TPU v7x, 256 devices: a whole 4x4x8 slice. The times are simulated.
256 devices in a mesh: sub: 16 (over z_hi, x, core), tile: 16 (over y, z_lo).
Axes of the slice: x: 4, y: 4, z: 8 (z_hi: 2, z_lo: 4; z = z_hi * 4 + z_lo), core: 2. Of those that a mesh axis runs over, the one named last changes fastest.
Arguments:
- echoes: bfloat16 [8192, 2, 8192], P(('sub', 'tile')), may hold values from -6 to 6
- chirp_ref: bfloat16 [2, 2048], replicated, may hold values from -0.09375 to 0.09375
- band_starts: int32 [32, 16], P('sub'), may hold values from 0 to 8064
- doppler_rates: float32 [16, 512], P('sub'), may hold values from -4096 to 4096
- slot_pulse: int32 [16, 2, 256], P('sub'), may hold values from 0 to 255, each once within a row
- interp_weights: bfloat16 [32, 2, 128, 64, 2048], P('sub', None, None, 'tile'), may hold values from -0.00390625 to 0.00390625
Outputs:
- sar_image: float32 [2, 64, 2048], P(None, 'tile', 'sub')
Inputs may be any that keep to these rules, and one draw needn't show every extreme that they name: `band_starts`: a band of 128 bins from each start lies inside the pulse of 8192 samples. `slot_pulse`: for each group and block, the 256 slots name each of the block's pulses once.
All inputs are finite; a program needn't handle non-finite values.
Results may differ from a plain program's by a relative error of at most 0.0037.
Values may be sent and summed in bfloat16 or wider, within the bound.
No kernel may reach another device: no remote copies, remote signals or barrier semaphores. Data moves between devices by JAX's collectives and lax.ppermute only.
A program may use at most 128 MiB of HBM per device.

v0:
```python
import jax
import jax.numpy as jnp
from jax import lax
from jax.sharding import PartitionSpec as P


def compress_pulses(echoes, chirp_ref):
    pulse_count = echoes.shape[0]
    pulse_len = echoes.shape[2]
    chirp_len = chirp_ref.shape[1]
    seg_len = min(chirp_len, 512)
    shifts = chirp_len // seg_len + 1
    seg_count = pulse_len // seg_len
    window_len = shifts * seg_len
    line_len = window_len + seg_len
    padded = jnp.concatenate([chirp_ref, jnp.zeros((2, line_len - chirp_len), jnp.bfloat16)], 1)
    tiled = jnp.tile(padded, (1, seg_len))[:, : seg_len * (line_len - 1)]
    toeplitz = tiled.reshape(2, seg_len, line_len - 1)[:, :, :window_len]
    table_real = toeplitz[0]
    table_imag = toeplitz[1]
    kernel_real = jnp.concatenate([table_real, table_imag], 1)
    kernel_imag = jnp.concatenate([-table_imag, table_real], 1)
    tail = jnp.zeros((pulse_count, shifts - 1, seg_len), jnp.bfloat16)
    part_real = jnp.concatenate([echoes[:, 0].reshape(pulse_count, seg_count, seg_len), tail], 1)
    part_imag = jnp.concatenate([echoes[:, 1].reshape(pulse_count, seg_count, seg_len), tail], 1)
    windows = jnp.concatenate(
        [part_real[:, step : step + seg_count] for step in range(shifts)]
        + [part_imag[:, step : step + seg_count] for step in range(shifts)],
        2,
    )
    dims = (((2,), (1,)), ((), ()))
    out_real = lax.dot_general(
        windows, kernel_real, dims, preferred_element_type=jnp.float32
    ).reshape(pulse_count, pulse_len)
    out_imag = lax.dot_general(
        windows, kernel_imag, dims, preferred_element_type=jnp.float32
    ).reshape(pulse_count, pulse_len)
    return jnp.stack([out_real.astype(jnp.bfloat16), out_imag.astype(jnp.bfloat16)], 1)


def phase_table(slot_ids, rate_row, col_pos):
    block_len = rate_row.shape[0]
    matches = slot_ids[:, None] == jnp.arange(block_len, dtype=jnp.int32)[None, :]
    pulse_rate = jnp.sum(jnp.where(matches, rate_row[None, :], 0.0), 1)
    angles = pulse_rate[:, None] * col_pos[None, :]
    return jnp.concatenate(
        [jnp.cos(angles).astype(jnp.bfloat16), jnp.sin(angles).astype(jnp.bfloat16)], 1
    )


def accumulate(band_rows, factors, band_len, col_count):
    product = lax.dot_general(
        band_rows, factors, (((0,), (0,)), ((), ())), preferred_element_type=jnp.float32
    )
    acc_real = product[:band_len, :col_count] - product[band_len:, col_count:]
    acc_imag = product[:band_len, col_count:] + product[band_len:, :col_count]
    return (acc_real, acc_imag)


def shards(echoes, chirp_ref, band_starts, doppler_rates, slot_pulse, interp_weights):
    pulse_len = echoes.shape[2]
    compressed = compress_pulses(echoes, chirp_ref)
    block_count = interp_weights.shape[0]
    band_len = interp_weights.shape[2]
    row_count = interp_weights.shape[3]
    col_count = interp_weights.shape[4]
    block_len = slot_pulse.shape[2]
    compressed = compressed.reshape(block_count, -1, 2, pulse_len)
    my_tile = lax.axis_index("tile")
    col_pos = (jnp.arange(col_count, dtype=jnp.float32) + 0.5) / col_count - 0.5
    empty = jnp.zeros((band_len, col_count), jnp.float32)
    focused_list = []
    for block in range(block_count):
        offset = band_starts[block, my_tile]
        slot_all = slot_pulse[0, block]
        rate_row = doppler_rates[0, block * block_len : (block + 1) * block_len]

        def fold_piece(running, pieces, first, offset=offset, slot_all=slot_all, rate_row=rate_row):
            count = pieces.shape[0]
            band_cut = lax.dynamic_slice_in_dim(pieces, offset, band_len, 2).reshape(
                count, 2 * band_len
            )
            return accumulate(
                band_cut, phase_table(slot_all, rate_row, col_pos), band_len, col_count
            )

        focused_list.append(
            fold_piece(
                (empty, empty),
                lax.all_gather(compressed[block], "tile", axis=0, tiled=True),
                jnp.int32(0),
            )
        )
    image_real = jnp.zeros((row_count, col_count), jnp.float32)
    image_imag = jnp.zeros((row_count, col_count), jnp.float32)
    for block in range(block_count):
        acc_real, acc_imag = focused_list[block]
        weight_real = interp_weights[block, 0].astype(jnp.float32)
        weight_imag = interp_weights[block, 1].astype(jnp.float32)
        image_real = image_real + jnp.sum(
            weight_real * acc_real[:, None, :] - weight_imag * acc_imag[:, None, :], 0
        )
        image_imag = image_imag + jnp.sum(
            weight_real * acc_imag[:, None, :] + weight_imag * acc_real[:, None, :], 0
        )
    partial_image = jnp.stack([image_real, image_imag])
    summed = lax.psum(partial_image, "sub")
    col_width = col_count // lax.axis_size("sub")
    return lax.dynamic_slice_in_dim(summed, lax.axis_index("sub") * col_width, col_width, 2)


def solution(mesh):
    in_specs = (
        P(("sub", "tile"), None, None),
        P(),
        P("sub", None),
        P("sub", None),
        P("sub", None, None),
        P("sub", None, None, "tile", None),
    )
    out_specs = P(None, "tile", "sub")
    return jax.shard_map(shards, mesh=mesh, in_specs=in_specs, out_specs=out_specs, check_vma=False)
```

profile of v0, /device:TPU:1, one launch (start us, length us, event | category | flops | bytes accessed | tf_op | source)
XLA Modules:
  0.0 659.5 jit_solution(4466715416030246036)
XLA Ops:
  6.5 0.0 all-gather.3.cloned.1.call-start
  6.5 0.7 concatenate.27
  7.2 0.8 broadcast_bitcast_fusion
  8.0 28.5 %copy.23 = bf16[1,2,512,3072]{3,1,2,0:T(2,128)(2,1)S(1)} copy(bf16[1,2,512,3072]{3,2,1,0:T(8,128)(2,1)S(1)} %broadcast_bitcast_fusion) | data formatting | bytes 12582912
  36.5 5.4 slice.129
  41.9 9.4 %reshape.99 = bf16[3144704]{0:T(1024)(128)(2,1)} reshape(bf16[2,1572352]{1,0:T(2,128)(2,1)} %slice.129) | data formatting | bytes 12578816
  51.3 15.1 %reshape.88 = bf16[2,512,3071]{2,1,0:T(8,128)(2,1)} reshape(bf16[3144704]{0:T(1024)(128)(2,1)} %reshape.99) | data formatting | bytes 12578816 | tf_op jit(solution)/shard_map/reshape | solution.py:18
  66.4 2.9 slice_bitcast_fusion.1
  69.3 0.0 copy-start
  69.3 3.5 fusion.40
  72.9 0.0 copy-done
  72.9 4.7 slice_reduce_fusion
  77.6 0.2 copy.21
  77.7 0.1 constant_dynamic-update-slice_fusion.1
  77.8 0.2 fusion.28
  78.0 0.2 fusion.29
  78.1 0.2 fusion.30
  78.3 0.2 fusion.31
  78.5 0.2 copy.22
  78.6 0.1 constant_dynamic-update-slice_fusion
  78.7 0.2 fusion.32
  78.9 0.2 fusion.33
  79.0 0.2 fusion.34
  79.2 0.2 fusion.35
  79.4 0.0 copy-start.2
  79.4 2.3 copy-done.2
  81.7 3.7 fusion.27
  85.4 1.3 convert_element_type.65
  86.7 0.8 constant_dynamic-update-slice_fusion.3
  87.5 6.2 fusion.26
  93.7 0.0 copy-start.5
  93.8 0.0 copy-start.3
  93.8 0.0 copy-start.4
  93.8 0.2 convert_element_type.67
  94.0 0.8 constant_dynamic-update-slice_fusion.2
  94.9 1.3 fusion.41
  96.2 1.4 copy.17
  97.5 0.0 all-gather.3.cloned.1.call-update
  97.5 0.0 all-gather.5.cloned.1.call-start
  97.6 1.4 copy.19
  99.0 0.0 all-gather.5.cloned.1.call-update
  99.0 0.0 all-reduce.5.cloned.1.call-start
  99.0 0.0 copy-done.5
  99.0 0.6 constant_dynamic-slice_fusion.3
  103.3 0.0 copy-done.3
  103.3 0.0 copy-done.4
  103.3 0.2 select_reduce_fusion
  103.6 16.2 %fusion.14 = (bf16[256,2048]{1,0:T(8,128)(2,1)S(1)}, bf16[256,2048]{1,0:T(8,128)(2,1)}, bf16[256,2048]{1,0:T(8,128)(2,1)S(1)}, bf16[256,2048]{1,0:T(8,128)(2,1)S(1)}) fusion(f32[2048]{0:T(1024)S(1)} %multiply_add_fusion, f32[256]{0:T(256)S(1)} %get-tuple-element.34, f32[256]{0:T(256)S(1)} %get-tuple-element.33), kind=kLoop, calls=%fused_computation.31 | loop fusion | flops 3145728 | bytes 4204544 | tf_op jit(solution)/shard_map/convert_element_type | solution.py:47
  119.8 169.7 %all-gather.3.cloned.1.call-done = bf16[256,2,8192]{2,1,0:T(2,128)(2,1)} async-done(((bf16[16,2,8192]{2,1,0:T(2,128)(2,1)}), bf16[256,2,8192]{2,1,0:T(2,128)(2,1)}) %all-gather.3.cloned.1.call-update) | async-done | bytes 8388624 | tf_op jit(solution)/shard_map/all_gather | solution.py:90
  289.5 1.2 constant_dynamic-slice_fusion.2
  290.7 0.1 copy.18
  290.8 1.9 fusion.18
  292.7 1.3 slice_add_fusion.1
  294.1 182.3 %all-gather.5.cloned.1.call-done = bf16[256,2,8192]{2,1,0:T(2,128)(2,1)} async-done(((bf16[16,2,8192]{2,1,0:T(2,128)(2,1)}), bf16[256,2,8192]{2,1,0:T(2,128)(2,1)}) %all-gather.5.cloned.1.call-update) | async-done | bytes 8388624 | tf_op jit(solution)/shard_map/all_gather | solution.py:90
  476.3 1.2 constant_dynamic-slice_fusion.1
  477.5 0.1 copy.20
  477.6 0.7 fusion.22
  478.3 0.3 slice_subtract_fusion
  478.7 0.9 copy-done.1
  479.6 8.9 %fusion.11 = (f32[4,2048]{1,0:T(4,128)S(1)}, f32[4,2048]{1,0:T(4,128)S(1)}, f32[4,2048]{1,0:T(4,128)S(1)}, f32[4,2048]{1,0:T(4,128)S(1)}) fusion(f32[128,2048]{1,0:T(8,128)S(1)} %get-tuple-element.18, f32[128,2048]{1,0:T(8,128)S(1)} %get-tuple-element.17, bf16[2,2,128,4,2048]{4,3,2,1,0:T(4,128)(2,1)} %param.11, f32[128,2048]{1,0:T(8,128)S(1)} %copy-done.1, ...), kind=kLoop, calls=%fused_computation.21 | loop fusion | flops 20938752 | bytes 12713984 | tf_op jit(solution)/shard_map/reduce_sum | solution.py:100
  488.5 0.6 pad_maximum_fusion
  489.1 0.0 all-reduce.5.cloned.1.call-update
  489.1 162.6 %all-reduce.5.cloned.1.call-done = f32[2,4,2048]{2,1,0:T(4,128)} async-done(((f32[2,4,2048]{2,1,0:T(4,128)}), f32[2,4,2048]{2,1,0:T(4,128)}) %all-reduce.5.cloned.1.call-update) | async-done | bytes 65552 | tf_op jit(solution)/shard_map/psum | solution.py:107
  651.7 1.3 constant_dynamic-slice_fusion
  (6 shorter events, 0.0 us)
Async XLA Ops:
  6.5 283.0 %all-gather.3.cloned.1.call-start = ((), (), s32[]{:S(2)}) async-start(), calls=%async_computation | async-start | bytes 8912896 | tf_op jit(solution)/shard_map/all_gather | solution.py:90
  69.3 3.6 copy-start
  79.4 2.3 copy-start.2
  93.7 5.3 copy-start.5
  93.8 9.5 %copy-start.3 = (f32[1,512]{1,0:T(1,128)S(1)}, f32[1,512]{1,0:T(1,128)}, u32[]{:S(2)}) copy-start(f32[1,512]{1,0:T(1,128)} %param.9) | copy-start | bytes 6148
  93.8 9.5 %copy-start.4 = (s32[1,2,256]{2,1,0:T(2,128)S(1)}, s32[1,2,256]{2,1,0:T(2,128)}, u32[]{:S(2)}) copy-start(s32[1,2,256]{2,1,0:T(2,128)} %param.10) | copy-start | bytes 6148
  97.5 378.8 %all-gather.5.cloned.1.call-start = ((), (), s32[]{:S(2)}) async-start(), calls=%async_computation.1 | async-start | bytes 8912896 | tf_op jit(solution)/shard_map/all_gather | solution.py:90
  99.0 552.7 %all-reduce.5.cloned.1.call-start = ((), (), s32[]{:S(2)}) async-start(), calls=%async_computation.2 | async-start | bytes 131072 | tf_op jit(solution)/shard_map/psum | solution.py:107
  478.3 1.2 copy-start.1
Sparse Core Ops, SparseCore 0:
  97.7 191.7 all-gather.2
  291.3 184.9 all-gather.4
  489.2 162.4 all-reduce.4
where the time goes:
time: 661 us; the launch traced here: 659 us
  waiting for transfers between devices  515 us (78%)
  local copies, waits for them, and re-layouts  84 us (13%)
  other arithmetic  31.2 us (5%)
  between operations  17 us (3%)
  matrix products  12.6 us (2%)
    all_gather x2, waiting for transfers between devices, shards(): lax.all_gather(compressed[block], 'tile', axis=0, tiled=True)  352 us
    psum x1, waiting for transfers between devices, shards(): summed = lax.psum(partial_image, 'sub')  163 us
    unnamed x31, local copies, waits for them, and re-layouts  47.2 us
    convert_element_type x1, other arithmetic, phase_table(): jnp.cos(angles).astype(jnp.bfloat16)  16.2 us
    reshape x1, local copies, waits for them, and re-layouts, compress_pulses(): toeplitz = tiled.reshape(2, seg_len, line_len - 1)[:, :, :window_len]  15.1 us
  transfers between devices with their start and end apart: 3, of which 3 were waited for; matrix products, arithmetic and copies ran while one was open for 3% of the time, Pallas kernels for 0%

commit v1 on v0

v1 whole, which is shorter than its diff:
```python
import functools

import jax
import jax.numpy as jnp
import numpy as np
from jax import lax
from jax.experimental import pallas as pl
from jax.experimental.pallas import tpu as pltpu
from jax.sharding import PartitionSpec as P

LANES = 128
VMEM_LIMIT = 40 * 1024 * 1024


def compress_kernel(starts_ref, chirp_ref, samples_ref, bands_ref, lhs_ref, toeplitz_ref, product_ref):
    span = toeplitz_ref.shape[1]
    blocks, tiles = starts_ref.shape
    rows = samples_ref.shape[1] // blocks
    half = rows // 2
    chunks = span // LANES
    chirp = chirp_ref[...].astype(jnp.float32)
    pad = jnp.zeros((1, span - chirp.shape[1]), jnp.float32)
    for part in range(2):
        line = jnp.concatenate([chirp[part : part + 1], pad], 1)
        shifted = pltpu.roll(
            jnp.broadcast_to(line, (LANES, span)), 0, 1, stride=1, stride_axis=0
        ).astype(jnp.bfloat16)
        base = part * 2 * LANES
        toeplitz_ref[base : base + LANES, :] = shifted
        toeplitz_ref[base + LANES : base + 2 * LANES, :LANES] = jnp.zeros((LANES, LANES), jnp.bfloat16)
        toeplitz_ref[base + LANES : base + 2 * LANES, LANES:] = shifted[:, : span - LANES]
    for block in range(blocks):
        for tile in range(tiles):
            first = starts_ref[block, tile] // LANES
            place = (block * tiles + tile) * rows
            for chunk in range(chunks):
                lhs_ref[place : place + rows, chunk * LANES : (chunk + 1) * LANES] = samples_ref[
                    first + chunk, block * rows : (block + 1) * rows, :
                ]
    product_ref[...] = lax.dot_general(
        lhs_ref[...], toeplitz_ref[...], (((1,), (1,)), ((), ())), preferred_element_type=jnp.float32
    )
    lane = lax.broadcasted_iota(jnp.int32, (half, LANES), 1)
    for block in range(blocks):
        for tile in range(tiles):
            place = (block * tiles + tile) * rows
            shift = starts_ref[block, tile] % LANES
            turn = (LANES - shift) % LANES
            keep = lane < LANES - shift

            def piece(part, column):
                top = place + part * half
                low = product_ref[top : top + half, column * 2 * LANES : column * 2 * LANES + LANES]
                high = product_ref[top : top + half, column * 2 * LANES + LANES : (column + 1) * 2 * LANES]
                return low, high

            rr, ri = piece(0, 0), piece(0, 1)
            ir, ii = piece(1, 0), piece(1, 1)
            for part, (low, high) in enumerate(
                ((rr[0] + ii[0], rr[1] + ii[1]), (ir[0] - ri[0], ir[1] - ri[1]))
            ):
                cut = jnp.where(keep, pltpu.roll(low, turn, 1), pltpu.roll(high, turn, 1))
                top = block * rows + part * half
                bands_ref[tile, top : top + half, :] = cut.astype(jnp.bfloat16)


def sine_cosine(angle):
    turns = jnp.round(angle * np.float32(2 / np.pi))
    rest = (angle - turns * np.float32(1.5703125)) - turns * np.float32(np.pi / 2 - 1.5703125)
    quarter = turns.astype(jnp.int32)
    sq = rest * rest
    sine = np.float32(1 / 362880) * sq + np.float32(-1 / 5040)
    sine = sine * sq + np.float32(1 / 120)
    sine = sine * sq + np.float32(-1 / 6)
    sine = sine * sq * rest + rest
    cosine = np.float32(1 / 40320) * sq + np.float32(-1 / 720)
    cosine = cosine * sq + np.float32(1 / 24)
    cosine = cosine * sq + np.float32(-1 / 2)
    cosine = cosine * sq + np.float32(1)
    odd = (quarter & 1) == 1
    sin_out = jnp.where(odd, cosine, sine)
    cos_out = jnp.where(odd, sine, cosine)
    sin_out = jnp.where((quarter & 2) == 2, -sin_out, sin_out)
    cos_out = jnp.where(((quarter + 1) & 2) == 2, -cos_out, cos_out)
    return sin_out, cos_out


def phase_kernel(rates_ref, slots_ref, table_ref):
    blocks, count = slots_ref.shape
    columns = table_ref.shape[2]
    row = lax.broadcasted_iota(jnp.int32, (count, count), 0)
    col = lax.broadcasted_iota(jnp.int32, (count, count), 1)
    lane = lax.broadcasted_iota(jnp.int32, (count, LANES), 1).astype(jnp.float32)
    place = (lane + 0.5) * np.float32(1 / columns) - 0.5
    for block in range(blocks):
        slots = slots_ref[block : block + 1, :].astype(jnp.float32)
        slot = jnp.sum(jnp.where(row == col, slots, 0.0), 1, keepdims=True)
        rates = rates_ref[:, block * count : (block + 1) * count]
        rate = jnp.sum(jnp.where(slot == col.astype(jnp.float32), rates, 0.0), 1, keepdims=True)
        rate = jnp.broadcast_to(rate, (count, LANES))
        for group in range(count // 32):
            span = slice(group * 32, group * 32 + 32)
            sine, cosine = sine_cosine(rate[span] * place[span])
            step_sine, step_cosine = sine_cosine(rate[span] * np.float32(LANES / columns))
            for chunk in range(columns // LANES):
                if chunk > 0:
                    sine, cosine = (
                        sine * step_cosine + cosine * step_sine,
                        cosine * step_cosine - sine * step_sine,
                    )
                lanes = slice(chunk * LANES, (chunk + 1) * LANES)
                table_ref[block, group * 32 : group * 32 + 32, lanes] = cosine.astype(jnp.bfloat16)
                table_ref[block, count + group * 32 : count + group * 32 + 32, lanes] = sine.astype(
                    jnp.bfloat16
                )


def image_kernel(bands_ref, table_ref, weights_ref, image_ref, focused_ref):
    blocks = table_ref.shape[0]
    sources, band_rows, band = bands_ref.shape
    rows = band_rows // blocks
    half = rows // 2
    count = sources * half
    columns = table_ref.shape[2]
    groups = columns // (4 * LANES)
    upper = lax.broadcasted_iota(jnp.int32, (8, LANES), 0) < 4
    zero = jnp.zeros((8, LANES), jnp.float32)
    image_rows = [[zero, zero, zero, zero] for _ in range(groups)]
    for block in range(blocks):
        real = bands_ref[:, block * rows : block * rows + half, :].reshape(count, band)
        imag = bands_ref[:, block * rows + half : (block + 1) * rows, :].reshape(count, band)
        top = jnp.concatenate([real, imag], 1)
        bottom = jnp.concatenate([-imag, real], 1)
        left = jnp.concatenate([top, bottom], 0)
        for group in range(groups):
            focused_ref[...] = lax.dot_general(
                left,
                table_ref[block, :, group * 4 * LANES : (group + 1) * 4 * LANES],
                (((0,), (0,)), ((), ())),
                preferred_element_type=jnp.float32,
            ).reshape(focused_ref.shape)

            def step(outer, sums):
                sums = list(sums)
                for inner in range(8):
                    k = outer * 8 + inner
                    weight_real = weights_ref[
                        block * 2 * band + k, group * 16 : group * 16 + 16, :
                    ].astype(jnp.float32)
                    weight_imag = weights_ref[
                        block * 2 * band + band + k, group * 16 : group * 16 + 16, :
                    ].astype(jnp.float32)
                    for pair in range(2):
                        wr = weight_real[pair * 8 : pair * 8 + 8]
                        wi = weight_imag[pair * 8 : pair * 8 + 8]

                        def value(row):
                            parts = [
                                jnp.broadcast_to(
                                    focused_ref[
                                        row,
                                        inner : inner + 1,
                                        (2 * pair + side) * LANES : (2 * pair + side + 1) * LANES,
                                    ],
                                    (8, LANES),
                                )
                                for side in range(2)
                            ]
                            return jnp.where(upper, parts[0], parts[1])

                        fr = value(outer)
                        fi = value(band // 8 + outer)
                        sums[2 * pair] = sums[2 * pair] + (wr * fr - wi * fi)
                        sums[2 * pair + 1] = sums[2 * pair + 1] + (wr * fi + wi * fr)
                return tuple(sums)

            image_rows[group] = list(
                lax.fori_loop(0, band // 8, step, tuple(image_rows[group]))
            )
    for group in range(groups):
        for pair in range(2):
            real, imag = image_rows[group][2 * pair], image_rows[group][2 * pair + 1]
            chunk = group * 4 + 2 * pair
            image_ref[chunk] = jnp.concatenate([real[:4], imag[:4]], 0)
            image_ref[chunk + 1] = jnp.concatenate([real[4:], imag[4:]], 0)


def vmem():
    return pl.BlockSpec(memory_space=pltpu.VMEM)


def partial_image(echoes, chirp_ref, band_starts, doppler_rates, slot_pulse, interp_weights):
    pulses, _, pulse_len = echoes.shape
    chirp_len = chirp_ref.shape[1]
    blocks, tiles = band_starts.shape
    _, _, band, image_rows, columns = interp_weights.shape
    count = slot_pulse.shape[2]
    chunks = pulse_len // LANES
    span = chirp_len + 2 * LANES
    params = pltpu.CompilerParams(vmem_limit_bytes=VMEM_LIMIT)
    half = pulses // blocks
    samples = echoes.reshape(blocks, half, 2, chunks, LANES).transpose(3, 0, 2, 1, 4)
    samples = samples.reshape(chunks, 2 * pulses, LANES)
    samples = jnp.pad(samples, ((0, span // LANES - 1), (0, 0), (0, 0)))
    bands = pl.pallas_call(
        compress_kernel,
        out_shape=jax.ShapeDtypeStruct((tiles, 2 * pulses, band), jnp.bfloat16),
        in_specs=[pl.BlockSpec(memory_space=pltpu.SMEM), vmem(), vmem()],
        out_specs=vmem(),
        scratch_shapes=[
            pltpu.VMEM((blocks * tiles * 2 * half, span), jnp.bfloat16),
            pltpu.VMEM((4 * LANES, span), jnp.bfloat16),
            pltpu.VMEM((blocks * tiles * 2 * half, 4 * LANES), jnp.float32),
        ],
        compiler_params=params,
        name="compress",
    )(band_starts, chirp_ref, samples)
    bands = lax.all_to_all(bands, "tile", 0, 0, tiled=True)
    table = pl.pallas_call(
        phase_kernel,
        out_shape=jax.ShapeDtypeStruct((blocks, 2 * count, columns), jnp.bfloat16),
        in_specs=[vmem(), vmem()],
        out_specs=vmem(),
        compiler_params=params,
        name="phase",
    )(doppler_rates, slot_pulse.reshape(blocks, count))
    weights = interp_weights.reshape(blocks, 2, band, image_rows, columns // LANES, LANES)
    weights = weights.transpose(0, 1, 2, 4, 3, 5).reshape(
        blocks * 2 * band, columns // LANES * image_rows, LANES
    )
    image = pl.pallas_call(
        image_kernel,
        out_shape=jax.ShapeDtypeStruct((columns // LANES, 2 * image_rows, LANES), jnp.float32),
        in_specs=[vmem(), vmem(), vmem()],
        out_specs=vmem(),
        scratch_shapes=[pltpu.VMEM((2 * band // 8, 8, 4 * LANES), jnp.float32)],
        compiler_params=params,
        name="image",
    )(bands, table, weights)
    return image


def shards(*args):
    image = partial_image(*args)
    pieces = lax.all_to_all(image, "sub", 0, 0, tiled=True)
    return jnp.sum(pieces, 0).reshape(2, -1, LANES)


def solution(mesh):
    in_specs = (
        P(("sub", "tile"), None, None),
        P(),
        P("sub", None),
        P("sub", None),
        P("sub", None, None),
        P("sub", None, None, "tile", None),
    )
    out_specs = P(None, "tile", "sub")
    return jax.shard_map(shards, mesh=mesh, in_specs=in_specs, out_specs=out_specs, check_vma=False)
```

time: 661 us -> 58.9 us (0.09)
  waiting for transfers between devices: 515 us -> 5.84 us
  local copies, waits for them, and re-layouts: 84 us -> 10.3 us
  other arithmetic: 31.2 us -> 0.61 us
  blocking collectives: 0 us -> 19.9 us
  between operations: 17 us -> 0.1 us
  Pallas kernels: 0 us -> 12.7 us
  matrix products: 12.6 us -> 0 us
  starting transfers between devices: 0.09 us -> 9.19 us
    all_gather x2 -> x0, waiting for transfers between devices: 352 us -> none  [shards(): lax.all_gather(compressed[block], 'tile', axis=0, tiled=True)]
    psum x1 -> x0, waiting for transfers between devices: 163 us -> none  [shards(): summed = lax.psum(partial_image, 'sub')]
    unnamed x31 -> x14, local copies, waits for them, and re-layouts: 47.2 us -> 7.52 us
    all_to_all x0 -> x1, blocking collectives: none -> 19.9 us  [shards(): pieces = lax.all_to_all(image, 'sub', 0, 0, tiled=True)]
    convert_element_type x1 -> x0, other arithmetic: 16.2 us -> none  [phase_table(): jnp.cos(angles).astype(jnp.bfloat16)]
    pallas_call x0 -> x3, Pallas kernels: none -> 12.7 us  [the longest x1 6.48 us: partial_image(): pl.pallas_call(image_kernel, out_shape=jax.ShapeDtypeStruct((columns // L...]
    dot_general x4 -> x0, matrix products: 12.6 us -> none  [the longest x1 6.2 us: compress_pulses(): lax.dot_general(windows, kernel_imag, dims, preferred_element_type=jnp.fl...]
    reshape x1 -> x2, local copies, waits for them, and re-layouts: 15.1 us -> 2.57 us  [partial_image(): echoes.reshape(blocks, half, 2, chunks, LANES).transpose(3, 0, 2, 1, 4)]
  transfers between devices with their start and end apart: 3 -> 1, of which waited for: 3 -> 1; matrix products, arithmetic and copies ran while one was open for 3% -> 0% of each run, Pallas kernels for 0% -> 3%
where the time goes in v1:
time: 58.9 us; the launch traced here: 58.6 us
  blocking collectives  19.9 us (34%)
  Pallas kernels  12.7 us (22%)
  local copies, waits for them, and re-layouts  10.3 us (17%)
  starting transfers between devices  9.19 us (16%)
  waiting for transfers between devices  5.84 us (10%)
  other arithmetic  0.61 us (1%)
    all_to_all x1, blocking collectives, shards(): pieces = lax.all_to_all(image, 'sub', 0, 0, tiled=True)  19.9 us
    all_to_all x1, starting transfers between devices, partial_image(): bands = lax.all_to_all(bands, 'tile', 0, 0, tiled=True)  9.19 us
    unnamed x14, local copies, waits for them, and re-layouts  7.52 us
    pallas_call x1, Pallas kernels, partial_image(): pl.pallas_call(image_kernel, out_shape=jax.ShapeDtypeStruct((columns // L...  6.48 us
    all_to_all x1, waiting for transfers between devices, partial_image(): bands = lax.all_to_all(bands, 'tile', 0, 0, tiled=True)  5.84 us
    pallas_call x1, Pallas kernels, partial_image(): pl.pallas_call(compress_kernel, out_shape=jax.ShapeDtypeStruct((tiles, 2...  4.33 us
    reshape x2, local copies, waits for them, and re-layouts, partial_image(): echoes.reshape(blocks, half, 2, chunks, LANES).transpose(3, 0, 2, 1, 4)  2.57 us
    pallas_call x1, Pallas kernels, partial_image(): pl.pallas_call(phase_kernel, out_shape=jax.ShapeDtypeStruct((blocks, 2 *...  1.88 us
  transfers between devices with their start and end apart: 1, of which 1 were waited for; matrix products, arithmetic and copies ran while one was open for 0% of the time, Pallas kernels for 3%

profile of v1, /device:TPU:1, one launch (start us, length us, event | category | flops | bytes accessed | tf_op | source)
XLA Modules:
  0.0 58.6 jit_solution(13774370818426076684)
XLA Ops:
  0.0 0.0 copy-start.6
  0.0 0.0 copy-start.3
  0.0 0.0 copy-start.5
  0.0 0.0 copy-start.4
  0.0 1.9 %reshape.18 = bf16[2,16,2,64,128]{4,3,2,1,0:T(8,128)(2,1)S(1)} reshape(bf16[32,2,8192]{2,1,0:T(2,128)(2,1)} %param.6) | data formatting | bytes 2097152 | tf_op jit(solution)/shard_map/reshape | solution.py:202
  1.9 0.7 %copy.7 = bf16[2,16,2,64,128]{4,1,2,0,3:T(8,128)(2,1)S(1)} copy(bf16[2,16,2,64,128]{4,3,2,1,0:T(8,128)(2,1)S(1)} %reshape.18) | data formatting | bytes 2097152 | tf_op jit(solution)/shard_map/reshape | solution.py:202
  2.6 0.2 pad.4.samples_ref
  2.8 0.0 copy-done.6
  2.8 0.0 copy-done.3
  2.8 4.3 %compress.1 = bf16[16,64,128]{2,1,0:T(8,128)(2,1)} custom-call(s32[2,16]{1,0:T(2,128)S(1)} %copy-done.6, bf16[2,2048]{1,0:T(2,128)(2,1)S(1)} %copy-done.3, bf16[81,64,128]{2,1,0:T(8,128)(2,1)S(1)} %pad.4.samples_ref), custom_call_target="tpu_custom_call" | custom-call | tf_op jit(solution)/shard_map/compress/pallas_call | solution.py:205
  7.2 9.2 %all-to-all-start = ((bf16[16,64,128]{2,1,0:T(8,128)(2,1)}), bf16[16,64,128]{2,1,0:T(8,128)(2,1)S(1)}, u32[]{:S(2)}, u32[]{:S(2)}) async-start(bf16[16,64,128]{2,1,0:T(8,128)(2,1)} %compress.1), calls=%async_computation | async-start | bytes 524288 | tf_op jit(solution)/shard_map/all_to_all | solution.py:218
  16.3 0.0 copy-done.5
  16.4 0.0 copy-done.4
  16.4 1.9 %phase.1.table_ref = bf16[2,512,2048]{2,1,0:T(8,128)(2,1)S(1)} custom-call(f32[1,512]{1,0:T(1,128)S(1)} %copy-done.4, s32[2,256]{1,0:T(2,128)S(1)} %bitcast.11), custom_call_target="tpu_custom_call" | custom-call | tf_op jit(solution)/shard_map/phase/pallas_call | solution.py:219
  18.3 0.0 copy-start
  18.3 1.9 %copy-done = bf16[2,512,2048]{2,1,0:T(8,128)(2,1)} copy-done((bf16[2,512,2048]{2,1,0:T(8,128)(2,1)}, bf16[2,512,2048]{2,1,0:T(8,128)(2,1)S(1)}, u32[]{:S(2)}) %copy-start) | copy-done | bytes 4194328
  20.2 5.8 %all-to-all-done.bands_ref = bf16[16,64,128]{2,1,0:T(8,128)(2,1)S(1)} async-done(((bf16[16,64,128]{2,1,0:T(8,128)(2,1)}), bf16[16,64,128]{2,1,0:T(8,128)(2,1)S(1)}, u32[]{:S(2)}, u32[]{:S(2)}) %all-to-all-start) | async-done | bytes 262176 | tf_op jit(solution)/shard_map/all_to_all | solution.py:218
  26.0 0.0 copy-start.1
  26.0 2.2 %copy-done.1 = bf16[2,512,2048]{2,1,0:T(8,128)(2,1)S(1)} copy-done((bf16[2,512,2048]{2,1,0:T(8,128)(2,1)S(1)}, bf16[2,512,2048]{2,1,0:T(8,128)(2,1)}, u32[]{:S(2)}) %copy-start.1) | copy-done | bytes 4194328
  28.2 0.0 copy-start.2
  28.2 3.4 %copy-done.2 = bf16[2,2,128,4,2048]{4,3,2,1,0:T(4,128)(2,1)S(1)} copy-done((bf16[2,2,128,4,2048]{4,3,2,1,0:T(4,128)(2,1)S(1)}, bf16[2,2,128,4,2048]{4,3,2,1,0:T(4,128)(2,1)}, u32[]{:S(2)}) %copy-start.2) | copy-done | bytes 8388632
  31.6 6.5 %image.1 = f32[16,8,128]{2,1,0:T(8,128)S(1)} custom-call(bf16[16,64,128]{2,1,0:T(8,128)(2,1)S(1)} %all-to-all-done.bands_ref, bf16[2,512,2048]{2,1,0:T(8,128)(2,1)S(1)} %copy-done.1, bf16[512,64,128]{2,1,0:T(8,128)(2,1)S(1)} %bitcast.10), custom_call_target="tpu_custom_call" | custom-call | tf_op jit(solution)/shard_map/image/pallas_call | solution.py:231
  38.1 19.9 %all_to_all.10 = f32[16,8,128]{2,1,0:T(8,128)S(1)} all-to-all(f32[16,8,128]{2,1,0:T(8,128)S(1)} %image.1), channel_id=1, replica_groups=mesh['sub'=16,'tile'=16] {'sub'}, dimensions={0} | all-to-all | bytes 131072 | tf_op jit(solution)/shard_map/all_to_all | solution.py:245
  58.0 0.6 %reduce_sum.9 = f32[8,128]{1,0:T(8,128)} reduce(f32[16,8,128]{2,1,0:T(8,128)S(1)} %all_to_all.10, f32[]{:T(128)} %constant.4.clone.1), dimensions={0}, to_apply=%region_0.1 | reduce | flops 15360 | bytes 69636 | tf_op jit(solution)/shard_map/reduce_sum | solution.py:246
Async XLA Ops:
  0.0 2.8 %copy-start.6 = (s32[2,16]{1,0:T(2,128)S(1)}, s32[2,16]{1,0:T(2,128)}, u32[]{:S(2)}) copy-start(s32[2,16]{1,0:T(2,128)} %starts_ref.1) | copy-start | bytes 388
  0.0 2.8 %copy-start.3 = (bf16[2,2048]{1,0:T(2,128)(2,1)S(1)}, bf16[2,2048]{1,0:T(2,128)(2,1)}, u32[]{:S(2)}) copy-start(bf16[2,2048]{1,0:T(2,128)(2,1)} %chirp_ref.1) | copy-start | bytes 24580
  0.0 16.3 %copy-start.5 = (s32[1,2,256]{2,1,0:T(2,128)S(1)}, s32[1,2,256]{2,1,0:T(2,128)}, u32[]{:S(2)}) copy-start(s32[1,2,256]{2,1,0:T(2,128)} %param.10) | copy-start | bytes 6148
  0.0 16.4 %copy-start.4 = (f32[1,512]{1,0:T(1,128)S(1)}, f32[1,512]{1,0:T(1,128)}, u32[]{:S(2)}) copy-start(f32[1,512]{1,0:T(1,128)} %rates_ref.1) | copy-start | bytes 6148
  7.2 18.9 %all-to-all-start = ((bf16[16,64,128]{2,1,0:T(8,128)(2,1)}), bf16[16,64,128]{2,1,0:T(8,128)(2,1)S(1)}, u32[]{:S(2)}, u32[]{:S(2)}) async-start(bf16[16,64,128]{2,1,0:T(8,128)(2,1)} %compress.1), calls=%async_computation | async-start | bytes 524288 | tf_op jit(solution)/shard_map/all_to_all | solution.py:218
  18.3 1.9 %copy-start = (bf16[2,512,2048]{2,1,0:T(8,128)(2,1)}, bf16[2,512,2048]{2,1,0:T(8,128)(2,1)S(1)}, u32[]{:S(2)}) copy-start(bf16[2,512,2048]{2,1,0:T(8,128)(2,1)S(1)} %phase.1.table_ref) | copy-start | bytes 12582916
  26.0 2.2 %copy-start.1 = (bf16[2,512,2048]{2,1,0:T(8,128)(2,1)S(1)}, bf16[2,512,2048]{2,1,0:T(8,128)(2,1)}, u32[]{:S(2)}) copy-start(bf16[2,512,2048]{2,1,0:T(8,128)(2,1)} %copy-done) | copy-start | bytes 12582916
  28.2 3.4 %copy-start.2 = (bf16[2,2,128,4,2048]{4,3,2,1,0:T(4,128)(2,1)S(1)}, bf16[2,2,128,4,2048]{4,3,2,1,0:T(4,128)(2,1)}, u32[]{:S(2)}) copy-start(bf16[2,2,128,4,2048]{4,3,2,1,0:T(4,128)(2,1)} %param.11) | copy-start | bytes 25165828

commit v2 on v1

v2 whole, which is shorter than its diff:
```python
import functools

import jax
import jax.numpy as jnp
import numpy as np
from jax import lax
from jax.experimental import pallas as pl
from jax.experimental.pallas import tpu as pltpu
from jax.sharding import PartitionSpec as P

LANES = 128
VMEM_LIMIT = 60 * 1024 * 1024


def compress_kernel(
    starts_ref, chirp_ref, echoes_ref, bands_ref, raw_ref, wide_ref, samples_ref, lhs_ref, toeplitz_ref, product_ref, sem
):
    fetch = pltpu.make_async_copy(echoes_ref, raw_ref, sem)
    fetch.start()
    span = toeplitz_ref.shape[1]
    blocks, tiles = starts_ref.shape
    pulses, lines, _ = raw_ref.shape
    half = pulses // blocks
    rows = 2 * half
    chunks = span // LANES
    chirp = chirp_ref[...].astype(jnp.float32)
    pad = jnp.zeros((1, span - chirp.shape[1]), jnp.float32)
    for part in range(2):
        line = jnp.concatenate([chirp[part : part + 1], pad], 1)
        shifted = pltpu.roll(
            jnp.broadcast_to(line, (LANES, span)), 0, 1, stride=1, stride_axis=0
        ).astype(jnp.bfloat16)
        base = part * 2 * LANES
        toeplitz_ref[base : base + LANES, :] = shifted
        toeplitz_ref[base + LANES : base + 2 * LANES, :LANES] = jnp.zeros((LANES, LANES), jnp.bfloat16)
        toeplitz_ref[base + LANES : base + 2 * LANES, LANES:] = shifted[:, : span - LANES]
    samples_ref[lines // 2 :] = jnp.zeros(
        (samples_ref.shape[0] - lines // 2, 2 * pulses, LANES), jnp.bfloat16
    )
    fetch.wait()
    wide_ref[...] = raw_ref[...].astype(jnp.float32).reshape(wide_ref.shape)
    for chunk in range(lines // 2):
        for block in range(blocks):
            for part in range(2):
                line = wide_ref[
                    pl.ds(block * half * lines + 2 * chunk + part, half, stride=lines), :
                ]
                top = block * rows + part * half
                samples_ref[chunk, top : top + half, :] = line.astype(jnp.bfloat16)
    for block in range(blocks):
        for tile in range(tiles):
            first = starts_ref[block, tile] // LANES
            place = (block * tiles + tile) * rows
            for chunk in range(chunks):
                lhs_ref[place : place + rows, chunk * LANES : (chunk + 1) * LANES] = samples_ref[
                    first + chunk, block * rows : (block + 1) * rows, :
                ]
    product_ref[...] = lax.dot_general(
        lhs_ref[...], toeplitz_ref[...], (((1,), (1,)), ((), ())), preferred_element_type=jnp.float32
    )
    lane = lax.broadcasted_iota(jnp.int32, (half, LANES), 1)
    for block in range(blocks):
        for tile in range(tiles):
            place = (block * tiles + tile) * rows
            shift = starts_ref[block, tile] % LANES
            turn = (LANES - shift) % LANES
            keep = lane < LANES - shift

            def piece(part, column):
                top = place + part * half
                low = product_ref[top : top + half, column * 2 * LANES : column * 2 * LANES + LANES]
                high = product_ref[top : top + half, column * 2 * LANES + LANES : (column + 1) * 2 * LANES]
                return low, high

            rr, ri = piece(0, 0), piece(0, 1)
            ir, ii = piece(1, 0), piece(1, 1)
            for part, (low, high) in enumerate(
                ((rr[0] + ii[0], rr[1] + ii[1]), (ir[0] - ri[0], ir[1] - ri[1]))
            ):
                cut = jnp.where(keep, pltpu.roll(low, turn, 1), pltpu.roll(high, turn, 1))
                top = block * rows + part * half
                bands_ref[tile, top : top + half, :] = cut.astype(jnp.bfloat16)


def sine_cosine(angle):
    turns = jnp.round(angle * np.float32(2 / np.pi))
    rest = (angle - turns * np.float32(1.5703125)) - turns * np.float32(np.pi / 2 - 1.5703125)
    quarter = turns.astype(jnp.int32)
    sq = rest * rest
    sine = np.float32(1 / 362880) * sq + np.float32(-1 / 5040)
    sine = sine * sq + np.float32(1 / 120)
    sine = sine * sq + np.float32(-1 / 6)
    sine = sine * sq * rest + rest
    cosine = np.float32(1 / 40320) * sq + np.float32(-1 / 720)
    cosine = cosine * sq + np.float32(1 / 24)
    cosine = cosine * sq + np.float32(-1 / 2)
    cosine = cosine * sq + np.float32(1)
    odd = (quarter & 1) == 1
    sin_out = jnp.where(odd, cosine, sine)
    cos_out = jnp.where(odd, sine, cosine)
    sin_out = jnp.where((quarter & 2) == 2, -sin_out, sin_out)
    cos_out = jnp.where(((quarter + 1) & 2) == 2, -cos_out, cos_out)
    return sin_out, cos_out


def phase_kernel(rates_ref, slots_ref, table_ref):
    count = slots_ref.shape[1]
    columns = table_ref.shape[2]
    block = pl.program_id(0)
    row = lax.broadcasted_iota(jnp.int32, (count, count), 0)
    col = lax.broadcasted_iota(jnp.int32, (count, count), 1)
    lane = lax.broadcasted_iota(jnp.int32, (count, LANES), 1).astype(jnp.float32)
    place = (lane + 0.5) * np.float32(1 / columns) - 0.5
    which = lax.broadcasted_iota(jnp.int32, slots_ref.shape, 0) == block
    slots = jnp.sum(jnp.where(which, slots_ref[...], 0), 0, keepdims=True).astype(jnp.float32)
    slot = jnp.sum(jnp.where(row == col, slots, 0.0), 1, keepdims=True)
    rates = rates_ref[...]
    rate = jnp.sum(jnp.where(slot == col.astype(jnp.float32), rates, 0.0), 1, keepdims=True)
    rate = jnp.broadcast_to(rate, (count, LANES))
    for group in range(count // 32):
        span = slice(group * 32, group * 32 + 32)
        sine, cosine = sine_cosine(rate[span] * place[span])
        step_sine, step_cosine = sine_cosine(rate[span] * np.float32(LANES / columns))
        for chunk in range(columns // LANES):
            if chunk > 0:
                sine, cosine = (
                    sine * step_cosine + cosine * step_sine,
                    cosine * step_cosine - sine * step_sine,
                )
            lanes = slice(chunk * LANES, (chunk + 1) * LANES)
            table_ref[0, group * 32 : group * 32 + 32, lanes] = cosine.astype(jnp.bfloat16)
            table_ref[0, count + group * 32 : count + group * 32 + 32, lanes] = sine.astype(
                jnp.bfloat16
            )


def image_kernel(me_ref, bands_ref, table_ref, weights_ref, *rest):
    *piece_refs, left_ref, focused_ref, image_ref = rest
    step_id = pl.program_id(0)
    blocks = table_ref.shape[0]
    sources, band_rows, band = bands_ref.shape
    rows = band_rows // blocks
    half = rows // 2
    count = sources * half

    @pl.when(step_id == 0)
    def _():
        for block in range(blocks):
            real = bands_ref[:, block * rows : block * rows + half, :].reshape(count, band)
            imag = bands_ref[:, block * rows + half : (block + 1) * rows, :].reshape(count, band)
            top = jnp.concatenate([real, imag], 1)
            bottom = jnp.concatenate([-imag, real], 1)
            left_ref[block] = jnp.concatenate([top, bottom], 0).T

    for block in range(blocks):
        focused_ref[block] = jnp.dot(
            left_ref[block], table_ref[block], preferred_element_type=jnp.float32
        ).reshape(focused_ref.shape[1:])
    upper = lax.broadcasted_iota(jnp.int32, (8, LANES), 0) < 4
    zero = jnp.zeros((8, LANES), jnp.float32)
    sums = (zero, zero)
    for block in range(blocks):

        def step(outer, sums):
            real, imag = sums
            for inner in range(8):
                k = outer * 8 + inner
                wr = weights_ref[block * 2 * band + k].astype(jnp.float32)
                wi = weights_ref[block * 2 * band + band + k].astype(jnp.float32)

                def value(row):
                    parts = [
                        jnp.broadcast_to(
                            focused_ref[
                                block, row, inner : inner + 1, side * LANES : (side + 1) * LANES
                            ],
                            (8, LANES),
                        )
                        for side in range(2)
                    ]
                    return jnp.where(upper, parts[0], parts[1])

                fr = value(outer)
                fi = value(band // 8 + outer)
                real = real + (wr * fr - wi * fi)
                imag = imag + (wr * fi + wi * fr)
            return real, imag

        sums = lax.fori_loop(0, band // 8, step, sums)
    real, imag = sums
    image_ref[2 * step_id] = jnp.concatenate([real[:4], imag[:4]], 0)
    image_ref[2 * step_id + 1] = jnp.concatenate([real[4:], imag[4:]], 0)

    @pl.when(step_id == pl.num_programs(0) - 1)
    def _():
        for index, piece_ref in enumerate(piece_refs):
            piece_ref[...] = image_ref[me_ref[0] ^ index]


def vmem():
    return pl.BlockSpec(memory_space=pltpu.VMEM)


def partial_image(echoes, chirp_ref, band_starts, doppler_rates, slot_pulse, interp_weights):
    pulses, _, pulse_len = echoes.shape
    chirp_len = chirp_ref.shape[1]
    blocks, tiles = band_starts.shape
    _, _, band, image_rows, columns = interp_weights.shape
    count = slot_pulse.shape[2]
    lines = 2 * pulse_len // LANES
    span = chirp_len + 2 * LANES
    places = columns // LANES
    params = pltpu.CompilerParams(vmem_limit_bytes=VMEM_LIMIT)
    samples = echoes.reshape(pulses, 2, pulse_len // LANES, LANES).transpose(0, 2, 1, 3)
    samples = samples.reshape(pulses, lines, LANES)
    bands = pl.pallas_call(
        compress_kernel,
        out_shape=jax.ShapeDtypeStruct((tiles, 2 * pulses, band), jnp.bfloat16),
        in_specs=[
            pl.BlockSpec(memory_space=pltpu.SMEM),
            vmem(),
            pl.BlockSpec(memory_space=pl.ANY),
        ],
        out_specs=vmem(),
        scratch_shapes=[
            pltpu.VMEM((pulses, lines, LANES), jnp.bfloat16),
            pltpu.VMEM((pulses * lines, LANES), jnp.float32),
            pltpu.VMEM((lines // 2 + span // LANES - 1, 2 * pulses, LANES), jnp.bfloat16),
            pltpu.VMEM((tiles * 2 * pulses, span), jnp.bfloat16),
            pltpu.VMEM((4 * LANES, span), jnp.bfloat16),
            pltpu.VMEM((tiles * 2 * pulses, 4 * LANES), jnp.float32),
            pltpu.SemaphoreType.DMA,
        ],
        compiler_params=params,
        name="compress",
    )(band_starts, chirp_ref, samples)
    bands = lax.all_to_all(bands, "tile", 0, 0, tiled=True)
    table = pl.pallas_call(
        phase_kernel,
        grid=(blocks,),
        out_shape=jax.ShapeDtypeStruct((blocks, 2 * count, columns), jnp.bfloat16),
        in_specs=[
            pl.BlockSpec((1, count), lambda i: (0, i)),
            pl.BlockSpec((blocks, count), lambda i: (0, 0)),
        ],
        out_specs=pl.BlockSpec((1, 2 * count, columns), lambda i: (i, 0, 0)),
        compiler_params=params,
        name="phase",
    )(doppler_rates, slot_pulse.reshape(blocks, count))
    weights = interp_weights.reshape(blocks, 2, band, image_rows, places, LANES)
    weights = weights.transpose(0, 1, 2, 4, 3, 5).reshape(
        blocks * 2 * band, places * image_rows, LANES
    )
    me = lax.axis_index("sub").astype(jnp.int32).reshape(1)
    return pl.pallas_call(
        image_kernel,
        grid=(places // 2,),
        out_shape=[jax.ShapeDtypeStruct((2 * image_rows, LANES), jnp.float32)] * places,
        in_specs=[
            pl.BlockSpec(memory_space=pltpu.SMEM),
            pl.BlockSpec((tiles, 2 * pulses, band), lambda i: (0, 0, 0)),
            pl.BlockSpec((blocks, 2 * count, 2 * LANES), lambda i: (0, 0, i)),
            pl.BlockSpec((blocks * 2 * band, 2 * image_rows, LANES), lambda i: (0, i, 0)),
        ],
        out_specs=[pl.BlockSpec((2 * image_rows, LANES), lambda i: (0, 0))] * places,
        scratch_shapes=[
            pltpu.VMEM((blocks, 2 * band, 2 * count), jnp.bfloat16),
            pltpu.VMEM((blocks, 2 * band // 8, 8, 2 * LANES), jnp.float32),
            pltpu.VMEM((places, 2 * image_rows, LANES), jnp.float32),
        ],
        compiler_params=params,
        name="image",
    )(me, bands, table, weights)


def shards(*args):
    pieces = partial_image(*args)
    size = len(pieces)
    total = pieces[0]
    for index in range(1, size):
        pairs = [(source, source ^ index) for source in range(size)]
        total = total + lax.ppermute(pieces[index], "sub", pairs)
    return total.reshape(2, -1, LANES)


def solution(mesh):
    in_specs = (
        P(("sub", "tile"), None, None),
        P(),
        P("sub", None),
        P("sub", None),
        P("sub", None, None),
        P("sub", None, None, "tile", None),
    )
    out_specs = P(None, "tile", "sub")
    return jax.shard_map(shards, mesh=mesh, in_specs=in_specs, out_specs=out_specs, check_vma=False)
```

time: 58.9 us -> 85.7 us (1.46)
  starting transfers between devices: 9.19 us -> 47.4 us
  blocking collectives: 19.9 us -> 0 us
  local copies, waits for them, and re-layouts: 10.3 us -> 0.71 us
  Pallas kernels: 12.7 us -> 22.2 us
  waiting for transfers between devices: 5.84 us -> 13.5 us
    ppermute x0 -> x15, starting transfers between devices: none -> 38.2 us  [shards(): total = total + lax.ppermute(pieces[index], 'sub', pairs)]
    all_to_all x1 -> x0, blocking collectives: 19.9 us -> none  [shards(): pieces = lax.all_to_all(image, 'sub', 0, 0, tiled=True)]
    ppermute x0 -> x15, waiting for transfers between devices: none -> 7.98 us  [shards(): total = total + lax.ppermute(pieces[index], 'sub', pairs)]
    pallas_call x2, Pallas kernels: 8.36 us -> 15.5 us  [the longest x1 11.3 us: partial_image(): pl.pallas_call(image_kernel, grid=(places // 2,), out_shape=[jax.ShapeDty...]
    unnamed x14 -> x2, local copies, waits for them, and re-layouts: 7.52 us -> 0.71 us
    reshape x2 -> x0, local copies, waits for them, and re-layouts: 2.57 us -> none  [partial_image(): echoes.reshape(blocks, half, 2, chunks, LANES).transpose(3, 0, 2, 1, 4)]
    pallas_call x1, Pallas kernels: 4.33 us -> 6.76 us  [partial_image(): pl.pallas_call(compress_kernel, out_shape=jax.ShapeDtypeStruct((tiles, 2...]
    add x0 -> x1, other arithmetic: none -> 1.3 us  [shards(): total = total + lax.ppermute(pieces[index], 'sub', pairs)]
  transfers between devices with their start and end apart: 1 -> 16, of which waited for: 1 -> 3; matrix products, arithmetic and copies ran while one was open for 0% -> 0% of each run, Pallas kernels for 3% -> 5%
where the time goes in v2:
time: 85.7 us; the launch traced here: 85.2 us
  starting transfers between devices  47.4 us (55%)
  Pallas kernels  22.2 us (26%)
  waiting for transfers between devices  13.5 us (16%)
  other arithmetic  1.3 us (2%)
    ppermute x15, starting transfers between devices, shards(): total = total + lax.ppermute(pieces[index], 'sub', pairs)  38.2 us
    pallas_call x1, Pallas kernels, partial_image(): pl.pallas_call(image_kernel, grid=(places // 2,), out_shape=[jax.ShapeDty...  11.3 us
    all_to_all x1, starting transfers between devices, partial_image(): bands = lax.all_to_all(bands, 'tile', 0, 0, tiled=True)  9.2 us
    ppermute x15, waiting for transfers between devices, shards(): total = total + lax.ppermute(pieces[index], 'sub', pairs)  7.98 us
    pallas_call x1, Pallas kernels, partial_image(): pl.pallas_call(compress_kernel, out_shape=jax.ShapeDtypeStruct((tiles, 2...  6.76 us
    all_to_all x1, waiting for transfers between devices, partial_image(): bands = lax.all_to_all(bands, 'tile', 0, 0, tiled=True)  5.56 us
    pallas_call x1, Pallas kernels, partial_image(): pl.pallas_call(phase_kernel, grid=(blocks,), out_shape=jax.ShapeDtypeStru...  4.13 us
  transfers between devices with their start and end apart: 16, of which 3 were waited for; matrix products, arithmetic and copies ran while one was open for 0% of the time, Pallas kernels for 5%

profile of v2, /device:TPU:1, one launch (start us, length us, event | category | flops | bytes accessed | tf_op | source)
XLA Modules:
  0.0 85.2 jit_solution(17334869562497098600)
XLA Ops:
  0.0 6.8 %compress.1 = bf16[16,64,128]{2,1,0:T(8,128)(2,1)} custom-call(s32[2,16]{1,0:T(2,128)} %starts_ref.1, bf16[2,2048]{1,0:T(2,128)(2,1)} %chirp_ref.1, bf16[32,128,128]{2,1,0:T(8,128)(2,1)} %bitcast.14), custom_call_target="tpu_custom_call" | custom-call | tf_op jit(solution)/shard_map/compress/pallas_call | solution.py:216
  6.8 9.2 %all-to-all-start = ((bf16[16,64,128]{2,1,0:T(8,128)(2,1)}), bf16[16,64,128]{2,1,0:T(8,128)(2,1)S(1)}, u32[]{:S(2)}, u32[]{:S(2)}) async-start(bf16[16,64,128]{2,1,0:T(8,128)(2,1)} %compress.1), calls=%async_computation | async-start | bytes 524288 | tf_op jit(solution)/shard_map/all_to_all | solution.py:237
  16.0 4.1 %phase.1.table_ref = bf16[2,512,2048]{2,1,0:T(8,128)(2,1)} custom-call(f32[1,512]{1,0:T(1,128)} %rates_ref.1, s32[2,256]{1,0:T(2,128)} %bitcast.15), custom_call_target="tpu_custom_call" | custom-call | tf_op jit(solution)/shard_map/phase/pallas_call | solution.py:238
  20.1 5.6 %all-to-all-done.bands_ref = bf16[16,64,128]{2,1,0:T(8,128)(2,1)S(1)} async-done(((bf16[16,64,128]{2,1,0:T(8,128)(2,1)}), bf16[16,64,128]{2,1,0:T(8,128)(2,1)S(1)}, u32[]{:S(2)}, u32[]{:S(2)}) %all-to-all-start) | async-done | bytes 262176 | tf_op jit(solution)/shard_map/all_to_all | solution.py:237
  25.7 0.0 copy-start
  25.7 0.7 copy-done
  26.4 11.3 %image.1 = (f32[8,128]{1,0:T(8,128)}, f32[8,128]{1,0:T(8,128)}, f32[8,128]{1,0:T(8,128)}, f32[8,128]{1,0:T(8,128)}, f32[8,128]{1,0:T(8,128)}, /*index=5*/f32[8,1...) custom-call(s32[1]{0:T(128)} %bitcast.me_ref, ...), custom_call_target="tpu_custom_call" | custom-call | tf_op jit(solution)/shard_map/image/pallas_call | solution.py:255
  37.7 2.2 %collective-permute-start = (f32[8,128]{1,0:T(8,128)}, f32[8,128]{1,0:T(8,128)S(1)}, u32[]{:S(2)}, u32[]{:S(2)}) collective-permute-start(f32[8,128]{1,0:T(8,128)} %get-tuple-element.22), channel_id=1, source_target_pairs={{0,16},{16,0},{32,48},{48,32},{64,80},{80,64},{96,112},{112,96},{1... | collective-permute-start | bytes 12296 | tf_op jit(solution)/shard_map/ppermute | solution.py:282
  40.0 1.2 %collective-permute-start.1 = (f32[8,128]{1,0:T(8,128)}, f32[8,128]{1,0:T(8,128)S(1)}, u32[]{:S(2)}, u32[]{:S(2)}) collective-permute-start(f32[8,128]{1,0:T(8,128)} %get-tuple-element.23), channel_id=1, source_target_pairs={{0,32},{16,48},{32,0},{48,16},{64,96},{80,112},{96,64},{112,80},{1... | collective-permute-start | bytes 12296 | tf_op jit(solution)/shard_map/ppermute | solution.py:282
  41.2 0.5 collective-permute-start.2
  41.7 2.7 %collective-permute-start.3 = (f32[8,128]{1,0:T(8,128)}, f32[8,128]{1,0:T(8,128)S(1)}, u32[]{:S(2)}, u32[]{:S(2)}) collective-permute-start(f32[8,128]{1,0:T(8,128)} %get-tuple-element.25), channel_id=1, source_target_pairs={{0,64},{16,80},{32,96},{48,112},{64,0},{80,16},{96,32},{112,48},{1... | collective-permute-start | bytes 12296 | tf_op jit(solution)/shard_map/ppermute | solution.py:282
  44.4 0.6 collective-permute-start.4
  45.0 0.0 collective-permute-done
  45.0 2.5 %collective-permute-start.5 = (f32[8,128]{1,0:T(8,128)}, f32[8,128]{1,0:T(8,128)S(1)}, u32[]{:S(2)}, u32[]{:S(2)}) collective-permute-start(f32[8,128]{1,0:T(8,128)} %get-tuple-element.27), channel_id=1, source_target_pairs={{0,96},{16,112},{32,64},{48,80},{64,32},{80,48},{96,0},{112,16},{1... | collective-permute-start | bytes 12296 | tf_op jit(solution)/shard_map/ppermute | solution.py:282
  47.5 0.0 collective-permute-done.1
  47.5 0.4 collective-permute-start.6
  47.9 0.0 collective-permute-done.2
  47.9 4.2 %collective-permute-start.7 = (f32[8,128]{1,0:T(8,128)}, f32[8,128]{1,0:T(8,128)S(1)}, u32[]{:S(2)}, u32[]{:S(2)}) collective-permute-start(f32[8,128]{1,0:T(8,128)} %get-tuple-element.29), channel_id=1, source_target_pairs={{0,128},{16,144},{32,160},{48,176},{64,192},{80,208},{96,224},{112... | collective-permute-start | bytes 12296 | tf_op jit(solution)/shard_map/ppermute | solution.py:282
  52.1 0.0 collective-permute-done.3
  52.1 1.5 %collective-permute-start.8 = (f32[8,128]{1,0:T(8,128)}, f32[8,128]{1,0:T(8,128)S(1)}, u32[]{:S(2)}, u32[]{:S(2)}) collective-permute-start(f32[8,128]{1,0:T(8,128)} %get-tuple-element.30), channel_id=1, source_target_pairs={{0,144},{16,128},{32,176},{48,160},{64,208},{80,192},{96,240},{112... | collective-permute-start | bytes 12296 | tf_op jit(solution)/shard_map/ppermute | solution.py:282
  53.6 0.0 collective-permute-done.4
  53.6 3.9 %collective-permute-start.9 = (f32[8,128]{1,0:T(8,128)}, f32[8,128]{1,0:T(8,128)S(1)}, u32[]{:S(2)}, u32[]{:S(2)}) collective-permute-start(f32[8,128]{1,0:T(8,128)} %get-tuple-element.31), channel_id=1, source_target_pairs={{0,160},{16,176},{32,128},{48,144},{64,224},{80,240},{96,192},{112... | collective-permute-start | bytes 12296 | tf_op jit(solution)/shard_map/ppermute | solution.py:282
  57.6 0.0 collective-permute-done.5
  57.6 2.6 %collective-permute-start.10 = (f32[8,128]{1,0:T(8,128)}, f32[8,128]{1,0:T(8,128)S(1)}, u32[]{:S(2)}, u32[]{:S(2)}) collective-permute-start(f32[8,128]{1,0:T(8,128)} %get-tuple-element.32), channel_id=1, source_target_pairs={{0,176},{16,160},{32,144},{48,128},{64,240},{80,224},{96,208},{112... | collective-permute-start | bytes 12296 | tf_op jit(solution)/shard_map/ppermute | solution.py:282
  60.1 0.0 collective-permute-done.6
  60.1 5.5 %collective-permute-start.11 = (f32[8,128]{1,0:T(8,128)}, f32[8,128]{1,0:T(8,128)S(1)}, u32[]{:S(2)}, u32[]{:S(2)}) collective-permute-start(f32[8,128]{1,0:T(8,128)} %get-tuple-element.33), channel_id=1, source_target_pairs={{0,192},{16,208},{32,224},{48,240},{64,128},{80,144},{96,160},{112... | collective-permute-start | bytes 12296 | tf_op jit(solution)/shard_map/ppermute | solution.py:282
  65.6 0.0 collective-permute-done.7
  65.6 2.6 %collective-permute-start.12 = (f32[8,128]{1,0:T(8,128)}, f32[8,128]{1,0:T(8,128)S(1)}, u32[]{:S(2)}, u32[]{:S(2)}) collective-permute-start(f32[8,128]{1,0:T(8,128)} %get-tuple-element.34), channel_id=1, source_target_pairs={{0,208},{16,192},{32,240},{48,224},{64,144},{80,128},{96,176},{112... | collective-permute-start | bytes 12296 | tf_op jit(solution)/shard_map/ppermute | solution.py:282
  68.2 0.0 collective-permute-done.8
  68.2 6.4 %collective-permute-start.13 = (f32[8,128]{1,0:T(8,128)}, f32[8,128]{1,0:T(8,128)S(1)}, u32[]{:S(2)}, u32[]{:S(2)}) collective-permute-start(f32[8,128]{1,0:T(8,128)} %get-tuple-element.35), channel_id=1, source_target_pairs={{0,224},{16,240},{32,192},{48,208},{64,160},{80,176},{96,128},{112... | collective-permute-start | bytes 12296 | tf_op jit(solution)/shard_map/ppermute | solution.py:282
  74.7 0.0 collective-permute-done.9
  74.7 1.3 %collective-permute-start.14 = (f32[8,128]{1,0:T(8,128)}, f32[8,128]{1,0:T(8,128)S(1)}, u32[]{:S(2)}, u32[]{:S(2)}) collective-permute-start(f32[8,128]{1,0:T(8,128)} %get-tuple-element.36), channel_id=1, source_target_pairs={{0,240},{16,224},{32,208},{48,192},{64,176},{80,160},{96,144},{112... | collective-permute-start | bytes 12296 | tf_op jit(solution)/shard_map/ppermute | solution.py:282
  76.0 0.0 collective-permute-done.10
  76.0 0.0 collective-permute-done.11
  76.0 0.0 collective-permute-done.12
  76.0 1.0 %collective-permute-done.13 = f32[8,128]{1,0:T(8,128)S(1)} collective-permute-done((f32[8,128]{1,0:T(8,128)}, f32[8,128]{1,0:T(8,128)S(1)}, u32[]{:S(2)}, u32[]{:S(2)}) %collective-permute-start.13) | collective-permute-done | bytes 4128 | tf_op jit(solution)/shard_map/ppermute | solution.py:282
  76.9 7.0 %collective-permute-done.14 = f32[8,128]{1,0:T(8,128)S(1)} collective-permute-done((f32[8,128]{1,0:T(8,128)}, f32[8,128]{1,0:T(8,128)S(1)}, u32[]{:S(2)}, u32[]{:S(2)}) %collective-permute-start.14) | collective-permute-done | bytes 4128 | tf_op jit(solution)/shard_map/ppermute | solution.py:282
  83.9 1.3 %add_add_fusion = f32[8,128]{1,0:T(8,128)} fusion(f32[8,128]{1,0:T(8,128)S(1)} %collective-permute-done.14, f32[8,128]{1,0:T(8,128)S(1)} %collective-permute-done.13, f32[8,128]{1,0:T(8,128)S(1)} %collective-permute-done.12, f32[8,128]{1,0:T(8,128)S(1)} %collective-permute-done.11, f32[8,128]{1,0:T(8,128)S(1)} %collective-permute-done.10, ...), kind=kLoop, calls=%fused_computation | loop fusion | flops 15360 | bytes 69632 | tf_op jit(solution)/shard_map/add | solution.py:282
Async XLA Ops:
  6.8 18.9 %all-to-all-start = ((bf16[16,64,128]{2,1,0:T(8,128)(2,1)}), bf16[16,64,128]{2,1,0:T(8,128)(2,1)S(1)}, u32[]{:S(2)}, u32[]{:S(2)}) async-start(bf16[16,64,128]{2,1,0:T(8,128)(2,1)} %compress.1), calls=%async_computation | async-start | bytes 524288 | tf_op jit(solution)/shard_map/all_to_all | solution.py:237
  25.7 0.7 copy-start
  37.7 7.3 %collective-permute-start = (f32[8,128]{1,0:T(8,128)}, f32[8,128]{1,0:T(8,128)S(1)}, u32[]{:S(2)}, u32[]{:S(2)}) collective-permute-start(f32[8,128]{1,0:T(8,128)} %get-tuple-element.22), channel_id=1, source_target_pairs={{0,16},{16,0},{32,48},{48,32},{64,80},{80,64},{96,112},{112,96},{1... | collective-permute-start | bytes 12296 | tf_op jit(solution)/shard_map/ppermute | solution.py:282
  40.0 7.5 %collective-permute-start.1 = (f32[8,128]{1,0:T(8,128)}, f32[8,128]{1,0:T(8,128)S(1)}, u32[]{:S(2)}, u32[]{:S(2)}) collective-permute-start(f32[8,128]{1,0:T(8,128)} %get-tuple-element.23), channel_id=1, source_target_pairs={{0,32},{16,48},{32,0},{48,16},{64,96},{80,112},{96,64},{112,80},{1... | collective-permute-start | bytes 12296 | tf_op jit(solution)/shard_map/ppermute | solution.py:282
  41.2 6.7 %collective-permute-start.2 = (f32[8,128]{1,0:T(8,128)}, f32[8,128]{1,0:T(8,128)S(1)}, u32[]{:S(2)}, u32[]{:S(2)}) collective-permute-start(f32[8,128]{1,0:T(8,128)} %get-tuple-element.24), channel_id=1, source_target_pairs={{0,48},{16,32},{32,16},{48,0},{64,112},{80,96},{96,80},{112,64},{1... | collective-permute-start | bytes 12296 | tf_op jit(solution)/shard_map/ppermute | solution.py:282
  41.7 10.4 %collective-permute-start.3 = (f32[8,128]{1,0:T(8,128)}, f32[8,128]{1,0:T(8,128)S(1)}, u32[]{:S(2)}, u32[]{:S(2)}) collective-permute-start(f32[8,128]{1,0:T(8,128)} %get-tuple-element.25), channel_id=1, source_target_pairs={{0,64},{16,80},{32,96},{48,112},{64,0},{80,16},{96,32},{112,48},{1... | collective-permute-start | bytes 12296 | tf_op jit(solution)/shard_map/ppermute | solution.py:282
  44.4 9.2 %collective-permute-start.4 = (f32[8,128]{1,0:T(8,128)}, f32[8,128]{1,0:T(8,128)S(1)}, u32[]{:S(2)}, u32[]{:S(2)}) collective-permute-start(f32[8,128]{1,0:T(8,128)} %get-tuple-element.26), channel_id=1, source_target_pairs={{0,80},{16,64},{32,112},{48,96},{64,16},{80,0},{96,48},{112,32},{1... | collective-permute-start | bytes 12296 | tf_op jit(solution)/shard_map/ppermute | solution.py:282
  45.0 12.6 %collective-permute-start.5 = (f32[8,128]{1,0:T(8,128)}, f32[8,128]{1,0:T(8,128)S(1)}, u32[]{:S(2)}, u32[]{:S(2)}) collective-permute-start(f32[8,128]{1,0:T(8,128)} %get-tuple-element.27), channel_id=1, source_target_pairs={{0,96},{16,112},{32,64},{48,80},{64,32},{80,48},{96,0},{112,16},{1... | collective-permute-start | bytes 12296 | tf_op jit(solution)/shard_map/ppermute | solution.py:282
  47.5 12.7 %collective-permute-start.6 = (f32[8,128]{1,0:T(8,128)}, f32[8,128]{1,0:T(8,128)S(1)}, u32[]{:S(2)}, u32[]{:S(2)}) collective-permute-start(f32[8,128]{1,0:T(8,128)} %get-tuple-element.28), channel_id=1, source_target_pairs={{0,112},{16,96},{32,80},{48,64},{64,48},{80,32},{96,16},{112,0},{1... | collective-permute-start | bytes 12296 | tf_op jit(solution)/shard_map/ppermute | solution.py:282
  47.9 17.7 %collective-permute-start.7 = (f32[8,128]{1,0:T(8,128)}, f32[8,128]{1,0:T(8,128)S(1)}, u32[]{:S(2)}, u32[]{:S(2)}) collective-permute-start(f32[8,128]{1,0:T(8,128)} %get-tuple-element.29), channel_id=1, source_target_pairs={{0,128},{16,144},{32,160},{48,176},{64,192},{80,208},{96,224},{112... | collective-permute-start | bytes 12296 | tf_op jit(solution)/shard_map/ppermute | solution.py:282
  52.1 16.1 %collective-permute-start.8 = (f32[8,128]{1,0:T(8,128)}, f32[8,128]{1,0:T(8,128)S(1)}, u32[]{:S(2)}, u32[]{:S(2)}) collective-permute-start(f32[8,128]{1,0:T(8,128)} %get-tuple-element.30), channel_id=1, source_target_pairs={{0,144},{16,128},{32,176},{48,160},{64,208},{80,192},{96,240},{112... | collective-permute-start | bytes 12296 | tf_op jit(solution)/shard_map/ppermute | solution.py:282
  53.6 21.0 %collective-permute-start.9 = (f32[8,128]{1,0:T(8,128)}, f32[8,128]{1,0:T(8,128)S(1)}, u32[]{:S(2)}, u32[]{:S(2)}) collective-permute-start(f32[8,128]{1,0:T(8,128)} %get-tuple-element.31), channel_id=1, source_target_pairs={{0,160},{16,176},{32,128},{48,144},{64,224},{80,240},{96,192},{112... | collective-permute-start | bytes 12296 | tf_op jit(solution)/shard_map/ppermute | solution.py:282
  57.6 18.4 %collective-permute-start.10 = (f32[8,128]{1,0:T(8,128)}, f32[8,128]{1,0:T(8,128)S(1)}, u32[]{:S(2)}, u32[]{:S(2)}) collective-permute-start(f32[8,128]{1,0:T(8,128)} %get-tuple-element.32), channel_id=1, source_target_pairs={{0,176},{16,160},{32,144},{48,128},{64,240},{80,224},{96,208},{112... | collective-permute-start | bytes 12296 | tf_op jit(solution)/shard_map/ppermute | solution.py:282
  60.1 15.8 %collective-permute-start.11 = (f32[8,128]{1,0:T(8,128)}, f32[8,128]{1,0:T(8,128)S(1)}, u32[]{:S(2)}, u32[]{:S(2)}) collective-permute-start(f32[8,128]{1,0:T(8,128)} %get-tuple-element.33), channel_id=1, source_target_pairs={{0,192},{16,208},{32,224},{48,240},{64,128},{80,144},{96,160},{112... | collective-permute-start | bytes 12296 | tf_op jit(solution)/shard_map/ppermute | solution.py:282
  65.6 10.4 %collective-permute-start.12 = (f32[8,128]{1,0:T(8,128)}, f32[8,128]{1,0:T(8,128)S(1)}, u32[]{:S(2)}, u32[]{:S(2)}) collective-permute-start(f32[8,128]{1,0:T(8,128)} %get-tuple-element.34), channel_id=1, source_target_pairs={{0,208},{16,192},{32,240},{48,224},{64,144},{80,128},{96,176},{112... | collective-permute-start | bytes 12296 | tf_op jit(solution)/shard_map/ppermute | solution.py:282
  68.2 8.7 %collective-permute-start.13 = (f32[8,128]{1,0:T(8,128)}, f32[8,128]{1,0:T(8,128)S(1)}, u32[]{:S(2)}, u32[]{:S(2)}) collective-permute-start(f32[8,128]{1,0:T(8,128)} %get-tuple-element.35), channel_id=1, source_target_pairs={{0,224},{16,240},{32,192},{48,208},{64,160},{80,176},{96,128},{112... | collective-permute-start | bytes 12296 | tf_op jit(solution)/shard_map/ppermute | solution.py:282
  74.7 9.3 %collective-permute-start.14 = (f32[8,128]{1,0:T(8,128)}, f32[8,128]{1,0:T(8,128)S(1)}, u32[]{:S(2)}, u32[]{:S(2)}) collective-permute-start(f32[8,128]{1,0:T(8,128)} %get-tuple-element.36), channel_id=1, source_target_pairs={{0,240},{16,224},{32,208},{48,192},{64,176},{80,160},{96,144},{112... | collective-permute-start | bytes 12296 | tf_op jit(solution)/shard_map/ppermute | solution.py:282

commit v3 on v2

--- a/solution.py
+++ b/solution.py
@@ -13,7 +13,7 @@
 
 
 def compress_kernel(
-    starts_ref, chirp_ref, echoes_ref, bands_ref, raw_ref, wide_ref, samples_ref, lhs_ref, toeplitz_ref, product_ref, sem
+    starts_ref, chirp_ref, echoes_ref, bands_ref, raw_ref, samples_ref, lhs_ref, toeplitz_ref, product_ref, sem
 ):
     fetch = pltpu.make_async_copy(echoes_ref, raw_ref, sem)
     fetch.start()
@@ -37,16 +37,27 @@
     samples_ref[lines // 2 :] = jnp.zeros(
         (samples_ref.shape[0] - lines // 2, 2 * pulses, LANES), jnp.bfloat16
     )
+    piece = 16
+    side = half * piece
+    row = lax.broadcasted_iota(jnp.int32, (side, side), 0)
+    col = lax.broadcasted_iota(jnp.int32, (side, side), 1)
+    order = jnp.where(col == (row % half) * piece + row // half, 1.0, 0.0).astype(jnp.bfloat16)
     fetch.wait()
-    wide_ref[...] = raw_ref[...].astype(jnp.float32).reshape(wide_ref.shape)
-    for chunk in range(lines // 2):
+    for group in range(lines // piece):
+        block_rows = jnp.concatenate(
+            [
+                raw_ref[block * half : (block + 1) * half, group * piece : (group + 1) * piece, :].reshape(
+                    side, LANES
+                )
+                for block in range(blocks)
+            ],
+            1,
+        )
+        moved = jnp.dot(order, block_rows, preferred_element_type=jnp.float32).astype(jnp.bfloat16)
         for block in range(blocks):
-            for part in range(2):
-                line = wide_ref[
-                    pl.ds(block * half * lines + 2 * chunk + part, half, stride=lines), :
-                ]
-                top = block * rows + part * half
-                samples_ref[chunk, top : top + half, :] = line.astype(jnp.bfloat16)
+            samples_ref[
+                group * piece // 2 : (group + 1) * piece // 2, block * rows : (block + 1) * rows, :
+            ] = moved[:, block * LANES : (block + 1) * LANES].reshape(piece // 2, rows, LANES)
     for block in range(blocks):
         for tile in range(tiles):
             first = starts_ref[block, tile] // LANES
@@ -105,7 +116,7 @@
 
 def phase_kernel(rates_ref, slots_ref, table_ref):
     count = slots_ref.shape[1]
-    columns = table_ref.shape[2]
+    columns = table_ref.shape[1] * table_ref.shape[3]
     block = pl.program_id(0)
     row = lax.broadcasted_iota(jnp.int32, (count, count), 0)
     col = lax.broadcasted_iota(jnp.int32, (count, count), 1)
@@ -127,74 +138,109 @@
                     sine * step_cosine + cosine * step_sine,
                     cosine * step_cosine - sine * step_sine,
                 )
-            lanes = slice(chunk * LANES, (chunk + 1) * LANES)
-            table_ref[0, group * 32 : group * 32 + 32, lanes] = cosine.astype(jnp.bfloat16)
-            table_ref[0, count + group * 32 : count + group * 32 + 32, lanes] = sine.astype(
-                jnp.bfloat16
+            lanes = slice(chunk % 2 * LANES, (chunk % 2 + 1) * LANES)
+            table_ref[0, chunk // 2, span, lanes] = cosine.astype(jnp.bfloat16)
+            table_ref[0, chunk // 2, count + group * 32 : count + group * 32 + 32, lanes] = (
+                sine.astype(jnp.bfloat16)
             )
 
 
-def image_kernel(me_ref, bands_ref, table_ref, weights_ref, *rest):
-    *piece_refs, left_ref, focused_ref, image_ref = rest
-    step_id = pl.program_id(0)
-    blocks = table_ref.shape[0]
+def image_kernel(
+    bands_ref, table_ref, weights_ref, image_ref, left_ref, near_table_ref, near_weights_ref, focused_ref, table_sem, weights_sem
+):
+    blocks, parts, _, width = table_ref.shape
     sources, band_rows, band = bands_ref.shape
     rows = band_rows // blocks
     half = rows // 2
     count = sources * half
-
-    @pl.when(step_id == 0)
-    def _():
-        for block in range(blocks):
-            real = bands_ref[:, block * rows : block * rows + half, :].reshape(count, band)
-            imag = bands_ref[:, block * rows + half : (block + 1) * rows, :].reshape(count, band)
-            top = jnp.concatenate([real, imag], 1)
-            bottom = jnp.concatenate([-imag, real], 1)
-            left_ref[block] = jnp.concatenate([top, bottom], 0).T
-
-    for block in range(blocks):
-        focused_ref[block] = jnp.dot(
-            left_ref[block], table_ref[block], preferred_element_type=jnp.float32
-        ).reshape(focused_ref.shape[1:])
+    places = image_ref.shape[0]
+    depth = band // parts
+
+    def table_copy(block, part):
+        return pltpu.make_async_copy(
+            table_ref.at[block, part], near_table_ref.at[block, part], table_sem.at[block, part]
+        )
+
+    def weights_copy(block, part, side):
+        span = pl.ds((block * 2 + side) * band + part * depth, depth)
+        return pltpu.make_async_copy(
+            weights_ref.at[span], near_weights_ref.at[span], weights_sem.at[block, part, side]
+        )
+
+    for block in range(blocks):
+        for part in range(parts):
+            table_copy(block, part).start()
+        for part in range(parts):
+            for side in range(2):
+                weights_copy(block, part, side).start()
+
+    for block in range(blocks):
+        real = bands_ref[:, block * rows : block * rows + half, :].reshape(count, band)
+        imag = bands_ref[:, block * rows + half : (block + 1) * rows, :].reshape(count, band)
+        top = jnp.concatenate([real, imag], 1)
+        bottom = jnp.concatenate([-imag, real], 1)
+        left_ref[block] = jnp.concatenate([top, bottom], 0).T
+
+    def focus(block, part):
+        table_copy(block, part).wait()
+        focused_ref[block, part] = jnp.dot(
+            left_ref[block], near_table_ref[block, part], preferred_element_type=jnp.float32
+        ).reshape(focused_ref.shape[2:])
+
+    for part in range(parts):
+        focus(0, part)
+
     upper = lax.broadcasted_iota(jnp.int32, (8, LANES), 0) < 4
-    zero = jnp.zeros((8, LANES), jnp.float32)
-    sums = (zero, zero)
-    for block in range(blocks):
-
-        def step(outer, sums):
-            real, imag = sums
-            for inner in range(8):
-                k = outer * 8 + inner
-                wr = weights_ref[block * 2 * band + k].astype(jnp.float32)
-                wi = weights_ref[block * 2 * band + band + k].astype(jnp.float32)
-
-                def value(row):
-                    parts = [
-                        jnp.broadcast_to(
-                            focused_ref[
-                                block, row, inner : inner + 1, side * LANES : (side + 1) * LANES
-                            ],
-                            (8, LANES),
-                        )
-                        for side in range(2)
-                    ]
-                    return jnp.where(upper, parts[0], parts[1])
-
-                fr = value(outer)
-                fi = value(band // 8 + outer)
-                real = real + (wr * fr - wi * fi)
-                imag = imag + (wr * fi + wi * fr)
-            return real, imag
-
-        sums = lax.fori_loop(0, band // 8, step, sums)
-    real, imag = sums
-    image_ref[2 * step_id] = jnp.concatenate([real[:4], imag[:4]], 0)
-    image_ref[2 * step_id + 1] = jnp.concatenate([real[4:], imag[4:]], 0)
-
-    @pl.when(step_id == pl.num_programs(0) - 1)
-    def _():
-        for index, piece_ref in enumerate(piece_refs):
-            piece_ref[...] = image_ref[me_ref[0] ^ index]
+    sums = tuple(jnp.zeros((8, LANES), jnp.float32) for _ in range(places))
+    for block in range(blocks):
+
+        def step(part, sums):
+            sums = list(sums)
+            for side in range(2):
+                weights_copy(block, part, side).wait()
+            if block + 1 < blocks:
+                focus(block + 1, part)
+            for inner in range(depth):
+                k = part * depth + inner
+                for pair in range(places // 4):
+                    span = slice(pair * 16, pair * 16 + 16)
+                    weight_real = near_weights_ref[block * 2 * band + k, span, :].astype(jnp.float32)
+                    weight_imag = near_weights_ref[
+                        (block * 2 + 1) * band + k, span, :
+                    ].astype(jnp.float32)
+                    for one in range(2):
+                        wr = weight_real[one * 8 : one * 8 + 8]
+                        wi = weight_imag[one * 8 : one * 8 + 8]
+
+                        def value(side):
+                            line = side * (band // 8) + part * (depth // 8) + inner // 8
+                            halves = [
+                                jnp.broadcast_to(
+                                    focused_ref[
+                                        block,
+                                        2 * pair + one,
+                                        line,
+                                        inner % 8 : inner % 8 + 1,
+                                        place * LANES : (place + 1) * LANES,
+                                    ],
+                                    (8, LANES),
+                                )
+                                for place in range(2)
+                            ]
+                            return jnp.where(upper, halves[0], halves[1])
+
+                        fr = value(0)
+                        fi = value(1)
+                        at = 2 * (2 * pair + one)
+                        sums[at] = sums[at] + (wr * fr - wi * fi)
+                        sums[at + 1] = sums[at + 1] + (wr * fi + wi * fr)
+            return tuple(sums)
+
+        sums = lax.fori_loop(0, parts, step, sums)
+    for pair in range(places // 2):
+        real, imag = sums[2 * pair], sums[2 * pair + 1]
+        image_ref[2 * pair] = jnp.concatenate([real[:4], imag[:4]], 0)
+        image_ref[2 * pair + 1] = jnp.concatenate([real[4:], imag[4:]], 0)
 
 
 def vmem():
@@ -210,6 +256,7 @@
     lines = 2 * pulse_len // LANES
     span = chirp_len + 2 * LANES
     places = columns // LANES
+    parts = places // 2
     params = pltpu.CompilerParams(vmem_limit_bytes=VMEM_LIMIT)
     samples = echoes.reshape(pulses, 2, pulse_len // LANES, LANES).transpose(0, 2, 1, 3)
     samples = samples.reshape(pulses, lines, LANES)
@@ -224,7 +271,6 @@
         out_specs=vmem(),
         scratch_shapes=[
             pltpu.VMEM((pulses, lines, LANES), jnp.bfloat16),
-            pltpu.VMEM((pulses * lines, LANES), jnp.float32),
             pltpu.VMEM((lines // 2 + span // LANES - 1, 2 * pulses, LANES), jnp.bfloat16),
             pltpu.VMEM((tiles * 2 * pulses, span), jnp.bfloat16),
             pltpu.VMEM((4 * LANES, span), jnp.bfloat16),
@@ -238,12 +284,12 @@
     table = pl.pallas_call(
         phase_kernel,
         grid=(blocks,),
-        out_shape=jax.ShapeDtypeStruct((blocks, 2 * count, columns), jnp.bfloat16),
+        out_shape=jax.ShapeDtypeStruct((blocks, parts, 2 * count, 2 * LANES), jnp.bfloat16),
         in_specs=[
             pl.BlockSpec((1, count), lambda i: (0, i)),
             pl.BlockSpec((blocks, count), lambda i: (0, 0)),
         ],
-        out_specs=pl.BlockSpec((1, 2 * count, columns), lambda i: (i, 0, 0)),
+        out_specs=pl.BlockSpec((1, parts, 2 * count, 2 * LANES), lambda i: (i, 0, 0, 0)),
         compiler_params=params,
         name="phase",
     )(doppler_rates, slot_pulse.reshape(blocks, count))
@@ -251,36 +297,32 @@
     weights = weights.transpose(0, 1, 2, 4, 3, 5).reshape(
         blocks * 2 * band, places * image_rows, LANES
     )
-    me = lax.axis_index("sub").astype(jnp.int32).reshape(1)
     return pl.pallas_call(
         image_kernel,
-        grid=(places // 2,),
-        out_shape=[jax.ShapeDtypeStruct((2 * image_rows, LANES), jnp.float32)] * places,
+        out_shape=jax.ShapeDtypeStruct((places, 2 * image_rows, LANES), jnp.float32),
         in_specs=[
-            pl.BlockSpec(memory_space=pltpu.SMEM),
-            pl.BlockSpec((tiles, 2 * pulses, band), lambda i: (0, 0, 0)),
-            pl.BlockSpec((blocks, 2 * count, 2 * LANES), lambda i: (0, 0, i)),
-            pl.BlockSpec((blocks * 2 * band, 2 * image_rows, LANES), lambda i: (0, i, 0)),
-        ],
-        out_specs=[pl.BlockSpec((2 * image_rows, LANES), lambda i: (0, 0))] * places,
+            vmem(),
+            pl.BlockSpec(memory_space=pl.ANY),
+            pl.BlockSpec(memory_space=pl.ANY),
+        ],
+        out_specs=vmem(),
         scratch_shapes=[
             pltpu.VMEM((blocks, 2 * band, 2 * count), jnp.bfloat16),
-            pltpu.VMEM((blocks, 2 * band // 8, 8, 2 * LANES), jnp.float32),
-            pltpu.VMEM((places, 2 * image_rows, LANES), jnp.float32),
+            pltpu.VMEM((blocks, parts, 2 * count, 2 * LANES), jnp.bfloat16),
+            pltpu.VMEM((blocks * 2 * band, places * image_rows, LANES), jnp.bfloat16),
+            pltpu.VMEM((blocks, parts, 2 * band // 8, 8, 2 * LANES), jnp.float32),
+            pltpu.SemaphoreType.DMA((blocks, parts)),
+            pltpu.SemaphoreType.DMA((blocks, parts, 2)),
         ],
         compiler_params=params,
         name="image",
-    )(me, bands, table, weights)
+    )(bands, table, weights)
 
 
 def shards(*args):
-    pieces = partial_image(*args)
-    size = len(pieces)
-    total = pieces[0]
-    for index in range(1, size):
-        pairs = [(source, source ^ index) for source in range(size)]
-        total = total + lax.ppermute(pieces[index], "sub", pairs)
-    return total.reshape(2, -1, LANES)
+    image = partial_image(*args)
+    pieces = lax.all_to_all(image, "sub", 0, 0, tiled=True)
+    return jnp.sum(pieces, 0).reshape(2, -1, LANES)
 
 
 def solution(mesh):

time: 85.7 us -> 58.2 us (0.68)
  starting transfers between devices: 47.4 us -> 9.21 us
  blocking collectives: 0 us -> 20.1 us
  waiting for transfers between devices: 13.5 us -> 5.58 us
    ppermute x15 -> x0, starting transfers between devices: 38.2 us -> none  [shards(): total = total + lax.ppermute(pieces[index], 'sub', pairs)]
    all_to_all x0 -> x1, blocking collectives: none -> 20.1 us  [shards(): pieces = lax.all_to_all(image, 'sub', 0, 0, tiled=True)]
    ppermute x15 -> x0, waiting for transfers between devices: 7.98 us -> none  [shards(): total = total + lax.ppermute(pieces[index], 'sub', pairs)]
    add x1 -> x0, other arithmetic: 1.3 us -> none  [shards(): total = total + lax.ppermute(pieces[index], 'sub', pairs)]
    pallas_call x1, Pallas kernels: 6.76 us -> 5.78 us  [partial_image(): pl.pallas_call(compress_kernel, out_shape=jax.ShapeDtypeStruct((tiles, 2...]
  transfers between devices with their start and end apart: 16 -> 1, of which waited for: 3 -> 1; matrix products, arithmetic and copies ran while one was open for 0% -> 0% of each run, Pallas kernels for 5% -> 7%
where the time goes in v3:
time: 58.2 us; the launch traced here: 57.8 us
  Pallas kernels  21.6 us (37%)
  blocking collectives  20.1 us (35%)
  starting transfers between devices  9.21 us (16%)
  waiting for transfers between devices  5.58 us (10%)
  local copies, waits for them, and re-layouts  0.69 us (1%)
  other arithmetic  0.61 us (1%)
    all_to_all x1, blocking collectives, shards(): pieces = lax.all_to_all(image, 'sub', 0, 0, tiled=True)  20.1 us
    pallas_call x1, Pallas kernels, partial_image(): pl.pallas_call(image_kernel, out_shape=jax.ShapeDtypeStruct((places, 2 *...  11.7 us
    all_to_all x1, starting transfers between devices, partial_image(): bands = lax.all_to_all(bands, 'tile', 0, 0, tiled=True)  9.21 us
    pallas_call x1, Pallas kernels, partial_image(): pl.pallas_call(compress_kernel, out_shape=jax.ShapeDtypeStruct((tiles, 2...  5.78 us
    all_to_all x1, waiting for transfers between devices, partial_image(): bands = lax.all_to_all(bands, 'tile', 0, 0, tiled=True)  5.58 us
    pallas_call x1, Pallas kernels, partial_image(): pl.pallas_call(phase_kernel, grid=(blocks,), out_shape=jax.ShapeDtypeStru...  4.11 us
  transfers between devices with their start and end apart: 1, of which 1 were waited for; matrix products, arithmetic and copies ran while one was open for 0% of the time, Pallas kernels for 7%

profile of v3, /device:TPU:1, one launch (start us, length us, event | category | flops | bytes accessed | tf_op | source)
XLA Modules:
  0.0 57.8 jit_solution(2465800336490201161)
XLA Ops:
  0.0 5.8 %compress.1 = bf16[16,64,128]{2,1,0:T(8,128)(2,1)} custom-call(s32[2,16]{1,0:T(2,128)} %starts_ref.1, bf16[2,2048]{1,0:T(2,128)(2,1)} %chirp_ref.1, bf16[32,128,128]{2,1,0:T(8,128)(2,1)} %bitcast.13), custom_call_target="tpu_custom_call" | custom-call | tf_op jit(solution)/shard_map/compress/pallas_call | solution.py:263
  5.8 9.2 %all-to-all-start = ((bf16[16,64,128]{2,1,0:T(8,128)(2,1)}), bf16[16,64,128]{2,1,0:T(8,128)(2,1)S(1)}, u32[]{:S(2)}, u32[]{:S(2)}) async-start(bf16[16,64,128]{2,1,0:T(8,128)(2,1)} %compress.1), calls=%async_computation | async-start | bytes 524288 | tf_op jit(solution)/shard_map/all_to_all | solution.py:283
  15.0 4.1 %phase.1.table_ref = bf16[2,8,512,256]{3,2,1,0:T(8,128)(2,1)} custom-call(f32[1,512]{1,0:T(1,128)} %rates_ref.1, s32[2,256]{1,0:T(2,128)} %bitcast.14), custom_call_target="tpu_custom_call" | custom-call | tf_op jit(solution)/shard_map/phase/pallas_call | solution.py:284
  19.1 5.6 %all-to-all-done.bands_ref = bf16[16,64,128]{2,1,0:T(8,128)(2,1)S(1)} async-done(((bf16[16,64,128]{2,1,0:T(8,128)(2,1)}), bf16[16,64,128]{2,1,0:T(8,128)(2,1)S(1)}, u32[]{:S(2)}, u32[]{:S(2)}) %all-to-all-start) | async-done | bytes 262176 | tf_op jit(solution)/shard_map/all_to_all | solution.py:283
  24.7 0.0 copy-start
  24.7 0.7 %copy-done = bf16[16,64,128]{2,1,0:T(8,128)(2,1)} copy-done((bf16[16,64,128]{2,1,0:T(8,128)(2,1)}, bf16[16,64,128]{2,1,0:T(8,128)(2,1)S(1)}, u32[]{:S(2)}) %copy-start) | copy-done | bytes 262168
  25.4 11.7 %image.1 = f32[16,8,128]{2,1,0:T(8,128)} custom-call(bf16[16,64,128]{2,1,0:T(8,128)(2,1)} %copy-done, bf16[2,8,512,256]{3,2,1,0:T(8,128)(2,1)} %phase.1.table_ref, bf16[512,64,128]{2,1,0:T(8,128)(2,1)} %bitcast.12), custom_call_target="tpu_custom_call" | custom-call | tf_op jit(solution)/shard_map/image/pallas_call | solution.py:300
  37.1 20.1 %all_to_all.10 = f32[16,8,128]{2,1,0:T(8,128)S(1)} all-to-all(f32[16,8,128]{2,1,0:T(8,128)} %image.1), channel_id=1, replica_groups=mesh['sub'=16,'tile'=16] {'sub'}, dimensions={0} | all-to-all | bytes 131072 | tf_op jit(solution)/shard_map/all_to_all | solution.py:324
  57.2 0.6 %reduce_sum.9 = f32[8,128]{1,0:T(8,128)} reduce(f32[16,8,128]{2,1,0:T(8,128)S(1)} %all_to_all.10, f32[]{:T(128)} %constant.0.clone.1), dimensions={0}, to_apply=%region_0.0 | reduce | flops 15360 | bytes 69636 | tf_op jit(solution)/shard_map/reduce_sum | solution.py:325
Async XLA Ops:
  5.8 18.9 %all-to-all-start = ((bf16[16,64,128]{2,1,0:T(8,128)(2,1)}), bf16[16,64,128]{2,1,0:T(8,128)(2,1)S(1)}, u32[]{:S(2)}, u32[]{:S(2)}) async-start(bf16[16,64,128]{2,1,0:T(8,128)(2,1)} %compress.1), calls=%async_computation | async-start | bytes 524288 | tf_op jit(solution)/shard_map/all_to_all | solution.py:283
  24.7 0.7 %copy-start = (bf16[16,64,128]{2,1,0:T(8,128)(2,1)}, bf16[16,64,128]{2,1,0:T(8,128)(2,1)S(1)}, u32[]{:S(2)}) copy-start(bf16[16,64,128]{2,1,0:T(8,128)(2,1)S(1)} %all-to-all-done.bands_ref) | copy-start | bytes 786436

commit v4 on v3

--- a/solution.py
+++ b/solution.py
@@ -9,16 +9,17 @@
 from jax.sharding import PartitionSpec as P
 
 LANES = 128
-VMEM_LIMIT = 60 * 1024 * 1024
 
 
 def compress_kernel(
-    starts_ref, chirp_ref, echoes_ref, bands_ref, raw_ref, samples_ref, lhs_ref, toeplitz_ref, product_ref, sem
+    me_ref, starts_ref, chirp_ref, echoes_ref, *rest
 ):
+    *bands_refs, raw_ref, samples_ref, lhs_ref, toeplitz_ref, product_ref, sem = rest
     fetch = pltpu.make_async_copy(echoes_ref, raw_ref, sem)
     fetch.start()
     span = toeplitz_ref.shape[1]
     blocks, tiles = starts_ref.shape
+    near = tiles // len(bands_refs)
     pulses, lines, _ = raw_ref.shape
     half = pulses // blocks
     rows = 2 * half
@@ -60,7 +61,7 @@
             ] = moved[:, block * LANES : (block + 1) * LANES].reshape(piece // 2, rows, LANES)
     for block in range(blocks):
         for tile in range(tiles):
-            first = starts_ref[block, tile] // LANES
+            first = starts_ref[block, me_ref[0] ^ tile] // LANES
             place = (block * tiles + tile) * rows
             for chunk in range(chunks):
                 lhs_ref[place : place + rows, chunk * LANES : (chunk + 1) * LANES] = samples_ref[
@@ -73,7 +74,7 @@
     for block in range(blocks):
         for tile in range(tiles):
             place = (block * tiles + tile) * rows
-            shift = starts_ref[block, tile] % LANES
+            shift = starts_ref[block, me_ref[0] ^ tile] % LANES
             turn = (LANES - shift) % LANES
             keep = lane < LANES - shift
 
@@ -90,7 +91,7 @@
             ):
                 cut = jnp.where(keep, pltpu.roll(low, turn, 1), pltpu.roll(high, turn, 1))
                 top = block * rows + part * half
-                bands_ref[tile, top : top + half, :] = cut.astype(jnp.bfloat16)
+                bands_refs[tile // near][tile % near, top : top + half, :] = cut.astype(jnp.bfloat16)
 
 
 def sine_cosine(angle):
@@ -115,64 +116,71 @@
 
 
 def phase_kernel(rates_ref, slots_ref, table_ref):
-    count = slots_ref.shape[1]
+    blocks, count = slots_ref.shape
     columns = table_ref.shape[1] * table_ref.shape[3]
-    block = pl.program_id(0)
     row = lax.broadcasted_iota(jnp.int32, (count, count), 0)
     col = lax.broadcasted_iota(jnp.int32, (count, count), 1)
     lane = lax.broadcasted_iota(jnp.int32, (count, LANES), 1).astype(jnp.float32)
     place = (lane + 0.5) * np.float32(1 / columns) - 0.5
-    which = lax.broadcasted_iota(jnp.int32, slots_ref.shape, 0) == block
-    slots = jnp.sum(jnp.where(which, slots_ref[...], 0), 0, keepdims=True).astype(jnp.float32)
-    slot = jnp.sum(jnp.where(row == col, slots, 0.0), 1, keepdims=True)
-    rates = rates_ref[...]
-    rate = jnp.sum(jnp.where(slot == col.astype(jnp.float32), rates, 0.0), 1, keepdims=True)
-    rate = jnp.broadcast_to(rate, (count, LANES))
-    for group in range(count // 32):
-        span = slice(group * 32, group * 32 + 32)
-        sine, cosine = sine_cosine(rate[span] * place[span])
-        step_sine, step_cosine = sine_cosine(rate[span] * np.float32(LANES / columns))
-        for chunk in range(columns // LANES):
-            if chunk > 0:
-                sine, cosine = (
-                    sine * step_cosine + cosine * step_sine,
-                    cosine * step_cosine - sine * step_sine,
+    for block in range(blocks):
+        slots = slots_ref[block : block + 1, :].astype(jnp.float32)
+        slot = jnp.sum(jnp.where(row == col, slots, 0.0), 1, keepdims=True)
+        rates = rates_ref[:, block * count : (block + 1) * count]
+        rate = jnp.sum(jnp.where(slot == col.astype(jnp.float32), rates, 0.0), 1, keepdims=True)
+        rate = jnp.broadcast_to(rate, (count, LANES))
+        for group in range(count // 32):
+            span = slice(group * 32, group * 32 + 32)
+            sine, cosine = sine_cosine(rate[span] * place[span])
+            step_sine, step_cosine = sine_cosine(rate[span] * np.float32(LANES / columns))
+            for chunk in range(columns // LANES):
+                if chunk > 0:
+                    sine, cosine = (
+                        sine * step_cosine + cosine * step_sine,
+                        cosine * step_cosine - sine * step_sine,
+                    )
+                lanes = slice(chunk % 2 * LANES, (chunk % 2 + 1) * LANES)
+                table_ref[block, chunk // 2, span, lanes] = cosine.astype(jnp.bfloat16)
+                table_ref[block, chunk // 2, count + group * 32 : count + group * 32 + 32, lanes] = (
+                    sine.astype(jnp.bfloat16)
                 )
-            lanes = slice(chunk % 2 * LANES, (chunk % 2 + 1) * LANES)
-            table_ref[0, chunk // 2, span, lanes] = cosine.astype(jnp.bfloat16)
-            table_ref[0, chunk // 2, count + group * 32 : count + group * 32 + 32, lanes] = (
-                sine.astype(jnp.bfloat16)
-            )
-
-
-def image_kernel(
-    bands_ref, table_ref, weights_ref, image_ref, left_ref, near_table_ref, near_weights_ref, focused_ref, table_sem, weights_sem
-):
+
+
+def relay_kernel(*refs):
+    near = refs[0].shape[0]
+    far = len(refs) - near + 1
+    for dz in range(1, near):
+        for dy in range(far):
+            refs[far + dz - 1][dy] = refs[dy][dz]
+
+
+def image_kernel(me_ref, table_ref, weights_ref, *rest):
+    *sources_refs, image_ref, bands_ref, left_ref, near_weights_ref, first_ref, second_ref, sem = rest
     blocks, parts, _, width = table_ref.shape
     sources, band_rows, band = bands_ref.shape
+    far_count = len(sources_refs) // 2 + 1
+    near_refs, far_refs = sources_refs[:far_count], sources_refs[far_count:]
+    near = sources // far_count
     rows = band_rows // blocks
     half = rows // 2
     count = sources * half
     places = image_ref.shape[0]
     depth = band // parts
-
-    def table_copy(block, part):
+    focused_refs = (first_ref, second_ref)
+    ahead = 4
+
+    def weights_copy(step, side):
+        span = pl.ds((step // parts * 2 + side) * band + step % parts * depth, depth)
         return pltpu.make_async_copy(
-            table_ref.at[block, part], near_table_ref.at[block, part], table_sem.at[block, part]
+            weights_ref.at[span], near_weights_ref.at[span], sem.at[step, side]
         )
 
-    def weights_copy(block, part, side):
-        span = pl.ds((block * 2 + side) * band + part * depth, depth)
-        return pltpu.make_async_copy(
-            weights_ref.at[span], near_weights_ref.at[span], weights_sem.at[block, part, side]
-        )
-
-    for block in range(blocks):
-        for part in range(parts):
-            table_copy(block, part).start()
-        for part in range(parts):
-            for side in range(2):
-                weights_copy(block, part, side).start()
+    for step in range(ahead):
+        for side in range(2):
+            weights_copy(step, side).start()
+    for dy in range(far_count):
+        bands_ref[me_ref[0] ^ (dy * near)] = near_refs[dy][0]
+        for dz in range(1, near):
+            bands_ref[me_ref[0] ^ (dy * near + dz)] = far_refs[dz - 1][dy]
 
     for block in range(blocks):
         real = bands_ref[:, block * rows : block * rows + half, :].reshape(count, band)
@@ -182,10 +190,10 @@
         left_ref[block] = jnp.concatenate([top, bottom], 0).T
 
     def focus(block, part):
-        table_copy(block, part).wait()
-        focused_ref[block, part] = jnp.dot(
-            left_ref[block], near_table_ref[block, part], preferred_element_type=jnp.float32
-        ).reshape(focused_ref.shape[2:])
+        target_ref = focused_refs[block]
+        target_ref[part] = jnp.dot(
+            left_ref[block], table_ref[block, part], preferred_element_type=jnp.float32
+        ).reshape(target_ref.shape[1:])
 
     for part in range(parts):
         focus(0, part)
@@ -193,11 +201,18 @@
     upper = lax.broadcasted_iota(jnp.int32, (8, LANES), 0) < 4
     sums = tuple(jnp.zeros((8, LANES), jnp.float32) for _ in range(places))
     for block in range(blocks):
+        focused_ref = focused_refs[block]
 
         def step(part, sums):
             sums = list(sums)
             for side in range(2):
-                weights_copy(block, part, side).wait()
+                weights_copy(block * parts + part, side).wait()
+
+            @pl.when(block * parts + part + ahead < blocks * parts)
+            def _():
+                for side in range(2):
+                    weights_copy(block * parts + part + ahead, side).start()
+
             if block + 1 < blocks:
                 focus(block + 1, part)
             for inner in range(depth):
@@ -217,7 +232,6 @@
                             halves = [
                                 jnp.broadcast_to(
                                     focused_ref[
-                                        block,
                                         2 * pair + one,
                                         line,
                                         inner % 8 : inner % 8 + 1,
@@ -243,6 +257,10 @@
         image_ref[2 * pair + 1] = jnp.concatenate([real[4:], imag[4:]], 0)
 
 
+def params(mib):
+    return pltpu.CompilerParams(vmem_limit_bytes=mib * 1024 * 1024)
+
+
 def vmem():
     return pl.BlockSpec(memory_space=pltpu.VMEM)
 
@@ -257,18 +275,22 @@
     span = chirp_len + 2 * LANES
     places = columns // LANES
     parts = places // 2
-    params = pltpu.CompilerParams(vmem_limit_bytes=VMEM_LIMIT)
     samples = echoes.reshape(pulses, 2, pulse_len // LANES, LANES).transpose(0, 2, 1, 3)
     samples = samples.reshape(pulses, lines, LANES)
+    smem = pl.BlockSpec(memory_space=pltpu.SMEM)
+    me = lax.axis_index("tile").astype(jnp.int32).reshape(1)
+    near = 4
+    far = tiles // near
     bands = pl.pallas_call(
         compress_kernel,
-        out_shape=jax.ShapeDtypeStruct((tiles, 2 * pulses, band), jnp.bfloat16),
+        out_shape=[jax.ShapeDtypeStruct((near, 2 * pulses, band), jnp.bfloat16)] * far,
         in_specs=[
-            pl.BlockSpec(memory_space=pltpu.SMEM),
+            smem,
+            smem,
             vmem(),
             pl.BlockSpec(memory_space=pl.ANY),
         ],
-        out_specs=vmem(),
+        out_specs=[vmem()] * far,
         scratch_shapes=[
             pltpu.VMEM((pulses, lines, LANES), jnp.bfloat16),
             pltpu.VMEM((lines // 2 + span // LANES - 1, 2 * pulses, LANES), jnp.bfloat16),
@@ -277,46 +299,52 @@
             pltpu.VMEM((tiles * 2 * pulses, 4 * LANES), jnp.float32),
             pltpu.SemaphoreType.DMA,
         ],
-        compiler_params=params,
+        compiler_params=params(60),
         name="compress",
-    )(band_starts, chirp_ref, samples)
-    bands = lax.all_to_all(bands, "tile", 0, 0, tiled=True)
-    table = pl.pallas_call(
-        phase_kernel,
-        grid=(blocks,),
-        out_shape=jax.ShapeDtypeStruct((blocks, parts, 2 * count, 2 * LANES), jnp.bfloat16),
-        in_specs=[
-            pl.BlockSpec((1, count), lambda i: (0, i)),
-            pl.BlockSpec((blocks, count), lambda i: (0, 0)),
-        ],
-        out_specs=pl.BlockSpec((1, parts, 2 * count, 2 * LANES), lambda i: (i, 0, 0, 0)),
-        compiler_params=params,
-        name="phase",
-    )(doppler_rates, slot_pulse.reshape(blocks, count))
+    )(me, band_starts, chirp_ref, samples)
+
+    def swap(value, distance):
+        return lax.ppermute(value, "tile", [(one, one ^ distance) for one in range(tiles)])
+
+    bands = [bands[0]] + [swap(bands[dy], dy * near) for dy in range(1, far)]
     weights = interp_weights.reshape(blocks, 2, band, image_rows, places, LANES)
     weights = weights.transpose(0, 1, 2, 4, 3, 5).reshape(
         blocks * 2 * band, places * image_rows, LANES
     )
+    table = pl.pallas_call(
+        phase_kernel,
+        out_shape=jax.ShapeDtypeStruct((blocks, parts, 2 * count, 2 * LANES), jnp.bfloat16),
+        in_specs=[vmem(), vmem()],
+        out_specs=vmem(),
+        compiler_params=params(16),
+        name="phase",
+    )(doppler_rates, slot_pulse.reshape(blocks, count))
+    passed = pl.pallas_call(
+        relay_kernel,
+        out_shape=[jax.ShapeDtypeStruct((far, 2 * pulses, band), jnp.bfloat16)] * (near - 1),
+        in_specs=[vmem()] * far,
+        out_specs=[vmem()] * (near - 1),
+        compiler_params=params(16),
+        name="relay",
+    )(*bands)
+    passed = [swap(passed[dz - 1], dz) for dz in range(1, near)]
+    sources = bands + passed
     return pl.pallas_call(
         image_kernel,
         out_shape=jax.ShapeDtypeStruct((places, 2 * image_rows, LANES), jnp.float32),
-        in_specs=[
-            vmem(),
-            pl.BlockSpec(memory_space=pl.ANY),
-            pl.BlockSpec(memory_space=pl.ANY),
-        ],
+        in_specs=[smem, vmem(), pl.BlockSpec(memory_space=pl.ANY)] + [vmem()] * len(sources),
         out_specs=vmem(),
         scratch_shapes=[
+            pltpu.VMEM((tiles, 2 * pulses, band), jnp.bfloat16),
             pltpu.VMEM((blocks, 2 * band, 2 * count), jnp.bfloat16),
-            pltpu.VMEM((blocks, parts, 2 * count, 2 * LANES), jnp.bfloat16),
-            pltpu.VMEM((blocks * 2 * band, places * image_rows, LANES), jnp.bfloat16),
-            pltpu.VMEM((blocks, parts, 2 * band // 8, 8, 2 * LANES), jnp.float32),
-            pltpu.SemaphoreType.DMA((blocks, parts)),
-            pltpu.SemaphoreType.DMA((blocks, parts, 2)),
+            pltpu.VMEM(weights.shape, jnp.bfloat16),
+            pltpu.VMEM((parts, 2 * band // 8, 8, 2 * LANES), jnp.float32),
+            pltpu.VMEM((parts, 2 * band // 8, 8, 2 * LANES), jnp.float32),
+            pltpu.SemaphoreType.DMA((blocks * parts, 2)),
         ],
-        compiler_params=params,
+        compiler_params=params(45),
         name="image",
-    )(bands, table, weights)
+    )(me, table, weights, *sources)
 
 
 def shards(*args):

time: 58.2 us -> 55.6 us (0.955)
  Pallas kernels: 21.6 us -> 14 us
  local copies, waits for them, and re-layouts: 0.69 us -> 3.04 us
  waiting for transfers between devices: 5.58 us -> 6.8 us
  blocking collectives: 20.1 us -> 21.2 us
    ppermute x0 -> x6, starting transfers between devices: none -> 9.55 us  [swap(): lax.ppermute(value, 'tile', [(one, one ^ distance) for one in range(tiles)])]
    all_to_all x1 -> x0, starting transfers between devices: 9.21 us -> none  [partial_image(): bands = lax.all_to_all(bands, 'tile', 0, 0, tiled=True)]
    ppermute x0 -> x6, waiting for transfers between devices: none -> 6.8 us  [swap(): lax.ppermute(value, 'tile', [(one, one ^ distance) for one in range(tiles)])]
    all_to_all x1 -> x0, waiting for transfers between devices: 5.58 us -> none  [partial_image(): bands = lax.all_to_all(bands, 'tile', 0, 0, tiled=True)]
    pallas_call x1, Pallas kernels: 11.7 us -> 6.32 us  [partial_image(): pl.pallas_call(image_kernel, out_shape=jax.ShapeDtypeStruct((places, 2 *...]
    unnamed x2 -> x8, local copies, waits for them, and re-layouts: 0.69 us -> 3.04 us
    pallas_call x2 -> x3, Pallas kernels: 9.89 us -> 7.63 us  [the longest x1 5.73 us: partial_image(): pl.pallas_call(compress_kernel, out_shape=[jax.ShapeDtypeStruct((near, 2...]
    all_to_all x1, blocking collectives: 20.1 us -> 21.2 us  [shards(): pieces = lax.all_to_all(image, 'sub', 0, 0, tiled=True)]
  transfers between devices with their start and end apart: 1 -> 6, of which waited for: 1 -> 3; matrix products, arithmetic and copies ran while one was open for 0% -> 0% of each run, Pallas kernels for 7% -> 3%
where the time goes in v4:
time: 55.6 us; the launch traced here: 55.2 us
  blocking collectives  21.2 us (38%)
  Pallas kernels  14 us (25%)
  starting transfers between devices  9.55 us (17%)
  waiting for transfers between devices  6.8 us (12%)
  local copies, waits for them, and re-layouts  3.04 us (5%)
  other arithmetic  0.61 us (1%)
    all_to_all x1, blocking collectives, shards(): pieces = lax.all_to_all(image, 'sub', 0, 0, tiled=True)  21.2 us
    ppermute x6, starting transfers between devices, swap(): lax.ppermute(value, 'tile', [(one, one ^ distance) for one in range(tiles)])  9.55 us
    ppermute x6, waiting for transfers between devices, swap(): lax.ppermute(value, 'tile', [(one, one ^ distance) for one in range(tiles)])  6.8 us
    pallas_call x1, Pallas kernels, partial_image(): pl.pallas_call(image_kernel, out_shape=jax.ShapeDtypeStruct((places, 2 *...  6.32 us
    pallas_call x1, Pallas kernels, partial_image(): pl.pallas_call(compress_kernel, out_shape=[jax.ShapeDtypeStruct((near, 2...  5.73 us
    unnamed x8, local copies, waits for them, and re-layouts  3.04 us
    pallas_call x1, Pallas kernels, partial_image(): pl.pallas_call(phase_kernel, out_shape=jax.ShapeDtypeStruct((blocks, part...  1.88 us
  transfers between devices with their start and end apart: 6, of which 3 were waited for; matrix products, arithmetic and copies ran while one was open for 0% of the time, Pallas kernels for 3%

profile of v4, /device:TPU:1, one launch (start us, length us, event | category | flops | bytes accessed | tf_op | source)
XLA Modules:
  0.0 55.2 jit_solution(11498214454514917280)
XLA Ops:
  0.0 5.7 %compress.1 = (bf16[4,64,128]{2,1,0:T(8,128)(2,1)}, bf16[4,64,128]{2,1,0:T(8,128)(2,1)}, bf16[4,64,128]{2,1,0:T(8,128)(2,1)}, bf16[4,64,128]{2,1,0:T(8,128)(2,1)}) custom-call(s32[1]{0:T(128)} %bitcast.me_ref, s32[2,16]{1,0:T(2,128)} %starts_ref.1, bf16[2,2048]{1,0:T(2,128)(2,1)} %chirp_ref.1, bf16[32,128,128]{2,1,0:T(8,128)(2,1)} %bitcast.15), custom_call_target="tpu_custom_call" | custom-call | tf_op jit(solution)/shard_map/compress/pallas_call | solution.py:284
  5.7 2.2 %collective-permute-start = (bf16[4,64,128]{2,1,0:T(8,128)(2,1)}, bf16[4,64,128]{2,1,0:T(8,128)(2,1)S(1)}, u32[]{:S(2)}, u32[]{:S(2)}) collective-permute-start(bf16[4,64,128]{2,1,0:T(8,128)(2,1)} %get-tuple-element.13), channel_id=1, source_target_pairs={{0,4},{1,5},{2,6},{3,7},{4,0},{5,1},{6,2},{7,3},{8,12},{9,13},{10,... | collective-permute-start | bytes 196616 | tf_op jit(solution)/shard_map/ppermute | solution.py:307
  8.0 2.6 %collective-permute-start.1 = (bf16[4,64,128]{2,1,0:T(8,128)(2,1)}, bf16[4,64,128]{2,1,0:T(8,128)(2,1)S(1)}, u32[]{:S(2)}, u32[]{:S(2)}) collective-permute-start(bf16[4,64,128]{2,1,0:T(8,128)(2,1)} %get-tuple-element.14), channel_id=1, source_target_pairs={{0,8},{1,9},{2,10},{3,11},{4,12},{5,13},{6,14},{7,15},{8,0},{9,1},... | collective-permute-start | bytes 196616 | tf_op jit(solution)/shard_map/ppermute | solution.py:307
  10.6 0.0 collective-permute-start.2
  10.6 0.0 collective-permute-done.refs_1_.rest_1_
  10.6 2.8 %collective-permute-done.1.refs_2_.rest_2_ = bf16[4,64,128]{2,1,0:T(8,128)(2,1)S(1)} collective-permute-done((bf16[4,64,128]{2,1,0:T(8,128)(2,1)}, bf16[4,64,128]{2,1,0:T(8,128)(2,1)S(1)}, u32[]{:S(2)}, u32[]{:S(2)}) %collective-permute-start.1) | collective-permute-done | bytes 65568 | tf_op jit(solution)/shard_map/ppermute | solution.py:307
  13.4 1.9 %collective-permute-done.2.refs_3_.rest_3_ = bf16[4,64,128]{2,1,0:T(8,128)(2,1)S(1)} collective-permute-done((bf16[4,64,128]{2,1,0:T(8,128)(2,1)}, bf16[4,64,128]{2,1,0:T(8,128)(2,1)S(1)}, u32[]{:S(2)}, u32[]{:S(2)}) %collective-permute-start.2) | collective-permute-done | bytes 65568 | tf_op jit(solution)/shard_map/ppermute | solution.py:307
  15.2 0.0 copy-start
  15.2 0.8 %copy-done = bf16[4,64,128]{2,1,0:T(8,128)(2,1)S(1)} copy-done((bf16[4,64,128]{2,1,0:T(8,128)(2,1)S(1)}, bf16[4,64,128]{2,1,0:T(8,128)(2,1)}, u32[]{:S(2)}) %copy-start) | copy-done | bytes 65560
  16.1 1.7 %collective-permute-start.3 = (bf16[4,64,128]{2,1,0:T(8,128)(2,1)S(1)}, bf16[4,64,128]{2,1,0:T(8,128)(2,1)S(1)}, u32[]{:S(2)}, u32[]{:S(2)}) collective-permute-start(bf16[4,64,128]{2,1,0:T(8,128)(2,1)S(1)} %get-tuple-element.16), channel_id=1, source_target_pairs={{0,1},{1,0},{2,3},{3,2},{4,5},{5,4},{6,7},{7,6},{8,9},{9,8},{10,11... | collective-permute-start | bytes 196616 | tf_op jit(solution)/shard_map/ppermute | solution.py:307
  17.8 3.0 %collective-permute-start.4 = (bf16[4,64,128]{2,1,0:T(8,128)(2,1)S(1)}, bf16[4,64,128]{2,1,0:T(8,128)(2,1)S(1)}, u32[]{:S(2)}, u32[]{:S(2)}) collective-permute-start(bf16[4,64,128]{2,1,0:T(8,128)(2,1)S(1)} %get-tuple-element.17), channel_id=1, source_target_pairs={{0,2},{1,3},{2,0},{3,1},{4,6},{5,7},{6,4},{7,5},{8,10},{9,11},{10,... | collective-permute-start | bytes 196616 | tf_op jit(solution)/shard_map/ppermute | solution.py:307
  20.8 0.0 collective-permute-start.5
  20.8 0.0 copy-start.2
  20.8 0.7 %copy-done.2 = f32[1,512]{1,0:T(1,128)S(1)} copy-done((f32[1,512]{1,0:T(1,128)S(1)}, f32[1,512]{1,0:T(1,128)}, u32[]{:S(2)}) %copy-start.2) | copy-done | bytes 2072
  21.5 0.0 copy-start.3
  21.5 0.7 %copy-done.3 = s32[1,2,256]{2,1,0:T(2,128)S(1)} copy-done((s32[1,2,256]{2,1,0:T(2,128)S(1)}, s32[1,2,256]{2,1,0:T(2,128)}, u32[]{:S(2)}) %copy-start.3) | copy-done | bytes 2072
  22.2 1.9 %phase.1.table_ref = bf16[2,8,512,256]{3,2,1,0:T(8,128)(2,1)S(1)} custom-call(f32[1,512]{1,0:T(1,128)S(1)} %copy-done.2, s32[2,256]{1,0:T(2,128)S(1)} %bitcast.13), custom_call_target="tpu_custom_call" | custom-call | tf_op jit(solution)/shard_map/phase/pallas_call | solution.py:314
  24.1 0.0 collective-permute-done.3.rest_4_
  24.1 0.0 collective-permute-done.4.rest_5_
  24.1 2.1 %collective-permute-done.5.rest_6_ = bf16[4,64,128]{2,1,0:T(8,128)(2,1)S(1)} collective-permute-done((bf16[4,64,128]{2,1,0:T(8,128)(2,1)S(1)}, bf16[4,64,128]{2,1,0:T(8,128)(2,1)S(1)}, u32[]{:S(2)}, u32[]{:S(2)}) %collective-permute-start.5) | collective-permute-done | bytes 65568 | tf_op jit(solution)/shard_map/ppermute | solution.py:307
  26.2 0.0 copy-start.1
  26.2 0.8 %copy-done.1 = bf16[4,64,128]{2,1,0:T(8,128)(2,1)S(1)} copy-done((bf16[4,64,128]{2,1,0:T(8,128)(2,1)S(1)}, bf16[4,64,128]{2,1,0:T(8,128)(2,1)}, u32[]{:S(2)}) %copy-start.1) | copy-done | bytes 65560
  27.1 6.3 %image.1 = f32[16,8,128]{2,1,0:T(8,128)S(1)} custom-call(s32[1]{0:T(128)} %bitcast.me_ref, bf16[2,8,512,256]{3,2,1,0:T(8,128)(2,1)S(1)} %phase.1.table_ref, bf16[512,64,128]{2,1,0:T(8,128)(2,1)} %bitcast.14, bf16[4,64,128]{2,1,0:T(8,128)(2,1)S(1)} %copy-done.1, bf16[4,64,128]{2,1,0:T(8,128)(2,1)S(1)} %collective-permute-done.refs_1_.rest_1_, ...), custom_call_target="tpu_custom_call" | custom-call | tf_op jit(solution)/shard_map/image/pallas_call | solution.py:332
  33.4 21.2 %all_to_all.5 = f32[16,8,128]{2,1,0:T(8,128)S(1)} all-to-all(f32[16,8,128]{2,1,0:T(8,128)S(1)} %image.1), channel_id=1, replica_groups=mesh['sub'=16,'tile'=16] {'sub'}, dimensions={0} | all-to-all | bytes 131072 | tf_op jit(solution)/shard_map/all_to_all | solution.py:352
  54.6 0.6 %reduce_sum.9 = f32[8,128]{1,0:T(8,128)} reduce(f32[16,8,128]{2,1,0:T(8,128)S(1)} %all_to_all.5, f32[]{:T(128)} %constant.1.clone.1), dimensions={0}, to_apply=%region_0.0 | reduce | flops 15360 | bytes 69636 | tf_op jit(solution)/shard_map/reduce_sum | solution.py:353
  (1 shorter events, 0.0 us)
Async XLA Ops:
  5.7 4.8 %collective-permute-start = (bf16[4,64,128]{2,1,0:T(8,128)(2,1)}, bf16[4,64,128]{2,1,0:T(8,128)(2,1)S(1)}, u32[]{:S(2)}, u32[]{:S(2)}) collective-permute-start(bf16[4,64,128]{2,1,0:T(8,128)(2,1)} %get-tuple-element.13), channel_id=1, source_target_pairs={{0,4},{1,5},{2,6},{3,7},{4,0},{5,1},{6,2},{7,3},{8,12},{9,13},{10,... | collective-permute-start | bytes 196616 | tf_op jit(solution)/shard_map/ppermute | solution.py:307
  8.0 5.4 %collective-permute-start.1 = (bf16[4,64,128]{2,1,0:T(8,128)(2,1)}, bf16[4,64,128]{2,1,0:T(8,128)(2,1)S(1)}, u32[]{:S(2)}, u32[]{:S(2)}) collective-permute-start(bf16[4,64,128]{2,1,0:T(8,128)(2,1)} %get-tuple-element.14), channel_id=1, source_target_pairs={{0,8},{1,9},{2,10},{3,11},{4,12},{5,13},{6,14},{7,15},{8,0},{9,1},... | collective-permute-start | bytes 196616 | tf_op jit(solution)/shard_map/ppermute | solution.py:307
  10.6 4.7 %collective-permute-start.2 = (bf16[4,64,128]{2,1,0:T(8,128)(2,1)}, bf16[4,64,128]{2,1,0:T(8,128)(2,1)S(1)}, u32[]{:S(2)}, u32[]{:S(2)}) collective-permute-start(bf16[4,64,128]{2,1,0:T(8,128)(2,1)} %get-tuple-element.15), channel_id=1, source_target_pairs={{0,12},{1,13},{2,14},{3,15},{4,8},{5,9},{6,10},{7,11},{8,4},{9,5},... | collective-permute-start | bytes 196616 | tf_op jit(solution)/shard_map/ppermute | solution.py:307
  15.2 0.8 %copy-start = (bf16[4,64,128]{2,1,0:T(8,128)(2,1)S(1)}, bf16[4,64,128]{2,1,0:T(8,128)(2,1)}, u32[]{:S(2)}) copy-start(bf16[4,64,128]{2,1,0:T(8,128)(2,1)} %get-tuple-element.12.refs_0_.rest_0_) | copy-start | bytes 196612
  16.1 8.0 %collective-permute-start.3 = (bf16[4,64,128]{2,1,0:T(8,128)(2,1)S(1)}, bf16[4,64,128]{2,1,0:T(8,128)(2,1)S(1)}, u32[]{:S(2)}, u32[]{:S(2)}) collective-permute-start(bf16[4,64,128]{2,1,0:T(8,128)(2,1)S(1)} %get-tuple-element.16), channel_id=1, source_target_pairs={{0,1},{1,0},{2,3},{3,2},{4,5},{5,4},{6,7},{7,6},{8,9},{9,8},{10,11... | collective-permute-start | bytes 196616 | tf_op jit(solution)/shard_map/ppermute | solution.py:307
  17.8 6.3 %collective-permute-start.4 = (bf16[4,64,128]{2,1,0:T(8,128)(2,1)S(1)}, bf16[4,64,128]{2,1,0:T(8,128)(2,1)S(1)}, u32[]{:S(2)}, u32[]{:S(2)}) collective-permute-start(bf16[4,64,128]{2,1,0:T(8,128)(2,1)S(1)} %get-tuple-element.17), channel_id=1, source_target_pairs={{0,2},{1,3},{2,0},{3,1},{4,6},{5,7},{6,4},{7,5},{8,10},{9,11},{10,... | collective-permute-start | bytes 196616 | tf_op jit(solution)/shard_map/ppermute | solution.py:307
  20.8 5.4 %collective-permute-start.5 = (bf16[4,64,128]{2,1,0:T(8,128)(2,1)S(1)}, bf16[4,64,128]{2,1,0:T(8,128)(2,1)S(1)}, u32[]{:S(2)}, u32[]{:S(2)}) collective-permute-start(bf16[4,64,128]{2,1,0:T(8,128)(2,1)S(1)} %get-tuple-element.18), channel_id=1, source_target_pairs={{0,3},{1,2},{2,1},{3,0},{4,7},{5,6},{6,5},{7,4},{8,11},{9,10},{10,... | collective-permute-start | bytes 196616 | tf_op jit(solution)/shard_map/ppermute | solution.py:307
  20.8 0.7 %copy-start.2 = (f32[1,512]{1,0:T(1,128)S(1)}, f32[1,512]{1,0:T(1,128)}, u32[]{:S(2)}) copy-start(f32[1,512]{1,0:T(1,128)} %rates_ref.1) | copy-start | bytes 6148
  21.5 0.7 %copy-start.3 = (s32[1,2,256]{2,1,0:T(2,128)S(1)}, s32[1,2,256]{2,1,0:T(2,128)}, u32[]{:S(2)}) copy-start(s32[1,2,256]{2,1,0:T(2,128)} %param.10) | copy-start | bytes 6148
  26.2 0.8 %copy-start.1 = (bf16[4,64,128]{2,1,0:T(8,128)(2,1)S(1)}, bf16[4,64,128]{2,1,0:T(8,128)(2,1)}, u32[]{:S(2)}) copy-start(bf16[4,64,128]{2,1,0:T(8,128)(2,1)} %get-tuple-element.12.refs_0_.rest_0_) | copy-start | bytes 196612

commit v5 on v4

v5 whole, which is shorter than its diff:
```python
import jax
import jax.numpy as jnp
import numpy as np
from jax import lax
from jax.experimental import pallas as pl
from jax.experimental.pallas import tpu as pltpu
from jax.sharding import PartitionSpec as P

LANES = 128


def compress_kernel(
    me_ref, starts_ref, chirp_hbm, rates_hbm, slots_hbm, echoes_ref, *rest
):
    (
        *bands_refs, rate_ref, chirp_ref, rates_ref, slots_ref, raw_ref, samples_ref, lhs_ref, toeplitz_ref,
        product_ref, sems,
    ) = rest
    fetches = [
        pltpu.make_async_copy(source, target, sems.at[index])
        for index, (source, target) in enumerate(
            (
                (chirp_hbm, chirp_ref),
                (rates_hbm, rates_ref),
                (slots_hbm, slots_ref),
                (echoes_ref, raw_ref),
            )
        )
    ]
    for fetch in fetches:
        fetch.start()
    span = toeplitz_ref.shape[1]
    blocks, tiles = starts_ref.shape
    near = tiles // len(bands_refs)
    pulses, lines, _ = raw_ref.shape
    half = pulses // blocks
    rows = 2 * half
    chunks = span // LANES
    fetches[0].wait()
    chirp = chirp_ref[...].astype(jnp.float32)
    pad = jnp.zeros((1, span - chirp.shape[1]), jnp.float32)
    for part in range(2):
        line = jnp.concatenate([chirp[part : part + 1], pad], 1)
        shifted = pltpu.roll(
            jnp.broadcast_to(line, (LANES, span)), 0, 1, stride=1, stride_axis=0
        ).astype(jnp.bfloat16)
        base = part * 2 * LANES
        toeplitz_ref[base : base + LANES, :] = shifted
        toeplitz_ref[base + LANES : base + 2 * LANES, :LANES] = jnp.zeros((LANES, LANES), jnp.bfloat16)
        toeplitz_ref[base + LANES : base + 2 * LANES, LANES:] = shifted[:, : span - LANES]
    fetches[1].wait()
    fetches[2].wait()
    count = slots_ref.shape[1]
    row = lax.broadcasted_iota(jnp.int32, (count, count), 0)
    col = lax.broadcasted_iota(jnp.int32, (count, count), 1)
    for block in range(blocks):
        slots = slots_ref[block : block + 1, :].astype(jnp.float32)
        slot = jnp.sum(jnp.where(row == col, slots, 0.0), 1, keepdims=True)
        rates = rates_ref[:, block * count : (block + 1) * count]
        rate = jnp.sum(jnp.where(slot == col.astype(jnp.float32), rates, 0.0), 1, keepdims=True)
        rate_ref[block] = jnp.broadcast_to(rate, (count, LANES))
    samples_ref[lines // 2 :] = jnp.zeros(
        (samples_ref.shape[0] - lines // 2, 2 * pulses, LANES), jnp.bfloat16
    )
    piece = 16
    side = half * piece
    row = lax.broadcasted_iota(jnp.int32, (side, side), 0)
    col = lax.broadcasted_iota(jnp.int32, (side, side), 1)
    order = jnp.where(col == (row % half) * piece + row // half, 1.0, 0.0).astype(jnp.bfloat16)
    fetches[3].wait()
    for group in range(lines // piece):
        block_rows = jnp.concatenate(
            [
                raw_ref[block * half : (block + 1) * half, group * piece : (group + 1) * piece, :].reshape(
                    side, LANES
                )
                for block in range(blocks)
            ],
            1,
        )
        moved = jnp.dot(order, block_rows, preferred_element_type=jnp.float32).astype(jnp.bfloat16)
        for block in range(blocks):
            samples_ref[
                group * piece // 2 : (group + 1) * piece // 2, block * rows : (block + 1) * rows, :
            ] = moved[:, block * LANES : (block + 1) * LANES].reshape(piece // 2, rows, LANES)
    for block in range(blocks):
        for tile in range(tiles):
            first = starts_ref[block, me_ref[0] ^ tile] // LANES
            place = (block * tiles + tile) * rows
            for chunk in range(chunks):
                lhs_ref[place : place + rows, chunk * LANES : (chunk + 1) * LANES] = samples_ref[
                    first + chunk, block * rows : (block + 1) * rows, :
                ]
    product_ref[...] = lax.dot_general(
        lhs_ref[...], toeplitz_ref[...], (((1,), (1,)), ((), ())), preferred_element_type=jnp.float32
    )
    lane = lax.broadcasted_iota(jnp.int32, (half, LANES), 1)
    for block in range(blocks):
        for tile in range(tiles):
            place = (block * tiles + tile) * rows
            shift = starts_ref[block, me_ref[0] ^ tile] % LANES
            turn = (LANES - shift) % LANES
            keep = lane < LANES - shift

            def piece(part, column):
                top = place + part * half
                low = product_ref[top : top + half, column * 2 * LANES : column * 2 * LANES + LANES]
                high = product_ref[top : top + half, column * 2 * LANES + LANES : (column + 1) * 2 * LANES]
                return low, high

            rr, ri = piece(0, 0), piece(0, 1)
            ir, ii = piece(1, 0), piece(1, 1)
            for part, (low, high) in enumerate(
                ((rr[0] + ii[0], rr[1] + ii[1]), (ir[0] - ri[0], ir[1] - ri[1]))
            ):
                cut = jnp.where(keep, pltpu.roll(low, turn, 1), pltpu.roll(high, turn, 1))
                top = block * rows + part * half
                bands_refs[tile // near][tile % near, top : top + half, :] = cut.astype(jnp.bfloat16)


def sine_cosine(angle):
    turns = jnp.round(angle * np.float32(2 / np.pi))
    rest = (angle - turns * np.float32(1.5703125)) - turns * np.float32(np.pi / 2 - 1.5703125)
    quarter = turns.astype(jnp.int32)
    sq = rest * rest
    sine = np.float32(1 / 362880) * sq + np.float32(-1 / 5040)
    sine = sine * sq + np.float32(1 / 120)
    sine = sine * sq + np.float32(-1 / 6)
    sine = sine * sq * rest + rest
    cosine = np.float32(1 / 40320) * sq + np.float32(-1 / 720)
    cosine = cosine * sq + np.float32(1 / 24)
    cosine = cosine * sq + np.float32(-1 / 2)
    cosine = cosine * sq + np.float32(1)
    odd = (quarter & 1) == 1
    sin_out = jnp.where(odd, cosine, sine)
    cos_out = jnp.where(odd, sine, cosine)
    sin_out = jnp.where((quarter & 2) == 2, -sin_out, sin_out)
    cos_out = jnp.where(((quarter + 1) & 2) == 2, -cos_out, cos_out)
    return sin_out, cos_out


def first_phase_kernel(rate_hbm, bands_hbm, table_ref, rate_ref, bands_ref, sems):
    fetches = [
        pltpu.make_async_copy(rate_hbm, rate_ref, sems.at[0]),
        pltpu.make_async_copy(bands_hbm, bands_ref, sems.at[1]),
    ]
    for fetch in fetches:
        fetch.start()
    fetches[0].wait()
    phase_table(0, rate_ref, table_ref)
    fetches[1].wait()


def second_phase_kernel(rate_ref, after_ref, table_ref):
    phase_table(1, rate_ref, table_ref)


def phase_table(block, rate_ref, table_ref):
    count = rate_ref.shape[1]
    columns = table_ref.shape[0] * table_ref.shape[2]
    lane = lax.broadcasted_iota(jnp.int32, (32, LANES), 1).astype(jnp.float32)
    place = (lane + 0.5) * np.float32(1 / columns) - 0.5
    for group in range(count // 32):
        span = slice(group * 32, group * 32 + 32)
        rate = rate_ref[block, span]
        sine, cosine = sine_cosine(rate * place)
        step_sine, step_cosine = sine_cosine(rate * np.float32(LANES / columns))
        for chunk in range(columns // LANES):
            if chunk > 0:
                sine, cosine = (
                    sine * step_cosine + cosine * step_sine,
                    cosine * step_cosine - sine * step_sine,
                )
            lanes = slice(chunk % 2 * LANES, (chunk % 2 + 1) * LANES)
            table_ref[chunk // 2, span, lanes] = cosine.astype(jnp.bfloat16)
            table_ref[chunk // 2, count + group * 32 : count + group * 32 + 32, lanes] = (
                sine.astype(jnp.bfloat16)
            )


def relay_kernel(after_ref, *refs):
    near = refs[0].shape[0]
    far = len(refs) - near + 1
    for dz in range(1, near):
        for dy in range(far):
            refs[far + dz - 1][dy] = refs[dy][dz]


def weighted_sum(side, table_refs, weights_ref, image_ref, left_ref, near_weights_ref, first_ref, second_ref, sem):
    blocks = len(table_refs)
    places, lines, _ = image_ref.shape
    image_rows = lines // 2
    parts = places // 2
    band = weights_ref.shape[0] // (2 * blocks)
    depth = band // parts
    held = places * image_rows
    focused_refs = (first_ref, second_ref)
    ahead = 3

    def weights_copy(step, part):
        span = pl.ds((step // parts * 2 + part) * band + step % parts * depth, depth)
        rows = pl.ds(pl.multiple_of(side * held, held), held)
        return pltpu.make_async_copy(
            weights_ref.at[span, rows], near_weights_ref.at[span], sem.at[step, part]
        )

    def focus(block, part):
        target_ref = focused_refs[block]
        target_ref[part] = jnp.dot(
            left_ref[block], table_refs[block][side * parts + part], preferred_element_type=jnp.float32
        ).reshape(target_ref.shape[1:])

    for step in range(ahead):
        for part in range(2):
            weights_copy(step, part).start()
    yield
    for part in range(parts):
        focus(0, part)

    upper = lax.broadcasted_iota(jnp.int32, (8, LANES), 0) < 4
    sums = tuple(jnp.zeros((8, LANES), jnp.float32) for _ in range(places))
    for block in range(blocks):
        focused_ref = focused_refs[block]

        def step(chunk, sums):
            sums = list(sums)
            now = block * parts + chunk
            for part in range(2):
                weights_copy(now, part).wait()

            @pl.when(now + ahead < blocks * parts)
            def _():
                for part in range(2):
                    weights_copy(now + ahead, part).start()

            if block + 1 < blocks:
                focus(block + 1, chunk)
            for line in range(depth // 8):
                for quad in range(places // 4):
                    held_rows = {}
                    for one in range(2):
                        for part in range(2):
                            held_rows[one, part] = focused_ref[
                                2 * quad + one, part * (band // 8) + chunk * (depth // 8) + line, :, LANES:
                            ]
                    for inner in range(8):
                        k = chunk * depth + line * 8 + inner
                        span = slice(quad * 16, quad * 16 + 16)
                        weight_real = near_weights_ref[block * 2 * band + k, span, :].astype(jnp.float32)
                        weight_imag = near_weights_ref[
                            (block * 2 + 1) * band + k, span, :
                        ].astype(jnp.float32)
                        for one in range(2):
                            wr = weight_real[one * 8 : one * 8 + 8]
                            wi = weight_imag[one * 8 : one * 8 + 8]

                            def value(part):
                                low = focused_ref[
                                    2 * quad + one,
                                    part * (band // 8) + chunk * (depth // 8) + line,
                                    inner : inner + 1,
                                    :LANES,
                                ]
                                high = held_rows[one, part][inner : inner + 1]
                                return jnp.where(
                                    upper,
                                    jnp.broadcast_to(low, (8, LANES)),
                                    jnp.broadcast_to(high, (8, LANES)),
                                )

                            fr = value(0)
                            fi = value(1)
                            at = 2 * (2 * quad + one)
                            sums[at] = sums[at] + (wr * fr - wi * fi)
                            sums[at + 1] = sums[at + 1] + (wr * fi + wi * fr)
            return tuple(sums)

        sums = lax.fori_loop(0, parts, step, sums)
    for pair in range(places // 2):
        real, imag = sums[2 * pair], sums[2 * pair + 1]
        image_ref[2 * pair] = jnp.concatenate([real[:image_rows], imag[:image_rows]], 0)
        image_ref[2 * pair + 1] = jnp.concatenate([real[image_rows:], imag[image_rows:]], 0)
    yield


def far_image_kernel(me_ref, sub_ref, first_table_ref, second_table_ref, weights_ref, *rest):
    *sources_refs, image_ref, left_ref, bands_ref, near_weights_ref, first_ref, second_ref, sem = rest
    work = weighted_sum(
        1 - (sub_ref[0] >> 3), (first_table_ref, second_table_ref), weights_ref, image_ref, left_ref,
        near_weights_ref, first_ref, second_ref, sem,
    )
    next(work)
    sources, band_rows, band = bands_ref.shape
    far_count = len(sources_refs) // 2 + 1
    near_refs, far_refs = sources_refs[:far_count], sources_refs[far_count:]
    near = sources // far_count
    blocks = left_ref.shape[0]
    rows = band_rows // blocks
    half = rows // 2
    count = sources * half
    for dy in range(far_count):
        bands_ref[me_ref[0] ^ (dy * near)] = near_refs[dy][0]
        for dz in range(1, near):
            bands_ref[me_ref[0] ^ (dy * near + dz)] = far_refs[dz - 1][dy]
    for block in range(blocks):
        real = bands_ref[:, block * rows : block * rows + half, :].reshape(count, band)
        imag = bands_ref[:, block * rows + half : (block + 1) * rows, :].reshape(count, band)
        top = jnp.concatenate([real, imag], 1)
        bottom = jnp.concatenate([-imag, real], 1)
        left_ref[block] = jnp.concatenate([top, bottom], 0).T
    next(work)


def near_image_kernel(
    sub_ref, first_table_ref, second_table_ref, weights_ref, left_ref, after_ref, image_ref,
    near_weights_ref, first_ref, second_ref, sem,
):
    work = weighted_sum(
        sub_ref[0] >> 3, (first_table_ref, second_table_ref), weights_ref, image_ref, left_ref,
        near_weights_ref, first_ref, second_ref, sem,
    )
    next(work)
    next(work)


def split_kernel(sub_ref, mine_ref, came_ref, *out_refs):
    width = out_refs[0].shape[0]
    for dx, out_ref in enumerate(out_refs):
        first = ((sub_ref[0] >> 1 & 3) ^ dx) * width
        for core in range(width):
            out_ref[core] = mine_ref[first + core] + came_ref[first + core]


def join_kernel(sub_ref, *refs):
    *piece_refs, keep_ref, send_ref = refs
    for out_ref, core in ((keep_ref, sub_ref[0] & 1), (send_ref, 1 - (sub_ref[0] & 1))):
        out_ref[...] = (piece_refs[0][core] + piece_refs[1][core]) + (
            piece_refs[2][core] + piece_refs[3][core]
        )


def params(mib):
    return pltpu.CompilerParams(vmem_limit_bytes=mib * 1024 * 1024)


def vmem():
    return pl.BlockSpec(memory_space=pltpu.VMEM)


def call(kernel, name, mib, out_shape, in_specs, scratch=()):
    multiple = isinstance(out_shape, list)
    return pl.pallas_call(
        kernel,
        out_shape=out_shape,
        in_specs=in_specs,
        out_specs=[vmem()] * len(out_shape) if multiple else vmem(),
        scratch_shapes=list(scratch),
        compiler_params=params(mib),
        name=name,
    )


def partial_image(echoes, chirp_ref, band_starts, doppler_rates, slot_pulse, interp_weights):
    pulses, _, pulse_len = echoes.shape
    chirp_len = chirp_ref.shape[1]
    blocks, tiles = band_starts.shape
    _, _, band, image_rows, columns = interp_weights.shape
    count = slot_pulse.shape[2]
    lines = 2 * pulse_len // LANES
    span = chirp_len + 2 * LANES
    places = columns // LANES
    parts = places // 2
    near = 4
    far = tiles // near
    smem = pl.BlockSpec(memory_space=pltpu.SMEM)
    anywhere = pl.BlockSpec(memory_space=pl.ANY)
    shape = jax.ShapeDtypeStruct
    sub = lax.axis_index("sub").astype(jnp.int32).reshape(1)
    me = lax.axis_index("tile").astype(jnp.int32).reshape(1)

    samples = echoes.reshape(pulses, 2, pulse_len // LANES, LANES).transpose(0, 2, 1, 3)
    samples = samples.reshape(pulses, lines, LANES)
    weights = interp_weights.reshape(blocks, 2, band, image_rows, places, LANES)
    weights = weights.transpose(0, 1, 2, 4, 3, 5).reshape(
        blocks * 2 * band, places * image_rows, LANES
    )
    own = shape((near, 2 * pulses, band), jnp.bfloat16)
    rates = shape((blocks, count, LANES), jnp.float32)
    *bands, rate = call(
        compress_kernel,
        "compress",
        60,
        [own] * far + [rates],
        [smem, smem] + [anywhere] * 4,
        [
            pltpu.VMEM((2, chirp_len), jnp.bfloat16),
            pltpu.VMEM((1, blocks * count), jnp.float32),
            pltpu.VMEM((blocks, count), jnp.int32),
            pltpu.VMEM((pulses, lines, LANES), jnp.bfloat16),
            pltpu.VMEM((lines // 2 + span // LANES - 1, 2 * pulses, LANES), jnp.bfloat16),
            pltpu.VMEM((tiles * 2 * pulses, span), jnp.bfloat16),
            pltpu.VMEM((4 * LANES, span), jnp.bfloat16),
            pltpu.VMEM((tiles * 2 * pulses, 4 * LANES), jnp.float32),
            pltpu.SemaphoreType.DMA((4,)),
        ],
    )(me, band_starts, chirp_ref, doppler_rates, slot_pulse.reshape(blocks, count), samples)

    def swap(value, distance):
        return lax.ppermute(value, "tile", [(one, one ^ distance) for one in range(tiles)])

    table = shape((parts, 2 * count, 2 * LANES), jnp.bfloat16)
    first_table, rate, mine = call(
        first_phase_kernel,
        "phase",
        16,
        [table, rates, own],
        [anywhere] * 2,
        [pltpu.SemaphoreType.DMA((2,))],
    )(rate, bands[0])
    bands = [mine] + [swap(bands[dy], dy * near) for dy in range(1, far)]
    passed = call(
        relay_kernel,
        "relay",
        16,
        [shape((far, 2 * pulses, band), jnp.bfloat16)] * (near - 1),
        [anywhere] + [vmem()] * far,
    )(first_table, *bands)
    second_table = call(second_phase_kernel, "phase", 16, table, [vmem(), anywhere])(rate, passed[0])
    passed = [swap(passed[dz - 1], dz) for dz in range(1, near)]
    sources = bands + passed
    half = shape((places // 2, 2 * image_rows, LANES), jnp.float32)
    near_weights = pltpu.VMEM((blocks * 2 * band, places // 2 * image_rows, LANES), jnp.bfloat16)
    focused = pltpu.VMEM((parts // 2, 2 * band // 8, 8, 2 * LANES), jnp.float32)
    sems = pltpu.SemaphoreType.DMA((blocks * parts // 2, 2))
    far_image, left = call(
        far_image_kernel,
        "far_image",
        45,
        [half, shape((blocks, 2 * band, 2 * count), jnp.bfloat16)],
        [smem, smem, vmem(), vmem(), anywhere] + [vmem()] * len(sources),
        [
            pltpu.VMEM((tiles, 2 * pulses, band), jnp.bfloat16),
            near_weights,
            focused,
            focused,
            sems,
        ],
    )(me, sub, first_table, second_table, weights, *sources)
    near_image = call(
        near_image_kernel,
        "near_image",
        45,
        half,
        [smem, vmem(), vmem(), anywhere, vmem(), anywhere],
        [near_weights, focused, focused, sems],
    )(sub, first_table, second_table, weights, left, far_image)
    return sub, far_image, near_image


def shards(*args):
    sub, far_image, near_image = partial_image(*args)
    smem = pl.BlockSpec(memory_space=pltpu.SMEM)
    size = 16

    def swap(value, distance):
        return lax.ppermute(value, "sub", [(one, one ^ distance) for one in range(size)])

    came = swap(far_image, 8)
    _, lines, _ = far_image.shape
    pair = jax.ShapeDtypeStruct((2, lines, LANES), jnp.float32)
    one = jax.ShapeDtypeStruct((lines, LANES), jnp.float32)
    pieces = call(split_kernel, "split", 16, [pair] * 4, [smem, vmem(), vmem()])(sub, near_image, came)
    pieces = [pieces[0]] + [swap(pieces[dx], 2 * dx) for dx in range(1, 4)]
    keep, send = call(join_kernel, "join", 16, [one, one], [smem] + [vmem()] * 4)(sub, *pieces)
    return (keep + swap(send, 1)).reshape(2, -1, LANES)


def solution(mesh):
    in_specs = (
        P(("sub", "tile"), None, None),
        P(),
        P("sub", None),
        P("sub", None),
        P("sub", None, None),
        P("sub", None, None, "tile", None),
    )
    out_specs = P(None, "tile", "sub")
    return jax.shard_map(shards, mesh=mesh, in_specs=in_specs, out_specs=out_specs, check_vma=False)
```

time: 55.6 us -> 52.4 us (0.942)
  blocking collectives: 21.2 us -> 0 us
  starting transfers between devices: 9.55 us -> 24.1 us
  waiting for transfers between devices: 6.8 us -> 9.56 us
  Pallas kernels: 14 us -> 15.9 us
  local copies, waits for them, and re-layouts: 3.04 us -> 1.79 us
    all_to_all x1 -> x0, blocking collectives: 21.2 us -> none  [shards(): pieces = lax.all_to_all(image, 'sub', 0, 0, tiled=True)]
    ppermute x0 -> x5, starting transfers between devices: none -> 14.6 us  [swap(): lax.ppermute(value, 'sub', [(one, one ^ distance) for one in range(size)])]
    ppermute x0 -> x5, waiting for transfers between devices: none -> 4.34 us  [swap(): lax.ppermute(value, 'sub', [(one, one ^ distance) for one in range(size)])]
    pallas_call x4 -> x8, Pallas kernels: 14 us -> 15.9 us  [the longest x1 6.05 us: partial_image(): call(compress_kernel, 'compress', 60, [own] * far + [rates], [smem, smem]...]
    ppermute x6, waiting for transfers between devices: 6.8 us -> 5.22 us  [swap(): lax.ppermute(value, 'tile', [(one, one ^ distance) for one in range(tiles)])]
    unnamed x8 -> x4, local copies, waits for them, and re-layouts: 3.04 us -> 1.79 us
    reduce_sum x1 -> x0, other arithmetic: 0.61 us -> none  [shards(): return jnp.sum(pieces, 0).reshape(2, -1, LANES)]
    add x0 -> x1, other arithmetic: none -> 0.59 us  [shards(): return (keep + swap(send, 1)).reshape(2, -1, LANES)]
  transfers between devices with their start and end apart: 6 -> 11, of which waited for: 3 -> 6; matrix products, arithmetic and copies ran while one was open for 0% -> 0% of each run, Pallas kernels for 3% -> 11%
where the time goes in v5:
time: 52.4 us; the launch traced here: 52.1 us
  starting transfers between devices  24.1 us (46%)
  Pallas kernels  15.9 us (30%)
  waiting for transfers between devices  9.56 us (18%)
  local copies, waits for them, and re-layouts  1.79 us (3%)
  other arithmetic  0.59 us (1%)
    ppermute x5, starting transfers between devices, swap(): lax.ppermute(value, 'sub', [(one, one ^ distance) for one in range(size)])  14.6 us
    ppermute x6, starting transfers between devices, swap(): lax.ppermute(value, 'tile', [(one, one ^ distance) for one in range(tiles)])  9.54 us
    pallas_call x1, Pallas kernels, partial_image(): call(compress_kernel, 'compress', 60, [own] * far + [rates], [smem, smem]...  6.05 us
    ppermute x6, waiting for transfers between devices, swap(): lax.ppermute(value, 'tile', [(one, one ^ distance) for one in range(tiles)])  5.22 us
    ppermute x5, waiting for transfers between devices, swap(): lax.ppermute(value, 'sub', [(one, one ^ distance) for one in range(size)])  4.34 us
    pallas_call x1, Pallas kernels, partial_image(): call(far_image_kernel, 'far_image', 45, [half, shape((blocks, 2 * band, 2...  4 us
    pallas_call x1, Pallas kernels, partial_image(): call(near_image_kernel, 'near_image', 45, half, [smem, vmem(), vmem(), an...  3.99 us
    unnamed x4, local copies, waits for them, and re-layouts  1.79 us
  transfers between devices with their start and end apart: 11, of which 6 were waited for; matrix products, arithmetic and copies ran while one was open for 0% of the time, Pallas kernels for 11%

profile of v5, /device:TPU:1, one launch (start us, length us, event | category | flops | bytes accessed | tf_op | source)
XLA Modules:
  0.0 52.1 jit_solution(525249251135681258)
XLA Ops:
  0.0 6.1 %compress.1 = (bf16[4,64,128]{2,1,0:T(8,128)(2,1)}, bf16[4,64,128]{2,1,0:T(8,128)(2,1)}, bf16[4,64,128]{2,1,0:T(8,128)(2,1)}, bf16[4,64,128]{2,1,0:T(8,128)(2,1)}, f32[2,256,128]{2,1,0:T(8,128)}) custom-call(s32[1]{0:T(128)} %bitcast.1.me_ref, s32[2,16]{1,0:T(2,128)} %starts_ref.1, bf16[2,2048]{1,0:T(2,128)(2,1)} %chirp_hbm.1, f32[1,512]{1,0:T(1,128)} %rates_hbm.1, ...), custom_call_target="tpu_custom_call" | custom-call | tf_op jit(solution)/shard_map/compress/pallas_call | solution.py:389
  6.1 2.2 %collective-permute-start = (bf16[4,64,128]{2,1,0:T(8,128)(2,1)}, bf16[4,64,128]{2,1,0:T(8,128)(2,1)S(1)}, u32[]{:S(2)}, u32[]{:S(2)}) collective-permute-start(bf16[4,64,128]{2,1,0:T(8,128)(2,1)} %get-tuple-element.29), channel_id=1, source_target_pairs={{0,4},{1,5},{2,6},{3,7},{4,0},{5,1},{6,2},{7,3},{8,12},{9,13},{10,... | collective-permute-start | bytes 196616 | tf_op jit(solution)/shard_map/ppermute | solution.py:409
  8.3 2.6 %collective-permute-start.1 = (bf16[4,64,128]{2,1,0:T(8,128)(2,1)}, bf16[4,64,128]{2,1,0:T(8,128)(2,1)S(1)}, u32[]{:S(2)}, u32[]{:S(2)}) collective-permute-start(bf16[4,64,128]{2,1,0:T(8,128)(2,1)} %get-tuple-element.30), channel_id=1, source_target_pairs={{0,8},{1,9},{2,10},{3,11},{4,12},{5,13},{6,14},{7,15},{8,0},{9,1},... | collective-permute-start | bytes 196616 | tf_op jit(solution)/shard_map/ppermute | solution.py:409
  10.9 0.0 collective-permute-start.2
  10.9 0.0 copy-start
  10.9 0.9 %copy-done = f32[2,256,128]{2,1,0:T(8,128)S(1)} copy-done((f32[2,256,128]{2,1,0:T(8,128)S(1)}, f32[2,256,128]{2,1,0:T(8,128)}, u32[]{:S(2)}) %copy-start) | copy-done | bytes 262168
  11.8 0.0 copy-start.1
  11.8 0.8 %copy-done.1 = bf16[4,64,128]{2,1,0:T(8,128)(2,1)S(1)} copy-done((bf16[4,64,128]{2,1,0:T(8,128)(2,1)S(1)}, bf16[4,64,128]{2,1,0:T(8,128)(2,1)}, u32[]{:S(2)}) %copy-start.1) | copy-done | bytes 65560
  12.7 1.0 %phase.2 = (bf16[8,512,256]{2,1,0:T(8,128)(2,1)S(1)}, f32[2,256,128]{2,1,0:T(8,128)S(1)}, bf16[4,64,128]{2,1,0:T(8,128)(2,1)S(1)}) custom-call(f32[2,256,128]{2,1,0:T(8,128)S(1)} %copy-done, bf16[4,64,128]{2,1,0:T(8,128)(2,1)S(1)} %copy-done.1), custom_call_target="tpu_custom_call" | custom-call | tf_op jit(solution)/shard_map/phase/pallas_call | solution.py:412
  13.7 0.0 collective-permute-done.refs_1_.rest_1_
  13.7 0.0 collective-permute-done.1.refs_2_.rest_2_
  13.7 1.9 %collective-permute-done.2.refs_3_.rest_3_ = bf16[4,64,128]{2,1,0:T(8,128)(2,1)S(1)} collective-permute-done((bf16[4,64,128]{2,1,0:T(8,128)(2,1)}, bf16[4,64,128]{2,1,0:T(8,128)(2,1)S(1)}, u32[]{:S(2)}, u32[]{:S(2)}) %collective-permute-start.2) | collective-permute-done | bytes 65568 | tf_op jit(solution)/shard_map/ppermute | solution.py:409
  15.6 3.1 %collective-permute-start.4 = (bf16[4,64,128]{2,1,0:T(8,128)(2,1)S(1)}, bf16[4,64,128]{2,1,0:T(8,128)(2,1)S(1)}, u32[]{:S(2)}, u32[]{:S(2)}) collective-permute-start(bf16[4,64,128]{2,1,0:T(8,128)(2,1)S(1)} %get-tuple-element.33), channel_id=1, source_target_pairs={{0,2},{1,3},{2,0},{3,1},{4,6},{5,7},{6,4},{7,5},{8,10},{9,11},{10,... | collective-permute-start | bytes 196616 | tf_op jit(solution)/shard_map/ppermute | solution.py:409
  18.7 1.4 %collective-permute-start.5 = (bf16[4,64,128]{2,1,0:T(8,128)(2,1)S(1)}, bf16[4,64,128]{2,1,0:T(8,128)(2,1)S(1)}, u32[]{:S(2)}, u32[]{:S(2)}) collective-permute-start(bf16[4,64,128]{2,1,0:T(8,128)(2,1)S(1)} %get-tuple-element.34), channel_id=1, source_target_pairs={{0,3},{1,2},{2,1},{3,0},{4,7},{5,6},{6,5},{7,4},{8,11},{9,10},{10,... | collective-permute-start | bytes 196616 | tf_op jit(solution)/shard_map/ppermute | solution.py:409
  20.1 0.2 collective-permute-start.3
  20.3 0.9 %phase.3.second_table_ref = bf16[8,512,256]{2,1,0:T(8,128)(2,1)S(1)} custom-call(f32[2,256,128]{2,1,0:T(8,128)S(1)} %get-tuple-element.27.rate_ref, bf16[4,64,128]{2,1,0:T(8,128)(2,1)S(1)} %get-tuple-element.32.after_ref), custom_call_target="tpu_custom_call" | custom-call | tf_op jit(solution)/shard_map/phase/pallas_call | solution.py:428
  21.1 0.0 collective-permute-done.4.rest_5_
  21.2 2.8 %collective-permute-done.5.rest_6_ = bf16[4,64,128]{2,1,0:T(8,128)(2,1)S(1)} collective-permute-done((bf16[4,64,128]{2,1,0:T(8,128)(2,1)S(1)}, bf16[4,64,128]{2,1,0:T(8,128)(2,1)S(1)}, u32[]{:S(2)}, u32[]{:S(2)}) %collective-permute-start.5) | collective-permute-done | bytes 65568 | tf_op jit(solution)/shard_map/ppermute | solution.py:409
  23.9 0.6 %collective-permute-done.3.rest_4_ = bf16[4,64,128]{2,1,0:T(8,128)(2,1)S(1)} collective-permute-done((bf16[4,64,128]{2,1,0:T(8,128)(2,1)S(1)}, bf16[4,64,128]{2,1,0:T(8,128)(2,1)S(1)}, u32[]{:S(2)}, u32[]{:S(2)}) %collective-permute-start.3) | collective-permute-done | bytes 65568 | tf_op jit(solution)/shard_map/ppermute | solution.py:409
  24.5 4.0 %far_image.1 = (f32[8,8,128]{2,1,0:T(8,128)S(1)}, bf16[2,256,512]{2,1,0:T(8,128)(2,1)S(1)}) custom-call(s32[1]{0:T(128)} %bitcast.1.me_ref, s32[1]{0:T(128)} %bitcast.sub_ref, bf16[8,512,256]{2,1,0:T(8,128)(2,1)S(1)} %get-tuple-element.26.after_ref.first_table_ref, bf16[8,512,256]{2,1,0:T(8,128)(2,1)S(1)} %phase.3.second_table_ref, ...), custom_call_target="tpu_custom_call" | custom-call | tf_op jit(solution)/shard_map/far_image/pallas_call | solution.py:435
  28.5 5.8 %collective-permute-start.6 = (f32[8,8,128]{2,1,0:T(8,128)S(1)}, f32[8,8,128]{2,1,0:T(8,128)S(1)}, u32[]{:S(2)}, u32[]{:S(2)}) collective-permute-start(f32[8,8,128]{2,1,0:T(8,128)S(1)} %get-tuple-element.36.after_ref), channel_id=1, source_target_pairs={{0,128},{16,144},{32,160},{48,176},{64,192},{80,208},{96,224},{112... | collective-permute-start | bytes 98312 | tf_op jit(solution)/shard_map/ppermute | solution.py:466
  34.2 4.0 %near_image.1.mine_ref = f32[8,8,128]{2,1,0:T(8,128)S(1)} custom-call(s32[1]{0:T(128)} %bitcast.sub_ref, bf16[8,512,256]{2,1,0:T(8,128)(2,1)S(1)} %get-tuple-element.26.after_ref.first_table_ref, bf16[8,512,256]{2,1,0:T(8,128)(2,1)S(1)} %phase.3.second_table_ref, bf16[512,64,128]{2,1,0:T(8,128)(2,1)} %bitcast.15, ...), custom_call_target="tpu_custom_call" | custom-call | tf_op jit(solution)/shard_map/near_image/pallas_call | solution.py:449
  38.2 0.0 collective-permute-done.6.came_ref
  38.3 1.3 %collective-permute-start.7 = (f32[2,8,128]{2,1,0:T(8,128)S(1)}, f32[2,8,128]{2,1,0:T(8,128)S(1)}, u32[]{:S(2)}, u32[]{:S(2)}) collective-permute-start(f32[2,8,128]{2,1,0:T(8,128)S(1)} %get-tuple-element.38), channel_id=1, source_target_pairs={{0,32},{16,48},{32,0},{48,16},{64,96},{80,112},{96,64},{112,80},{1... | collective-permute-start | bytes 24584 | tf_op jit(solution)/shard_map/ppermute | solution.py:466
  39.6 2.5 %collective-permute-start.8 = (f32[2,8,128]{2,1,0:T(8,128)S(1)}, f32[2,8,128]{2,1,0:T(8,128)S(1)}, u32[]{:S(2)}, u32[]{:S(2)}) collective-permute-start(f32[2,8,128]{2,1,0:T(8,128)S(1)} %get-tuple-element.39), channel_id=1, source_target_pairs={{0,64},{16,80},{32,96},{48,112},{64,0},{80,16},{96,32},{112,48},{1... | collective-permute-start | bytes 24584 | tf_op jit(solution)/shard_map/ppermute | solution.py:466
  42.0 0.2 collective-permute-start.9
  42.2 0.0 collective-permute-done.7.refs_1_
  42.2 1.4 %collective-permute-done.8.refs_2_ = f32[2,8,128]{2,1,0:T(8,128)S(1)} collective-permute-done((f32[2,8,128]{2,1,0:T(8,128)S(1)}, f32[2,8,128]{2,1,0:T(8,128)S(1)}, u32[]{:S(2)}, u32[]{:S(2)}) %collective-permute-start.8) | collective-permute-done | bytes 8224 | tf_op jit(solution)/shard_map/ppermute | solution.py:466
  43.6 2.2 %collective-permute-done.9.refs_3_ = f32[2,8,128]{2,1,0:T(8,128)S(1)} collective-permute-done((f32[2,8,128]{2,1,0:T(8,128)S(1)}, f32[2,8,128]{2,1,0:T(8,128)S(1)}, u32[]{:S(2)}, u32[]{:S(2)}) %collective-permute-start.9) | collective-permute-done | bytes 8224 | tf_op jit(solution)/shard_map/ppermute | solution.py:466
  45.7 4.9 %collective-permute-start.10 = (f32[8,128]{1,0:T(8,128)S(1)}, f32[8,128]{1,0:T(8,128)S(1)}, u32[]{:S(2)}, u32[]{:S(2)}) collective-permute-start(f32[8,128]{1,0:T(8,128)S(1)} %get-tuple-element.42), channel_id=1, source_target_pairs={{0,16},{16,0},{32,48},{48,32},{64,80},{80,64},{96,112},{112,96},{1... | collective-permute-start | bytes 12296 | tf_op jit(solution)/shard_map/ppermute | solution.py:466
  50.6 0.8 %collective-permute-done.10 = f32[8,128]{1,0:T(8,128)S(1)} collective-permute-done((f32[8,128]{1,0:T(8,128)S(1)}, f32[8,128]{1,0:T(8,128)S(1)}, u32[]{:S(2)}, u32[]{:S(2)}) %collective-permute-start.10) | collective-permute-done | bytes 4128 | tf_op jit(solution)/shard_map/ppermute | solution.py:466
  51.5 0.6 %add.3 = f32[8,128]{1,0:T(8,128)} add(f32[8,128]{1,0:T(8,128)S(1)} %get-tuple-element.41, f32[8,128]{1,0:T(8,128)S(1)} %collective-permute-done.10) | non-fusion elementwise | flops 1024 | bytes 12288 | tf_op jit(solution)/shard_map/add | solution.py:475
  (3 shorter events, 0.0 us)
Async XLA Ops:
  6.1 7.6 %collective-permute-start = (bf16[4,64,128]{2,1,0:T(8,128)(2,1)}, bf16[4,64,128]{2,1,0:T(8,128)(2,1)S(1)}, u32[]{:S(2)}, u32[]{:S(2)}) collective-permute-start(bf16[4,64,128]{2,1,0:T(8,128)(2,1)} %get-tuple-element.29), channel_id=1, source_target_pairs={{0,4},{1,5},{2,6},{3,7},{4,0},{5,1},{6,2},{7,3},{8,12},{9,13},{10,... | collective-permute-start | bytes 196616 | tf_op jit(solution)/shard_map/ppermute | solution.py:409
  8.3 5.4 %collective-permute-start.1 = (bf16[4,64,128]{2,1,0:T(8,128)(2,1)}, bf16[4,64,128]{2,1,0:T(8,128)(2,1)S(1)}, u32[]{:S(2)}, u32[]{:S(2)}) collective-permute-start(bf16[4,64,128]{2,1,0:T(8,128)(2,1)} %get-tuple-element.30), channel_id=1, source_target_pairs={{0,8},{1,9},{2,10},{3,11},{4,12},{5,13},{6,14},{7,15},{8,0},{9,1},... | collective-permute-start | bytes 196616 | tf_op jit(solution)/shard_map/ppermute | solution.py:409
  10.9 4.7 %collective-permute-start.2 = (bf16[4,64,128]{2,1,0:T(8,128)(2,1)}, bf16[4,64,128]{2,1,0:T(8,128)(2,1)S(1)}, u32[]{:S(2)}, u32[]{:S(2)}) collective-permute-start(bf16[4,64,128]{2,1,0:T(8,128)(2,1)} %get-tuple-element.31), channel_id=1, source_target_pairs={{0,12},{1,13},{2,14},{3,15},{4,8},{5,9},{6,10},{7,11},{8,4},{9,5},... | collective-permute-start | bytes 196616 | tf_op jit(solution)/shard_map/ppermute | solution.py:409
  10.9 1.0 %copy-start = (f32[2,256,128]{2,1,0:T(8,128)S(1)}, f32[2,256,128]{2,1,0:T(8,128)}, u32[]{:S(2)}) copy-start(f32[2,256,128]{2,1,0:T(8,128)} %get-tuple-element.24.rate_hbm) | copy-start | bytes 786436
  11.8 0.8 %copy-start.1 = (bf16[4,64,128]{2,1,0:T(8,128)(2,1)S(1)}, bf16[4,64,128]{2,1,0:T(8,128)(2,1)}, u32[]{:S(2)}) copy-start(bf16[4,64,128]{2,1,0:T(8,128)(2,1)} %get-tuple-element.25.bands_hbm) | copy-start | bytes 196612
  15.6 5.6 %collective-permute-start.4 = (bf16[4,64,128]{2,1,0:T(8,128)(2,1)S(1)}, bf16[4,64,128]{2,1,0:T(8,128)(2,1)S(1)}, u32[]{:S(2)}, u32[]{:S(2)}) collective-permute-start(bf16[4,64,128]{2,1,0:T(8,128)(2,1)S(1)} %get-tuple-element.33), channel_id=1, source_target_pairs={{0,2},{1,3},{2,0},{3,1},{4,6},{5,7},{6,4},{7,5},{8,10},{9,11},{10,... | collective-permute-start | bytes 196616 | tf_op jit(solution)/shard_map/ppermute | solution.py:409
  18.7 5.3 %collective-permute-start.5 = (bf16[4,64,128]{2,1,0:T(8,128)(2,1)S(1)}, bf16[4,64,128]{2,1,0:T(8,128)(2,1)S(1)}, u32[]{:S(2)}, u32[]{:S(2)}) collective-permute-start(bf16[4,64,128]{2,1,0:T(8,128)(2,1)S(1)} %get-tuple-element.34), channel_id=1, source_target_pairs={{0,3},{1,2},{2,1},{3,0},{4,7},{5,6},{6,5},{7,4},{8,11},{9,10},{10,... | collective-permute-start | bytes 196616 | tf_op jit(solution)/shard_map/ppermute | solution.py:409
  20.1 4.4 %collective-permute-start.3 = (bf16[4,64,128]{2,1,0:T(8,128)(2,1)S(1)}, bf16[4,64,128]{2,1,0:T(8,128)(2,1)S(1)}, u32[]{:S(2)}, u32[]{:S(2)}) collective-permute-start(bf16[4,64,128]{2,1,0:T(8,128)(2,1)S(1)} %get-tuple-element.32.after_ref), channel_id=1, source_target_pairs={{0,1},{1,0},{2,3},{3,2},{4,5},{5,4},{6,7},{7,6},{8,9},{9,8},{10,11... | collective-permute-start | bytes 196616 | tf_op jit(solution)/shard_map/ppermute | solution.py:409
  28.5 9.8 %collective-permute-start.6 = (f32[8,8,128]{2,1,0:T(8,128)S(1)}, f32[8,8,128]{2,1,0:T(8,128)S(1)}, u32[]{:S(2)}, u32[]{:S(2)}) collective-permute-start(f32[8,8,128]{2,1,0:T(8,128)S(1)} %get-tuple-element.36.after_ref), channel_id=1, source_target_pairs={{0,128},{16,144},{32,160},{48,176},{64,192},{80,208},{96,224},{112... | collective-permute-start | bytes 98312 | tf_op jit(solution)/shard_map/ppermute | solution.py:466
  38.3 3.9 %collective-permute-start.7 = (f32[2,8,128]{2,1,0:T(8,128)S(1)}, f32[2,8,128]{2,1,0:T(8,128)S(1)}, u32[]{:S(2)}, u32[]{:S(2)}) collective-permute-start(f32[2,8,128]{2,1,0:T(8,128)S(1)} %get-tuple-element.38), channel_id=1, source_target_pairs={{0,32},{16,48},{32,0},{48,16},{64,96},{80,112},{96,64},{112,80},{1... | collective-permute-start | bytes 24584 | tf_op jit(solution)/shard_map/ppermute | solution.py:466
  39.6 4.0 %collective-permute-start.8 = (f32[2,8,128]{2,1,0:T(8,128)S(1)}, f32[2,8,128]{2,1,0:T(8,128)S(1)}, u32[]{:S(2)}, u32[]{:S(2)}) collective-permute-start(f32[2,8,128]{2,1,0:T(8,128)S(1)} %get-tuple-element.39), channel_id=1, source_target_pairs={{0,64},{16,80},{32,96},{48,112},{64,0},{80,16},{96,32},{112,48},{1... | collective-permute-start | bytes 24584 | tf_op jit(solution)/shard_map/ppermute | solution.py:466
  42.0 3.7 %collective-permute-start.9 = (f32[2,8,128]{2,1,0:T(8,128)S(1)}, f32[2,8,128]{2,1,0:T(8,128)S(1)}, u32[]{:S(2)}, u32[]{:S(2)}) collective-permute-start(f32[2,8,128]{2,1,0:T(8,128)S(1)} %get-tuple-element.40), channel_id=1, source_target_pairs={{0,96},{16,112},{32,64},{48,80},{64,32},{80,48},{96,0},{112,16},{1... | collective-permute-start | bytes 24584 | tf_op jit(solution)/shard_map/ppermute | solution.py:466
  45.7 5.7 %collective-permute-start.10 = (f32[8,128]{1,0:T(8,128)S(1)}, f32[8,128]{1,0:T(8,128)S(1)}, u32[]{:S(2)}, u32[]{:S(2)}) collective-permute-start(f32[8,128]{1,0:T(8,128)S(1)} %get-tuple-element.42), channel_id=1, source_target_pairs={{0,16},{16,0},{32,48},{48,32},{64,80},{80,64},{96,112},{112,96},{1... | collective-permute-start | bytes 12296 | tf_op jit(solution)/shard_map/ppermute | solution.py:466

commit v6 on v5

v6 whole, which is shorter than its diff:
```python
import jax
import jax.numpy as jnp
import numpy as np
from jax import lax
from jax.experimental import pallas as pl
from jax.experimental.pallas import tpu as pltpu
from jax.sharding import PartitionSpec as P

LANES = 128


def compress_kernel(
    me_ref, starts_ref, chirp_hbm, rates_hbm, slots_hbm, echoes_ref, *rest
):
    (
        *bands_refs, extra_ref, chirp_ref, rates_ref, slots_ref, raw_ref, samples_ref, lhs_ref, toeplitz_ref,
        product_ref, sems,
    ) = rest
    fetches = [
        pltpu.make_async_copy(source, target, sems.at[index])
        for index, (source, target) in enumerate(
            (
                (chirp_hbm, chirp_ref),
                (rates_hbm, rates_ref),
                (slots_hbm, slots_ref),
                (echoes_ref, raw_ref),
            )
        )
    ]
    for fetch in fetches:
        fetch.start()
    span = toeplitz_ref.shape[1]
    blocks, tiles = starts_ref.shape
    near = tiles // (len(bands_refs) + 1)
    pulses, lines, _ = raw_ref.shape
    half = pulses // blocks
    rows = 2 * half
    chunks = span // LANES
    fetches[0].wait()
    chirp = chirp_ref[...].astype(jnp.float32)
    pad = jnp.zeros((1, span - chirp.shape[1]), jnp.float32)
    for part in range(2):
        line = jnp.concatenate([chirp[part : part + 1], pad], 1)
        shifted = pltpu.roll(
            jnp.broadcast_to(line, (LANES, span)), 0, 1, stride=1, stride_axis=0
        ).astype(jnp.bfloat16)
        base = part * 2 * LANES
        toeplitz_ref[base : base + LANES, :] = shifted
        toeplitz_ref[base + LANES : base + 2 * LANES, :LANES] = jnp.zeros((LANES, LANES), jnp.bfloat16)
        toeplitz_ref[base + LANES : base + 2 * LANES, LANES:] = shifted[:, : span - LANES]
    fetches[1].wait()
    fetches[2].wait()
    count = slots_ref.shape[1]
    row = lax.broadcasted_iota(jnp.int32, (count, count), 0)
    col = lax.broadcasted_iota(jnp.int32, (count, count), 1)
    for block in range(blocks):
        slots = slots_ref[block : block + 1, :].astype(jnp.float32)
        slot = jnp.sum(jnp.where(row == col, slots, 0.0), 1, keepdims=True)
        rates = rates_ref[:, block * count : (block + 1) * count]
        rate = jnp.sum(jnp.where(slot == col.astype(jnp.float32), rates, 0.0), 1, keepdims=True)
        extra_ref[block * count : (block + 1) * count, :] = jnp.broadcast_to(rate, (count, LANES))
    samples_ref[lines // 2 :] = jnp.zeros(
        (samples_ref.shape[0] - lines // 2, 2 * pulses, LANES), jnp.bfloat16
    )
    piece = 16
    side = half * piece
    row = lax.broadcasted_iota(jnp.int32, (side, side), 0)
    col = lax.broadcasted_iota(jnp.int32, (side, side), 1)
    order = jnp.where(col == (row % half) * piece + row // half, 1.0, 0.0).astype(jnp.bfloat16)
    fetches[3].wait()
    for group in range(lines // piece):
        block_rows = jnp.concatenate(
            [
                raw_ref[block * half : (block + 1) * half, group * piece : (group + 1) * piece, :].reshape(
                    side, LANES
                )
                for block in range(blocks)
            ],
            1,
        )
        moved = jnp.dot(order, block_rows, preferred_element_type=jnp.float32).astype(jnp.bfloat16)
        for block in range(blocks):
            samples_ref[
                group * piece // 2 : (group + 1) * piece // 2, block * rows : (block + 1) * rows, :
            ] = moved[:, block * LANES : (block + 1) * LANES].reshape(piece // 2, rows, LANES)
    for block in range(blocks):
        for tile in range(tiles):
            first = starts_ref[block, me_ref[0] ^ tile] // LANES
            place = (block * tiles + tile) * rows
            for chunk in range(chunks):
                lhs_ref[place : place + rows, chunk * LANES : (chunk + 1) * LANES] = samples_ref[
                    first + chunk, block * rows : (block + 1) * rows, :
                ]
    product_ref[...] = lax.dot_general(
        lhs_ref[...], toeplitz_ref[...], (((1,), (1,)), ((), ())), preferred_element_type=jnp.float32
    )
    lane = lax.broadcasted_iota(jnp.int32, (half, LANES), 1)
    for block in range(blocks):
        for tile in range(tiles):
            place = (block * tiles + tile) * rows
            shift = starts_ref[block, me_ref[0] ^ tile] % LANES
            turn = (LANES - shift) % LANES
            keep = lane < LANES - shift

            def piece(part, column):
                top = place + part * half
                low = product_ref[top : top + half, column * 2 * LANES : column * 2 * LANES + LANES]
                high = product_ref[top : top + half, column * 2 * LANES + LANES : (column + 1) * 2 * LANES]
                return low, high

            rr, ri = piece(0, 0), piece(0, 1)
            ir, ii = piece(1, 0), piece(1, 1)
            for part, (low, high) in enumerate(
                ((rr[0] + ii[0], rr[1] + ii[1]), (ir[0] - ri[0], ir[1] - ri[1]))
            ):
                cut = jnp.where(keep, pltpu.roll(low, turn, 1), pltpu.roll(high, turn, 1))
                top = block * rows + part * half
                cut = cut.astype(jnp.bfloat16)
                if tile < near:
                    top += blocks * count + tile * 2 * pulses
                    extra_ref[top : top + half, :] = cut.astype(jnp.float32)
                else:
                    bands_refs[tile // near - 1][tile % near, top : top + half, :] = cut


def sine_cosine(angle):
    turns = jnp.round(angle * np.float32(2 / np.pi))
    rest = (angle - turns * np.float32(1.5703125)) - turns * np.float32(np.pi / 2 - 1.5703125)
    quarter = turns.astype(jnp.int32)
    sq = rest * rest
    sine = np.float32(1 / 362880) * sq + np.float32(-1 / 5040)
    sine = sine * sq + np.float32(1 / 120)
    sine = sine * sq + np.float32(-1 / 6)
    sine = sine * sq * rest + rest
    cosine = np.float32(1 / 40320) * sq + np.float32(-1 / 720)
    cosine = cosine * sq + np.float32(1 / 24)
    cosine = cosine * sq + np.float32(-1 / 2)
    cosine = cosine * sq + np.float32(1)
    odd = (quarter & 1) == 1
    sin_out = jnp.where(odd, cosine, sine)
    cos_out = jnp.where(odd, sine, cosine)
    sin_out = jnp.where((quarter & 2) == 2, -sin_out, sin_out)
    cos_out = jnp.where(((quarter + 1) & 2) == 2, -cos_out, cos_out)
    return sin_out, cos_out


def phase_kernel(extra_ref, first_table_ref, second_table_ref, bands_ref):
    count = first_table_ref.shape[1] // 2
    bands_ref[...] = extra_ref[2 * count :].astype(jnp.bfloat16).reshape(bands_ref.shape)
    phase_table(0, extra_ref, first_table_ref)
    phase_table(1, extra_ref, second_table_ref)


def turn_kernel(weights_ref, after_ref, first_ref, second_ref):
    band = first_ref.shape[2]
    lines = first_ref.shape[1]
    size = 16
    side = size * size
    row = lax.broadcasted_iota(jnp.int32, (side, side), 0)
    col = lax.broadcasted_iota(jnp.int32, (side, side), 1)
    order = jnp.where(col == (row % size) * size + row // size, 1.0, 0.0).astype(jnp.bfloat16)
    for block, out_ref in enumerate((first_ref, second_ref)):
        for part in range(2):

            def step(chunk, carry, block=block, part=part, out_ref=out_ref):
                first = pl.multiple_of(chunk * size, size)
                for pair in range(lines // (2 * size)):
                    tops = [(2 * pair + one) * size for one in range(2)]
                    block_rows = jnp.concatenate(
                        [
                            weights_ref[
                                pl.ds((block * 2 + part) * band + first, size), top : top + size, :
                            ].reshape(side, LANES)
                            for top in tops
                        ],
                        1,
                    )
                    moved = jnp.dot(order, block_rows, preferred_element_type=jnp.float32).astype(
                        jnp.bfloat16
                    )
                    for one, top in enumerate(tops):
                        out_ref[part, top : top + size, pl.ds(first, size), :] = moved[
                            :, one * LANES : (one + 1) * LANES
                        ].reshape(size, size, LANES)
                return carry

            lax.fori_loop(0, band // size, step, 0, unroll=True)


def phase_table(block, rate_ref, table_ref):
    count = table_ref.shape[1] // 2
    columns = table_ref.shape[0] * table_ref.shape[2]
    lane = lax.broadcasted_iota(jnp.int32, (32, LANES), 1).astype(jnp.float32)
    place = (lane + 0.5) * np.float32(1 / columns) - 0.5
    for group in range(count // 32):
        span = slice(group * 32, group * 32 + 32)
        rate = rate_ref[block * count + group * 32 : block * count + group * 32 + 32, :]
        sine, cosine = sine_cosine(rate * place)
        step_sine, step_cosine = sine_cosine(rate * np.float32(LANES / columns))
        for chunk in range(columns // LANES):
            if chunk > 0:
                sine, cosine = (
                    sine * step_cosine + cosine * step_sine,
                    cosine * step_cosine - sine * step_sine,
                )
            lanes = slice(chunk % 2 * LANES, (chunk % 2 + 1) * LANES)
            table_ref[chunk // 2, span, lanes] = cosine.astype(jnp.bfloat16)
            table_ref[chunk // 2, count + group * 32 : count + group * 32 + 32, lanes] = (
                sine.astype(jnp.bfloat16)
            )


def relay_kernel(after_ref, *refs):
    near = refs[0].shape[0]
    far = len(refs) - near + 1
    for dz in range(1, near):
        for dy in range(far):
            refs[far + dz - 1][dy] = refs[dy][dz]


def weighted_sum(side, table_refs, weights_refs, image_ref, left_ref, focused_refs):
    blocks = len(table_refs)
    places, lines, _ = image_ref.shape
    image_rows = lines // 2
    pairs = places // 2
    band = weights_refs[0].shape[2]

    def focus(pair):
        for block in range(blocks):
            focused_refs[pair % 2 * blocks + block][...] = jnp.dot(
                left_ref[block], table_refs[block][side * pairs + pair], preferred_element_type=jnp.float32
            )

    focus(0)
    for pair in range(pairs):
        if pair + 1 < pairs:
            focus(pair + 1)
        for place in range(2):
            lanes = slice(place * LANES, (place + 1) * LANES)
            real = [jnp.zeros((8, LANES), jnp.float32)] * image_rows
            imag = [jnp.zeros((8, LANES), jnp.float32)] * image_rows
            for block in range(blocks):
                focused_ref = focused_refs[pair % 2 * blocks + block]
                for k in range(0, band, 16):
                    focus_real = focused_ref[k : k + 16, lanes]
                    focus_imag = focused_ref[band + k : band + k + 16, lanes]
                    for row in range(image_rows):
                        line = (side * places + 2 * pair + place) * image_rows + row
                        weight_real = weights_refs[block][0, line, k : k + 16, :].astype(jnp.float32)
                        weight_imag = weights_refs[block][1, line, k : k + 16, :].astype(jnp.float32)
                        for first in (0, 8):
                            part = slice(first, first + 8)
                            wr, wi = weight_real[part], weight_imag[part]
                            fr, fi = focus_real[part], focus_imag[part]
                            real[row] = real[row] + (wr * fr - wi * fi)
                            imag[row] = imag[row] + (wr * fi + wi * fr)
            image_ref[2 * pair + place] = jnp.concatenate(
                [jnp.sum(one, 0, keepdims=True) for one in real + imag], 0
            )


def far_image_kernel(
    me_ref, sub_ref, first_table_ref, second_table_ref, first_weights_ref, second_weights_ref, *rest
):
    *sources_refs, image_ref, left_ref, bands_ref, one_ref, two_ref, three_ref, four_ref = rest
    sources, band_rows, band = bands_ref.shape
    far_count = len(sources_refs) // 2 + 1
    near_refs, far_refs = sources_refs[:far_count], sources_refs[far_count:]
    near = sources // far_count
    blocks = left_ref.shape[0]
    rows = band_rows // blocks
    half = rows // 2
    count = sources * half
    for dy in range(far_count):
        bands_ref[me_ref[0] ^ (dy * near)] = near_refs[dy][0]
        for dz in range(1, near):
            bands_ref[me_ref[0] ^ (dy * near + dz)] = far_refs[dz - 1][dy]
    for block in range(blocks):
        real = bands_ref[:, block * rows : block * rows + half, :].reshape(count, band)
        imag = bands_ref[:, block * rows + half : (block + 1) * rows, :].reshape(count, band)
        top = jnp.concatenate([real, imag], 1)
        bottom = jnp.concatenate([-imag, real], 1)
        left_ref[block] = jnp.concatenate([top, bottom], 0).T
    weighted_sum(
        1 - (sub_ref[0] >> 3),
        (first_table_ref, second_table_ref),
        (first_weights_ref, second_weights_ref),
        image_ref,
        left_ref,
        (one_ref, two_ref, three_ref, four_ref),
    )


def near_image_kernel(
    sub_ref, first_table_ref, second_table_ref, first_weights_ref, second_weights_ref, left_ref, after_ref,
    image_ref, one_ref, two_ref, three_ref, four_ref,
):
    weighted_sum(
        sub_ref[0] >> 3,
        (first_table_ref, second_table_ref),
        (first_weights_ref, second_weights_ref),
        image_ref,
        left_ref,
        (one_ref, two_ref, three_ref, four_ref),
    )


def params(mib):
    return pltpu.CompilerParams(vmem_limit_bytes=mib * 1024 * 1024)


def vmem():
    return pl.BlockSpec(memory_space=pltpu.VMEM)


def call(kernel, name, mib, out_shape, in_specs, scratch=(), flops=0):
    multiple = isinstance(out_shape, list)
    return pl.pallas_call(
        kernel,
        out_shape=out_shape,
        in_specs=in_specs,
        out_specs=[vmem()] * len(out_shape) if multiple else vmem(),
        scratch_shapes=list(scratch),
        compiler_params=params(mib),
        cost_estimate=pl.CostEstimate(flops=flops, bytes_accessed=0, transcendentals=0),
        name=name,
    )


def partial_image(echoes, chirp_ref, band_starts, doppler_rates, slot_pulse, interp_weights):
    pulses, _, pulse_len = echoes.shape
    chirp_len = chirp_ref.shape[1]
    blocks, tiles = band_starts.shape
    _, _, band, image_rows, columns = interp_weights.shape
    count = slot_pulse.shape[2]
    lines = 2 * pulse_len // LANES
    span = chirp_len + 2 * LANES
    places = columns // LANES
    parts = places // 2
    near = 4
    far = tiles // near
    smem = pl.BlockSpec(memory_space=pltpu.SMEM)
    anywhere = pl.BlockSpec(memory_space=pl.ANY)
    shape = jax.ShapeDtypeStruct
    sub = lax.axis_index("sub").astype(jnp.int32).reshape(1)
    me = lax.axis_index("tile").astype(jnp.int32).reshape(1)

    samples = echoes.reshape(pulses, 2, pulse_len // LANES, LANES).transpose(0, 2, 1, 3)
    samples = samples.reshape(pulses, lines, LANES)
    weights = interp_weights.reshape(blocks, 2, band, image_rows, places, LANES)
    weights = weights.transpose(0, 1, 2, 4, 3, 5).reshape(
        blocks * 2 * band, places * image_rows, LANES
    )
    own = shape((near, 2 * pulses, band), jnp.bfloat16)
    extras = shape((blocks * count + near * 2 * pulses, LANES), jnp.float32)
    *bands, extra = call(
        compress_kernel,
        "compress",
        60,
        [own] * (far - 1) + [extras],
        [smem, smem] + [anywhere] * 4,
        [
            pltpu.VMEM((2, chirp_len), jnp.bfloat16),
            pltpu.VMEM((1, blocks * count), jnp.float32),
            pltpu.VMEM((blocks, count), jnp.int32),
            pltpu.VMEM((pulses, lines, LANES), jnp.bfloat16),
            pltpu.VMEM((lines // 2 + span // LANES - 1, 2 * pulses, LANES), jnp.bfloat16),
            pltpu.VMEM((tiles * 2 * pulses, span), jnp.bfloat16),
            pltpu.VMEM((4 * LANES, span), jnp.bfloat16),
            pltpu.VMEM((tiles * 2 * pulses, 4 * LANES), jnp.float32),
            pltpu.SemaphoreType.DMA((4,)),
        ],
        flops=6 * 10**9,
    )(me, band_starts, chirp_ref, doppler_rates, slot_pulse.reshape(blocks, count), samples)

    def swap(value, distance):
        return lax.ppermute(value, "tile", [(one, one ^ distance) for one in range(tiles)])

    table = shape((parts, 2 * count, 2 * LANES), jnp.bfloat16)
    turned = shape((2, places * image_rows, band, LANES), jnp.bfloat16)
    first_table, second_table, mine = call(phase_kernel, "phase", 12, [table, table, own], [vmem()], flops=4 * 10**9)(extra)
    bands = [mine] + [swap(bands[dy - 1], dy * near) for dy in range(1, far)]
    passed = call(
        relay_kernel,
        "relay",
        16,
        [shape((far, 2 * pulses, band), jnp.bfloat16)] * (near - 1),
        [anywhere] + [vmem()] * far,
    )(first_table, *bands)
    first_weights, second_weights = call(turn_kernel, "turn", 12, [turned, turned], [vmem(), anywhere], flops=4 * 10**9)(
        weights, passed[0]
    )
    passed = [swap(passed[dz - 1], dz) for dz in range(1, near)]
    sources = bands + passed
    half = shape((places // 2, 2 * image_rows, LANES), jnp.float32)
    focused = [pltpu.VMEM((2 * band, 2 * LANES), jnp.float32)] * (2 * blocks)
    far_image, left = call(
        far_image_kernel,
        "far_image",
        12,
        [half, shape((blocks, 2 * band, 2 * count), jnp.bfloat16)],
        [smem, smem] + [vmem()] * (4 + len(sources)),
        [pltpu.VMEM((tiles, 2 * pulses, band), jnp.bfloat16)] + focused,
        flops=3 * 10**9,
    )(me, sub, first_table, second_table, first_weights, second_weights, *sources)
    near_image = call(
        near_image_kernel, "near_image", 12, half, [smem] + [vmem()] * 5 + [anywhere], focused, flops=3 * 10**9
    )(sub, first_table, second_table, first_weights, second_weights, left, far_image)
    return sub, far_image, near_image


def shards(*args):
    _, far_image, near_image = partial_image(*args)
    size = 16
    half = size // 2
    came = lax.ppermute(far_image, "sub", [(one, one ^ half) for one in range(size)])
    groups = [list(range(half)), list(range(half, size))]
    pieces = lax.all_to_all(near_image + came, "sub", 0, 0, axis_index_groups=groups, tiled=True)
    return jnp.sum(pieces, 0).reshape(2, -1, LANES)


def solution(mesh):
    in_specs = (
        P(("sub", "tile"), None, None),
        P(),
        P("sub", None),
        P("sub", None),
        P("sub", None, None),
        P("sub", None, None, "tile", None),
    )
    out_specs = P(None, "tile", "sub")
    return jax.shard_map(shards, mesh=mesh, in_specs=in_specs, out_specs=out_specs, check_vma=False)
```

time: 52.4 us -> 49 us (0.935)
  blocking collectives: 0 us -> 12 us
  starting transfers between devices: 24.1 us -> 14.7 us
  waiting for transfers between devices: 9.56 us -> 0.64 us
  local copies, waits for them, and re-layouts: 1.79 us -> 5.7 us
  Pallas kernels: 15.9 us -> 14.9 us
    all_to_all x0 -> x1, blocking collectives: none -> 12 us  [shards(): lax.all_to_all(near_image + came, 'sub', 0, 0, axis_index_groups=groups,...]
    ppermute x5 -> x1, starting transfers between devices: 14.6 us -> 5.19 us  [shards(): lax.ppermute(far_image, 'sub', [(one, one ^ half) for one in range(size)])]
    ppermute x6, waiting for transfers between devices: 5.22 us -> 0.63 us  [swap(): lax.ppermute(value, 'tile', [(one, one ^ distance) for one in range(tiles)])]
    ppermute x5 -> x1, waiting for transfers between devices: 4.34 us -> 0.01 us  [shards(): lax.ppermute(far_image, 'sub', [(one, one ^ half) for one in range(size)])]
    unnamed x4 -> x8, local copies, waits for them, and re-layouts: 1.79 us -> 5.7 us
    pallas_call x7 -> x5, Pallas kernels: 15.9 us -> 14.9 us  [the longest x1 6.01 us: partial_image(): call(compress_kernel, 'compress', 60, [own] * (far - 1) + [extras], [smem...]
    reduce_sum x0 -> x1, other arithmetic: none -> 0.6 us  [shards(): return jnp.sum(pieces, 0).reshape(2, -1, LANES)]
    add x1, other arithmetic: 0.59 us -> 0.01 us  [shards(): near_image + came]
  transfers between devices with their start and end apart: 11 -> 7, of which waited for: 6 -> 1; matrix products, arithmetic and copies ran while one was open for 0% -> 0% of each run, Pallas kernels for 11% -> 13%
where the time goes in v6:
time: 49 us; the launch traced here: 48.7 us
  Pallas kernels  14.9 us (30%)
  starting transfers between devices  14.7 us (30%)
  blocking collectives  12 us (24%)
  local copies, waits for them, and re-layouts  5.7 us (12%)
  waiting for transfers between devices  0.64 us (1%)
  other arithmetic  0.61 us (1%)
    all_to_all x1, blocking collectives, shards(): lax.all_to_all(near_image + came, 'sub', 0, 0, axis_index_groups=groups,...  12 us
    ppermute x6, starting transfers between devices, swap(): lax.ppermute(value, 'tile', [(one, one ^ distance) for one in range(tiles)])  9.55 us
    pallas_call x1, Pallas kernels, partial_image(): call(compress_kernel, 'compress', 60, [own] * (far - 1) + [extras], [smem...  6.01 us
    unnamed x8, local copies, waits for them, and re-layouts  5.7 us
    ppermute x1, starting transfers between devices, shards(): lax.ppermute(far_image, 'sub', [(one, one ^ half) for one in range(size)])  5.19 us
    pallas_call x1, Pallas kernels, partial_image(): call(near_image_kernel, 'near_image', 12, half, [smem] + [vmem()] * 5 + [...  2.51 us
    pallas_call x1, Pallas kernels, partial_image(): call(far_image_kernel, 'far_image', 12, [half, shape((blocks, 2 * band, 2...  2.35 us
    pallas_call x1, Pallas kernels, partial_image(): call(turn_kernel, 'turn', 12, [turned, turned], [vmem(), anywhere], flops...  2.35 us
  transfers between devices with their start and end apart: 7, of which 1 were waited for; matrix products, arithmetic and copies ran while one was open for 0% of the time, Pallas kernels for 13%

profile of v6, /device:TPU:1, one launch (start us, length us, event | category | flops | bytes accessed | tf_op | source)
XLA Modules:
  0.0 48.7 jit_solution(6910139245851648624)
XLA Ops:
  0.0 6.0 %compress.1 = (bf16[4,64,128]{2,1,0:T(8,128)(2,1)}, bf16[4,64,128]{2,1,0:T(8,128)(2,1)}, bf16[4,64,128]{2,1,0:T(8,128)(2,1)}, f32[768,128]{1,0:T(8,128)}) custom-call(s32[1]{0:T(128)} %bitcast.1.me_ref, s32[2,16]{1,0:T(2,128)} %starts_ref.1, bf16[2,2048]{1,0:T(2,128)(2,1)} %chirp_hbm.1, f32[1,512]{1,0:T(1,128)} %rates_hbm.1, s32[2,256]{1,0:T(2,128)} %bitcast.16, ...), custom_call_target="tpu_custom_call" | custom-call | flops 6000000000 | tf_op jit(solution)/shard_map/compress/pallas_call | solution.py:356
  6.0 2.2 %collective-permute-start = (bf16[4,64,128]{2,1,0:T(8,128)(2,1)}, bf16[4,64,128]{2,1,0:T(8,128)(2,1)S(1)}, u32[]{:S(2)}, u32[]{:S(2)}) collective-permute-start(bf16[4,64,128]{2,1,0:T(8,128)(2,1)} %get-tuple-element.23), channel_id=1, source_target_pairs={{0,4},{1,5},{2,6},{3,7},{4,0},{5,1},{6,2},{7,3},{8,12},{9,13},{10,... | collective-permute-start | bytes 196616 | tf_op jit(solution)/shard_map/ppermute | solution.py:377
  8.2 2.6 %collective-permute-start.1 = (bf16[4,64,128]{2,1,0:T(8,128)(2,1)}, bf16[4,64,128]{2,1,0:T(8,128)(2,1)S(1)}, u32[]{:S(2)}, u32[]{:S(2)}) collective-permute-start(bf16[4,64,128]{2,1,0:T(8,128)(2,1)} %get-tuple-element.24), channel_id=1, source_target_pairs={{0,8},{1,9},{2,10},{3,11},{4,12},{5,13},{6,14},{7,15},{8,0},{9,1},... | collective-permute-start | bytes 196616 | tf_op jit(solution)/shard_map/ppermute | solution.py:377
  10.9 0.0 collective-permute-start.2
  10.9 0.0 copy-start.3
  10.9 1.0 %copy-done.3 = f32[768,128]{1,0:T(8,128)S(1)} copy-done((f32[768,128]{1,0:T(8,128)S(1)}, f32[768,128]{1,0:T(8,128)}, u32[]{:S(2)}) %copy-start.3) | copy-done | bytes 393240
  11.9 1.7 %phase.1 = (bf16[8,512,256]{2,1,0:T(8,128)(2,1)S(1)}, bf16[8,512,256]{2,1,0:T(8,128)(2,1)S(1)}, bf16[4,64,128]{2,1,0:T(8,128)(2,1)S(1)}) custom-call(f32[768,128]{1,0:T(8,128)S(1)} %copy-done.3), custom_call_target="tpu_custom_call" | custom-call | flops 4000000000 | tf_op jit(solution)/shard_map/phase/pallas_call | solution.py:381
  13.6 0.0 copy-start
  13.6 1.3 %copy-done = bf16[8,512,256]{2,1,0:T(8,128)(2,1)} copy-done((bf16[8,512,256]{2,1,0:T(8,128)(2,1)}, bf16[8,512,256]{2,1,0:T(8,128)(2,1)S(1)}, u32[]{:S(2)}) %copy-start) | copy-done | bytes 2097176
  14.9 0.0 collective-permute-done.refs_1_.rest_1_
  14.9 0.0 collective-permute-done.1.refs_2_.rest_2_
  14.9 0.6 %collective-permute-done.2.refs_3_.rest_3_ = bf16[4,64,128]{2,1,0:T(8,128)(2,1)S(1)} collective-permute-done((bf16[4,64,128]{2,1,0:T(8,128)(2,1)}, bf16[4,64,128]{2,1,0:T(8,128)(2,1)S(1)}, u32[]{:S(2)}, u32[]{:S(2)}) %collective-permute-start.2) | collective-permute-done | bytes 65568 | tf_op jit(solution)/shard_map/ppermute | solution.py:377
  15.5 3.1 %collective-permute-start.4 = (bf16[4,64,128]{2,1,0:T(8,128)(2,1)S(1)}, bf16[4,64,128]{2,1,0:T(8,128)(2,1)S(1)}, u32[]{:S(2)}, u32[]{:S(2)}) collective-permute-start(bf16[4,64,128]{2,1,0:T(8,128)(2,1)S(1)} %get-tuple-element.29), channel_id=1, source_target_pairs={{0,2},{1,3},{2,0},{3,1},{4,6},{5,7},{6,4},{7,5},{8,10},{9,11},{10,... | collective-permute-start | bytes 196616 | tf_op jit(solution)/shard_map/ppermute | solution.py:377
  18.6 1.5 %collective-permute-start.5 = (bf16[4,64,128]{2,1,0:T(8,128)(2,1)S(1)}, bf16[4,64,128]{2,1,0:T(8,128)(2,1)S(1)}, u32[]{:S(2)}, u32[]{:S(2)}) collective-permute-start(bf16[4,64,128]{2,1,0:T(8,128)(2,1)S(1)} %get-tuple-element.30), channel_id=1, source_target_pairs={{0,3},{1,2},{2,1},{3,0},{4,7},{5,6},{6,5},{7,4},{8,11},{9,10},{10,... | collective-permute-start | bytes 196616 | tf_op jit(solution)/shard_map/ppermute | solution.py:377
  20.1 0.2 collective-permute-start.3
  20.3 0.0 copy-start.2
  20.3 3.4 %copy-done.2 = bf16[2,2,128,4,2048]{4,3,2,1,0:T(4,128)(2,1)S(1)} copy-done((bf16[2,2,128,4,2048]{4,3,2,1,0:T(4,128)(2,1)S(1)}, bf16[2,2,128,4,2048]{4,3,2,1,0:T(4,128)(2,1)}, u32[]{:S(2)}) %copy-start.2) | copy-done | bytes 8388632
  23.6 0.0 copy-start.1
  23.6 2.3 %turn.1 = (bf16[2,64,128,128]{3,2,1,0:T(8,128)(2,1)S(1)}, bf16[2,64,128,128]{3,2,1,0:T(8,128)(2,1)S(1)}) custom-call(bf16[512,64,128]{2,1,0:T(8,128)(2,1)S(1)} %bitcast.14, bf16[4,64,128]{2,1,0:T(8,128)(2,1)S(1)} %get-tuple-element.26.after_ref), custom_call_target="tpu_custom_call" | custom-call | flops 4000000000 | tf_op jit(solution)/shard_map/turn/pallas_call | solution.py:390
  26.0 0.0 collective-permute-done.4.rest_5_
  26.0 0.0 collective-permute-done.5.rest_6_
  26.0 0.0 collective-permute-done.3.rest_4_
  26.0 0.0 copy-done.1
  26.0 2.4 %far_image.1 = (f32[8,8,128]{2,1,0:T(8,128)S(1)}, bf16[2,256,512]{2,1,0:T(8,128)(2,1)S(1)}) custom-call(s32[1]{0:T(128)} %bitcast.1.me_ref, s32[1]{0:T(128)} %bitcast.sub_ref, bf16[8,512,256]{2,1,0:T(8,128)(2,1)S(1)} %get-tuple-element.20.after_ref.first_table_ref, bf16[8,512,256]{2,1,0:T(8,128)(2,1)S(1)} %copy-done.1, ...), custom_call_target="tpu_custom_call" | custom-call | flops 3000000000 | tf_op jit(solution)/shard_map/far_image/pallas_call | solution.py:397
  28.4 5.2 %collective-permute-start.6 = (f32[8,8,128]{2,1,0:T(8,128)S(1)}, f32[8,8,128]{2,1,0:T(8,128)S(1)}, u32[]{:S(2)}, u32[]{:S(2)}) collective-permute-start(f32[8,8,128]{2,1,0:T(8,128)S(1)} %get-tuple-element.32.after_ref), channel_id=1, source_target_pairs={{0,128},{16,144},{32,160},{48,176},{64,192},{80,208},{96,224},{112... | collective-permute-start | bytes 98312 | tf_op jit(solution)/shard_map/ppermute | solution.py:416
  33.6 2.5 %near_image.1 = f32[8,8,128]{2,1,0:T(8,128)S(1)} custom-call(s32[1]{0:T(128)} %bitcast.sub_ref, bf16[8,512,256]{2,1,0:T(8,128)(2,1)S(1)} %get-tuple-element.20.after_ref.first_table_ref, bf16[8,512,256]{2,1,0:T(8,128)(2,1)S(1)} %copy-done.1, bf16[2,64,128,128]{3,2,1,0:T(8,128)(2,1)S(1)} %get-tuple-element.27.first_weights_ref, ...), custom_call_target="tpu_custom_call" | custom-call | flops 3000000000 | tf_op jit(solution)/shard_map/near_image/pallas_call | solution.py:406
  36.1 0.0 collective-permute-done.6
  36.1 12.0 %all_to_all.5 = f32[8,8,128]{2,1,0:T(8,128)S(1)} all-to-all(f32[8,8,128]{2,1,0:T(8,128)S(1)} %add.3), channel_id=1, replica_groups={{0,16,32,48,64,80,96,112},{128,144,160,176,192,208,224,240},{1,17,33,49..., dimensions={0} | all-to-all | bytes 65536 | tf_op jit(solution)/shard_map/all_to_all | solution.py:418
  48.1 0.6 %reduce_sum.9 = f32[8,128]{1,0:T(8,128)} reduce(f32[8,8,128]{2,1,0:T(8,128)S(1)} %all_to_all.5, f32[]{:T(128)} %constant.8.clone.1), dimensions={0}, to_apply=%region_0.0 | reduce | flops 7168 | bytes 36868 | tf_op jit(solution)/shard_map/reduce_sum | solution.py:419
  (2 shorter events, 0.0 us)
Async XLA Ops:
  6.0 8.9 %collective-permute-start = (bf16[4,64,128]{2,1,0:T(8,128)(2,1)}, bf16[4,64,128]{2,1,0:T(8,128)(2,1)S(1)}, u32[]{:S(2)}, u32[]{:S(2)}) collective-permute-start(bf16[4,64,128]{2,1,0:T(8,128)(2,1)} %get-tuple-element.23), channel_id=1, source_target_pairs={{0,4},{1,5},{2,6},{3,7},{4,0},{5,1},{6,2},{7,3},{8,12},{9,13},{10,... | collective-permute-start | bytes 196616 | tf_op jit(solution)/shard_map/ppermute | solution.py:377
  8.2 6.7 %collective-permute-start.1 = (bf16[4,64,128]{2,1,0:T(8,128)(2,1)}, bf16[4,64,128]{2,1,0:T(8,128)(2,1)S(1)}, u32[]{:S(2)}, u32[]{:S(2)}) collective-permute-start(bf16[4,64,128]{2,1,0:T(8,128)(2,1)} %get-tuple-element.24), channel_id=1, source_target_pairs={{0,8},{1,9},{2,10},{3,11},{4,12},{5,13},{6,14},{7,15},{8,0},{9,1},... | collective-permute-start | bytes 196616 | tf_op jit(solution)/shard_map/ppermute | solution.py:377
  10.9 4.7 %collective-permute-start.2 = (bf16[4,64,128]{2,1,0:T(8,128)(2,1)}, bf16[4,64,128]{2,1,0:T(8,128)(2,1)S(1)}, u32[]{:S(2)}, u32[]{:S(2)}) collective-permute-start(bf16[4,64,128]{2,1,0:T(8,128)(2,1)} %get-tuple-element.25), channel_id=1, source_target_pairs={{0,12},{1,13},{2,14},{3,15},{4,8},{5,9},{6,10},{7,11},{8,4},{9,5},... | collective-permute-start | bytes 196616 | tf_op jit(solution)/shard_map/ppermute | solution.py:377
  10.9 1.0 %copy-start.3 = (f32[768,128]{1,0:T(8,128)S(1)}, f32[768,128]{1,0:T(8,128)}, u32[]{:S(2)}) copy-start(f32[768,128]{1,0:T(8,128)} %get-tuple-element.19.extra_ref) | copy-start | bytes 1179652
  13.6 1.3 %copy-start = (bf16[8,512,256]{2,1,0:T(8,128)(2,1)}, bf16[8,512,256]{2,1,0:T(8,128)(2,1)S(1)}, u32[]{:S(2)}) copy-start(bf16[8,512,256]{2,1,0:T(8,128)(2,1)S(1)} %get-tuple-element.21.second_table_ref) | copy-start | bytes 6291460
  15.5 10.5 %collective-permute-start.4 = (bf16[4,64,128]{2,1,0:T(8,128)(2,1)S(1)}, bf16[4,64,128]{2,1,0:T(8,128)(2,1)S(1)}, u32[]{:S(2)}, u32[]{:S(2)}) collective-permute-start(bf16[4,64,128]{2,1,0:T(8,128)(2,1)S(1)} %get-tuple-element.29), channel_id=1, source_target_pairs={{0,2},{1,3},{2,0},{3,1},{4,6},{5,7},{6,4},{7,5},{8,10},{9,11},{10,... | collective-permute-start | bytes 196616 | tf_op jit(solution)/shard_map/ppermute | solution.py:377
  18.6 7.4 %collective-permute-start.5 = (bf16[4,64,128]{2,1,0:T(8,128)(2,1)S(1)}, bf16[4,64,128]{2,1,0:T(8,128)(2,1)S(1)}, u32[]{:S(2)}, u32[]{:S(2)}) collective-permute-start(bf16[4,64,128]{2,1,0:T(8,128)(2,1)S(1)} %get-tuple-element.30), channel_id=1, source_target_pairs={{0,3},{1,2},{2,1},{3,0},{4,7},{5,6},{6,5},{7,4},{8,11},{9,10},{10,... | collective-permute-start | bytes 196616 | tf_op jit(solution)/shard_map/ppermute | solution.py:377
  20.1 6.0 %collective-permute-start.3 = (bf16[4,64,128]{2,1,0:T(8,128)(2,1)S(1)}, bf16[4,64,128]{2,1,0:T(8,128)(2,1)S(1)}, u32[]{:S(2)}, u32[]{:S(2)}) collective-permute-start(bf16[4,64,128]{2,1,0:T(8,128)(2,1)S(1)} %get-tuple-element.26.after_ref), channel_id=1, source_target_pairs={{0,1},{1,0},{2,3},{3,2},{4,5},{5,4},{6,7},{7,6},{8,9},{9,8},{10,11... | collective-permute-start | bytes 196616 | tf_op jit(solution)/shard_map/ppermute | solution.py:377
  20.3 3.4 %copy-start.2 = (bf16[2,2,128,4,2048]{4,3,2,1,0:T(4,128)(2,1)S(1)}, bf16[2,2,128,4,2048]{4,3,2,1,0:T(4,128)(2,1)}, u32[]{:S(2)}) copy-start(bf16[2,2,128,4,2048]{4,3,2,1,0:T(4,128)(2,1)} %param.11) | copy-start | bytes 25165828
  23.6 2.4 %copy-start.1 = (bf16[8,512,256]{2,1,0:T(8,128)(2,1)S(1)}, bf16[8,512,256]{2,1,0:T(8,128)(2,1)}, u32[]{:S(2)}) copy-start(bf16[8,512,256]{2,1,0:T(8,128)(2,1)} %copy-done) | copy-start | bytes 6291460
  28.4 7.7 %collective-permute-start.6 = (f32[8,8,128]{2,1,0:T(8,128)S(1)}, f32[8,8,128]{2,1,0:T(8,128)S(1)}, u32[]{:S(2)}, u32[]{:S(2)}) collective-permute-start(f32[8,8,128]{2,1,0:T(8,128)S(1)} %get-tuple-element.32.after_ref), channel_id=1, source_target_pairs={{0,128},{16,144},{32,160},{48,176},{64,192},{80,208},{96,224},{112... | collective-permute-start | bytes 98312 | tf_op jit(solution)/shard_map/ppermute | solution.py:416

commit v7 on v6

--- a/solution.py
+++ b/solution.py
@@ -10,11 +10,11 @@
 
 
 def compress_kernel(
-    me_ref, starts_ref, chirp_hbm, rates_hbm, slots_hbm, echoes_ref, *rest
+    me_ref, sub_ref, starts_ref, chirp_hbm, rates_hbm, slots_hbm, echoes_ref, *rest
 ):
     (
-        *bands_refs, extra_ref, chirp_ref, rates_ref, slots_ref, raw_ref, samples_ref, lhs_ref, toeplitz_ref,
-        product_ref, sems,
+        *bands_refs, extra_ref, chirp_ref, rates_ref, slots_ref, raw_ref, samples_ref, toeplitz_ref,
+        lhs_a, lhs_b, lhs_c, lhs_d, sems,
     ) = rest
     fetches = [
         pltpu.make_async_copy(source, target, sems.at[index])
@@ -36,6 +36,14 @@
     half = pulses // blocks
     rows = 2 * half
     chunks = span // LANES
+    samples_ref[lines // 2 :] = jnp.zeros(
+        (samples_ref.shape[0] - lines // 2, 2 * pulses, LANES), jnp.bfloat16
+    )
+    piece = 16
+    side = half * piece
+    row = lax.broadcasted_iota(jnp.int32, (side, side), 0)
+    col = lax.broadcasted_iota(jnp.int32, (side, side), 1)
+    order = jnp.where(col == (row % half) * piece + row // half, 1.0, 0.0).astype(jnp.bfloat16)
     fetches[0].wait()
     chirp = chirp_ref[...].astype(jnp.float32)
     pad = jnp.zeros((1, span - chirp.shape[1]), jnp.float32)
@@ -59,14 +67,6 @@
         rates = rates_ref[:, block * count : (block + 1) * count]
         rate = jnp.sum(jnp.where(slot == col.astype(jnp.float32), rates, 0.0), 1, keepdims=True)
         extra_ref[block * count : (block + 1) * count, :] = jnp.broadcast_to(rate, (count, LANES))
-    samples_ref[lines // 2 :] = jnp.zeros(
-        (samples_ref.shape[0] - lines // 2, 2 * pulses, LANES), jnp.bfloat16
-    )
-    piece = 16
-    side = half * piece
-    row = lax.broadcasted_iota(jnp.int32, (side, side), 0)
-    col = lax.broadcasted_iota(jnp.int32, (side, side), 1)
-    order = jnp.where(col == (row % half) * piece + row // half, 1.0, 0.0).astype(jnp.bfloat16)
     fetches[3].wait()
     for group in range(lines // piece):
         block_rows = jnp.concatenate(
@@ -83,44 +83,59 @@
             samples_ref[
                 group * piece // 2 : (group + 1) * piece // 2, block * rows : (block + 1) * rows, :
             ] = moved[:, block * LANES : (block + 1) * LANES].reshape(piece // 2, rows, LANES)
-    for block in range(blocks):
-        for tile in range(tiles):
-            first = starts_ref[block, me_ref[0] ^ tile] // LANES
-            place = (block * tiles + tile) * rows
-            for chunk in range(chunks):
-                lhs_ref[place : place + rows, chunk * LANES : (chunk + 1) * LANES] = samples_ref[
-                    first + chunk, block * rows : (block + 1) * rows, :
-                ]
-    product_ref[...] = lax.dot_general(
-        lhs_ref[...], toeplitz_ref[...], (((1,), (1,)), ((), ())), preferred_element_type=jnp.float32
-    )
     lane = lax.broadcasted_iota(jnp.int32, (half, LANES), 1)
-    for block in range(blocks):
-        for tile in range(tiles):
-            place = (block * tiles + tile) * rows
-            shift = starts_ref[block, me_ref[0] ^ tile] % LANES
-            turn = (LANES - shift) % LANES
-            keep = lane < LANES - shift
-
-            def piece(part, column):
-                top = place + part * half
-                low = product_ref[top : top + half, column * 2 * LANES : column * 2 * LANES + LANES]
-                high = product_ref[top : top + half, column * 2 * LANES + LANES : (column + 1) * 2 * LANES]
-                return low, high
-
-            rr, ri = piece(0, 0), piece(0, 1)
-            ir, ii = piece(1, 0), piece(1, 1)
-            for part, (low, high) in enumerate(
-                ((rr[0] + ii[0], rr[1] + ii[1]), (ir[0] - ri[0], ir[1] - ri[1]))
-            ):
-                cut = jnp.where(keep, pltpu.roll(low, turn, 1), pltpu.roll(high, turn, 1))
-                top = block * rows + part * half
-                cut = cut.astype(jnp.bfloat16)
-                if tile < near:
-                    top += blocks * count + tile * 2 * pulses
-                    extra_ref[top : top + half, :] = cut.astype(jnp.float32)
-                else:
-                    bands_refs[tile // near - 1][tile % near, top : top + half, :] = cut
+    lhs_refs = (lhs_a, lhs_b, lhs_c, lhs_d)
+
+    def gather(dy):
+        for dz in range(near):
+            for block in range(blocks):
+                first = starts_ref[block, me_ref[0] ^ (dy * near + dz)] // LANES
+                place = (dz * blocks + block) * rows
+                for chunk in range(chunks):
+                    lhs_refs[dy][place : place + rows, chunk * LANES : (chunk + 1) * LANES] = samples_ref[
+                        first + chunk, block * rows : (block + 1) * rows, :
+                    ]
+
+    def correlate(dy):
+        return lax.dot_general(
+            lhs_refs[dy][...],
+            toeplitz_ref[...],
+            (((1,), (1,)), ((), ())),
+            preferred_element_type=jnp.float32,
+        )
+
+    def cut(dy, product):
+        for dz in range(near):
+            for block in range(blocks):
+                place = (dz * blocks + block) * rows
+                shift = starts_ref[block, me_ref[0] ^ (dy * near + dz)] % LANES
+                turn = (LANES - shift) % LANES
+                keep = lane < LANES - shift
+
+                def piece(part, column):
+                    rows_of = product[place + part * half : place + (part + 1) * half]
+                    left = column * 2 * LANES
+                    return rows_of[:, left : left + LANES], rows_of[:, left + LANES : left + 2 * LANES]
+
+                rr, ri = piece(0, 0), piece(0, 1)
+                ir, ii = piece(1, 0), piece(1, 1)
+                for part, (low, high) in enumerate(
+                    ((rr[0] + ii[0], rr[1] + ii[1]), (ir[0] - ri[0], ir[1] - ri[1]))
+                ):
+                    band = jnp.where(keep, pltpu.roll(low, turn, 1), pltpu.roll(high, turn, 1))
+                    band = band.astype(jnp.bfloat16)
+                    top = block * rows + part * half
+                    if dy == 0:
+                        top += blocks * count + dz * 2 * pulses
+                        extra_ref[top : top + half, :] = band.astype(jnp.float32)
+                    else:
+                        bands_refs[dy - 1][dz, top : top + half, :] = band
+
+    gather(0)
+    for dy in range(len(lhs_refs)):
+        if dy + 1 < len(lhs_refs):
+            gather(dy + 1)
+        cut(dy, correlate(dy))
 
 
 def sine_cosine(angle):
@@ -358,20 +373,21 @@
         "compress",
         60,
         [own] * (far - 1) + [extras],
-        [smem, smem] + [anywhere] * 4,
+        [smem] * 3 + [anywhere] * 4,
         [
             pltpu.VMEM((2, chirp_len), jnp.bfloat16),
             pltpu.VMEM((1, blocks * count), jnp.float32),
             pltpu.VMEM((blocks, count), jnp.int32),
             pltpu.VMEM((pulses, lines, LANES), jnp.bfloat16),
             pltpu.VMEM((lines // 2 + span // LANES - 1, 2 * pulses, LANES), jnp.bfloat16),
-            pltpu.VMEM((tiles * 2 * pulses, span), jnp.bfloat16),
             pltpu.VMEM((4 * LANES, span), jnp.bfloat16),
-            pltpu.VMEM((tiles * 2 * pulses, 4 * LANES), jnp.float32),
+        ]
+        + [pltpu.VMEM((near * 2 * pulses, span), jnp.bfloat16)] * far
+        + [
             pltpu.SemaphoreType.DMA((4,)),
         ],
         flops=6 * 10**9,
-    )(me, band_starts, chirp_ref, doppler_rates, slot_pulse.reshape(blocks, count), samples)
+    )(me, sub, band_starts, chirp_ref, doppler_rates, slot_pulse.reshape(blocks, count), samples)
 
     def swap(value, distance):
         return lax.ppermute(value, "tile", [(one, one ^ distance) for one in range(tiles)])

time: 49 us -> 48 us (0.980)
  local copies, waits for them, and re-layouts: 5.7 us -> 1 us
  waiting for transfers between devices: 0.64 us -> 3.78 us
  starting transfers between devices: 14.7 us -> 15.3 us
    unnamed x8 -> x4, local copies, waits for them, and re-layouts: 5.7 us -> 1 us
    ppermute x6, waiting for transfers between devices: 0.63 us -> 3.78 us  [swap(): lax.ppermute(value, 'tile', [(one, one ^ distance) for one in range(tiles)])]
    ppermute x1, starting transfers between devices: 5.19 us -> 5.75 us  [shards(): lax.ppermute(far_image, 'sub', [(one, one ^ half) for one in range(size)])]
  transfers between devices with their start and end apart: 7 -> 7, of which waited for: 1 -> 4; matrix products, arithmetic and copies ran while one was open for 0% -> 0% of each run, Pallas kernels for 13% -> 14%
where the time goes in v7:
time: 48 us; the launch traced here: 47.8 us
  starting transfers between devices  15.3 us (32%)
  Pallas kernels  15.1 us (31%)
  blocking collectives  12 us (25%)
  waiting for transfers between devices  3.78 us (8%)
  local copies, waits for them, and re-layouts  1 us (2%)
  other arithmetic  0.61 us (1%)
    all_to_all x1, blocking collectives, shards(): lax.all_to_all(near_image + came, 'sub', 0, 0, axis_index_groups=groups,...  12 us
    ppermute x6, starting transfers between devices, swap(): lax.ppermute(value, 'tile', [(one, one ^ distance) for one in range(tiles)])  9.55 us
    pallas_call x1, Pallas kernels, partial_image(): call(compress_kernel, 'compress', 60, [own] * (far - 1) + [extras], [smem...  6.13 us
    ppermute x1, starting transfers between devices, shards(): lax.ppermute(far_image, 'sub', [(one, one ^ half) for one in range(size)])  5.75 us
    ppermute x6, waiting for transfers between devices, swap(): lax.ppermute(value, 'tile', [(one, one ^ distance) for one in range(tiles)])  3.78 us
    pallas_call x1, Pallas kernels, partial_image(): call(near_image_kernel, 'near_image', 12, half, [smem] + [vmem()] * 5 + [...  2.51 us
    pallas_call x1, Pallas kernels, partial_image(): call(turn_kernel, 'turn', 12, [turned, turned], [vmem(), anywhere], flops...  2.35 us
    pallas_call x1, Pallas kernels, partial_image(): call(far_image_kernel, 'far_image', 12, [half, shape((blocks, 2 * band, 2...  2.34 us
  transfers between devices with their start and end apart: 7, of which 4 were waited for; matrix products, arithmetic and copies ran while one was open for 0% of the time, Pallas kernels for 14%

profile of v7, /device:TPU:1, one launch (start us, length us, event | category | flops | bytes accessed | tf_op | source)
XLA Modules:
  0.0 47.8 jit_solution(16037570361071956867)
XLA Ops:
  0.0 6.1 %compress.1 = (bf16[4,64,128]{2,1,0:T(8,128)(2,1)}, bf16[4,64,128]{2,1,0:T(8,128)(2,1)}, bf16[4,64,128]{2,1,0:T(8,128)(2,1)}, f32[768,128]{1,0:T(8,128)}) custom-call(s32[1]{0:T(128)} %bitcast.1.me_ref, s32[1]{0:T(128)} %bitcast.sub_ref, s32[2,16]{1,0:T(2,128)} %starts_ref.1, bf16[2,2048]{1,0:T(2,128)(2,1)} %chirp_hbm.1, f32[1,512]{1,0:T(1,128)} %rates_hbm.1, ...), custom_call_target="tpu_custom_call" | custom-call | flops 6000000000 | tf_op jit(solution)/shard_map/compress/pallas_call | solution.py:371
  6.1 2.2 %collective-permute-start = (bf16[4,64,128]{2,1,0:T(8,128)(2,1)}, bf16[4,64,128]{2,1,0:T(8,128)(2,1)S(1)}, u32[]{:S(2)}, u32[]{:S(2)}) collective-permute-start(bf16[4,64,128]{2,1,0:T(8,128)(2,1)} %get-tuple-element.23), channel_id=1, source_target_pairs={{0,4},{1,5},{2,6},{3,7},{4,0},{5,1},{6,2},{7,3},{8,12},{9,13},{10,... | collective-permute-start | bytes 196616 | tf_op jit(solution)/shard_map/ppermute | solution.py:393
  8.4 2.6 %collective-permute-start.1 = (bf16[4,64,128]{2,1,0:T(8,128)(2,1)}, bf16[4,64,128]{2,1,0:T(8,128)(2,1)S(1)}, u32[]{:S(2)}, u32[]{:S(2)}) collective-permute-start(bf16[4,64,128]{2,1,0:T(8,128)(2,1)} %get-tuple-element.24), channel_id=1, source_target_pairs={{0,8},{1,9},{2,10},{3,11},{4,12},{5,13},{6,14},{7,15},{8,0},{9,1},... | collective-permute-start | bytes 196616 | tf_op jit(solution)/shard_map/ppermute | solution.py:393
  11.0 0.0 collective-permute-start.2
  11.0 0.0 copy-start.1
  11.0 1.0 %copy-done.1 = f32[768,128]{1,0:T(8,128)S(1)} copy-done((f32[768,128]{1,0:T(8,128)S(1)}, f32[768,128]{1,0:T(8,128)}, u32[]{:S(2)}) %copy-start.1) | copy-done | bytes 393240
  12.0 0.0 copy-start
  12.0 1.7 %phase.1 = (bf16[8,512,256]{2,1,0:T(8,128)(2,1)S(1)}, bf16[8,512,256]{2,1,0:T(8,128)(2,1)S(1)}, bf16[4,64,128]{2,1,0:T(8,128)(2,1)S(1)}) custom-call(f32[768,128]{1,0:T(8,128)S(1)} %copy-done.1), custom_call_target="tpu_custom_call" | custom-call | flops 4000000000 | tf_op jit(solution)/shard_map/phase/pallas_call | solution.py:397
  13.7 0.0 collective-permute-done.refs_1_.rest_1_
  13.7 0.1 collective-permute-done.1.refs_2_.rest_2_
  13.8 1.9 %collective-permute-done.2.refs_3_.rest_3_ = bf16[4,64,128]{2,1,0:T(8,128)(2,1)S(1)} collective-permute-done((bf16[4,64,128]{2,1,0:T(8,128)(2,1)}, bf16[4,64,128]{2,1,0:T(8,128)(2,1)S(1)}, u32[]{:S(2)}, u32[]{:S(2)}) %collective-permute-start.2) | collective-permute-done | bytes 65568 | tf_op jit(solution)/shard_map/ppermute | solution.py:393
  15.7 3.1 %collective-permute-start.4 = (bf16[4,64,128]{2,1,0:T(8,128)(2,1)S(1)}, bf16[4,64,128]{2,1,0:T(8,128)(2,1)S(1)}, u32[]{:S(2)}, u32[]{:S(2)}) collective-permute-start(bf16[4,64,128]{2,1,0:T(8,128)(2,1)S(1)} %get-tuple-element.29), channel_id=1, source_target_pairs={{0,2},{1,3},{2,0},{3,1},{4,6},{5,7},{6,4},{7,5},{8,10},{9,11},{10,... | collective-permute-start | bytes 196616 | tf_op jit(solution)/shard_map/ppermute | solution.py:393
  18.7 1.5 %collective-permute-start.5 = (bf16[4,64,128]{2,1,0:T(8,128)(2,1)S(1)}, bf16[4,64,128]{2,1,0:T(8,128)(2,1)S(1)}, u32[]{:S(2)}, u32[]{:S(2)}) collective-permute-start(bf16[4,64,128]{2,1,0:T(8,128)(2,1)S(1)} %get-tuple-element.30), channel_id=1, source_target_pairs={{0,3},{1,2},{2,1},{3,0},{4,7},{5,6},{6,5},{7,4},{8,11},{9,10},{10,... | collective-permute-start | bytes 196616 | tf_op jit(solution)/shard_map/ppermute | solution.py:393
  20.2 0.2 collective-permute-start.3
  20.4 0.0 copy-done
  20.4 2.3 %turn.1 = (bf16[2,64,128,128]{3,2,1,0:T(8,128)(2,1)S(1)}, bf16[2,64,128,128]{3,2,1,0:T(8,128)(2,1)S(1)}) custom-call(bf16[512,64,128]{2,1,0:T(8,128)(2,1)S(1)} %bitcast.14, bf16[4,64,128]{2,1,0:T(8,128)(2,1)S(1)} %get-tuple-element.26.after_ref), custom_call_target="tpu_custom_call" | custom-call | flops 4000000000 | tf_op jit(solution)/shard_map/turn/pallas_call | solution.py:406
  22.7 0.0 collective-permute-done.4.rest_5_
  22.8 1.2 %collective-permute-done.5.rest_6_ = bf16[4,64,128]{2,1,0:T(8,128)(2,1)S(1)} collective-permute-done((bf16[4,64,128]{2,1,0:T(8,128)(2,1)S(1)}, bf16[4,64,128]{2,1,0:T(8,128)(2,1)S(1)}, u32[]{:S(2)}, u32[]{:S(2)}) %collective-permute-start.5) | collective-permute-done | bytes 65568 | tf_op jit(solution)/shard_map/ppermute | solution.py:393
  24.0 0.6 %collective-permute-done.3.rest_4_ = bf16[4,64,128]{2,1,0:T(8,128)(2,1)S(1)} collective-permute-done((bf16[4,64,128]{2,1,0:T(8,128)(2,1)S(1)}, bf16[4,64,128]{2,1,0:T(8,128)(2,1)S(1)}, u32[]{:S(2)}, u32[]{:S(2)}) %collective-permute-start.3) | collective-permute-done | bytes 65568 | tf_op jit(solution)/shard_map/ppermute | solution.py:393
  24.6 2.3 %far_image.1 = (f32[8,8,128]{2,1,0:T(8,128)S(1)}, bf16[2,256,512]{2,1,0:T(8,128)(2,1)S(1)}) custom-call(s32[1]{0:T(128)} %bitcast.1.me_ref, s32[1]{0:T(128)} %bitcast.sub_ref, bf16[8,512,256]{2,1,0:T(8,128)(2,1)S(1)} %get-tuple-element.20.after_ref.first_table_ref, bf16[8,512,256]{2,1,0:T(8,128)(2,1)S(1)} %get-tuple-element.21.second_table_ref, ...), custom_call_target="tpu_custom_call" | custom-call | flops 3000000000 | tf_op jit(solution)/shard_map/far_image/pallas_call | solution.py:413
  26.9 5.8 %collective-permute-start.6 = (f32[8,8,128]{2,1,0:T(8,128)S(1)}, f32[8,8,128]{2,1,0:T(8,128)S(1)}, u32[]{:S(2)}, u32[]{:S(2)}) collective-permute-start(f32[8,8,128]{2,1,0:T(8,128)S(1)} %get-tuple-element.32.after_ref), channel_id=1, source_target_pairs={{0,128},{16,144},{32,160},{48,176},{64,192},{80,208},{96,224},{112... | collective-permute-start | bytes 98312 | tf_op jit(solution)/shard_map/ppermute | solution.py:432
  32.7 2.5 %near_image.1 = f32[8,8,128]{2,1,0:T(8,128)S(1)} custom-call(s32[1]{0:T(128)} %bitcast.sub_ref, bf16[8,512,256]{2,1,0:T(8,128)(2,1)S(1)} %get-tuple-element.20.after_ref.first_table_ref, bf16[8,512,256]{2,1,0:T(8,128)(2,1)S(1)} %get-tuple-element.21.second_table_ref, bf16[2,64,128,128]{3,2,1,0:T(8,128)(2,1)S(1)} %get-tuple-element.27.first_weights_ref, ...), custom_call_target="tpu_custom_call" | custom-call | flops 3000000000 | tf_op jit(solution)/shard_map/near_image/pallas_call | solution.py:422
  35.2 0.0 collective-permute-done.6
  35.2 12.0 %all_to_all.5 = f32[8,8,128]{2,1,0:T(8,128)S(1)} all-to-all(f32[8,8,128]{2,1,0:T(8,128)S(1)} %add.3), channel_id=1, replica_groups={{0,16,32,48,64,80,96,112},{128,144,160,176,192,208,224,240},{1,17,33,49..., dimensions={0} | all-to-all | bytes 65536 | tf_op jit(solution)/shard_map/all_to_all | solution.py:434
  47.2 0.6 %reduce_sum.9 = f32[8,128]{1,0:T(8,128)} reduce(f32[8,8,128]{2,1,0:T(8,128)S(1)} %all_to_all.5, f32[]{:T(128)} %constant.8.clone.1), dimensions={0}, to_apply=%region_0.0 | reduce | flops 7168 | bytes 36868 | tf_op jit(solution)/shard_map/reduce_sum | solution.py:435
  (2 shorter events, 0.0 us)
Async XLA Ops:
  6.1 7.6 %collective-permute-start = (bf16[4,64,128]{2,1,0:T(8,128)(2,1)}, bf16[4,64,128]{2,1,0:T(8,128)(2,1)S(1)}, u32[]{:S(2)}, u32[]{:S(2)}) collective-permute-start(bf16[4,64,128]{2,1,0:T(8,128)(2,1)} %get-tuple-element.23), channel_id=1, source_target_pairs={{0,4},{1,5},{2,6},{3,7},{4,0},{5,1},{6,2},{7,3},{8,12},{9,13},{10,... | collective-permute-start | bytes 196616 | tf_op jit(solution)/shard_map/ppermute | solution.py:393
  8.4 5.4 %collective-permute-start.1 = (bf16[4,64,128]{2,1,0:T(8,128)(2,1)}, bf16[4,64,128]{2,1,0:T(8,128)(2,1)S(1)}, u32[]{:S(2)}, u32[]{:S(2)}) collective-permute-start(bf16[4,64,128]{2,1,0:T(8,128)(2,1)} %get-tuple-element.24), channel_id=1, source_target_pairs={{0,8},{1,9},{2,10},{3,11},{4,12},{5,13},{6,14},{7,15},{8,0},{9,1},... | collective-permute-start | bytes 196616 | tf_op jit(solution)/shard_map/ppermute | solution.py:393
  11.0 4.7 %collective-permute-start.2 = (bf16[4,64,128]{2,1,0:T(8,128)(2,1)}, bf16[4,64,128]{2,1,0:T(8,128)(2,1)S(1)}, u32[]{:S(2)}, u32[]{:S(2)}) collective-permute-start(bf16[4,64,128]{2,1,0:T(8,128)(2,1)} %get-tuple-element.25), channel_id=1, source_target_pairs={{0,12},{1,13},{2,14},{3,15},{4,8},{5,9},{6,10},{7,11},{8,4},{9,5},... | collective-permute-start | bytes 196616 | tf_op jit(solution)/shard_map/ppermute | solution.py:393
  11.0 1.0 %copy-start.1 = (f32[768,128]{1,0:T(8,128)S(1)}, f32[768,128]{1,0:T(8,128)}, u32[]{:S(2)}) copy-start(f32[768,128]{1,0:T(8,128)} %get-tuple-element.19.extra_ref) | copy-start | bytes 1179652
  12.0 8.4 %copy-start = (bf16[2,2,128,4,2048]{4,3,2,1,0:T(4,128)(2,1)S(1)}, bf16[2,2,128,4,2048]{4,3,2,1,0:T(4,128)(2,1)}, u32[]{:S(2)}) copy-start(bf16[2,2,128,4,2048]{4,3,2,1,0:T(4,128)(2,1)} %param.11) | copy-start | bytes 25165828
  15.7 7.1 %collective-permute-start.4 = (bf16[4,64,128]{2,1,0:T(8,128)(2,1)S(1)}, bf16[4,64,128]{2,1,0:T(8,128)(2,1)S(1)}, u32[]{:S(2)}, u32[]{:S(2)}) collective-permute-start(bf16[4,64,128]{2,1,0:T(8,128)(2,1)S(1)} %get-tuple-element.29), channel_id=1, source_target_pairs={{0,2},{1,3},{2,0},{3,1},{4,6},{5,7},{6,4},{7,5},{8,10},{9,11},{10,... | collective-permute-start | bytes 196616 | tf_op jit(solution)/shard_map/ppermute | solution.py:393
  18.7 5.3 %collective-permute-start.5 = (bf16[4,64,128]{2,1,0:T(8,128)(2,1)S(1)}, bf16[4,64,128]{2,1,0:T(8,128)(2,1)S(1)}, u32[]{:S(2)}, u32[]{:S(2)}) collective-permute-start(bf16[4,64,128]{2,1,0:T(8,128)(2,1)S(1)} %get-tuple-element.30), channel_id=1, source_target_pairs={{0,3},{1,2},{2,1},{3,0},{4,7},{5,6},{6,5},{7,4},{8,11},{9,10},{10,... | collective-permute-start | bytes 196616 | tf_op jit(solution)/shard_map/ppermute | solution.py:393
  20.2 4.4 %collective-permute-start.3 = (bf16[4,64,128]{2,1,0:T(8,128)(2,1)S(1)}, bf16[4,64,128]{2,1,0:T(8,128)(2,1)S(1)}, u32[]{:S(2)}, u32[]{:S(2)}) collective-permute-start(bf16[4,64,128]{2,1,0:T(8,128)(2,1)S(1)} %get-tuple-element.26.after_ref), channel_id=1, source_target_pairs={{0,1},{1,0},{2,3},{3,2},{4,5},{5,4},{6,7},{7,6},{8,9},{9,8},{10,11... | collective-permute-start | bytes 196616 | tf_op jit(solution)/shard_map/ppermute | solution.py:393
  26.9 8.3 %collective-permute-start.6 = (f32[8,8,128]{2,1,0:T(8,128)S(1)}, f32[8,8,128]{2,1,0:T(8,128)S(1)}, u32[]{:S(2)}, u32[]{:S(2)}) collective-permute-start(f32[8,8,128]{2,1,0:T(8,128)S(1)} %get-tuple-element.32.after_ref), channel_id=1, source_target_pairs={{0,128},{16,144},{32,160},{48,176},{64,192},{80,208},{96,224},{112... | collective-permute-start | bytes 98312 | tf_op jit(solution)/shard_map/ppermute | solution.py:432

commit v8 on v7

--- a/solution.py
+++ b/solution.py
@@ -43,8 +43,9 @@
     side = half * piece
     row = lax.broadcasted_iota(jnp.int32, (side, side), 0)
     col = lax.broadcasted_iota(jnp.int32, (side, side), 1)
-    order = jnp.where(col == (row % half) * piece + row // half, 1.0, 0.0).astype(jnp.bfloat16)
-    fetches[0].wait()
+    order = jnp.where(col == (row & (half - 1)) * piece + (row >> 4), 1.0, 0.0).astype(jnp.bfloat16)
+    for fetch in fetches[:3]:
+        fetch.wait()
     chirp = chirp_ref[...].astype(jnp.float32)
     pad = jnp.zeros((1, span - chirp.shape[1]), jnp.float32)
     for part in range(2):
@@ -52,12 +53,7 @@
         shifted = pltpu.roll(
             jnp.broadcast_to(line, (LANES, span)), 0, 1, stride=1, stride_axis=0
         ).astype(jnp.bfloat16)
-        base = part * 2 * LANES
-        toeplitz_ref[base : base + LANES, :] = shifted
-        toeplitz_ref[base + LANES : base + 2 * LANES, :LANES] = jnp.zeros((LANES, LANES), jnp.bfloat16)
-        toeplitz_ref[base + LANES : base + 2 * LANES, LANES:] = shifted[:, : span - LANES]
-    fetches[1].wait()
-    fetches[2].wait()
+        toeplitz_ref[part * LANES : (part + 1) * LANES, :] = shifted
     count = slots_ref.shape[1]
     row = lax.broadcasted_iota(jnp.int32, (count, count), 0)
     col = lax.broadcasted_iota(jnp.int32, (count, count), 1)
@@ -83,18 +79,30 @@
             samples_ref[
                 group * piece // 2 : (group + 1) * piece // 2, block * rows : (block + 1) * rows, :
             ] = moved[:, block * LANES : (block + 1) * LANES].reshape(piece // 2, rows, LANES)
-    lane = lax.broadcasted_iota(jnp.int32, (half, LANES), 1)
+    lane = lax.broadcasted_iota(jnp.int32, (rows, LANES), 1)
     lhs_refs = (lhs_a, lhs_b, lhs_c, lhs_d)
 
     def gather(dy):
         for dz in range(near):
             for block in range(blocks):
-                first = starts_ref[block, me_ref[0] ^ (dy * near + dz)] // LANES
+                start = starts_ref[block, me_ref[0] ^ (dy * near + dz)]
+                first = start >> 7
+                shift = start & (LANES - 1)
+                turn = (LANES - shift) & (LANES - 1)
+                keep = lane < LANES - shift
                 place = (dz * blocks + block) * rows
+
+                def rolled(chunk):
+                    line = samples_ref[first + chunk, block * rows : (block + 1) * rows, :]
+                    return pltpu.roll(line, turn, 1)
+
+                low = rolled(0)
                 for chunk in range(chunks):
-                    lhs_refs[dy][place : place + rows, chunk * LANES : (chunk + 1) * LANES] = samples_ref[
-                        first + chunk, block * rows : (block + 1) * rows, :
-                    ]
+                    high = rolled(chunk + 1)
+                    lhs_refs[dy][place : place + rows, chunk * LANES : (chunk + 1) * LANES] = jnp.where(
+                        keep, low, high
+                    )
+                    low = high
 
     def correlate(dy):
         return lax.dot_general(
@@ -108,21 +116,11 @@
         for dz in range(near):
             for block in range(blocks):
                 place = (dz * blocks + block) * rows
-                shift = starts_ref[block, me_ref[0] ^ (dy * near + dz)] % LANES
-                turn = (LANES - shift) % LANES
-                keep = lane < LANES - shift
-
-                def piece(part, column):
-                    rows_of = product[place + part * half : place + (part + 1) * half]
-                    left = column * 2 * LANES
-                    return rows_of[:, left : left + LANES], rows_of[:, left + LANES : left + 2 * LANES]
-
-                rr, ri = piece(0, 0), piece(0, 1)
-                ir, ii = piece(1, 0), piece(1, 1)
-                for part, (low, high) in enumerate(
-                    ((rr[0] + ii[0], rr[1] + ii[1]), (ir[0] - ri[0], ir[1] - ri[1]))
+                real = product[place : place + half]
+                imag = product[place + half : place + rows]
+                for part, band in enumerate(
+                    (real[:, :LANES] + imag[:, LANES:], imag[:, :LANES] - real[:, LANES:])
                 ):
-                    band = jnp.where(keep, pltpu.roll(low, turn, 1), pltpu.roll(high, turn, 1))
                     band = band.astype(jnp.bfloat16)
                     top = block * rows + part * half
                     if dy == 0:
@@ -173,7 +171,7 @@
     side = size * size
     row = lax.broadcasted_iota(jnp.int32, (side, side), 0)
     col = lax.broadcasted_iota(jnp.int32, (side, side), 1)
-    order = jnp.where(col == (row % size) * size + row // size, 1.0, 0.0).astype(jnp.bfloat16)
+    order = jnp.where(col == (row & (size - 1)) * size + (row >> 4), 1.0, 0.0).astype(jnp.bfloat16)
     for block, out_ref in enumerate((first_ref, second_ref)):
         for part in range(2):
 
@@ -349,7 +347,7 @@
     _, _, band, image_rows, columns = interp_weights.shape
     count = slot_pulse.shape[2]
     lines = 2 * pulse_len // LANES
-    span = chirp_len + 2 * LANES
+    span = chirp_len + LANES
     places = columns // LANES
     parts = places // 2
     near = 4
@@ -379,8 +377,8 @@
             pltpu.VMEM((1, blocks * count), jnp.float32),
             pltpu.VMEM((blocks, count), jnp.int32),
             pltpu.VMEM((pulses, lines, LANES), jnp.bfloat16),
-            pltpu.VMEM((lines // 2 + span // LANES - 1, 2 * pulses, LANES), jnp.bfloat16),
-            pltpu.VMEM((4 * LANES, span), jnp.bfloat16),
+            pltpu.VMEM((lines // 2 + span // LANES, 2 * pulses, LANES), jnp.bfloat16),
+            pltpu.VMEM((2 * LANES, span), jnp.bfloat16),
         ]
         + [pltpu.VMEM((near * 2 * pulses, span), jnp.bfloat16)] * far
         + [

time: 48 us -> 46.9 us (0.977)
  Pallas kernels: 15.1 us -> 14 us
    pallas_call x1, Pallas kernels: 6.13 us -> 5.07 us  [partial_image(): call(compress_kernel, 'compress', 60, [own] * (far - 1) + [extras], [smem...]
where the time goes in v8:
time: 46.9 us; the launch traced here: 46.8 us
  starting transfers between devices  15.3 us (33%)
  Pallas kernels  14 us (30%)
  blocking collectives  12 us (26%)
  waiting for transfers between devices  3.77 us (8%)
  local copies, waits for them, and re-layouts  1 us (2%)
  other arithmetic  0.61 us (1%)
    all_to_all x1, blocking collectives, shards(): lax.all_to_all(near_image + came, 'sub', 0, 0, axis_index_groups=groups,...  12 us
    ppermute x6, starting transfers between devices, swap(): lax.ppermute(value, 'tile', [(one, one ^ distance) for one in range(tiles)])  9.56 us
    ppermute x1, starting transfers between devices, shards(): lax.ppermute(far_image, 'sub', [(one, one ^ half) for one in range(size)])  5.75 us
    pallas_call x1, Pallas kernels, partial_image(): call(compress_kernel, 'compress', 60, [own] * (far - 1) + [extras], [smem...  5.07 us
    ppermute x6, waiting for transfers between devices, swap(): lax.ppermute(value, 'tile', [(one, one ^ distance) for one in range(tiles)])  3.77 us
    pallas_call x1, Pallas kernels, partial_image(): call(near_image_kernel, 'near_image', 12, half, [smem] + [vmem()] * 5 + [...  2.51 us
    pallas_call x1, Pallas kernels, partial_image(): call(turn_kernel, 'turn', 12, [turned, turned], [vmem(), anywhere], flops...  2.35 us
    pallas_call x1, Pallas kernels, partial_image(): call(far_image_kernel, 'far_image', 12, [half, shape((blocks, 2 * band, 2...  2.34 us
  transfers between devices with their start and end apart: 7, of which 4 were waited for; matrix products, arithmetic and copies ran while one was open for 0% of the time, Pallas kernels for 14%

profile of v8, /device:TPU:1, one launch (start us, length us, event | category | flops | bytes accessed | tf_op | source)
XLA Modules:
  0.0 46.8 jit_solution(7169000472797664600)
XLA Ops:
  0.0 5.1 %compress.1 = (bf16[4,64,128]{2,1,0:T(8,128)(2,1)}, bf16[4,64,128]{2,1,0:T(8,128)(2,1)}, bf16[4,64,128]{2,1,0:T(8,128)(2,1)}, f32[768,128]{1,0:T(8,128)}) custom-call(s32[1]{0:T(128)} %bitcast.1.me_ref, s32[1]{0:T(128)} %bitcast.sub_ref, s32[2,16]{1,0:T(2,128)} %starts_ref.1, bf16[2,2048]{1,0:T(2,128)(2,1)} %chirp_hbm.1, f32[1,512]{1,0:T(1,128)} %rates_hbm.1, ...), custom_call_target="tpu_custom_call" | custom-call | flops 6000000000 | tf_op jit(solution)/shard_map/compress/pallas_call | solution.py:369
  5.1 2.2 %collective-permute-start = (bf16[4,64,128]{2,1,0:T(8,128)(2,1)}, bf16[4,64,128]{2,1,0:T(8,128)(2,1)S(1)}, u32[]{:S(2)}, u32[]{:S(2)}) collective-permute-start(bf16[4,64,128]{2,1,0:T(8,128)(2,1)} %get-tuple-element.23), channel_id=1, source_target_pairs={{0,4},{1,5},{2,6},{3,7},{4,0},{5,1},{6,2},{7,3},{8,12},{9,13},{10,... | collective-permute-start | bytes 196616 | tf_op jit(solution)/shard_map/ppermute | solution.py:391
  7.3 2.6 %collective-permute-start.1 = (bf16[4,64,128]{2,1,0:T(8,128)(2,1)}, bf16[4,64,128]{2,1,0:T(8,128)(2,1)S(1)}, u32[]{:S(2)}, u32[]{:S(2)}) collective-permute-start(bf16[4,64,128]{2,1,0:T(8,128)(2,1)} %get-tuple-element.24), channel_id=1, source_target_pairs={{0,8},{1,9},{2,10},{3,11},{4,12},{5,13},{6,14},{7,15},{8,0},{9,1},... | collective-permute-start | bytes 196616 | tf_op jit(solution)/shard_map/ppermute | solution.py:391
  9.9 0.0 collective-permute-start.2
  9.9 0.0 copy-start.1
  9.9 1.0 %copy-done.1 = f32[768,128]{1,0:T(8,128)S(1)} copy-done((f32[768,128]{1,0:T(8,128)S(1)}, f32[768,128]{1,0:T(8,128)}, u32[]{:S(2)}) %copy-start.1) | copy-done | bytes 393240
  10.9 0.0 copy-start
  10.9 1.7 %phase.1 = (bf16[8,512,256]{2,1,0:T(8,128)(2,1)S(1)}, bf16[8,512,256]{2,1,0:T(8,128)(2,1)S(1)}, bf16[4,64,128]{2,1,0:T(8,128)(2,1)S(1)}) custom-call(f32[768,128]{1,0:T(8,128)S(1)} %copy-done.1), custom_call_target="tpu_custom_call" | custom-call | flops 4000000000 | tf_op jit(solution)/shard_map/phase/pallas_call | solution.py:395
  12.6 0.0 collective-permute-done.refs_1_.rest_1_
  12.6 0.1 collective-permute-done.1.refs_2_.rest_2_
  12.7 1.9 %collective-permute-done.2.refs_3_.rest_3_ = bf16[4,64,128]{2,1,0:T(8,128)(2,1)S(1)} collective-permute-done((bf16[4,64,128]{2,1,0:T(8,128)(2,1)}, bf16[4,64,128]{2,1,0:T(8,128)(2,1)S(1)}, u32[]{:S(2)}, u32[]{:S(2)}) %collective-permute-start.2) | collective-permute-done | bytes 65568 | tf_op jit(solution)/shard_map/ppermute | solution.py:391
  14.6 3.1 %collective-permute-start.4 = (bf16[4,64,128]{2,1,0:T(8,128)(2,1)S(1)}, bf16[4,64,128]{2,1,0:T(8,128)(2,1)S(1)}, u32[]{:S(2)}, u32[]{:S(2)}) collective-permute-start(bf16[4,64,128]{2,1,0:T(8,128)(2,1)S(1)} %get-tuple-element.29), channel_id=1, source_target_pairs={{0,2},{1,3},{2,0},{3,1},{4,6},{5,7},{6,4},{7,5},{8,10},{9,11},{10,... | collective-permute-start | bytes 196616 | tf_op jit(solution)/shard_map/ppermute | solution.py:391
  17.7 1.5 %collective-permute-start.5 = (bf16[4,64,128]{2,1,0:T(8,128)(2,1)S(1)}, bf16[4,64,128]{2,1,0:T(8,128)(2,1)S(1)}, u32[]{:S(2)}, u32[]{:S(2)}) collective-permute-start(bf16[4,64,128]{2,1,0:T(8,128)(2,1)S(1)} %get-tuple-element.30), channel_id=1, source_target_pairs={{0,3},{1,2},{2,1},{3,0},{4,7},{5,6},{6,5},{7,4},{8,11},{9,10},{10,... | collective-permute-start | bytes 196616 | tf_op jit(solution)/shard_map/ppermute | solution.py:391
  19.1 0.2 collective-permute-start.3
  19.3 0.0 copy-done
  19.3 2.3 %turn.1 = (bf16[2,64,128,128]{3,2,1,0:T(8,128)(2,1)S(1)}, bf16[2,64,128,128]{3,2,1,0:T(8,128)(2,1)S(1)}) custom-call(bf16[512,64,128]{2,1,0:T(8,128)(2,1)S(1)} %bitcast.14, bf16[4,64,128]{2,1,0:T(8,128)(2,1)S(1)} %get-tuple-element.26.after_ref), custom_call_target="tpu_custom_call" | custom-call | flops 4000000000 | tf_op jit(solution)/shard_map/turn/pallas_call | solution.py:404
  21.7 0.0 collective-permute-done.4.rest_5_
  21.7 1.2 %collective-permute-done.5.rest_6_ = bf16[4,64,128]{2,1,0:T(8,128)(2,1)S(1)} collective-permute-done((bf16[4,64,128]{2,1,0:T(8,128)(2,1)S(1)}, bf16[4,64,128]{2,1,0:T(8,128)(2,1)S(1)}, u32[]{:S(2)}, u32[]{:S(2)}) %collective-permute-start.5) | collective-permute-done | bytes 65568 | tf_op jit(solution)/shard_map/ppermute | solution.py:391
  22.9 0.6 %collective-permute-done.3.rest_4_ = bf16[4,64,128]{2,1,0:T(8,128)(2,1)S(1)} collective-permute-done((bf16[4,64,128]{2,1,0:T(8,128)(2,1)S(1)}, bf16[4,64,128]{2,1,0:T(8,128)(2,1)S(1)}, u32[]{:S(2)}, u32[]{:S(2)}) %collective-permute-start.3) | collective-permute-done | bytes 65568 | tf_op jit(solution)/shard_map/ppermute | solution.py:391
  23.5 2.3 %far_image.1 = (f32[8,8,128]{2,1,0:T(8,128)S(1)}, bf16[2,256,512]{2,1,0:T(8,128)(2,1)S(1)}) custom-call(s32[1]{0:T(128)} %bitcast.1.me_ref, s32[1]{0:T(128)} %bitcast.sub_ref, bf16[8,512,256]{2,1,0:T(8,128)(2,1)S(1)} %get-tuple-element.20.after_ref.first_table_ref, bf16[8,512,256]{2,1,0:T(8,128)(2,1)S(1)} %get-tuple-element.21.second_table_ref, ...), custom_call_target="tpu_custom_call" | custom-call | flops 3000000000 | tf_op jit(solution)/shard_map/far_image/pallas_call | solution.py:411
  25.9 5.8 %collective-permute-start.6 = (f32[8,8,128]{2,1,0:T(8,128)S(1)}, f32[8,8,128]{2,1,0:T(8,128)S(1)}, u32[]{:S(2)}, u32[]{:S(2)}) collective-permute-start(f32[8,8,128]{2,1,0:T(8,128)S(1)} %get-tuple-element.32.after_ref), channel_id=1, source_target_pairs={{0,128},{16,144},{32,160},{48,176},{64,192},{80,208},{96,224},{112... | collective-permute-start | bytes 98312 | tf_op jit(solution)/shard_map/ppermute | solution.py:430
  31.6 2.5 %near_image.1 = f32[8,8,128]{2,1,0:T(8,128)S(1)} custom-call(s32[1]{0:T(128)} %bitcast.sub_ref, bf16[8,512,256]{2,1,0:T(8,128)(2,1)S(1)} %get-tuple-element.20.after_ref.first_table_ref, bf16[8,512,256]{2,1,0:T(8,128)(2,1)S(1)} %get-tuple-element.21.second_table_ref, bf16[2,64,128,128]{3,2,1,0:T(8,128)(2,1)S(1)} %get-tuple-element.27.first_weights_ref, ...), custom_call_target="tpu_custom_call" | custom-call | flops 3000000000 | tf_op jit(solution)/shard_map/near_image/pallas_call | solution.py:420
  34.1 0.0 collective-permute-done.6
  34.2 12.0 %all_to_all.5 = f32[8,8,128]{2,1,0:T(8,128)S(1)} all-to-all(f32[8,8,128]{2,1,0:T(8,128)S(1)} %add.3), channel_id=1, replica_groups={{0,16,32,48,64,80,96,112},{128,144,160,176,192,208,224,240},{1,17,33,49..., dimensions={0} | all-to-all | bytes 65536 | tf_op jit(solution)/shard_map/all_to_all | solution.py:432
  46.2 0.6 %reduce_sum.9 = f32[8,128]{1,0:T(8,128)} reduce(f32[8,8,128]{2,1,0:T(8,128)S(1)} %all_to_all.5, f32[]{:T(128)} %constant.8.clone.1), dimensions={0}, to_apply=%region_0.0 | reduce | flops 7168 | bytes 36868 | tf_op jit(solution)/shard_map/reduce_sum | solution.py:433
  (2 shorter events, 0.0 us)
Async XLA Ops:
  5.1 7.6 %collective-permute-start = (bf16[4,64,128]{2,1,0:T(8,128)(2,1)}, bf16[4,64,128]{2,1,0:T(8,128)(2,1)S(1)}, u32[]{:S(2)}, u32[]{:S(2)}) collective-permute-start(bf16[4,64,128]{2,1,0:T(8,128)(2,1)} %get-tuple-element.23), channel_id=1, source_target_pairs={{0,4},{1,5},{2,6},{3,7},{4,0},{5,1},{6,2},{7,3},{8,12},{9,13},{10,... | collective-permute-start | bytes 196616 | tf_op jit(solution)/shard_map/ppermute | solution.py:391
  7.3 5.4 %collective-permute-start.1 = (bf16[4,64,128]{2,1,0:T(8,128)(2,1)}, bf16[4,64,128]{2,1,0:T(8,128)(2,1)S(1)}, u32[]{:S(2)}, u32[]{:S(2)}) collective-permute-start(bf16[4,64,128]{2,1,0:T(8,128)(2,1)} %get-tuple-element.24), channel_id=1, source_target_pairs={{0,8},{1,9},{2,10},{3,11},{4,12},{5,13},{6,14},{7,15},{8,0},{9,1},... | collective-permute-start | bytes 196616 | tf_op jit(solution)/shard_map/ppermute | solution.py:391
  9.9 4.7 %collective-permute-start.2 = (bf16[4,64,128]{2,1,0:T(8,128)(2,1)}, bf16[4,64,128]{2,1,0:T(8,128)(2,1)S(1)}, u32[]{:S(2)}, u32[]{:S(2)}) collective-permute-start(bf16[4,64,128]{2,1,0:T(8,128)(2,1)} %get-tuple-element.25), channel_id=1, source_target_pairs={{0,12},{1,13},{2,14},{3,15},{4,8},{5,9},{6,10},{7,11},{8,4},{9,5},... | collective-permute-start | bytes 196616 | tf_op jit(solution)/shard_map/ppermute | solution.py:391
  9.9 1.0 %copy-start.1 = (f32[768,128]{1,0:T(8,128)S(1)}, f32[768,128]{1,0:T(8,128)}, u32[]{:S(2)}) copy-start(f32[768,128]{1,0:T(8,128)} %get-tuple-element.19.extra_ref) | copy-start | bytes 1179652
  10.9 8.4 %copy-start = (bf16[2,2,128,4,2048]{4,3,2,1,0:T(4,128)(2,1)S(1)}, bf16[2,2,128,4,2048]{4,3,2,1,0:T(4,128)(2,1)}, u32[]{:S(2)}) copy-start(bf16[2,2,128,4,2048]{4,3,2,1,0:T(4,128)(2,1)} %param.11) | copy-start | bytes 25165828
  14.6 7.1 %collective-permute-start.4 = (bf16[4,64,128]{2,1,0:T(8,128)(2,1)S(1)}, bf16[4,64,128]{2,1,0:T(8,128)(2,1)S(1)}, u32[]{:S(2)}, u32[]{:S(2)}) collective-permute-start(bf16[4,64,128]{2,1,0:T(8,128)(2,1)S(1)} %get-tuple-element.29), channel_id=1, source_target_pairs={{0,2},{1,3},{2,0},{3,1},{4,6},{5,7},{6,4},{7,5},{8,10},{9,11},{10,... | collective-permute-start | bytes 196616 | tf_op jit(solution)/shard_map/ppermute | solution.py:391
  17.7 5.3 %collective-permute-start.5 = (bf16[4,64,128]{2,1,0:T(8,128)(2,1)S(1)}, bf16[4,64,128]{2,1,0:T(8,128)(2,1)S(1)}, u32[]{:S(2)}, u32[]{:S(2)}) collective-permute-start(bf16[4,64,128]{2,1,0:T(8,128)(2,1)S(1)} %get-tuple-element.30), channel_id=1, source_target_pairs={{0,3},{1,2},{2,1},{3,0},{4,7},{5,6},{6,5},{7,4},{8,11},{9,10},{10,... | collective-permute-start | bytes 196616 | tf_op jit(solution)/shard_map/ppermute | solution.py:391
  19.1 4.4 %collective-permute-start.3 = (bf16[4,64,128]{2,1,0:T(8,128)(2,1)S(1)}, bf16[4,64,128]{2,1,0:T(8,128)(2,1)S(1)}, u32[]{:S(2)}, u32[]{:S(2)}) collective-permute-start(bf16[4,64,128]{2,1,0:T(8,128)(2,1)S(1)} %get-tuple-element.26.after_ref), channel_id=1, source_target_pairs={{0,1},{1,0},{2,3},{3,2},{4,5},{5,4},{6,7},{7,6},{8,9},{9,8},{10,11... | collective-permute-start | bytes 196616 | tf_op jit(solution)/shard_map/ppermute | solution.py:391
  25.9 8.3 %collective-permute-start.6 = (f32[8,8,128]{2,1,0:T(8,128)S(1)}, f32[8,8,128]{2,1,0:T(8,128)S(1)}, u32[]{:S(2)}, u32[]{:S(2)}) collective-permute-start(f32[8,8,128]{2,1,0:T(8,128)S(1)} %get-tuple-element.32.after_ref), channel_id=1, source_target_pairs={{0,128},{16,144},{32,160},{48,176},{64,192},{80,208},{96,224},{112... | collective-permute-start | bytes 98312 | tf_op jit(solution)/shard_map/ppermute | solution.py:430

commit v9 on v8

--- a/solution.py
+++ b/solution.py
@@ -85,7 +85,7 @@
     def gather(dy):
         for dz in range(near):
             for block in range(blocks):
-                start = starts_ref[block, me_ref[0] ^ (dy * near + dz)]
+                start = starts_ref[block, me_ref[0] ^ distance_of(sub_ref[0], dy, dz, near)]
                 first = start >> 7
                 shift = start & (LANES - 1)
                 turn = (LANES - shift) & (LANES - 1)
@@ -134,6 +134,10 @@
         if dy + 1 < len(lhs_refs):
             gather(dy + 1)
         cut(dy, correlate(dy))
+
+
+def distance_of(sub, first, second, near):
+    return jnp.where((sub & 1) == 1, first * near + second, second * near + first)
 
 
 def sine_cosine(angle):
@@ -285,9 +289,9 @@
     half = rows // 2
     count = sources * half
     for dy in range(far_count):
-        bands_ref[me_ref[0] ^ (dy * near)] = near_refs[dy][0]
+        bands_ref[me_ref[0] ^ distance_of(sub_ref[0], dy, 0, near)] = near_refs[dy][0]
         for dz in range(1, near):
-            bands_ref[me_ref[0] ^ (dy * near + dz)] = far_refs[dz - 1][dy]
+            bands_ref[me_ref[0] ^ distance_of(sub_ref[0], dy, dz, near)] = far_refs[dz - 1][dy]
     for block in range(blocks):
         real = bands_ref[:, block * rows : block * rows + half, :].reshape(count, band)
         imag = bands_ref[:, block * rows + half : (block + 1) * rows, :].reshape(count, band)
@@ -387,13 +391,20 @@
         flops=6 * 10**9,
     )(me, sub, band_starts, chirp_ref, doppler_rates, slot_pulse.reshape(blocks, count), samples)
 
-    def swap(value, distance):
-        return lax.ppermute(value, "tile", [(one, one ^ distance) for one in range(tiles)])
+    subs = lax.axis_size("sub")
+
+    def swap(value, by_core):
+        pairs = [
+            (one * tiles + tile, one * tiles + (tile ^ by_core[one & 1]))
+            for one in range(subs)
+            for tile in range(tiles)
+        ]
+        return lax.ppermute(value, ("sub", "tile"), pairs)
 
     table = shape((parts, 2 * count, 2 * LANES), jnp.bfloat16)
     turned = shape((2, places * image_rows, band, LANES), jnp.bfloat16)
     first_table, second_table, mine = call(phase_kernel, "phase", 12, [table, table, own], [vmem()], flops=4 * 10**9)(extra)
-    bands = [mine] + [swap(bands[dy - 1], dy * near) for dy in range(1, far)]
+    bands = [mine] + [swap(bands[dy - 1], (dy, dy * near)) for dy in range(1, far)]
     passed = call(
         relay_kernel,
         "relay",
@@ -404,7 +415,7 @@
     first_weights, second_weights = call(turn_kernel, "turn", 12, [turned, turned], [vmem(), anywhere], flops=4 * 10**9)(
         weights, passed[0]
     )
-    passed = [swap(passed[dz - 1], dz) for dz in range(1, near)]
+    passed = [swap(passed[dz - 1], (dz * near, dz)) for dz in range(1, near)]
     sources = bands + passed
     half = shape((places // 2, 2 * image_rows, LANES), jnp.float32)
     focused = [pltpu.VMEM((2 * band, 2 * LANES), jnp.float32)] * (2 * blocks)

time: 46.9 us -> 47 us (level)
  blocking collectives: 12 us -> 13.2 us
  starting transfers between devices: 15.3 us -> 14.6 us
    all_to_all x1, blocking collectives: 12 us -> 13.2 us  [shards(): lax.all_to_all(near_image + came, 'sub', 0, 0, axis_index_groups=groups,...]
    ppermute x1, starting transfers between devices: 5.75 us -> 5.08 us  [shards(): lax.ppermute(far_image, 'sub', [(one, one ^ half) for one in range(size)])]
  transfers between devices with their start and end apart: 7 -> 7, of which waited for: 4 -> 3; matrix products, arithmetic and copies ran while one was open for 0% -> 0% of each run, Pallas kernels for 14% -> 14%
where the time goes in v9:
time: 47 us; the launch traced here: 46.8 us
  starting transfers between devices  14.6 us (31%)
  Pallas kernels  14 us (30%)
  blocking collectives  13.2 us (28%)
  waiting for transfers between devices  3.37 us (7%)
  local copies, waits for them, and re-layouts  1 us (2%)
  other arithmetic  0.61 us (1%)
    all_to_all x1, blocking collectives, shards(): lax.all_to_all(near_image + came, 'sub', 0, 0, axis_index_groups=groups,...  13.2 us
    ppermute x6, starting transfers between devices, swap(): return lax.ppermute(value, ('sub', 'tile'), pairs)  9.55 us
    ppermute x1, starting transfers between devices, shards(): lax.ppermute(far_image, 'sub', [(one, one ^ half) for one in range(size)])  5.08 us
    pallas_call x1, Pallas kernels, partial_image(): call(compress_kernel, 'compress', 60, [own] * (far - 1) + [extras], [smem...  5.07 us
    ppermute x6, waiting for transfers between devices, swap(): return lax.ppermute(value, ('sub', 'tile'), pairs)  3.36 us
    pallas_call x1, Pallas kernels, partial_image(): call(near_image_kernel, 'near_image', 12, half, [smem] + [vmem()] * 5 + [...  2.51 us
    pallas_call x1, Pallas kernels, partial_image(): call(turn_kernel, 'turn', 12, [turned, turned], [vmem(), anywhere], flops...  2.35 us
    pallas_call x1, Pallas kernels, partial_image(): call(far_image_kernel, 'far_image', 12, [half, shape((blocks, 2 * band, 2...  2.34 us
  transfers between devices with their start and end apart: 7, of which 3 were waited for; matrix products, arithmetic and copies ran while one was open for 0% of the time, Pallas kernels for 14%

profile of v9, /device:TPU:1, one launch (start us, length us, event | category | flops | bytes accessed | tf_op | source)
XLA Modules:
  0.0 46.8 jit_solution(12625437822482281951)
XLA Ops:
  0.0 5.1 %compress.1 = (bf16[4,64,128]{2,1,0:T(8,128)(2,1)}, bf16[4,64,128]{2,1,0:T(8,128)(2,1)}, bf16[4,64,128]{2,1,0:T(8,128)(2,1)}, f32[768,128]{1,0:T(8,128)}) custom-call(s32[1]{0:T(128)} %bitcast.1.me_ref, s32[1]{0:T(128)} %bitcast.sub_ref, s32[2,16]{1,0:T(2,128)} %starts_ref.1, bf16[2,2048]{1,0:T(2,128)(2,1)} %chirp_hbm.1, f32[1,512]{1,0:T(1,128)} %rates_hbm.1, ...), custom_call_target="tpu_custom_call" | custom-call | flops 6000000000 | tf_op jit(solution)/shard_map/compress/pallas_call | solution.py:373
  5.1 2.2 %collective-permute-start = (bf16[4,64,128]{2,1,0:T(8,128)(2,1)}, bf16[4,64,128]{2,1,0:T(8,128)(2,1)S(1)}, u32[]{:S(2)}, u32[]{:S(2)}) collective-permute-start(bf16[4,64,128]{2,1,0:T(8,128)(2,1)} %get-tuple-element.23), channel_id=1, source_target_pairs={{0,1},{1,0},{2,3},{3,2},{4,5},{5,4},{6,7},{7,6},{8,9},{9,8},{10,11... | collective-permute-start | bytes 196616 | tf_op jit(solution)/shard_map/ppermute | solution.py:402
  7.3 2.6 %collective-permute-start.1 = (bf16[4,64,128]{2,1,0:T(8,128)(2,1)}, bf16[4,64,128]{2,1,0:T(8,128)(2,1)S(1)}, u32[]{:S(2)}, u32[]{:S(2)}) collective-permute-start(bf16[4,64,128]{2,1,0:T(8,128)(2,1)} %get-tuple-element.24), channel_id=1, source_target_pairs={{0,2},{1,3},{2,0},{3,1},{4,6},{5,7},{6,4},{7,5},{8,10},{9,11},{10,... | collective-permute-start | bytes 196616 | tf_op jit(solution)/shard_map/ppermute | solution.py:402
  9.9 0.0 collective-permute-start.2
  9.9 0.0 copy-start.1
  9.9 1.0 %copy-done.1 = f32[768,128]{1,0:T(8,128)S(1)} copy-done((f32[768,128]{1,0:T(8,128)S(1)}, f32[768,128]{1,0:T(8,128)}, u32[]{:S(2)}) %copy-start.1) | copy-done | bytes 393240
  10.9 0.0 copy-start
  10.9 1.7 %phase.1 = (bf16[8,512,256]{2,1,0:T(8,128)(2,1)S(1)}, bf16[8,512,256]{2,1,0:T(8,128)(2,1)S(1)}, bf16[4,64,128]{2,1,0:T(8,128)(2,1)S(1)}) custom-call(f32[768,128]{1,0:T(8,128)S(1)} %copy-done.1), custom_call_target="tpu_custom_call" | custom-call | flops 4000000000 | tf_op jit(solution)/shard_map/phase/pallas_call | solution.py:406
  12.6 0.0 collective-permute-done.refs_1_.rest_1_
  12.6 0.0 collective-permute-done.1.refs_2_.rest_2_
  12.6 1.8 %collective-permute-done.2.refs_3_.rest_3_ = bf16[4,64,128]{2,1,0:T(8,128)(2,1)S(1)} collective-permute-done((bf16[4,64,128]{2,1,0:T(8,128)(2,1)}, bf16[4,64,128]{2,1,0:T(8,128)(2,1)S(1)}, u32[]{:S(2)}, u32[]{:S(2)}) %collective-permute-start.2) | collective-permute-done | bytes 65568 | tf_op jit(solution)/shard_map/ppermute | solution.py:402
  14.5 3.1 %collective-permute-start.4 = (bf16[4,64,128]{2,1,0:T(8,128)(2,1)S(1)}, bf16[4,64,128]{2,1,0:T(8,128)(2,1)S(1)}, u32[]{:S(2)}, u32[]{:S(2)}) collective-permute-start(bf16[4,64,128]{2,1,0:T(8,128)(2,1)S(1)} %get-tuple-element.29), channel_id=1, source_target_pairs={{0,8},{1,9},{2,10},{3,11},{4,12},{5,13},{6,14},{7,15},{8,0},{9,1},... | collective-permute-start | bytes 196616 | tf_op jit(solution)/shard_map/ppermute | solution.py:402
  17.5 1.5 %collective-permute-start.5 = (bf16[4,64,128]{2,1,0:T(8,128)(2,1)S(1)}, bf16[4,64,128]{2,1,0:T(8,128)(2,1)S(1)}, u32[]{:S(2)}, u32[]{:S(2)}) collective-permute-start(bf16[4,64,128]{2,1,0:T(8,128)(2,1)S(1)} %get-tuple-element.30), channel_id=1, source_target_pairs={{0,12},{1,13},{2,14},{3,15},{4,8},{5,9},{6,10},{7,11},{8,4},{9,5},... | collective-permute-start | bytes 196616 | tf_op jit(solution)/shard_map/ppermute | solution.py:402
  19.0 0.2 collective-permute-start.3
  19.2 0.0 copy-done
  19.2 2.3 %turn.1 = (bf16[2,64,128,128]{3,2,1,0:T(8,128)(2,1)S(1)}, bf16[2,64,128,128]{3,2,1,0:T(8,128)(2,1)S(1)}) custom-call(bf16[512,64,128]{2,1,0:T(8,128)(2,1)S(1)} %bitcast.14, bf16[4,64,128]{2,1,0:T(8,128)(2,1)S(1)} %get-tuple-element.26.after_ref), custom_call_target="tpu_custom_call" | custom-call | flops 4000000000 | tf_op jit(solution)/shard_map/turn/pallas_call | solution.py:415
  21.5 0.0 collective-permute-done.4.rest_5_
  21.6 1.1 %collective-permute-done.5.rest_6_ = bf16[4,64,128]{2,1,0:T(8,128)(2,1)S(1)} collective-permute-done((bf16[4,64,128]{2,1,0:T(8,128)(2,1)S(1)}, bf16[4,64,128]{2,1,0:T(8,128)(2,1)S(1)}, u32[]{:S(2)}, u32[]{:S(2)}) %collective-permute-start.5) | collective-permute-done | bytes 65568 | tf_op jit(solution)/shard_map/ppermute | solution.py:402
  22.6 0.5 %collective-permute-done.3.rest_4_ = bf16[4,64,128]{2,1,0:T(8,128)(2,1)S(1)} collective-permute-done((bf16[4,64,128]{2,1,0:T(8,128)(2,1)S(1)}, bf16[4,64,128]{2,1,0:T(8,128)(2,1)S(1)}, u32[]{:S(2)}, u32[]{:S(2)}) %collective-permute-start.3) | collective-permute-done | bytes 65568 | tf_op jit(solution)/shard_map/ppermute | solution.py:402
  23.1 2.3 %far_image.1 = (f32[8,8,128]{2,1,0:T(8,128)S(1)}, bf16[2,256,512]{2,1,0:T(8,128)(2,1)S(1)}) custom-call(s32[1]{0:T(128)} %bitcast.1.me_ref, s32[1]{0:T(128)} %bitcast.sub_ref, bf16[8,512,256]{2,1,0:T(8,128)(2,1)S(1)} %get-tuple-element.20.after_ref.first_table_ref, bf16[8,512,256]{2,1,0:T(8,128)(2,1)S(1)} %get-tuple-element.21.second_table_ref, ...), custom_call_target="tpu_custom_call" | custom-call | flops 3000000000 | tf_op jit(solution)/shard_map/far_image/pallas_call | solution.py:422
  25.5 5.1 %collective-permute-start.6 = (f32[8,8,128]{2,1,0:T(8,128)S(1)}, f32[8,8,128]{2,1,0:T(8,128)S(1)}, u32[]{:S(2)}, u32[]{:S(2)}) collective-permute-start(f32[8,8,128]{2,1,0:T(8,128)S(1)} %get-tuple-element.32.after_ref), channel_id=1, source_target_pairs={{0,128},{16,144},{32,160},{48,176},{64,192},{80,208},{96,224},{112... | collective-permute-start | bytes 98312 | tf_op jit(solution)/shard_map/ppermute | solution.py:441
  30.5 2.5 %near_image.1 = f32[8,8,128]{2,1,0:T(8,128)S(1)} custom-call(s32[1]{0:T(128)} %bitcast.sub_ref, bf16[8,512,256]{2,1,0:T(8,128)(2,1)S(1)} %get-tuple-element.20.after_ref.first_table_ref, bf16[8,512,256]{2,1,0:T(8,128)(2,1)S(1)} %get-tuple-element.21.second_table_ref, bf16[2,64,128,128]{3,2,1,0:T(8,128)(2,1)S(1)} %get-tuple-element.27.first_weights_ref, ...), custom_call_target="tpu_custom_call" | custom-call | flops 3000000000 | tf_op jit(solution)/shard_map/near_image/pallas_call | solution.py:431
  33.1 0.0 collective-permute-done.6
  33.1 13.2 %all_to_all.5 = f32[8,8,128]{2,1,0:T(8,128)S(1)} all-to-all(f32[8,8,128]{2,1,0:T(8,128)S(1)} %add.3), channel_id=1, replica_groups={{0,16,32,48,64,80,96,112},{128,144,160,176,192,208,224,240},{1,17,33,49..., dimensions={0} | all-to-all | bytes 65536 | tf_op jit(solution)/shard_map/all_to_all | solution.py:443
  46.2 0.6 %reduce_sum.9 = f32[8,128]{1,0:T(8,128)} reduce(f32[8,8,128]{2,1,0:T(8,128)S(1)} %all_to_all.5, f32[]{:T(128)} %constant.8.clone.1), dimensions={0}, to_apply=%region_0.0 | reduce | flops 7168 | bytes 36868 | tf_op jit(solution)/shard_map/reduce_sum | solution.py:444
  (2 shorter events, 0.0 us)
Async XLA Ops:
  5.1 7.6 %collective-permute-start = (bf16[4,64,128]{2,1,0:T(8,128)(2,1)}, bf16[4,64,128]{2,1,0:T(8,128)(2,1)S(1)}, u32[]{:S(2)}, u32[]{:S(2)}) collective-permute-start(bf16[4,64,128]{2,1,0:T(8,128)(2,1)} %get-tuple-element.23), channel_id=1, source_target_pairs={{0,1},{1,0},{2,3},{3,2},{4,5},{5,4},{6,7},{7,6},{8,9},{9,8},{10,11... | collective-permute-start | bytes 196616 | tf_op jit(solution)/shard_map/ppermute | solution.py:402
  7.3 5.4 %collective-permute-start.1 = (bf16[4,64,128]{2,1,0:T(8,128)(2,1)}, bf16[4,64,128]{2,1,0:T(8,128)(2,1)S(1)}, u32[]{:S(2)}, u32[]{:S(2)}) collective-permute-start(bf16[4,64,128]{2,1,0:T(8,128)(2,1)} %get-tuple-element.24), channel_id=1, source_target_pairs={{0,2},{1,3},{2,0},{3,1},{4,6},{5,7},{6,4},{7,5},{8,10},{9,11},{10,... | collective-permute-start | bytes 196616 | tf_op jit(solution)/shard_map/ppermute | solution.py:402
  9.9 4.5 %collective-permute-start.2 = (bf16[4,64,128]{2,1,0:T(8,128)(2,1)}, bf16[4,64,128]{2,1,0:T(8,128)(2,1)S(1)}, u32[]{:S(2)}, u32[]{:S(2)}) collective-permute-start(bf16[4,64,128]{2,1,0:T(8,128)(2,1)} %get-tuple-element.25), channel_id=1, source_target_pairs={{0,3},{1,2},{2,1},{3,0},{4,7},{5,6},{6,5},{7,4},{8,11},{9,10},{10,... | collective-permute-start | bytes 196616 | tf_op jit(solution)/shard_map/ppermute | solution.py:402
  9.9 1.0 %copy-start.1 = (f32[768,128]{1,0:T(8,128)S(1)}, f32[768,128]{1,0:T(8,128)}, u32[]{:S(2)}) copy-start(f32[768,128]{1,0:T(8,128)} %get-tuple-element.19.extra_ref) | copy-start | bytes 1179652
  10.9 8.3 %copy-start = (bf16[2,2,128,4,2048]{4,3,2,1,0:T(4,128)(2,1)S(1)}, bf16[2,2,128,4,2048]{4,3,2,1,0:T(4,128)(2,1)}, u32[]{:S(2)}) copy-start(bf16[2,2,128,4,2048]{4,3,2,1,0:T(4,128)(2,1)} %param.11) | copy-start | bytes 25165828
  14.5 7.1 %collective-permute-start.4 = (bf16[4,64,128]{2,1,0:T(8,128)(2,1)S(1)}, bf16[4,64,128]{2,1,0:T(8,128)(2,1)S(1)}, u32[]{:S(2)}, u32[]{:S(2)}) collective-permute-start(bf16[4,64,128]{2,1,0:T(8,128)(2,1)S(1)} %get-tuple-element.29), channel_id=1, source_target_pairs={{0,8},{1,9},{2,10},{3,11},{4,12},{5,13},{6,14},{7,15},{8,0},{9,1},... | collective-permute-start | bytes 196616 | tf_op jit(solution)/shard_map/ppermute | solution.py:402
  17.5 5.1 %collective-permute-start.5 = (bf16[4,64,128]{2,1,0:T(8,128)(2,1)S(1)}, bf16[4,64,128]{2,1,0:T(8,128)(2,1)S(1)}, u32[]{:S(2)}, u32[]{:S(2)}) collective-permute-start(bf16[4,64,128]{2,1,0:T(8,128)(2,1)S(1)} %get-tuple-element.30), channel_id=1, source_target_pairs={{0,12},{1,13},{2,14},{3,15},{4,8},{5,9},{6,10},{7,11},{8,4},{9,5},... | collective-permute-start | bytes 196616 | tf_op jit(solution)/shard_map/ppermute | solution.py:402
  19.0 4.1 %collective-permute-start.3 = (bf16[4,64,128]{2,1,0:T(8,128)(2,1)S(1)}, bf16[4,64,128]{2,1,0:T(8,128)(2,1)S(1)}, u32[]{:S(2)}, u32[]{:S(2)}) collective-permute-start(bf16[4,64,128]{2,1,0:T(8,128)(2,1)S(1)} %get-tuple-element.26.after_ref), channel_id=1, source_target_pairs={{0,4},{1,5},{2,6},{3,7},{4,0},{5,1},{6,2},{7,3},{8,12},{9,13},{10,... | collective-permute-start | bytes 196616 | tf_op jit(solution)/shard_map/ppermute | solution.py:402
  25.5 7.6 %collective-permute-start.6 = (f32[8,8,128]{2,1,0:T(8,128)S(1)}, f32[8,8,128]{2,1,0:T(8,128)S(1)}, u32[]{:S(2)}, u32[]{:S(2)}) collective-permute-start(f32[8,8,128]{2,1,0:T(8,128)S(1)} %get-tuple-element.32.after_ref), channel_id=1, source_target_pairs={{0,128},{16,144},{32,160},{48,176},{64,192},{80,208},{96,224},{112... | collective-permute-start | bytes 98312 | tf_op jit(solution)/shard_map/ppermute | solution.py:441

commit v10 on v9

--- a/solution.py
+++ b/solution.py
@@ -1,3 +1,5 @@
+import functools
+
 import jax
 import jax.numpy as jnp
 import numpy as np
@@ -136,8 +138,16 @@
         cut(dy, correlate(dy))
 
 
+FIRST_Z, FIRST_Y = (0, 3, 2, 1), (0, 2, 1, 3)
+SECOND_Z, SECOND_Y = (0, 1, 3, 2), (0, 3, 2, 1)
+
+
 def distance_of(sub, first, second, near):
-    return jnp.where((sub & 1) == 1, first * near + second, second * near + first)
+    return jnp.where(
+        (sub & 1) == 1,
+        FIRST_Y[first] * near + SECOND_Z[second],
+        SECOND_Y[second] * near + FIRST_Z[first],
+    )
 
 
 def sine_cosine(angle):
@@ -168,9 +178,10 @@
     phase_table(1, extra_ref, second_table_ref)
 
 
-def turn_kernel(weights_ref, after_ref, first_ref, second_ref):
+def turn_kernel(far, sub_ref, weights_ref, after_ref, first_ref, second_ref):
     band = first_ref.shape[2]
     lines = first_ref.shape[1]
+    offset = ((sub_ref[0] >> 3) ^ far) * lines
     size = 16
     side = size * size
     row = lax.broadcasted_iota(jnp.int32, (side, side), 0)
@@ -186,7 +197,9 @@
                     block_rows = jnp.concatenate(
                         [
                             weights_ref[
-                                pl.ds((block * 2 + part) * band + first, size), top : top + size, :
+                                pl.ds((block * 2 + part) * band + first, size),
+                                pl.ds(pl.multiple_of(offset + top, size), size),
+                                :,
                             ].reshape(side, LANES)
                             for top in tops
                         ],
@@ -262,7 +275,7 @@
                     focus_real = focused_ref[k : k + 16, lanes]
                     focus_imag = focused_ref[band + k : band + k + 16, lanes]
                     for row in range(image_rows):
-                        line = (side * places + 2 * pair + place) * image_rows + row
+                        line = (2 * pair + place) * image_rows + row
                         weight_real = weights_refs[block][0, line, k : k + 16, :].astype(jnp.float32)
                         weight_imag = weights_refs[block][1, line, k : k + 16, :].astype(jnp.float32)
                         for first in (0, 8):
@@ -402,9 +415,22 @@
         return lax.ppermute(value, ("sub", "tile"), pairs)
 
     table = shape((parts, 2 * count, 2 * LANES), jnp.bfloat16)
-    turned = shape((2, places * image_rows, band, LANES), jnp.bfloat16)
+    turned = shape((2, places // 2 * image_rows, band, LANES), jnp.bfloat16)
+
+    def turn(far, after):
+        return call(
+            functools.partial(turn_kernel, far),
+            "turn",
+            12,
+            [turned, turned],
+            [smem, vmem(), anywhere],
+            flops=2 * 10**9,
+        )(sub, weights, after)
+
     first_table, second_table, mine = call(phase_kernel, "phase", 12, [table, table, own], [vmem()], flops=4 * 10**9)(extra)
-    bands = [mine] + [swap(bands[dy - 1], (dy, dy * near)) for dy in range(1, far)]
+    bands = [mine] + [
+        swap(bands[dy - 1], (FIRST_Z[dy], FIRST_Y[dy] * near)) for dy in range(1, far)
+    ]
     passed = call(
         relay_kernel,
         "relay",
@@ -412,10 +438,8 @@
         [shape((far, 2 * pulses, band), jnp.bfloat16)] * (near - 1),
         [anywhere] + [vmem()] * far,
     )(first_table, *bands)
-    first_weights, second_weights = call(turn_kernel, "turn", 12, [turned, turned], [vmem(), anywhere], flops=4 * 10**9)(
-        weights, passed[0]
-    )
-    passed = [swap(passed[dz - 1], (dz * near, dz)) for dz in range(1, near)]
+    far_weights = turn(1, passed[0])
+    passed = [swap(passed[dz - 1], (SECOND_Y[dz] * near, SECOND_Z[dz])) for dz in range(1, near)]
     sources = bands + passed
     half = shape((places // 2, 2 * image_rows, LANES), jnp.float32)
     focused = [pltpu.VMEM((2 * band, 2 * LANES), jnp.float32)] * (2 * blocks)
@@ -427,10 +451,11 @@
         [smem, smem] + [vmem()] * (4 + len(sources)),
         [pltpu.VMEM((tiles, 2 * pulses, band), jnp.bfloat16)] + focused,
         flops=3 * 10**9,
-    )(me, sub, first_table, second_table, first_weights, second_weights, *sources)
+    )(me, sub, first_table, second_table, *far_weights, *sources)
+    near_weights = turn(0, far_image)
     near_image = call(
         near_image_kernel, "near_image", 12, half, [smem] + [vmem()] * 5 + [anywhere], focused, flops=3 * 10**9
-    )(sub, first_table, second_table, first_weights, second_weights, left, far_image)
+    )(sub, first_table, second_table, *near_weights, left, far_image)
     return sub, far_image, near_image
 
 

time: 47 us -> 47.2 us (level)
  blocking collectives: 13.2 us -> 12.5 us
  waiting for transfers between devices: 3.37 us -> 3.93 us
    all_to_all x1, blocking collectives: 13.2 us -> 12.5 us  [shards(): lax.all_to_all(near_image + came, 'sub', 0, 0, axis_index_groups=groups,...]
    ppermute x6, waiting for transfers between devices: 3.36 us -> 3.92 us  [swap(): return lax.ppermute(value, ('sub', 'tile'), pairs)]
    pallas_call x1 -> x2, Pallas kernels: 2.35 us -> 2.52 us  [turn(): call(functools.partial(turn_kernel, far), 'turn', 12, [turned, turned], [...]
    unnamed x4 -> x6, local copies, waits for them, and re-layouts: 1 us -> 1.15 us
  transfers between devices with their start and end apart: 7 -> 7, of which waited for: 3 -> 2; matrix products, arithmetic and copies ran while one was open for 0% -> 0% of each run, Pallas kernels for 14% -> 14%
where the time goes in v10:
time: 47.2 us; the launch traced here: 47 us
  starting transfers between devices  14.4 us (31%)
  Pallas kernels  14.3 us (30%)
  blocking collectives  12.5 us (26%)
  waiting for transfers between devices  3.93 us (8%)
  local copies, waits for them, and re-layouts  1.15 us (2%)
  other arithmetic  0.61 us (1%)
    all_to_all x1, blocking collectives, shards(): lax.all_to_all(near_image + came, 'sub', 0, 0, axis_index_groups=groups,...  12.5 us
    ppermute x6, starting transfers between devices, swap(): return lax.ppermute(value, ('sub', 'tile'), pairs)  9.24 us
    ppermute x1, starting transfers between devices, shards(): lax.ppermute(far_image, 'sub', [(one, one ^ half) for one in range(size)])  5.13 us
    pallas_call x1, Pallas kernels, partial_image(): call(compress_kernel, 'compress', 60, [own] * (far - 1) + [extras], [smem...  5.08 us
    ppermute x6, waiting for transfers between devices, swap(): return lax.ppermute(value, ('sub', 'tile'), pairs)  3.92 us
    pallas_call x1, Pallas kernels, partial_image(): call(near_image_kernel, 'near_image', 12, half, [smem] + [vmem()] * 5 + [...  2.58 us
    pallas_call x2, Pallas kernels, turn(): call(functools.partial(turn_kernel, far), 'turn', 12, [turned, turned], [...  2.52 us
    pallas_call x1, Pallas kernels, partial_image(): call(far_image_kernel, 'far_image', 12, [half, shape((blocks, 2 * band, 2...  2.41 us
  transfers between devices with their start and end apart: 7, of which 2 were waited for; matrix products, arithmetic and copies ran while one was open for 0% of the time, Pallas kernels for 14%

profile of v10, /device:TPU:1, one launch (start us, length us, event | category | flops | bytes accessed | tf_op | source)
XLA Modules:
  0.0 47.0 jit_solution(13565987858051044537)
XLA Ops:
  0.0 5.1 %compress.1 = (bf16[4,64,128]{2,1,0:T(8,128)(2,1)}, bf16[4,64,128]{2,1,0:T(8,128)(2,1)}, bf16[4,64,128]{2,1,0:T(8,128)(2,1)}, f32[768,128]{1,0:T(8,128)}) custom-call(s32[1]{0:T(128)} %bitcast.1.me_ref, s32[1]{0:T(128)} %bitcast.sub_ref, s32[2,16]{1,0:T(2,128)} %starts_ref.1, bf16[2,2048]{1,0:T(2,128)(2,1)} %chirp_hbm.1, f32[1,512]{1,0:T(1,128)} %rates_hbm.1, ...), custom_call_target="tpu_custom_call" | custom-call | flops 6000000000 | tf_op jit(solution)/shard_map/compress/pallas_call | solution.py:386
  5.1 3.8 %collective-permute-start = (bf16[4,64,128]{2,1,0:T(8,128)(2,1)}, bf16[4,64,128]{2,1,0:T(8,128)(2,1)S(1)}, u32[]{:S(2)}, u32[]{:S(2)}) collective-permute-start(bf16[4,64,128]{2,1,0:T(8,128)(2,1)} %get-tuple-element.25), channel_id=1, source_target_pairs={{0,3},{1,2},{2,1},{3,0},{4,7},{5,6},{6,5},{7,4},{8,11},{9,10},{10,... | collective-permute-start | bytes 196616 | tf_op jit(solution)/shard_map/ppermute | solution.py:415
  8.9 0.4 collective-permute-start.1
  9.3 0.4 collective-permute-start.2
  9.7 0.0 slice-start
  9.7 0.0 copy-start
  9.7 1.1 %copy-done = f32[768,128]{1,0:T(8,128)S(1)} copy-done((f32[768,128]{1,0:T(8,128)S(1)}, f32[768,128]{1,0:T(8,128)}, u32[]{:S(2)}) %copy-start) | copy-done | bytes 393240
  10.8 0.0 slice-start.1
  10.8 1.7 %phase.1 = (bf16[8,512,256]{2,1,0:T(8,128)(2,1)S(1)}, bf16[8,512,256]{2,1,0:T(8,128)(2,1)S(1)}, bf16[4,64,128]{2,1,0:T(8,128)(2,1)S(1)}) custom-call(f32[768,128]{1,0:T(8,128)S(1)} %copy-done), custom_call_target="tpu_custom_call" | custom-call | flops 4000000000 | tf_op jit(solution)/shard_map/phase/pallas_call | solution.py:430
  12.6 0.0 collective-permute-done.refs_1_.rest_1_
  12.6 0.0 collective-permute-done.1.refs_2_.rest_2_
  12.6 1.6 %collective-permute-done.2.refs_3_.rest_3_ = bf16[4,64,128]{2,1,0:T(8,128)(2,1)S(1)} collective-permute-done((bf16[4,64,128]{2,1,0:T(8,128)(2,1)}, bf16[4,64,128]{2,1,0:T(8,128)(2,1)S(1)}, u32[]{:S(2)}, u32[]{:S(2)}) %collective-permute-start.2) | collective-permute-done | bytes 65568 | tf_op jit(solution)/shard_map/ppermute | solution.py:415
  14.2 4.2 %collective-permute-start.4 = (bf16[4,64,128]{2,1,0:T(8,128)(2,1)S(1)}, bf16[4,64,128]{2,1,0:T(8,128)(2,1)S(1)}, u32[]{:S(2)}, u32[]{:S(2)}) collective-permute-start(bf16[4,64,128]{2,1,0:T(8,128)(2,1)S(1)} %get-tuple-element.31), channel_id=1, source_target_pairs={{0,8},{1,9},{2,10},{3,11},{4,12},{5,13},{6,14},{7,15},{8,0},{9,1},... | collective-permute-start | bytes 196616 | tf_op jit(solution)/shard_map/ppermute | solution.py:415
  18.4 0.0 collective-permute-start.5
  18.4 0.4 collective-permute-start.3
  18.8 0.0 slice-done
  18.8 0.0 slice-done.1
  18.8 1.3 %turn.2 = (bf16[2,32,128,128]{3,2,1,0:T(8,128)(2,1)S(1)}, bf16[2,32,128,128]{3,2,1,0:T(8,128)(2,1)S(1)}) custom-call(s32[1]{0:T(128)} %bitcast.sub_ref, bf16[512,64,128]{2,1,0:T(8,128)(2,1)S(1)} %bitcast.16, bf16[4,64,128]{2,1,0:T(8,128)(2,1)S(1)} %get-tuple-element.28.after_ref), custom_call_target="tpu_custom_call" | custom-call | flops 2000000000 | tf_op jit(solution)/shard_map/turn/pallas_call | solution.py:421
  20.1 0.0 collective-permute-done.4.rest_5_
  20.1 2.3 %collective-permute-done.5.rest_6_ = bf16[4,64,128]{2,1,0:T(8,128)(2,1)S(1)} collective-permute-done((bf16[4,64,128]{2,1,0:T(8,128)(2,1)S(1)}, bf16[4,64,128]{2,1,0:T(8,128)(2,1)S(1)}, u32[]{:S(2)}, u32[]{:S(2)}) %collective-permute-start.5) | collective-permute-done | bytes 65568 | tf_op jit(solution)/shard_map/ppermute | solution.py:415
  22.4 0.0 collective-permute-done.3.rest_4_
  22.4 2.4 %far_image.1 = (f32[8,8,128]{2,1,0:T(8,128)S(1)}, bf16[2,256,512]{2,1,0:T(8,128)(2,1)S(1)}) custom-call(s32[1]{0:T(128)} %bitcast.1.me_ref, s32[1]{0:T(128)} %bitcast.sub_ref, bf16[8,512,256]{2,1,0:T(8,128)(2,1)S(1)} %get-tuple-element.22.after_ref.first_table_ref, bf16[8,512,256]{2,1,0:T(8,128)(2,1)S(1)} %get-tuple-element.23.second_table_ref, ...), custom_call_target="tpu_custom_call" | custom-call | flops 3000000000 | tf_op jit(solution)/shard_map/far_image/pallas_call | solution.py:446
  24.8 5.1 %collective-permute-start.6 = (f32[8,8,128]{2,1,0:T(8,128)S(1)}, f32[8,8,128]{2,1,0:T(8,128)S(1)}, u32[]{:S(2)}, u32[]{:S(2)}) collective-permute-start(f32[8,8,128]{2,1,0:T(8,128)S(1)} %get-tuple-element.33.after_ref), channel_id=1, source_target_pairs={{0,128},{16,144},{32,160},{48,176},{64,192},{80,208},{96,224},{112... | collective-permute-start | bytes 98312 | tf_op jit(solution)/shard_map/ppermute | solution.py:466
  30.0 1.3 %turn.3 = (bf16[2,32,128,128]{3,2,1,0:T(8,128)(2,1)S(1)}, bf16[2,32,128,128]{3,2,1,0:T(8,128)(2,1)S(1)}) custom-call(s32[1]{0:T(128)} %bitcast.sub_ref, bf16[512,64,128]{2,1,0:T(8,128)(2,1)S(1)} %bitcast.17, f32[8,8,128]{2,1,0:T(8,128)S(1)} %get-tuple-element.33.after_ref), custom_call_target="tpu_custom_call" | custom-call | flops 2000000000 | tf_op jit(solution)/shard_map/turn/pallas_call | solution.py:421
  31.2 2.6 %near_image.1 = f32[8,8,128]{2,1,0:T(8,128)S(1)} custom-call(s32[1]{0:T(128)} %bitcast.sub_ref, bf16[8,512,256]{2,1,0:T(8,128)(2,1)S(1)} %get-tuple-element.22.after_ref.first_table_ref, bf16[8,512,256]{2,1,0:T(8,128)(2,1)S(1)} %get-tuple-element.23.second_table_ref, bf16[2,32,128,128]{3,2,1,0:T(8,128)(2,1)S(1)} %get-tuple-element.34.first_weights_ref, ...), custom_call_target="tpu_custom_call" | custom-call | flops 3000000000 | tf_op jit(solution)/shard_map/near_image/pallas_call | solution.py:456
  33.8 0.0 collective-permute-done.6
  33.9 12.5 %all_to_all.5 = f32[8,8,128]{2,1,0:T(8,128)S(1)} all-to-all(f32[8,8,128]{2,1,0:T(8,128)S(1)} %add.3), channel_id=1, replica_groups={{0,16,32,48,64,80,96,112},{128,144,160,176,192,208,224,240},{1,17,33,49..., dimensions={0} | all-to-all | bytes 65536 | tf_op jit(solution)/shard_map/all_to_all | solution.py:468
  46.4 0.6 %reduce_sum.9 = f32[8,128]{1,0:T(8,128)} reduce(f32[8,8,128]{2,1,0:T(8,128)S(1)} %all_to_all.5, f32[]{:T(128)} %constant.8.clone.1), dimensions={0}, to_apply=%region_0.0 | reduce | flops 7168 | bytes 36868 | tf_op jit(solution)/shard_map/reduce_sum | solution.py:469
  (3 shorter events, 0.0 us)
Async XLA Ops:
  5.1 7.5 %collective-permute-start = (bf16[4,64,128]{2,1,0:T(8,128)(2,1)}, bf16[4,64,128]{2,1,0:T(8,128)(2,1)S(1)}, u32[]{:S(2)}, u32[]{:S(2)}) collective-permute-start(bf16[4,64,128]{2,1,0:T(8,128)(2,1)} %get-tuple-element.25), channel_id=1, source_target_pairs={{0,3},{1,2},{2,1},{3,0},{4,7},{5,6},{6,5},{7,4},{8,11},{9,10},{10,... | collective-permute-start | bytes 196616 | tf_op jit(solution)/shard_map/ppermute | solution.py:415
  8.9 3.7 %collective-permute-start.1 = (bf16[4,64,128]{2,1,0:T(8,128)(2,1)}, bf16[4,64,128]{2,1,0:T(8,128)(2,1)S(1)}, u32[]{:S(2)}, u32[]{:S(2)}) collective-permute-start(bf16[4,64,128]{2,1,0:T(8,128)(2,1)} %get-tuple-element.26), channel_id=1, source_target_pairs={{0,2},{1,3},{2,0},{3,1},{4,6},{5,7},{6,4},{7,5},{8,10},{9,11},{10,... | collective-permute-start | bytes 196616 | tf_op jit(solution)/shard_map/ppermute | solution.py:415
  9.3 4.8 %collective-permute-start.2 = (bf16[4,64,128]{2,1,0:T(8,128)(2,1)}, bf16[4,64,128]{2,1,0:T(8,128)(2,1)S(1)}, u32[]{:S(2)}, u32[]{:S(2)}) collective-permute-start(bf16[4,64,128]{2,1,0:T(8,128)(2,1)} %get-tuple-element.27), channel_id=1, source_target_pairs={{0,1},{1,0},{2,3},{3,2},{4,5},{5,4},{6,7},{7,6},{8,9},{9,8},{10,11... | collective-permute-start | bytes 196616 | tf_op jit(solution)/shard_map/ppermute | solution.py:415
  9.7 9.1 %slice-start = ((s8[8388608]{0:T(1024)(128)(4,1)}), s8[4194304]{0:T(1024)(128)(4,1)S(1)}, s32[]{:S(2)}) async-start(s8[8388608]{0:T(1024)(128)(4,1)} %bitcast.14), calls=%async_computation.1 | async-start | bytes 8388608
  9.7 1.1 %copy-start = (f32[768,128]{1,0:T(8,128)S(1)}, f32[768,128]{1,0:T(8,128)}, u32[]{:S(2)}) copy-start(f32[768,128]{1,0:T(8,128)} %get-tuple-element.21.extra_ref) | copy-start | bytes 1179652
  10.8 8.0 %slice-start.1 = ((s8[8388608]{0:T(1024)(128)(4,1)}), s8[4194304]{0:T(1024)(128)(4,1)S(1)}, s32[]{:S(2)}) async-start(s8[8388608]{0:T(1024)(128)(4,1)} %bitcast.14), calls=%async_computation.2 | async-start | bytes 8388608
  14.2 5.9 %collective-permute-start.4 = (bf16[4,64,128]{2,1,0:T(8,128)(2,1)S(1)}, bf16[4,64,128]{2,1,0:T(8,128)(2,1)S(1)}, u32[]{:S(2)}, u32[]{:S(2)}) collective-permute-start(bf16[4,64,128]{2,1,0:T(8,128)(2,1)S(1)} %get-tuple-element.31), channel_id=1, source_target_pairs={{0,8},{1,9},{2,10},{3,11},{4,12},{5,13},{6,14},{7,15},{8,0},{9,1},... | collective-permute-start | bytes 196616 | tf_op jit(solution)/shard_map/ppermute | solution.py:415
  18.4 4.0 %collective-permute-start.5 = (bf16[4,64,128]{2,1,0:T(8,128)(2,1)S(1)}, bf16[4,64,128]{2,1,0:T(8,128)(2,1)S(1)}, u32[]{:S(2)}, u32[]{:S(2)}) collective-permute-start(bf16[4,64,128]{2,1,0:T(8,128)(2,1)S(1)} %get-tuple-element.32), channel_id=1, source_target_pairs={{0,4},{1,5},{2,6},{3,7},{4,0},{5,1},{6,2},{7,3},{8,12},{9,13},{10,... | collective-permute-start | bytes 196616 | tf_op jit(solution)/shard_map/ppermute | solution.py:415
  18.4 4.0 %collective-permute-start.3 = (bf16[4,64,128]{2,1,0:T(8,128)(2,1)S(1)}, bf16[4,64,128]{2,1,0:T(8,128)(2,1)S(1)}, u32[]{:S(2)}, u32[]{:S(2)}) collective-permute-start(bf16[4,64,128]{2,1,0:T(8,128)(2,1)S(1)} %get-tuple-element.28.after_ref), channel_id=1, source_target_pairs={{0,12},{1,13},{2,14},{3,15},{4,8},{5,9},{6,10},{7,11},{8,4},{9,5},... | collective-permute-start | bytes 196616 | tf_op jit(solution)/shard_map/ppermute | solution.py:415
  24.8 9.0 %collective-permute-start.6 = (f32[8,8,128]{2,1,0:T(8,128)S(1)}, f32[8,8,128]{2,1,0:T(8,128)S(1)}, u32[]{:S(2)}, u32[]{:S(2)}) collective-permute-start(f32[8,8,128]{2,1,0:T(8,128)S(1)} %get-tuple-element.33.after_ref), channel_id=1, source_target_pairs={{0,128},{16,144},{32,160},{48,176},{64,192},{80,208},{96,224},{112... | collective-permute-start | bytes 98312 | tf_op jit(solution)/shard_map/ppermute | solution.py:466

commit v11 on v9

--- a/solution.py
+++ b/solution.py
@@ -51,9 +51,12 @@
     for part in range(2):
         line = jnp.concatenate([chirp[part : part + 1], pad], 1)
         shifted = pltpu.roll(
-            jnp.broadcast_to(line, (LANES, span)), 0, 1, stride=1, stride_axis=0
+            jnp.broadcast_to(line, (16, span)), 0, 1, stride=1, stride_axis=0
         ).astype(jnp.bfloat16)
-        toeplitz_ref[part * LANES : (part + 1) * LANES, :] = shifted
+        for first in range(0, LANES, 16):
+            toeplitz_ref[part * LANES + first : part * LANES + first + 16, :] = (
+                pltpu.roll(shifted, first, 1) if first > 0 else shifted
+            )
     count = slots_ref.shape[1]
     row = lax.broadcasted_iota(jnp.int32, (count, count), 0)
     col = lax.broadcasted_iota(jnp.int32, (count, count), 1)
@@ -136,8 +139,16 @@
         cut(dy, correlate(dy))
 
 
+FIRST_Z, FIRST_Y = (0, 3, 2, 1), (0, 2, 1, 3)
+SECOND_Z, SECOND_Y = (0, 1, 3, 2), (0, 3, 2, 1)
+
+
 def distance_of(sub, first, second, near):
-    return jnp.where((sub & 1) == 1, first * near + second, second * near + first)
+    return jnp.where(
+        (sub & 1) == 1,
+        FIRST_Y[first] * near + SECOND_Z[second],
+        SECOND_Y[second] * near + FIRST_Z[first],
+    )
 
 
 def sine_cosine(angle):
@@ -237,9 +248,9 @@
 
 def weighted_sum(side, table_refs, weights_refs, image_ref, left_ref, focused_refs):
     blocks = len(table_refs)
-    places, lines, _ = image_ref.shape
-    image_rows = lines // 2
-    pairs = places // 2
+    pairs, lines, _ = image_ref.shape
+    places = 2 * pairs
+    image_rows = lines // 4
     band = weights_refs[0].shape[2]
 
     def focus(pair):
@@ -252,6 +263,7 @@
     for pair in range(pairs):
         if pair + 1 < pairs:
             focus(pair + 1)
+        sums = []
         for place in range(2):
             lanes = slice(place * LANES, (place + 1) * LANES)
             real = [jnp.zeros((8, LANES), jnp.float32)] * image_rows
@@ -271,9 +283,10 @@
                             fr, fi = focus_real[part], focus_imag[part]
                             real[row] = real[row] + (wr * fr - wi * fi)
                             imag[row] = imag[row] + (wr * fi + wi * fr)
-            image_ref[2 * pair + place] = jnp.concatenate(
-                [jnp.sum(one, 0, keepdims=True) for one in real + imag], 0
+            sums.append(
+                jnp.concatenate([jnp.sum(one, 0, keepdims=True) for one in real + imag], 0)
             )
+        image_ref[pair] = jnp.concatenate(sums, 0).astype(image_ref.dtype)
 
 
 def far_image_kernel(
@@ -404,7 +417,9 @@
     table = shape((parts, 2 * count, 2 * LANES), jnp.bfloat16)
     turned = shape((2, places * image_rows, band, LANES), jnp.bfloat16)
     first_table, second_table, mine = call(phase_kernel, "phase", 12, [table, table, own], [vmem()], flops=4 * 10**9)(extra)
-    bands = [mine] + [swap(bands[dy - 1], (dy, dy * near)) for dy in range(1, far)]
+    bands = [mine] + [
+        swap(bands[dy - 1], (FIRST_Z[dy], FIRST_Y[dy] * near)) for dy in range(1, far)
+    ]
     passed = call(
         relay_kernel,
         "relay",
@@ -415,21 +430,21 @@
     first_weights, second_weights = call(turn_kernel, "turn", 12, [turned, turned], [vmem(), anywhere], flops=4 * 10**9)(
         weights, passed[0]
     )
-    passed = [swap(passed[dz - 1], (dz * near, dz)) for dz in range(1, near)]
+    passed = [swap(passed[dz - 1], (SECOND_Y[dz] * near, SECOND_Z[dz])) for dz in range(1, near)]
     sources = bands + passed
-    half = shape((places // 2, 2 * image_rows, LANES), jnp.float32)
+    half = (places // 4, 4 * image_rows, LANES)
     focused = [pltpu.VMEM((2 * band, 2 * LANES), jnp.float32)] * (2 * blocks)
     far_image, left = call(
         far_image_kernel,
         "far_image",
         12,
-        [half, shape((blocks, 2 * band, 2 * count), jnp.bfloat16)],
+        [shape(half, jnp.bfloat16), shape((blocks, 2 * band, 2 * count), jnp.bfloat16)],
         [smem, smem] + [vmem()] * (4 + len(sources)),
         [pltpu.VMEM((tiles, 2 * pulses, band), jnp.bfloat16)] + focused,
         flops=3 * 10**9,
     )(me, sub, first_table, second_table, first_weights, second_weights, *sources)
     near_image = call(
-        near_image_kernel, "near_image", 12, half, [smem] + [vmem()] * 5 + [anywhere], focused, flops=3 * 10**9
+        near_image_kernel, "near_image", 12, shape(half, jnp.float32), [smem] + [vmem()] * 5 + [anywhere], focused, flops=3 * 10**9
     )(sub, first_table, second_table, first_weights, second_weights, left, far_image)
     return sub, far_image, near_image
 
@@ -440,7 +455,8 @@
     half = size // 2
     came = lax.ppermute(far_image, "sub", [(one, one ^ half) for one in range(size)])
     groups = [list(range(half)), list(range(half, size))]
-    pieces = lax.all_to_all(near_image + came, "sub", 0, 0, axis_index_groups=groups, tiled=True)
+    held = (near_image + came.astype(jnp.float32)).reshape(half, -1, LANES)
+    pieces = lax.all_to_all(held, "sub", 0, 0, axis_index_groups=groups, tiled=True)
     return jnp.sum(pieces, 0).reshape(2, -1, LANES)
 
 

time: 47 us -> 45.9 us (0.977)
  blocking collectives: 13.2 us -> 12.7 us
  transfers between devices with their start and end apart: 7 -> 7, of which waited for: 3 -> 2; matrix products, arithmetic and copies ran while one was open for 0% -> 0% of each run, Pallas kernels for 14% -> 14%
where the time goes in v11:
time: 45.9 us; the launch traced here: 45.8 us
  starting transfers between devices  14.2 us (31%)
  Pallas kernels  14.1 us (31%)
  blocking collectives  12.7 us (28%)
  waiting for transfers between devices  2.99 us (7%)
  local copies, waits for them, and re-layouts  1 us (2%)
  other arithmetic  0.61 us (1%)
    all_to_all x1, blocking collectives, shards(): lax.all_to_all(held, 'sub', 0, 0, axis_index_groups=groups, tiled=True)  12.7 us
    ppermute x6, starting transfers between devices, swap(): return lax.ppermute(value, ('sub', 'tile'), pairs)  9.24 us
    pallas_call x1, Pallas kernels, partial_image(): call(compress_kernel, 'compress', 60, [own] * (far - 1) + [extras], [smem...  5.2 us
    ppermute x1, starting transfers between devices, shards(): lax.ppermute(far_image, 'sub', [(one, one ^ half) for one in range(size)])  4.95 us
    ppermute x6, waiting for transfers between devices, swap(): return lax.ppermute(value, ('sub', 'tile'), pairs)  2.99 us
    pallas_call x1, Pallas kernels, partial_image(): call(near_image_kernel, 'near_image', 12, shape(half, jnp.float32), [smem...  2.51 us
    pallas_call x1, Pallas kernels, partial_image(): call(far_image_kernel, 'far_image', 12, [shape(half, jnp.bfloat16), shape...  2.35 us
    pallas_call x1, Pallas kernels, partial_image(): call(turn_kernel, 'turn', 12, [turned, turned], [vmem(), anywhere], flops...  2.35 us
  transfers between devices with their start and end apart: 7, of which 2 were waited for; matrix products, arithmetic and copies ran while one was open for 0% of the time, Pallas kernels for 14%

profile of v11, /device:TPU:1, one launch (start us, length us, event | category | flops | bytes accessed | tf_op | source)
XLA Modules:
  0.0 45.8 jit_solution(7886673276707287789)
XLA Ops:
  0.0 5.2 %compress.1 = (bf16[4,64,128]{2,1,0:T(8,128)(2,1)}, bf16[4,64,128]{2,1,0:T(8,128)(2,1)}, bf16[4,64,128]{2,1,0:T(8,128)(2,1)}, f32[768,128]{1,0:T(8,128)}) custom-call(s32[1]{0:T(128)} %bitcast.1.me_ref, s32[1]{0:T(128)} %bitcast.sub_ref, s32[2,16]{1,0:T(2,128)} %starts_ref.1, bf16[2,2048]{1,0:T(2,128)(2,1)} %chirp_hbm.1, f32[1,512]{1,0:T(1,128)} %rates_hbm.1, ...), custom_call_target="tpu_custom_call" | custom-call | flops 6000000000 | tf_op jit(solution)/shard_map/compress/pallas_call | solution.py:386
  5.2 3.8 %collective-permute-start = (bf16[4,64,128]{2,1,0:T(8,128)(2,1)}, bf16[4,64,128]{2,1,0:T(8,128)(2,1)S(1)}, u32[]{:S(2)}, u32[]{:S(2)}) collective-permute-start(bf16[4,64,128]{2,1,0:T(8,128)(2,1)} %get-tuple-element.23), channel_id=1, source_target_pairs={{0,3},{1,2},{2,1},{3,0},{4,7},{5,6},{6,5},{7,4},{8,11},{9,10},{10,... | collective-permute-start | bytes 196616 | tf_op jit(solution)/shard_map/ppermute | solution.py:415
  9.0 0.4 collective-permute-start.1
  9.4 0.4 collective-permute-start.2
  9.8 0.0 copy-start.1
  9.8 1.0 %copy-done.1 = f32[768,128]{1,0:T(8,128)S(1)} copy-done((f32[768,128]{1,0:T(8,128)S(1)}, f32[768,128]{1,0:T(8,128)}, u32[]{:S(2)}) %copy-start.1) | copy-done | bytes 393240
  10.8 0.0 copy-start
  10.8 1.7 %phase.1 = (bf16[8,512,256]{2,1,0:T(8,128)(2,1)S(1)}, bf16[8,512,256]{2,1,0:T(8,128)(2,1)S(1)}, bf16[4,64,128]{2,1,0:T(8,128)(2,1)S(1)}) custom-call(f32[768,128]{1,0:T(8,128)S(1)} %copy-done.1), custom_call_target="tpu_custom_call" | custom-call | flops 4000000000 | tf_op jit(solution)/shard_map/phase/pallas_call | solution.py:419
  12.5 0.0 collective-permute-done.refs_1_.rest_1_
  12.5 0.0 collective-permute-done.1.refs_2_.rest_2_
  12.6 1.7 %collective-permute-done.2.refs_3_.rest_3_ = bf16[4,64,128]{2,1,0:T(8,128)(2,1)S(1)} collective-permute-done((bf16[4,64,128]{2,1,0:T(8,128)(2,1)}, bf16[4,64,128]{2,1,0:T(8,128)(2,1)S(1)}, u32[]{:S(2)}, u32[]{:S(2)}) %collective-permute-start.2) | collective-permute-done | bytes 65568 | tf_op jit(solution)/shard_map/ppermute | solution.py:415
  14.3 4.2 %collective-permute-start.4 = (bf16[4,64,128]{2,1,0:T(8,128)(2,1)S(1)}, bf16[4,64,128]{2,1,0:T(8,128)(2,1)S(1)}, u32[]{:S(2)}, u32[]{:S(2)}) collective-permute-start(bf16[4,64,128]{2,1,0:T(8,128)(2,1)S(1)} %get-tuple-element.29), channel_id=1, source_target_pairs={{0,8},{1,9},{2,10},{3,11},{4,12},{5,13},{6,14},{7,15},{8,0},{9,1},... | collective-permute-start | bytes 196616 | tf_op jit(solution)/shard_map/ppermute | solution.py:415
  18.5 0.0 collective-permute-start.5
  18.5 0.4 collective-permute-start.3
  18.9 0.0 copy-done
  18.9 2.3 %turn.1 = (bf16[2,64,128,128]{3,2,1,0:T(8,128)(2,1)S(1)}, bf16[2,64,128,128]{3,2,1,0:T(8,128)(2,1)S(1)}) custom-call(bf16[512,64,128]{2,1,0:T(8,128)(2,1)S(1)} %bitcast.15, bf16[4,64,128]{2,1,0:T(8,128)(2,1)S(1)} %get-tuple-element.26.after_ref), custom_call_target="tpu_custom_call" | custom-call | flops 4000000000 | tf_op jit(solution)/shard_map/turn/pallas_call | solution.py:430
  21.3 0.0 collective-permute-done.4.rest_5_
  21.3 1.3 %collective-permute-done.5.rest_6_ = bf16[4,64,128]{2,1,0:T(8,128)(2,1)S(1)} collective-permute-done((bf16[4,64,128]{2,1,0:T(8,128)(2,1)S(1)}, bf16[4,64,128]{2,1,0:T(8,128)(2,1)S(1)}, u32[]{:S(2)}, u32[]{:S(2)}) %collective-permute-start.5) | collective-permute-done | bytes 65568 | tf_op jit(solution)/shard_map/ppermute | solution.py:415
  22.6 0.0 collective-permute-done.3.rest_4_
  22.6 2.3 %far_image.1 = (bf16[4,16,128]{2,1,0:T(8,128)(2,1)S(1)}, bf16[2,256,512]{2,1,0:T(8,128)(2,1)S(1)}) custom-call(s32[1]{0:T(128)} %bitcast.1.me_ref, s32[1]{0:T(128)} %bitcast.sub_ref, bf16[8,512,256]{2,1,0:T(8,128)(2,1)S(1)} %get-tuple-element.20.after_ref.first_table_ref, bf16[8,512,256]{2,1,0:T(8,128)(2,1)S(1)} %get-tuple-element.21.second_table_ref, ...), custom_call_target="tpu_custom_call" | custom-call | flops 3000000000 | tf_op jit(solution)/shard_map/far_image/pallas_call | solution.py:437
  24.9 5.0 %collective-permute-start.6 = (bf16[4,16,128]{2,1,0:T(8,128)(2,1)S(1)}, bf16[4,16,128]{2,1,0:T(8,128)(2,1)S(1)}, u32[]{:S(2)}, u32[]{:S(2)}) collective-permute-start(bf16[4,16,128]{2,1,0:T(8,128)(2,1)S(1)} %get-tuple-element.32.after_ref), channel_id=1, source_target_pairs={{0,128},{16,144},{32,160},{48,176},{64,192},{80,208},{96,224},{112... | collective-permute-start | bytes 49160 | tf_op jit(solution)/shard_map/ppermute | solution.py:456
  29.9 2.5 %near_image.1 = f32[4,16,128]{2,1,0:T(8,128)S(1)} custom-call(s32[1]{0:T(128)} %bitcast.sub_ref, bf16[8,512,256]{2,1,0:T(8,128)(2,1)S(1)} %get-tuple-element.20.after_ref.first_table_ref, bf16[8,512,256]{2,1,0:T(8,128)(2,1)S(1)} %get-tuple-element.21.second_table_ref, bf16[2,64,128,128]{3,2,1,0:T(8,128)(2,1)S(1)} %get-tuple-element.27.first_weights_ref, ...), custom_call_target="tpu_custom_call" | custom-call | flops 3000000000 | tf_op jit(solution)/shard_map/near_image/pallas_call | solution.py:446
  32.4 0.0 collective-permute-done.6
  32.4 12.7 %all_to_all.5 = f32[8,8,128]{2,1,0:T(8,128)S(1)} all-to-all(f32[8,8,128]{2,1,0:T(8,128)S(1)} %bitcast.16), channel_id=1, replica_groups={{0,16,32,48,64,80,96,112},{128,144,160,176,192,208,224,240},{1,17,33,49..., dimensions={0} | all-to-all | bytes 65536 | tf_op jit(solution)/shard_map/all_to_all | solution.py:459
  45.2 0.6 %reduce_sum.9 = f32[8,128]{1,0:T(8,128)} reduce(f32[8,8,128]{2,1,0:T(8,128)S(1)} %all_to_all.5, f32[]{:T(128)} %constant.8.clone.1), dimensions={0}, to_apply=%region_0.0 | reduce | flops 7168 | bytes 36868 | tf_op jit(solution)/shard_map/reduce_sum | solution.py:460
  (2 shorter events, 0.0 us)
Async XLA Ops:
  5.2 7.3 %collective-permute-start = (bf16[4,64,128]{2,1,0:T(8,128)(2,1)}, bf16[4,64,128]{2,1,0:T(8,128)(2,1)S(1)}, u32[]{:S(2)}, u32[]{:S(2)}) collective-permute-start(bf16[4,64,128]{2,1,0:T(8,128)(2,1)} %get-tuple-element.23), channel_id=1, source_target_pairs={{0,3},{1,2},{2,1},{3,0},{4,7},{5,6},{6,5},{7,4},{8,11},{9,10},{10,... | collective-permute-start | bytes 196616 | tf_op jit(solution)/shard_map/ppermute | solution.py:415
  9.0 3.5 %collective-permute-start.1 = (bf16[4,64,128]{2,1,0:T(8,128)(2,1)}, bf16[4,64,128]{2,1,0:T(8,128)(2,1)S(1)}, u32[]{:S(2)}, u32[]{:S(2)}) collective-permute-start(bf16[4,64,128]{2,1,0:T(8,128)(2,1)} %get-tuple-element.24), channel_id=1, source_target_pairs={{0,2},{1,3},{2,0},{3,1},{4,6},{5,7},{6,4},{7,5},{8,10},{9,11},{10,... | collective-permute-start | bytes 196616 | tf_op jit(solution)/shard_map/ppermute | solution.py:415
  9.4 4.8 %collective-permute-start.2 = (bf16[4,64,128]{2,1,0:T(8,128)(2,1)}, bf16[4,64,128]{2,1,0:T(8,128)(2,1)S(1)}, u32[]{:S(2)}, u32[]{:S(2)}) collective-permute-start(bf16[4,64,128]{2,1,0:T(8,128)(2,1)} %get-tuple-element.25), channel_id=1, source_target_pairs={{0,1},{1,0},{2,3},{3,2},{4,5},{5,4},{6,7},{7,6},{8,9},{9,8},{10,11... | collective-permute-start | bytes 196616 | tf_op jit(solution)/shard_map/ppermute | solution.py:415
  9.8 1.0 %copy-start.1 = (f32[768,128]{1,0:T(8,128)S(1)}, f32[768,128]{1,0:T(8,128)}, u32[]{:S(2)}) copy-start(f32[768,128]{1,0:T(8,128)} %get-tuple-element.19.extra_ref) | copy-start | bytes 1179652
  10.8 8.1 %copy-start = (bf16[2,2,128,4,2048]{4,3,2,1,0:T(4,128)(2,1)S(1)}, bf16[2,2,128,4,2048]{4,3,2,1,0:T(4,128)(2,1)}, u32[]{:S(2)}) copy-start(bf16[2,2,128,4,2048]{4,3,2,1,0:T(4,128)(2,1)} %param.11) | copy-start | bytes 25165828
  14.3 7.0 %collective-permute-start.4 = (bf16[4,64,128]{2,1,0:T(8,128)(2,1)S(1)}, bf16[4,64,128]{2,1,0:T(8,128)(2,1)S(1)}, u32[]{:S(2)}, u32[]{:S(2)}) collective-permute-start(bf16[4,64,128]{2,1,0:T(8,128)(2,1)S(1)} %get-tuple-element.29), channel_id=1, source_target_pairs={{0,8},{1,9},{2,10},{3,11},{4,12},{5,13},{6,14},{7,15},{8,0},{9,1},... | collective-permute-start | bytes 196616 | tf_op jit(solution)/shard_map/ppermute | solution.py:415
  18.5 4.0 %collective-permute-start.5 = (bf16[4,64,128]{2,1,0:T(8,128)(2,1)S(1)}, bf16[4,64,128]{2,1,0:T(8,128)(2,1)S(1)}, u32[]{:S(2)}, u32[]{:S(2)}) collective-permute-start(bf16[4,64,128]{2,1,0:T(8,128)(2,1)S(1)} %get-tuple-element.30), channel_id=1, source_target_pairs={{0,4},{1,5},{2,6},{3,7},{4,0},{5,1},{6,2},{7,3},{8,12},{9,13},{10,... | collective-permute-start | bytes 196616 | tf_op jit(solution)/shard_map/ppermute | solution.py:415
  18.5 4.0 %collective-permute-start.3 = (bf16[4,64,128]{2,1,0:T(8,128)(2,1)S(1)}, bf16[4,64,128]{2,1,0:T(8,128)(2,1)S(1)}, u32[]{:S(2)}, u32[]{:S(2)}) collective-permute-start(bf16[4,64,128]{2,1,0:T(8,128)(2,1)S(1)} %get-tuple-element.26.after_ref), channel_id=1, source_target_pairs={{0,12},{1,13},{2,14},{3,15},{4,8},{5,9},{6,10},{7,11},{8,4},{9,5},... | collective-permute-start | bytes 196616 | tf_op jit(solution)/shard_map/ppermute | solution.py:415
  24.9 7.5 %collective-permute-start.6 = (bf16[4,16,128]{2,1,0:T(8,128)(2,1)S(1)}, bf16[4,16,128]{2,1,0:T(8,128)(2,1)S(1)}, u32[]{:S(2)}, u32[]{:S(2)}) collective-permute-start(bf16[4,16,128]{2,1,0:T(8,128)(2,1)S(1)} %get-tuple-element.32.after_ref), channel_id=1, source_target_pairs={{0,128},{16,144},{32,160},{48,176},{64,192},{80,208},{96,224},{112... | collective-permute-start | bytes 49160 | tf_op jit(solution)/shard_map/ppermute | solution.py:456

commit v12 on v11

--- a/solution.py
+++ b/solution.py
@@ -44,19 +44,16 @@
     row = lax.broadcasted_iota(jnp.int32, (side, side), 0)
     col = lax.broadcasted_iota(jnp.int32, (side, side), 1)
     order = jnp.where(col == (row & (half - 1)) * piece + (row >> 4), 1.0, 0.0).astype(jnp.bfloat16)
-    for fetch in fetches[:3]:
+    for fetch in fetches:
         fetch.wait()
     chirp = chirp_ref[...].astype(jnp.float32)
     pad = jnp.zeros((1, span - chirp.shape[1]), jnp.float32)
     for part in range(2):
         line = jnp.concatenate([chirp[part : part + 1], pad], 1)
         shifted = pltpu.roll(
-            jnp.broadcast_to(line, (16, span)), 0, 1, stride=1, stride_axis=0
+            jnp.broadcast_to(line, (LANES, span)), 0, 1, stride=1, stride_axis=0
         ).astype(jnp.bfloat16)
-        for first in range(0, LANES, 16):
-            toeplitz_ref[part * LANES + first : part * LANES + first + 16, :] = (
-                pltpu.roll(shifted, first, 1) if first > 0 else shifted
-            )
+        toeplitz_ref[part * LANES : (part + 1) * LANES, :] = shifted
     count = slots_ref.shape[1]
     row = lax.broadcasted_iota(jnp.int32, (count, count), 0)
     col = lax.broadcasted_iota(jnp.int32, (count, count), 1)
@@ -66,7 +63,6 @@
         rates = rates_ref[:, block * count : (block + 1) * count]
         rate = jnp.sum(jnp.where(slot == col.astype(jnp.float32), rates, 0.0), 1, keepdims=True)
         extra_ref[block * count : (block + 1) * count, :] = jnp.broadcast_to(rate, (count, LANES))
-    fetches[3].wait()
     for group in range(lines // piece):
         block_rows = jnp.concatenate(
             [
@@ -145,7 +141,7 @@
 
 def distance_of(sub, first, second, near):
     return jnp.where(
-        (sub & 1) == 1,
+        (sub & 1) == 0,
         FIRST_Y[first] * near + SECOND_Z[second],
         SECOND_Y[second] * near + FIRST_Z[first],
     )
@@ -408,7 +404,7 @@
 
     def swap(value, by_core):
         pairs = [
-            (one * tiles + tile, one * tiles + (tile ^ by_core[one & 1]))
+            (one * tiles + tile, one * tiles + (tile ^ by_core[1 - (one & 1)]))
             for one in range(subs)
             for tile in range(tiles)
         ]

time: 45.9 us -> 46.1 us (level)
  no operation moved by 1% of the time
where the time goes in v12:
time: 46.1 us; the launch traced here: 46 us
  starting transfers between devices  14.4 us (31%)
  Pallas kernels  14.1 us (31%)
  blocking collectives  12.6 us (27%)
  waiting for transfers between devices  3.19 us (7%)
  local copies, waits for them, and re-layouts  1 us (2%)
  other arithmetic  0.61 us (1%)
    all_to_all x1, blocking collectives, shards(): lax.all_to_all(held, 'sub', 0, 0, axis_index_groups=groups, tiled=True)  12.6 us
    ppermute x6, starting transfers between devices, swap(): return lax.ppermute(value, ('sub', 'tile'), pairs)  9.42 us
    pallas_call x1, Pallas kernels, partial_image(): call(compress_kernel, 'compress', 60, [own] * (far - 1) + [extras], [smem...  5.21 us
    ppermute x1, starting transfers between devices, shards(): lax.ppermute(far_image, 'sub', [(one, one ^ half) for one in range(size)])  4.94 us
    ppermute x6, waiting for transfers between devices, swap(): return lax.ppermute(value, ('sub', 'tile'), pairs)  3.19 us
    pallas_call x1, Pallas kernels, partial_image(): call(near_image_kernel, 'near_image', 12, shape(half, jnp.float32), [smem...  2.51 us
    pallas_call x1, Pallas kernels, partial_image(): call(far_image_kernel, 'far_image', 12, [shape(half, jnp.bfloat16), shape...  2.35 us
    pallas_call x1, Pallas kernels, partial_image(): call(turn_kernel, 'turn', 12, [turned, turned], [vmem(), anywhere], flops...  2.35 us
  transfers between devices with their start and end apart: 7, of which 2 were waited for; matrix products, arithmetic and copies ran while one was open for 0% of the time, Pallas kernels for 14%

profile of v12, /device:TPU:1, one launch (start us, length us, event | category | flops | bytes accessed | tf_op | source)
XLA Modules:
  0.0 46.0 jit_solution(50181590115450377)
XLA Ops:
  0.0 5.2 %compress.1 = (bf16[4,64,128]{2,1,0:T(8,128)(2,1)}, bf16[4,64,128]{2,1,0:T(8,128)(2,1)}, bf16[4,64,128]{2,1,0:T(8,128)(2,1)}, f32[768,128]{1,0:T(8,128)}) custom-call(s32[1]{0:T(128)} %bitcast.1.me_ref, s32[1]{0:T(128)} %bitcast.sub_ref, s32[2,16]{1,0:T(2,128)} %starts_ref.1, bf16[2,2048]{1,0:T(2,128)(2,1)} %chirp_hbm.1, f32[1,512]{1,0:T(1,128)} %rates_hbm.1, ...), custom_call_target="tpu_custom_call" | custom-call | flops 6000000000 | tf_op jit(solution)/shard_map/compress/pallas_call | solution.py:382
  5.2 5.3 %collective-permute-start = (bf16[4,64,128]{2,1,0:T(8,128)(2,1)}, bf16[4,64,128]{2,1,0:T(8,128)(2,1)S(1)}, u32[]{:S(2)}, u32[]{:S(2)}) collective-permute-start(bf16[4,64,128]{2,1,0:T(8,128)(2,1)} %get-tuple-element.23), channel_id=1, source_target_pairs={{0,8},{1,9},{2,10},{3,11},{4,12},{5,13},{6,14},{7,15},{8,0},{9,1},... | collective-permute-start | bytes 196616 | tf_op jit(solution)/shard_map/ppermute | solution.py:411
  10.5 0.0 collective-permute-start.1
  10.5 0.4 collective-permute-start.2
  10.9 0.0 copy-start.1
  10.9 1.0 %copy-done.1 = f32[768,128]{1,0:T(8,128)S(1)} copy-done((f32[768,128]{1,0:T(8,128)S(1)}, f32[768,128]{1,0:T(8,128)}, u32[]{:S(2)}) %copy-start.1) | copy-done | bytes 393240
  11.9 0.0 copy-start
  11.9 1.7 %phase.1 = (bf16[8,512,256]{2,1,0:T(8,128)(2,1)S(1)}, bf16[8,512,256]{2,1,0:T(8,128)(2,1)S(1)}, bf16[4,64,128]{2,1,0:T(8,128)(2,1)S(1)}) custom-call(f32[768,128]{1,0:T(8,128)S(1)} %copy-done.1), custom_call_target="tpu_custom_call" | custom-call | flops 4000000000 | tf_op jit(solution)/shard_map/phase/pallas_call | solution.py:415
  13.6 0.0 collective-permute-done.refs_1_.rest_1_
  13.6 1.1 %collective-permute-done.1.refs_2_.rest_2_ = bf16[4,64,128]{2,1,0:T(8,128)(2,1)S(1)} collective-permute-done((bf16[4,64,128]{2,1,0:T(8,128)(2,1)}, bf16[4,64,128]{2,1,0:T(8,128)(2,1)S(1)}, u32[]{:S(2)}, u32[]{:S(2)}) %collective-permute-start.1) | collective-permute-done | bytes 65568 | tf_op jit(solution)/shard_map/ppermute | solution.py:411
  14.7 0.0 collective-permute-done.2.refs_3_.rest_3_
  14.7 3.0 %collective-permute-start.4 = (bf16[4,64,128]{2,1,0:T(8,128)(2,1)S(1)}, bf16[4,64,128]{2,1,0:T(8,128)(2,1)S(1)}, u32[]{:S(2)}, u32[]{:S(2)}) collective-permute-start(bf16[4,64,128]{2,1,0:T(8,128)(2,1)S(1)} %get-tuple-element.29), channel_id=1, source_target_pairs={{0,3},{1,2},{2,1},{3,0},{4,7},{5,6},{6,5},{7,4},{8,11},{9,10},{10,... | collective-permute-start | bytes 196616 | tf_op jit(solution)/shard_map/ppermute | solution.py:411
  17.7 0.6 %collective-permute-start.5 = (bf16[4,64,128]{2,1,0:T(8,128)(2,1)S(1)}, bf16[4,64,128]{2,1,0:T(8,128)(2,1)S(1)}, u32[]{:S(2)}, u32[]{:S(2)}) collective-permute-start(bf16[4,64,128]{2,1,0:T(8,128)(2,1)S(1)} %get-tuple-element.30), channel_id=1, source_target_pairs={{0,2},{1,3},{2,0},{3,1},{4,6},{5,7},{6,4},{7,5},{8,10},{9,11},{10,... | collective-permute-start | bytes 196616 | tf_op jit(solution)/shard_map/ppermute | solution.py:411
  18.4 0.2 collective-permute-start.3
  18.5 0.0 copy-done
  18.5 2.3 %turn.1 = (bf16[2,64,128,128]{3,2,1,0:T(8,128)(2,1)S(1)}, bf16[2,64,128,128]{3,2,1,0:T(8,128)(2,1)S(1)}) custom-call(bf16[512,64,128]{2,1,0:T(8,128)(2,1)S(1)} %bitcast.15, bf16[4,64,128]{2,1,0:T(8,128)(2,1)S(1)} %get-tuple-element.26.after_ref), custom_call_target="tpu_custom_call" | custom-call | flops 4000000000 | tf_op jit(solution)/shard_map/turn/pallas_call | solution.py:426
  20.9 0.0 collective-permute-done.4.rest_5_
  20.9 0.0 collective-permute-done.5.rest_6_
  20.9 2.1 %collective-permute-done.3.rest_4_ = bf16[4,64,128]{2,1,0:T(8,128)(2,1)S(1)} collective-permute-done((bf16[4,64,128]{2,1,0:T(8,128)(2,1)S(1)}, bf16[4,64,128]{2,1,0:T(8,128)(2,1)S(1)}, u32[]{:S(2)}, u32[]{:S(2)}) %collective-permute-start.3) | collective-permute-done | bytes 65568 | tf_op jit(solution)/shard_map/ppermute | solution.py:411
  23.0 2.3 %far_image.1 = (bf16[4,16,128]{2,1,0:T(8,128)(2,1)S(1)}, bf16[2,256,512]{2,1,0:T(8,128)(2,1)S(1)}) custom-call(s32[1]{0:T(128)} %bitcast.1.me_ref, s32[1]{0:T(128)} %bitcast.sub_ref, bf16[8,512,256]{2,1,0:T(8,128)(2,1)S(1)} %get-tuple-element.20.after_ref.first_table_ref, bf16[8,512,256]{2,1,0:T(8,128)(2,1)S(1)} %get-tuple-element.21.second_table_ref, ...), custom_call_target="tpu_custom_call" | custom-call | flops 3000000000 | tf_op jit(solution)/shard_map/far_image/pallas_call | solution.py:433
  25.3 4.9 %collective-permute-start.6 = (bf16[4,16,128]{2,1,0:T(8,128)(2,1)S(1)}, bf16[4,16,128]{2,1,0:T(8,128)(2,1)S(1)}, u32[]{:S(2)}, u32[]{:S(2)}) collective-permute-start(bf16[4,16,128]{2,1,0:T(8,128)(2,1)S(1)} %get-tuple-element.32.after_ref), channel_id=1, source_target_pairs={{0,128},{16,144},{32,160},{48,176},{64,192},{80,208},{96,224},{112... | collective-permute-start | bytes 49160 | tf_op jit(solution)/shard_map/ppermute | solution.py:452
  30.2 2.5 %near_image.1 = f32[4,16,128]{2,1,0:T(8,128)S(1)} custom-call(s32[1]{0:T(128)} %bitcast.sub_ref, bf16[8,512,256]{2,1,0:T(8,128)(2,1)S(1)} %get-tuple-element.20.after_ref.first_table_ref, bf16[8,512,256]{2,1,0:T(8,128)(2,1)S(1)} %get-tuple-element.21.second_table_ref, bf16[2,64,128,128]{3,2,1,0:T(8,128)(2,1)S(1)} %get-tuple-element.27.first_weights_ref, ...), custom_call_target="tpu_custom_call" | custom-call | flops 3000000000 | tf_op jit(solution)/shard_map/near_image/pallas_call | solution.py:442
  32.8 0.0 collective-permute-done.6
  32.8 12.6 %all_to_all.5 = f32[8,8,128]{2,1,0:T(8,128)S(1)} all-to-all(f32[8,8,128]{2,1,0:T(8,128)S(1)} %bitcast.16), channel_id=1, replica_groups={{0,16,32,48,64,80,96,112},{128,144,160,176,192,208,224,240},{1,17,33,49..., dimensions={0} | all-to-all | bytes 65536 | tf_op jit(solution)/shard_map/all_to_all | solution.py:455
  45.3 0.6 %reduce_sum.9 = f32[8,128]{1,0:T(8,128)} reduce(f32[8,8,128]{2,1,0:T(8,128)S(1)} %all_to_all.5, f32[]{:T(128)} %constant.8.clone.1), dimensions={0}, to_apply=%region_0.0 | reduce | flops 7168 | bytes 36868 | tf_op jit(solution)/shard_map/reduce_sum | solution.py:456
  (2 shorter events, 0.0 us)
Async XLA Ops:
  5.2 8.4 %collective-permute-start = (bf16[4,64,128]{2,1,0:T(8,128)(2,1)}, bf16[4,64,128]{2,1,0:T(8,128)(2,1)S(1)}, u32[]{:S(2)}, u32[]{:S(2)}) collective-permute-start(bf16[4,64,128]{2,1,0:T(8,128)(2,1)} %get-tuple-element.23), channel_id=1, source_target_pairs={{0,8},{1,9},{2,10},{3,11},{4,12},{5,13},{6,14},{7,15},{8,0},{9,1},... | collective-permute-start | bytes 196616 | tf_op jit(solution)/shard_map/ppermute | solution.py:411
  10.5 4.2 %collective-permute-start.1 = (bf16[4,64,128]{2,1,0:T(8,128)(2,1)}, bf16[4,64,128]{2,1,0:T(8,128)(2,1)S(1)}, u32[]{:S(2)}, u32[]{:S(2)}) collective-permute-start(bf16[4,64,128]{2,1,0:T(8,128)(2,1)} %get-tuple-element.24), channel_id=1, source_target_pairs={{0,4},{1,5},{2,6},{3,7},{4,0},{5,1},{6,2},{7,3},{8,12},{9,13},{10,... | collective-permute-start | bytes 196616 | tf_op jit(solution)/shard_map/ppermute | solution.py:411
  10.5 4.2 %collective-permute-start.2 = (bf16[4,64,128]{2,1,0:T(8,128)(2,1)}, bf16[4,64,128]{2,1,0:T(8,128)(2,1)S(1)}, u32[]{:S(2)}, u32[]{:S(2)}) collective-permute-start(bf16[4,64,128]{2,1,0:T(8,128)(2,1)} %get-tuple-element.25), channel_id=1, source_target_pairs={{0,12},{1,13},{2,14},{3,15},{4,8},{5,9},{6,10},{7,11},{8,4},{9,5},... | collective-permute-start | bytes 196616 | tf_op jit(solution)/shard_map/ppermute | solution.py:411
  10.9 1.0 %copy-start.1 = (f32[768,128]{1,0:T(8,128)S(1)}, f32[768,128]{1,0:T(8,128)}, u32[]{:S(2)}) copy-start(f32[768,128]{1,0:T(8,128)} %get-tuple-element.19.extra_ref) | copy-start | bytes 1179652
  11.9 6.6 %copy-start = (bf16[2,2,128,4,2048]{4,3,2,1,0:T(4,128)(2,1)S(1)}, bf16[2,2,128,4,2048]{4,3,2,1,0:T(4,128)(2,1)}, u32[]{:S(2)}) copy-start(bf16[2,2,128,4,2048]{4,3,2,1,0:T(4,128)(2,1)} %param.11) | copy-start | bytes 25165828
  14.7 6.1 %collective-permute-start.4 = (bf16[4,64,128]{2,1,0:T(8,128)(2,1)S(1)}, bf16[4,64,128]{2,1,0:T(8,128)(2,1)S(1)}, u32[]{:S(2)}, u32[]{:S(2)}) collective-permute-start(bf16[4,64,128]{2,1,0:T(8,128)(2,1)S(1)} %get-tuple-element.29), channel_id=1, source_target_pairs={{0,3},{1,2},{2,1},{3,0},{4,7},{5,6},{6,5},{7,4},{8,11},{9,10},{10,... | collective-permute-start | bytes 196616 | tf_op jit(solution)/shard_map/ppermute | solution.py:411
  17.7 3.1 %collective-permute-start.5 = (bf16[4,64,128]{2,1,0:T(8,128)(2,1)S(1)}, bf16[4,64,128]{2,1,0:T(8,128)(2,1)S(1)}, u32[]{:S(2)}, u32[]{:S(2)}) collective-permute-start(bf16[4,64,128]{2,1,0:T(8,128)(2,1)S(1)} %get-tuple-element.30), channel_id=1, source_target_pairs={{0,2},{1,3},{2,0},{3,1},{4,6},{5,7},{6,4},{7,5},{8,10},{9,11},{10,... | collective-permute-start | bytes 196616 | tf_op jit(solution)/shard_map/ppermute | solution.py:411
  18.4 4.6 %collective-permute-start.3 = (bf16[4,64,128]{2,1,0:T(8,128)(2,1)S(1)}, bf16[4,64,128]{2,1,0:T(8,128)(2,1)S(1)}, u32[]{:S(2)}, u32[]{:S(2)}) collective-permute-start(bf16[4,64,128]{2,1,0:T(8,128)(2,1)S(1)} %get-tuple-element.26.after_ref), channel_id=1, source_target_pairs={{0,1},{1,0},{2,3},{3,2},{4,5},{5,4},{6,7},{7,6},{8,9},{9,8},{10,11... | collective-permute-start | bytes 196616 | tf_op jit(solution)/shard_map/ppermute | solution.py:411
  25.3 7.5 %collective-permute-start.6 = (bf16[4,16,128]{2,1,0:T(8,128)(2,1)S(1)}, bf16[4,16,128]{2,1,0:T(8,128)(2,1)S(1)}, u32[]{:S(2)}, u32[]{:S(2)}) collective-permute-start(bf16[4,16,128]{2,1,0:T(8,128)(2,1)S(1)} %get-tuple-element.32.after_ref), channel_id=1, source_target_pairs={{0,128},{16,144},{32,160},{48,176},{64,192},{80,208},{96,224},{112... | collective-permute-start | bytes 49160 | tf_op jit(solution)/shard_map/ppermute | solution.py:452

commit v13 on v12

--- a/solution.py
+++ b/solution.py
@@ -199,9 +199,7 @@
                         ],
                         1,
                     )
-                    moved = jnp.dot(order, block_rows, preferred_element_type=jnp.float32).astype(
-                        jnp.bfloat16
-                    )
+                    moved = jnp.dot(order, block_rows, preferred_element_type=jnp.float32)
                     for one, top in enumerate(tops):
                         out_ref[part, top : top + size, pl.ds(first, size), :] = moved[
                             :, one * LANES : (one + 1) * LANES
@@ -214,6 +212,7 @@
 def phase_table(block, rate_ref, table_ref):
     count = table_ref.shape[1] // 2
     columns = table_ref.shape[0] * table_ref.shape[2]
+    per_half = table_ref.shape[2] // LANES
     lane = lax.broadcasted_iota(jnp.int32, (32, LANES), 1).astype(jnp.float32)
     place = (lane + 0.5) * np.float32(1 / columns) - 0.5
     for group in range(count // 32):
@@ -227,10 +226,11 @@
                     sine * step_cosine + cosine * step_sine,
                     cosine * step_cosine - sine * step_sine,
                 )
-            lanes = slice(chunk % 2 * LANES, (chunk % 2 + 1) * LANES)
-            table_ref[chunk // 2, span, lanes] = cosine.astype(jnp.bfloat16)
-            table_ref[chunk // 2, count + group * 32 : count + group * 32 + 32, lanes] = (
-                sine.astype(jnp.bfloat16)
+            side, place_of = chunk // per_half, chunk % per_half
+            lanes = slice(place_of * LANES, (place_of + 1) * LANES)
+            table_ref[side, span, lanes] = cosine.astype(jnp.bfloat16)
+            table_ref[side, count + group * 32 : count + group * 32 + 32, lanes] = sine.astype(
+                jnp.bfloat16
             )
 
 
@@ -242,53 +242,47 @@
             refs[far + dz - 1][dy] = refs[dy][dz]
 
 
-def weighted_sum(side, table_refs, weights_refs, image_ref, left_ref, focused_refs):
+def weighted_sum(side, table_refs, weights_refs, image_ref, left_ref, focused_refs, partial_ref):
     blocks = len(table_refs)
     pairs, lines, _ = image_ref.shape
     places = 2 * pairs
     image_rows = lines // 4
     band = weights_refs[0].shape[2]
-
-    def focus(pair):
-        for block in range(blocks):
-            focused_refs[pair % 2 * blocks + block][...] = jnp.dot(
-                left_ref[block], table_refs[block][side * pairs + pair], preferred_element_type=jnp.float32
-            )
-
-    focus(0)
-    for pair in range(pairs):
-        if pair + 1 < pairs:
-            focus(pair + 1)
-        sums = []
-        for place in range(2):
+    for block in range(blocks):
+        focused_refs[block][...] = jnp.dot(
+            left_ref[block], table_refs[block][side], preferred_element_type=jnp.float32
+        )
+    for block in range(blocks):
+        for place in range(places):
             lanes = slice(place * LANES, (place + 1) * LANES)
-            real = [jnp.zeros((8, LANES), jnp.float32)] * image_rows
-            imag = [jnp.zeros((8, LANES), jnp.float32)] * image_rows
-            for block in range(blocks):
-                focused_ref = focused_refs[pair % 2 * blocks + block]
-                for k in range(0, band, 16):
-                    focus_real = focused_ref[k : k + 16, lanes]
-                    focus_imag = focused_ref[band + k : band + k + 16, lanes]
-                    for row in range(image_rows):
-                        line = (side * places + 2 * pair + place) * image_rows + row
-                        weight_real = weights_refs[block][0, line, k : k + 16, :].astype(jnp.float32)
-                        weight_imag = weights_refs[block][1, line, k : k + 16, :].astype(jnp.float32)
-                        for first in (0, 8):
-                            part = slice(first, first + 8)
-                            wr, wi = weight_real[part], weight_imag[part]
-                            fr, fi = focus_real[part], focus_imag[part]
-                            real[row] = real[row] + (wr * fr - wi * fi)
-                            imag[row] = imag[row] + (wr * fi + wi * fr)
-            sums.append(
-                jnp.concatenate([jnp.sum(one, 0, keepdims=True) for one in real + imag], 0)
-            )
-        image_ref[pair] = jnp.concatenate(sums, 0).astype(image_ref.dtype)
+            if block == 0:
+                sums = [jnp.zeros((8, LANES), jnp.float32)] * (2 * image_rows)
+            else:
+                sums = [partial_ref[place, one] for one in range(2 * image_rows)]
+            for k in range(0, band, 8):
+                fr = focused_refs[block][k : k + 8, lanes]
+                fi = focused_refs[block][band + k : band + k + 8, lanes]
+                for row in range(image_rows):
+                    line = (side * places + place) * image_rows + row
+                    wr = weights_refs[block][0, line, k : k + 8, :]
+                    wi = weights_refs[block][1, line, k : k + 8, :]
+                    sums[row] = sums[row] + (wr * fr - wi * fi)
+                    sums[image_rows + row] = sums[image_rows + row] + (wr * fi + wi * fr)
+            if block + 1 < blocks:
+                for one in range(2 * image_rows):
+                    partial_ref[place, one] = sums[one]
+            else:
+                rows = jnp.concatenate([jnp.sum(one, 0, keepdims=True) for one in sums], 0)
+                if place % 2 == 0:
+                    upper = rows
+                else:
+                    image_ref[place // 2] = jnp.concatenate([upper, rows], 0).astype(image_ref.dtype)
 
 
 def far_image_kernel(
     me_ref, sub_ref, first_table_ref, second_table_ref, first_weights_ref, second_weights_ref, *rest
 ):
-    *sources_refs, image_ref, left_ref, bands_ref, one_ref, two_ref, three_ref, four_ref = rest
+    *sources_refs, image_ref, left_ref, bands_ref, one_ref, two_ref, partial_ref = rest
     sources, band_rows, band = bands_ref.shape
     far_count = len(sources_refs) // 2 + 1
     near_refs, far_refs = sources_refs[:far_count], sources_refs[far_count:]
@@ -313,13 +307,14 @@
         (first_weights_ref, second_weights_ref),
         image_ref,
         left_ref,
-        (one_ref, two_ref, three_ref, four_ref),
+        (one_ref, two_ref),
+        partial_ref,
     )
 
 
 def near_image_kernel(
     sub_ref, first_table_ref, second_table_ref, first_weights_ref, second_weights_ref, left_ref, after_ref,
-    image_ref, one_ref, two_ref, three_ref, four_ref,
+    image_ref, one_ref, two_ref, partial_ref,
 ):
     weighted_sum(
         sub_ref[0] >> 3,
@@ -327,7 +322,8 @@
         (first_weights_ref, second_weights_ref),
         image_ref,
         left_ref,
-        (one_ref, two_ref, three_ref, four_ref),
+        (one_ref, two_ref),
+        partial_ref,
     )
 
 
@@ -410,8 +406,8 @@
         ]
         return lax.ppermute(value, ("sub", "tile"), pairs)
 
-    table = shape((parts, 2 * count, 2 * LANES), jnp.bfloat16)
-    turned = shape((2, places * image_rows, band, LANES), jnp.bfloat16)
+    table = shape((2, 2 * count, columns // 2), jnp.bfloat16)
+    turned = shape((2, places * image_rows, band, LANES), jnp.float32)
     first_table, second_table, mine = call(phase_kernel, "phase", 12, [table, table, own], [vmem()], flops=4 * 10**9)(extra)
     bands = [mine] + [
         swap(bands[dy - 1], (FIRST_Z[dy], FIRST_Y[dy] * near)) for dy in range(1, far)
@@ -429,7 +425,9 @@
     passed = [swap(passed[dz - 1], (SECOND_Y[dz] * near, SECOND_Z[dz])) for dz in range(1, near)]
     sources = bands + passed
     half = (places // 4, 4 * image_rows, LANES)
-    focused = [pltpu.VMEM((2 * band, 2 * LANES), jnp.float32)] * (2 * blocks)
+    focused = [pltpu.VMEM((2 * band, columns // 2), jnp.float32)] * blocks + [
+        pltpu.VMEM((places // 2, 2 * image_rows, 8, LANES), jnp.float32)
+    ]
     far_image, left = call(
         far_image_kernel,
         "far_image",

time: 46.1 us -> 46.3 us (level)
  no operation moved by 1% of the time
where the time goes in v13:
time: 46.3 us; the launch traced here: 46.1 us
  starting transfers between devices  14.4 us (31%)
  Pallas kernels  14.2 us (31%)
  blocking collectives  12.6 us (27%)
  waiting for transfers between devices  3.2 us (7%)
  local copies, waits for them, and re-layouts  1 us (2%)
  other arithmetic  0.61 us (1%)
    all_to_all x1, blocking collectives, shards(): lax.all_to_all(held, 'sub', 0, 0, axis_index_groups=groups, tiled=True)  12.6 us
    ppermute x6, starting transfers between devices, swap(): return lax.ppermute(value, ('sub', 'tile'), pairs)  9.42 us
    pallas_call x1, Pallas kernels, partial_image(): call(compress_kernel, 'compress', 60, [own] * (far - 1) + [extras], [smem...  5.21 us
    ppermute x1, starting transfers between devices, shards(): lax.ppermute(far_image, 'sub', [(one, one ^ half) for one in range(size)])  4.93 us
    ppermute x6, waiting for transfers between devices, swap(): return lax.ppermute(value, ('sub', 'tile'), pairs)  3.19 us
    pallas_call x1, Pallas kernels, partial_image(): call(far_image_kernel, 'far_image', 12, [shape(half, jnp.bfloat16), shape...  2.51 us
    pallas_call x1, Pallas kernels, partial_image(): call(near_image_kernel, 'near_image', 12, shape(half, jnp.float32), [smem...  2.44 us
    pallas_call x1, Pallas kernels, partial_image(): call(turn_kernel, 'turn', 12, [turned, turned], [vmem(), anywhere], flops...  2.35 us
  transfers between devices with their start and end apart: 7, of which 2 were waited for; matrix products, arithmetic and copies ran while one was open for 0% of the time, Pallas kernels for 14%

profile of v13, /device:TPU:1, one launch (start us, length us, event | category | flops | bytes accessed | tf_op | source)
XLA Modules:
  0.0 46.1 jit_solution(5745516323416091911)
XLA Ops:
  0.0 5.2 %compress.1 = (bf16[4,64,128]{2,1,0:T(8,128)(2,1)}, bf16[4,64,128]{2,1,0:T(8,128)(2,1)}, bf16[4,64,128]{2,1,0:T(8,128)(2,1)}, f32[768,128]{1,0:T(8,128)}) custom-call(s32[1]{0:T(128)} %bitcast.1.me_ref, s32[1]{0:T(128)} %bitcast.sub_ref, s32[2,16]{1,0:T(2,128)} %starts_ref.1, bf16[2,2048]{1,0:T(2,128)(2,1)} %chirp_hbm.1, f32[1,512]{1,0:T(1,128)} %rates_hbm.1, ...), custom_call_target="tpu_custom_call" | custom-call | flops 6000000000 | tf_op jit(solution)/shard_map/compress/pallas_call | solution.py:378
  5.2 5.3 %collective-permute-start = (bf16[4,64,128]{2,1,0:T(8,128)(2,1)}, bf16[4,64,128]{2,1,0:T(8,128)(2,1)S(1)}, u32[]{:S(2)}, u32[]{:S(2)}) collective-permute-start(bf16[4,64,128]{2,1,0:T(8,128)(2,1)} %get-tuple-element.23), channel_id=1, source_target_pairs={{0,8},{1,9},{2,10},{3,11},{4,12},{5,13},{6,14},{7,15},{8,0},{9,1},... | collective-permute-start | bytes 196616 | tf_op jit(solution)/shard_map/ppermute | solution.py:407
  10.5 0.0 collective-permute-start.1
  10.5 0.4 collective-permute-start.2
  10.9 0.0 copy-start.1
  10.9 1.0 %copy-done.1 = f32[768,128]{1,0:T(8,128)S(1)} copy-done((f32[768,128]{1,0:T(8,128)S(1)}, f32[768,128]{1,0:T(8,128)}, u32[]{:S(2)}) %copy-start.1) | copy-done | bytes 393240
  11.9 0.0 copy-start
  11.9 1.7 %phase.1 = (bf16[2,512,1024]{2,1,0:T(8,128)(2,1)S(1)}, bf16[2,512,1024]{2,1,0:T(8,128)(2,1)S(1)}, bf16[4,64,128]{2,1,0:T(8,128)(2,1)S(1)}) custom-call(f32[768,128]{1,0:T(8,128)S(1)} %copy-done.1), custom_call_target="tpu_custom_call" | custom-call | flops 4000000000 | tf_op jit(solution)/shard_map/phase/pallas_call | solution.py:411
  13.6 0.0 collective-permute-done.refs_1_.rest_1_
  13.6 1.1 %collective-permute-done.1.refs_2_.rest_2_ = bf16[4,64,128]{2,1,0:T(8,128)(2,1)S(1)} collective-permute-done((bf16[4,64,128]{2,1,0:T(8,128)(2,1)}, bf16[4,64,128]{2,1,0:T(8,128)(2,1)S(1)}, u32[]{:S(2)}, u32[]{:S(2)}) %collective-permute-start.1) | collective-permute-done | bytes 65568 | tf_op jit(solution)/shard_map/ppermute | solution.py:407
  14.7 0.0 collective-permute-done.2.refs_3_.rest_3_
  14.7 3.0 %collective-permute-start.4 = (bf16[4,64,128]{2,1,0:T(8,128)(2,1)S(1)}, bf16[4,64,128]{2,1,0:T(8,128)(2,1)S(1)}, u32[]{:S(2)}, u32[]{:S(2)}) collective-permute-start(bf16[4,64,128]{2,1,0:T(8,128)(2,1)S(1)} %get-tuple-element.29), channel_id=1, source_target_pairs={{0,3},{1,2},{2,1},{3,0},{4,7},{5,6},{6,5},{7,4},{8,11},{9,10},{10,... | collective-permute-start | bytes 196616 | tf_op jit(solution)/shard_map/ppermute | solution.py:407
  17.7 0.6 %collective-permute-start.5 = (bf16[4,64,128]{2,1,0:T(8,128)(2,1)S(1)}, bf16[4,64,128]{2,1,0:T(8,128)(2,1)S(1)}, u32[]{:S(2)}, u32[]{:S(2)}) collective-permute-start(bf16[4,64,128]{2,1,0:T(8,128)(2,1)S(1)} %get-tuple-element.30), channel_id=1, source_target_pairs={{0,2},{1,3},{2,0},{3,1},{4,6},{5,7},{6,4},{7,5},{8,10},{9,11},{10,... | collective-permute-start | bytes 196616 | tf_op jit(solution)/shard_map/ppermute | solution.py:407
  18.3 0.2 collective-permute-start.3
  18.5 0.0 copy-done
  18.5 2.3 %turn.1 = (f32[2,64,128,128]{3,2,1,0:T(8,128)S(1)}, f32[2,64,128,128]{3,2,1,0:T(8,128)S(1)}) custom-call(bf16[512,64,128]{2,1,0:T(8,128)(2,1)S(1)} %bitcast.15, bf16[4,64,128]{2,1,0:T(8,128)(2,1)S(1)} %get-tuple-element.26.after_ref), custom_call_target="tpu_custom_call" | custom-call | flops 4000000000 | tf_op jit(solution)/shard_map/turn/pallas_call | solution.py:422
  20.9 0.0 collective-permute-done.4.rest_5_
  20.9 0.0 collective-permute-done.5.rest_6_
  20.9 2.1 %collective-permute-done.3.rest_4_ = bf16[4,64,128]{2,1,0:T(8,128)(2,1)S(1)} collective-permute-done((bf16[4,64,128]{2,1,0:T(8,128)(2,1)S(1)}, bf16[4,64,128]{2,1,0:T(8,128)(2,1)S(1)}, u32[]{:S(2)}, u32[]{:S(2)}) %collective-permute-start.3) | collective-permute-done | bytes 65568 | tf_op jit(solution)/shard_map/ppermute | solution.py:407
  23.0 2.5 %far_image.1 = (bf16[4,16,128]{2,1,0:T(8,128)(2,1)S(1)}, bf16[2,256,512]{2,1,0:T(8,128)(2,1)S(1)}) custom-call(s32[1]{0:T(128)} %bitcast.1.me_ref, s32[1]{0:T(128)} %bitcast.sub_ref, bf16[2,512,1024]{2,1,0:T(8,128)(2,1)S(1)} %get-tuple-element.20.after_ref.first_table_ref, bf16[2,512,1024]{2,1,0:T(8,128)(2,1)S(1)} %get-tuple-element.21.second_table_ref, ...), custom_call_target="tpu_custom_call" | custom-call | flops 3000000000 | tf_op jit(solution)/shard_map/far_image/pallas_call | solution.py:431
  25.5 4.9 %collective-permute-start.6 = (bf16[4,16,128]{2,1,0:T(8,128)(2,1)S(1)}, bf16[4,16,128]{2,1,0:T(8,128)(2,1)S(1)}, u32[]{:S(2)}, u32[]{:S(2)}) collective-permute-start(bf16[4,16,128]{2,1,0:T(8,128)(2,1)S(1)} %get-tuple-element.32.after_ref), channel_id=1, source_target_pairs={{0,128},{16,144},{32,160},{48,176},{64,192},{80,208},{96,224},{112... | collective-permute-start | bytes 49160 | tf_op jit(solution)/shard_map/ppermute | solution.py:450
  30.4 2.4 %near_image.1 = f32[4,16,128]{2,1,0:T(8,128)S(1)} custom-call(s32[1]{0:T(128)} %bitcast.sub_ref, bf16[2,512,1024]{2,1,0:T(8,128)(2,1)S(1)} %get-tuple-element.20.after_ref.first_table_ref, bf16[2,512,1024]{2,1,0:T(8,128)(2,1)S(1)} %get-tuple-element.21.second_table_ref, f32[2,64,128,128]{3,2,1,0:T(8,128)S(1)} %get-tuple-element.27.first_weights_ref, ...), custom_call_target="tpu_custom_call" | custom-call | flops 3000000000 | tf_op jit(solution)/shard_map/near_image/pallas_call | solution.py:440
  32.9 0.0 collective-permute-done.6
  32.9 12.6 %all_to_all.5 = f32[8,8,128]{2,1,0:T(8,128)S(1)} all-to-all(f32[8,8,128]{2,1,0:T(8,128)S(1)} %bitcast.16), channel_id=1, replica_groups={{0,16,32,48,64,80,96,112},{128,144,160,176,192,208,224,240},{1,17,33,49..., dimensions={0} | all-to-all | bytes 65536 | tf_op jit(solution)/shard_map/all_to_all | solution.py:453
  45.5 0.6 %reduce_sum.9 = f32[8,128]{1,0:T(8,128)} reduce(f32[8,8,128]{2,1,0:T(8,128)S(1)} %all_to_all.5, f32[]{:T(128)} %constant.8.clone.1), dimensions={0}, to_apply=%region_0.0 | reduce | flops 7168 | bytes 36868 | tf_op jit(solution)/shard_map/reduce_sum | solution.py:454
  (2 shorter events, 0.0 us)
Async XLA Ops:
  5.2 8.4 %collective-permute-start = (bf16[4,64,128]{2,1,0:T(8,128)(2,1)}, bf16[4,64,128]{2,1,0:T(8,128)(2,1)S(1)}, u32[]{:S(2)}, u32[]{:S(2)}) collective-permute-start(bf16[4,64,128]{2,1,0:T(8,128)(2,1)} %get-tuple-element.23), channel_id=1, source_target_pairs={{0,8},{1,9},{2,10},{3,11},{4,12},{5,13},{6,14},{7,15},{8,0},{9,1},... | collective-permute-start | bytes 196616 | tf_op jit(solution)/shard_map/ppermute | solution.py:407
  10.5 4.2 %collective-permute-start.1 = (bf16[4,64,128]{2,1,0:T(8,128)(2,1)}, bf16[4,64,128]{2,1,0:T(8,128)(2,1)S(1)}, u32[]{:S(2)}, u32[]{:S(2)}) collective-permute-start(bf16[4,64,128]{2,1,0:T(8,128)(2,1)} %get-tuple-element.24), channel_id=1, source_target_pairs={{0,4},{1,5},{2,6},{3,7},{4,0},{5,1},{6,2},{7,3},{8,12},{9,13},{10,... | collective-permute-start | bytes 196616 | tf_op jit(solution)/shard_map/ppermute | solution.py:407
  10.5 4.2 %collective-permute-start.2 = (bf16[4,64,128]{2,1,0:T(8,128)(2,1)}, bf16[4,64,128]{2,1,0:T(8,128)(2,1)S(1)}, u32[]{:S(2)}, u32[]{:S(2)}) collective-permute-start(bf16[4,64,128]{2,1,0:T(8,128)(2,1)} %get-tuple-element.25), channel_id=1, source_target_pairs={{0,12},{1,13},{2,14},{3,15},{4,8},{5,9},{6,10},{7,11},{8,4},{9,5},... | collective-permute-start | bytes 196616 | tf_op jit(solution)/shard_map/ppermute | solution.py:407
  10.9 1.0 %copy-start.1 = (f32[768,128]{1,0:T(8,128)S(1)}, f32[768,128]{1,0:T(8,128)}, u32[]{:S(2)}) copy-start(f32[768,128]{1,0:T(8,128)} %get-tuple-element.19.extra_ref) | copy-start | bytes 1179652
  11.9 6.7 %copy-start = (bf16[2,2,128,4,2048]{4,3,2,1,0:T(4,128)(2,1)S(1)}, bf16[2,2,128,4,2048]{4,3,2,1,0:T(4,128)(2,1)}, u32[]{:S(2)}) copy-start(bf16[2,2,128,4,2048]{4,3,2,1,0:T(4,128)(2,1)} %param.11) | copy-start | bytes 25165828
  14.7 6.1 %collective-permute-start.4 = (bf16[4,64,128]{2,1,0:T(8,128)(2,1)S(1)}, bf16[4,64,128]{2,1,0:T(8,128)(2,1)S(1)}, u32[]{:S(2)}, u32[]{:S(2)}) collective-permute-start(bf16[4,64,128]{2,1,0:T(8,128)(2,1)S(1)} %get-tuple-element.29), channel_id=1, source_target_pairs={{0,3},{1,2},{2,1},{3,0},{4,7},{5,6},{6,5},{7,4},{8,11},{9,10},{10,... | collective-permute-start | bytes 196616 | tf_op jit(solution)/shard_map/ppermute | solution.py:407
  17.7 3.1 %collective-permute-start.5 = (bf16[4,64,128]{2,1,0:T(8,128)(2,1)S(1)}, bf16[4,64,128]{2,1,0:T(8,128)(2,1)S(1)}, u32[]{:S(2)}, u32[]{:S(2)}) collective-permute-start(bf16[4,64,128]{2,1,0:T(8,128)(2,1)S(1)} %get-tuple-element.30), channel_id=1, source_target_pairs={{0,2},{1,3},{2,0},{3,1},{4,6},{5,7},{6,4},{7,5},{8,10},{9,11},{10,... | collective-permute-start | bytes 196616 | tf_op jit(solution)/shard_map/ppermute | solution.py:407
  18.3 4.6 %collective-permute-start.3 = (bf16[4,64,128]{2,1,0:T(8,128)(2,1)S(1)}, bf16[4,64,128]{2,1,0:T(8,128)(2,1)S(1)}, u32[]{:S(2)}, u32[]{:S(2)}) collective-permute-start(bf16[4,64,128]{2,1,0:T(8,128)(2,1)S(1)} %get-tuple-element.26.after_ref), channel_id=1, source_target_pairs={{0,1},{1,0},{2,3},{3,2},{4,5},{5,4},{6,7},{7,6},{8,9},{9,8},{10,11... | collective-permute-start | bytes 196616 | tf_op jit(solution)/shard_map/ppermute | solution.py:407
  25.5 7.4 %collective-permute-start.6 = (bf16[4,16,128]{2,1,0:T(8,128)(2,1)S(1)}, bf16[4,16,128]{2,1,0:T(8,128)(2,1)S(1)}, u32[]{:S(2)}, u32[]{:S(2)}) collective-permute-start(bf16[4,16,128]{2,1,0:T(8,128)(2,1)S(1)} %get-tuple-element.32.after_ref), channel_id=1, source_target_pairs={{0,128},{16,144},{32,160},{48,176},{64,192},{80,208},{96,224},{112... | collective-permute-start | bytes 49160 | tf_op jit(solution)/shard_map/ppermute | solution.py:450

commit v14 on v13

--- a/solution.py
+++ b/solution.py
@@ -212,7 +212,6 @@
 def phase_table(block, rate_ref, table_ref):
     count = table_ref.shape[1] // 2
     columns = table_ref.shape[0] * table_ref.shape[2]
-    per_half = table_ref.shape[2] // LANES
     lane = lax.broadcasted_iota(jnp.int32, (32, LANES), 1).astype(jnp.float32)
     place = (lane + 0.5) * np.float32(1 / columns) - 0.5
     for group in range(count // 32):
@@ -226,7 +225,7 @@
                     sine * step_cosine + cosine * step_sine,
                     cosine * step_cosine - sine * step_sine,
                 )
-            side, place_of = chunk // per_half, chunk % per_half
+            side, place_of = chunk % 2, chunk // 2
             lanes = slice(place_of * LANES, (place_of + 1) * LANES)
             table_ref[side, span, lanes] = cosine.astype(jnp.bfloat16)
             table_ref[side, count + group * 32 : count + group * 32 + 32, lanes] = sine.astype(
@@ -263,7 +262,7 @@
                 fr = focused_refs[block][k : k + 8, lanes]
                 fi = focused_refs[block][band + k : band + k + 8, lanes]
                 for row in range(image_rows):
-                    line = (side * places + place) * image_rows + row
+                    line = (2 * place + side) * image_rows + row
                     wr = weights_refs[block][0, line, k : k + 8, :]
                     wi = weights_refs[block][1, line, k : k + 8, :]
                     sums[row] = sums[row] + (wr * fr - wi * fi)
@@ -302,7 +301,7 @@
         bottom = jnp.concatenate([-imag, real], 1)
         left_ref[block] = jnp.concatenate([top, bottom], 0).T
     weighted_sum(
-        1 - (sub_ref[0] >> 3),
+        1 - (sub_ref[0] & 1),
         (first_table_ref, second_table_ref),
         (first_weights_ref, second_weights_ref),
         image_ref,
@@ -317,7 +316,7 @@
     image_ref, one_ref, two_ref, partial_ref,
 ):
     weighted_sum(
-        sub_ref[0] >> 3,
+        sub_ref[0] & 1,
         (first_table_ref, second_table_ref),
         (first_weights_ref, second_weights_ref),
         image_ref,
@@ -432,7 +431,7 @@
         far_image_kernel,
         "far_image",
         12,
-        [shape(half, jnp.bfloat16), shape((blocks, 2 * band, 2 * count), jnp.bfloat16)],
+        [shape(half, jnp.float32), shape((blocks, 2 * band, 2 * count), jnp.bfloat16)],
         [smem, smem] + [vmem()] * (4 + len(sources)),
         [pltpu.VMEM((tiles, 2 * pulses, band), jnp.bfloat16)] + focused,
         flops=3 * 10**9,
@@ -447,9 +446,9 @@
     _, far_image, near_image = partial_image(*args)
     size = 16
     half = size // 2
-    came = lax.ppermute(far_image, "sub", [(one, one ^ half) for one in range(size)])
-    groups = [list(range(half)), list(range(half, size))]
-    held = (near_image + came.astype(jnp.float32)).reshape(half, -1, LANES)
+    came = lax.ppermute(far_image, "sub", [(one, one ^ 1) for one in range(size)])
+    groups = [list(range(0, size, 2)), list(range(1, size, 2))]
+    held = (near_image + came).reshape(half, -1, LANES)
     pieces = lax.all_to_all(held, "sub", 0, 0, axis_index_groups=groups, tiled=True)
     return jnp.sum(pieces, 0).reshape(2, -1, LANES)
 

time: 46.3 us -> 49.5 us (1.069)
  blocking collectives: 12.6 us -> 17.1 us
  starting transfers between devices: 14.4 us -> 13 us
    all_to_all x1, blocking collectives: 12.6 us -> 17.1 us  [shards(): lax.all_to_all(held, 'sub', 0, 0, axis_index_groups=groups, tiled=True)]
    ppermute x1, starting transfers between devices: 4.93 us -> 3.59 us  [shards(): lax.ppermute(far_image, 'sub', [(one, one ^ 1) for one in range(size)])]
  transfers between devices with their start and end apart: 7 -> 7, of which waited for: 2 -> 2; matrix products, arithmetic and copies ran while one was open for 0% -> 0% of each run, Pallas kernels for 14% -> 13%
where the time goes in v14:
time: 49.5 us; the launch traced here: 49.3 us
  blocking collectives  17.1 us (35%)
  Pallas kernels  14.3 us (29%)
  starting transfers between devices  13 us (26%)
  waiting for transfers between devices  3.17 us (6%)
  local copies, waits for them, and re-layouts  1 us (2%)
  other arithmetic  0.61 us (1%)
    all_to_all x1, blocking collectives, shards(): lax.all_to_all(held, 'sub', 0, 0, axis_index_groups=groups, tiled=True)  17.1 us
    ppermute x6, starting transfers between devices, swap(): return lax.ppermute(value, ('sub', 'tile'), pairs)  9.42 us
    pallas_call x1, Pallas kernels, partial_image(): call(compress_kernel, 'compress', 60, [own] * (far - 1) + [extras], [smem...  5.22 us
    ppermute x1, starting transfers between devices, shards(): lax.ppermute(far_image, 'sub', [(one, one ^ 1) for one in range(size)])  3.59 us
    ppermute x6, waiting for transfers between devices, swap(): return lax.ppermute(value, ('sub', 'tile'), pairs)  3.17 us
    pallas_call x1, Pallas kernels, partial_image(): call(far_image_kernel, 'far_image', 12, [shape(half, jnp.float32), shape(...  2.52 us
    pallas_call x1, Pallas kernels, partial_image(): call(near_image_kernel, 'near_image', 12, shape(half, jnp.float32), [smem...  2.44 us
    pallas_call x1, Pallas kernels, partial_image(): call(turn_kernel, 'turn', 12, [turned, turned], [vmem(), anywhere], flops...  2.35 us
  transfers between devices with their start and end apart: 7, of which 2 were waited for; matrix products, arithmetic and copies ran while one was open for 0% of the time, Pallas kernels for 13%

profile of v14, /device:TPU:1, one launch (start us, length us, event | category | flops | bytes accessed | tf_op | source)
XLA Modules:
  0.0 49.3 jit_solution(13062276744133742900)
XLA Ops:
  0.0 5.2 %compress.1 = (bf16[4,64,128]{2,1,0:T(8,128)(2,1)}, bf16[4,64,128]{2,1,0:T(8,128)(2,1)}, bf16[4,64,128]{2,1,0:T(8,128)(2,1)}, f32[768,128]{1,0:T(8,128)}) custom-call(s32[1]{0:T(128)} %bitcast.1.me_ref, s32[1]{0:T(128)} %bitcast.sub_ref, s32[2,16]{1,0:T(2,128)} %starts_ref.1, bf16[2,2048]{1,0:T(2,128)(2,1)} %chirp_hbm.1, f32[1,512]{1,0:T(1,128)} %rates_hbm.1, ...), custom_call_target="tpu_custom_call" | custom-call | flops 6000000000 | tf_op jit(solution)/shard_map/compress/pallas_call | solution.py:377
  5.2 5.3 %collective-permute-start = (bf16[4,64,128]{2,1,0:T(8,128)(2,1)}, bf16[4,64,128]{2,1,0:T(8,128)(2,1)S(1)}, u32[]{:S(2)}, u32[]{:S(2)}) collective-permute-start(bf16[4,64,128]{2,1,0:T(8,128)(2,1)} %get-tuple-element.23), channel_id=1, source_target_pairs={{0,8},{1,9},{2,10},{3,11},{4,12},{5,13},{6,14},{7,15},{8,0},{9,1},... | collective-permute-start | bytes 196616 | tf_op jit(solution)/shard_map/ppermute | solution.py:406
  10.5 0.0 collective-permute-start.1
  10.5 0.4 collective-permute-start.2
  10.9 0.0 copy-start.1
  10.9 1.0 %copy-done.1 = f32[768,128]{1,0:T(8,128)S(1)} copy-done((f32[768,128]{1,0:T(8,128)S(1)}, f32[768,128]{1,0:T(8,128)}, u32[]{:S(2)}) %copy-start.1) | copy-done | bytes 393240
  11.9 0.0 copy-start
  11.9 1.7 %phase.1 = (bf16[2,512,1024]{2,1,0:T(8,128)(2,1)S(1)}, bf16[2,512,1024]{2,1,0:T(8,128)(2,1)S(1)}, bf16[4,64,128]{2,1,0:T(8,128)(2,1)S(1)}) custom-call(f32[768,128]{1,0:T(8,128)S(1)} %copy-done.1), custom_call_target="tpu_custom_call" | custom-call | flops 4000000000 | tf_op jit(solution)/shard_map/phase/pallas_call | solution.py:410
  13.6 0.0 collective-permute-done.refs_1_.rest_1_
  13.6 1.1 %collective-permute-done.1.refs_2_.rest_2_ = bf16[4,64,128]{2,1,0:T(8,128)(2,1)S(1)} collective-permute-done((bf16[4,64,128]{2,1,0:T(8,128)(2,1)}, bf16[4,64,128]{2,1,0:T(8,128)(2,1)S(1)}, u32[]{:S(2)}, u32[]{:S(2)}) %collective-permute-start.1) | collective-permute-done | bytes 65568 | tf_op jit(solution)/shard_map/ppermute | solution.py:406
  14.7 0.0 collective-permute-done.2.refs_3_.rest_3_
  14.7 3.0 %collective-permute-start.4 = (bf16[4,64,128]{2,1,0:T(8,128)(2,1)S(1)}, bf16[4,64,128]{2,1,0:T(8,128)(2,1)S(1)}, u32[]{:S(2)}, u32[]{:S(2)}) collective-permute-start(bf16[4,64,128]{2,1,0:T(8,128)(2,1)S(1)} %get-tuple-element.29), channel_id=1, source_target_pairs={{0,3},{1,2},{2,1},{3,0},{4,7},{5,6},{6,5},{7,4},{8,11},{9,10},{10,... | collective-permute-start | bytes 196616 | tf_op jit(solution)/shard_map/ppermute | solution.py:406
  17.7 0.6 %collective-permute-start.5 = (bf16[4,64,128]{2,1,0:T(8,128)(2,1)S(1)}, bf16[4,64,128]{2,1,0:T(8,128)(2,1)S(1)}, u32[]{:S(2)}, u32[]{:S(2)}) collective-permute-start(bf16[4,64,128]{2,1,0:T(8,128)(2,1)S(1)} %get-tuple-element.30), channel_id=1, source_target_pairs={{0,2},{1,3},{2,0},{3,1},{4,6},{5,7},{6,4},{7,5},{8,10},{9,11},{10,... | collective-permute-start | bytes 196616 | tf_op jit(solution)/shard_map/ppermute | solution.py:406
  18.4 0.2 collective-permute-start.3
  18.5 0.0 copy-done
  18.5 2.3 %turn.1 = (f32[2,64,128,128]{3,2,1,0:T(8,128)S(1)}, f32[2,64,128,128]{3,2,1,0:T(8,128)S(1)}) custom-call(bf16[512,64,128]{2,1,0:T(8,128)(2,1)S(1)} %bitcast.15, bf16[4,64,128]{2,1,0:T(8,128)(2,1)S(1)} %get-tuple-element.26.after_ref), custom_call_target="tpu_custom_call" | custom-call | flops 4000000000 | tf_op jit(solution)/shard_map/turn/pallas_call | solution.py:421
  20.9 0.0 collective-permute-done.4.rest_5_
  20.9 0.0 collective-permute-done.5.rest_6_
  20.9 2.1 %collective-permute-done.3.rest_4_ = bf16[4,64,128]{2,1,0:T(8,128)(2,1)S(1)} collective-permute-done((bf16[4,64,128]{2,1,0:T(8,128)(2,1)S(1)}, bf16[4,64,128]{2,1,0:T(8,128)(2,1)S(1)}, u32[]{:S(2)}, u32[]{:S(2)}) %collective-permute-start.3) | collective-permute-done | bytes 65568 | tf_op jit(solution)/shard_map/ppermute | solution.py:406
  23.0 2.5 %far_image.1 = (f32[4,16,128]{2,1,0:T(8,128)S(1)}, bf16[2,256,512]{2,1,0:T(8,128)(2,1)S(1)}) custom-call(s32[1]{0:T(128)} %bitcast.1.me_ref, s32[1]{0:T(128)} %bitcast.sub_ref, bf16[2,512,1024]{2,1,0:T(8,128)(2,1)S(1)} %get-tuple-element.20.after_ref.first_table_ref, bf16[2,512,1024]{2,1,0:T(8,128)(2,1)S(1)} %get-tuple-element.21.second_table_ref, ...), custom_call_target="tpu_custom_call" | custom-call | flops 3000000000 | tf_op jit(solution)/shard_map/far_image/pallas_call | solution.py:430
  25.5 3.6 %collective-permute-start.6 = (f32[4,16,128]{2,1,0:T(8,128)S(1)}, f32[4,16,128]{2,1,0:T(8,128)S(1)}, u32[]{:S(2)}, u32[]{:S(2)}) collective-permute-start(f32[4,16,128]{2,1,0:T(8,128)S(1)} %get-tuple-element.32.after_ref), channel_id=1, source_target_pairs={{0,16},{16,0},{32,48},{48,32},{64,80},{80,64},{96,112},{112,96},{1... | collective-permute-start | bytes 98312 | tf_op jit(solution)/shard_map/ppermute | solution.py:449
  29.1 2.4 %near_image.1 = f32[4,16,128]{2,1,0:T(8,128)S(1)} custom-call(s32[1]{0:T(128)} %bitcast.sub_ref, bf16[2,512,1024]{2,1,0:T(8,128)(2,1)S(1)} %get-tuple-element.20.after_ref.first_table_ref, bf16[2,512,1024]{2,1,0:T(8,128)(2,1)S(1)} %get-tuple-element.21.second_table_ref, f32[2,64,128,128]{3,2,1,0:T(8,128)S(1)} %get-tuple-element.27.first_weights_ref, ...), custom_call_target="tpu_custom_call" | custom-call | flops 3000000000 | tf_op jit(solution)/shard_map/near_image/pallas_call | solution.py:439
  31.5 0.0 collective-permute-done.6
  31.5 17.1 %all_to_all.5 = f32[8,8,128]{2,1,0:T(8,128)S(1)} all-to-all(f32[8,8,128]{2,1,0:T(8,128)S(1)} %bitcast.16), channel_id=1, replica_groups={{0,32,64,96,128,160,192,224},{16,48,80,112,144,176,208,240},{1,33,65,97..., dimensions={0} | all-to-all | bytes 65536 | tf_op jit(solution)/shard_map/all_to_all | solution.py:452
  48.7 0.6 %reduce_sum.9 = f32[8,128]{1,0:T(8,128)} reduce(f32[8,8,128]{2,1,0:T(8,128)S(1)} %all_to_all.5, f32[]{:T(128)} %constant.8.clone.1), dimensions={0}, to_apply=%region_0.0 | reduce | flops 7168 | bytes 36868 | tf_op jit(solution)/shard_map/reduce_sum | solution.py:453
  (2 shorter events, 0.0 us)
Async XLA Ops:
  5.2 8.4 %collective-permute-start = (bf16[4,64,128]{2,1,0:T(8,128)(2,1)}, bf16[4,64,128]{2,1,0:T(8,128)(2,1)S(1)}, u32[]{:S(2)}, u32[]{:S(2)}) collective-permute-start(bf16[4,64,128]{2,1,0:T(8,128)(2,1)} %get-tuple-element.23), channel_id=1, source_target_pairs={{0,8},{1,9},{2,10},{3,11},{4,12},{5,13},{6,14},{7,15},{8,0},{9,1},... | collective-permute-start | bytes 196616 | tf_op jit(solution)/shard_map/ppermute | solution.py:406
  10.5 4.2 %collective-permute-start.1 = (bf16[4,64,128]{2,1,0:T(8,128)(2,1)}, bf16[4,64,128]{2,1,0:T(8,128)(2,1)S(1)}, u32[]{:S(2)}, u32[]{:S(2)}) collective-permute-start(bf16[4,64,128]{2,1,0:T(8,128)(2,1)} %get-tuple-element.24), channel_id=1, source_target_pairs={{0,4},{1,5},{2,6},{3,7},{4,0},{5,1},{6,2},{7,3},{8,12},{9,13},{10,... | collective-permute-start | bytes 196616 | tf_op jit(solution)/shard_map/ppermute | solution.py:406
  10.5 4.2 %collective-permute-start.2 = (bf16[4,64,128]{2,1,0:T(8,128)(2,1)}, bf16[4,64,128]{2,1,0:T(8,128)(2,1)S(1)}, u32[]{:S(2)}, u32[]{:S(2)}) collective-permute-start(bf16[4,64,128]{2,1,0:T(8,128)(2,1)} %get-tuple-element.25), channel_id=1, source_target_pairs={{0,12},{1,13},{2,14},{3,15},{4,8},{5,9},{6,10},{7,11},{8,4},{9,5},... | collective-permute-start | bytes 196616 | tf_op jit(solution)/shard_map/ppermute | solution.py:406
  10.9 1.0 %copy-start.1 = (f32[768,128]{1,0:T(8,128)S(1)}, f32[768,128]{1,0:T(8,128)}, u32[]{:S(2)}) copy-start(f32[768,128]{1,0:T(8,128)} %get-tuple-element.19.extra_ref) | copy-start | bytes 1179652
  11.9 6.7 %copy-start = (bf16[2,2,128,4,2048]{4,3,2,1,0:T(4,128)(2,1)S(1)}, bf16[2,2,128,4,2048]{4,3,2,1,0:T(4,128)(2,1)}, u32[]{:S(2)}) copy-start(bf16[2,2,128,4,2048]{4,3,2,1,0:T(4,128)(2,1)} %param.11) | copy-start | bytes 25165828
  14.7 6.1 %collective-permute-start.4 = (bf16[4,64,128]{2,1,0:T(8,128)(2,1)S(1)}, bf16[4,64,128]{2,1,0:T(8,128)(2,1)S(1)}, u32[]{:S(2)}, u32[]{:S(2)}) collective-permute-start(bf16[4,64,128]{2,1,0:T(8,128)(2,1)S(1)} %get-tuple-element.29), channel_id=1, source_target_pairs={{0,3},{1,2},{2,1},{3,0},{4,7},{5,6},{6,5},{7,4},{8,11},{9,10},{10,... | collective-permute-start | bytes 196616 | tf_op jit(solution)/shard_map/ppermute | solution.py:406
  17.7 3.2 %collective-permute-start.5 = (bf16[4,64,128]{2,1,0:T(8,128)(2,1)S(1)}, bf16[4,64,128]{2,1,0:T(8,128)(2,1)S(1)}, u32[]{:S(2)}, u32[]{:S(2)}) collective-permute-start(bf16[4,64,128]{2,1,0:T(8,128)(2,1)S(1)} %get-tuple-element.30), channel_id=1, source_target_pairs={{0,2},{1,3},{2,0},{3,1},{4,6},{5,7},{6,4},{7,5},{8,10},{9,11},{10,... | collective-permute-start | bytes 196616 | tf_op jit(solution)/shard_map/ppermute | solution.py:406
  18.4 4.6 %collective-permute-start.3 = (bf16[4,64,128]{2,1,0:T(8,128)(2,1)S(1)}, bf16[4,64,128]{2,1,0:T(8,128)(2,1)S(1)}, u32[]{:S(2)}, u32[]{:S(2)}) collective-permute-start(bf16[4,64,128]{2,1,0:T(8,128)(2,1)S(1)} %get-tuple-element.26.after_ref), channel_id=1, source_target_pairs={{0,1},{1,0},{2,3},{3,2},{4,5},{5,4},{6,7},{7,6},{8,9},{9,8},{10,11... | collective-permute-start | bytes 196616 | tf_op jit(solution)/shard_map/ppermute | solution.py:406
  25.5 6.0 %collective-permute-start.6 = (f32[4,16,128]{2,1,0:T(8,128)S(1)}, f32[4,16,128]{2,1,0:T(8,128)S(1)}, u32[]{:S(2)}, u32[]{:S(2)}) collective-permute-start(f32[4,16,128]{2,1,0:T(8,128)S(1)} %get-tuple-element.32.after_ref), channel_id=1, source_target_pairs={{0,16},{16,0},{32,48},{48,32},{64,80},{80,64},{96,112},{112,96},{1... | collective-permute-start | bytes 98312 | tf_op jit(solution)/shard_map/ppermute | solution.py:449

commit v15 on v12

--- a/solution.py
+++ b/solution.py
@@ -242,6 +242,19 @@
             refs[far + dz - 1][dy] = refs[dy][dz]
 
 
+def fold_rows(values):
+    row = lax.broadcasted_iota(jnp.int32, values[0].shape, 0)
+    shift = 1
+    while len(values) > 1:
+        low = (row & shift) == 0
+        values = [
+            jnp.where(low, first, second) + pltpu.roll(jnp.where(low, second, first), 8 - shift, 0)
+            for first, second in zip(values[::2], values[1::2])
+        ]
+        shift *= 2
+    return values[0]
+
+
 def weighted_sum(side, table_refs, weights_refs, image_ref, left_ref, focused_refs):
     blocks = len(table_refs)
     pairs, lines, _ = image_ref.shape
@@ -279,9 +292,7 @@
                             fr, fi = focus_real[part], focus_imag[part]
                             real[row] = real[row] + (wr * fr - wi * fi)
                             imag[row] = imag[row] + (wr * fi + wi * fr)
-            sums.append(
-                jnp.concatenate([jnp.sum(one, 0, keepdims=True) for one in real + imag], 0)
-            )
+            sums.append(fold_rows(real + imag))
         image_ref[pair] = jnp.concatenate(sums, 0).astype(image_ref.dtype)
 
 

time: 46.1 us -> 46.1 us (level)
  no operation moved by 1% of the time
where the time goes in v15:
time: 46.1 us; the launch traced here: 45.9 us
  starting transfers between devices  14.4 us (31%)
  Pallas kernels  14.1 us (31%)
  blocking collectives  12.6 us (27%)
  waiting for transfers between devices  3.19 us (7%)
  local copies, waits for them, and re-layouts  1 us (2%)
  other arithmetic  0.61 us (1%)
    all_to_all x1, blocking collectives, shards(): lax.all_to_all(held, 'sub', 0, 0, axis_index_groups=groups, tiled=True)  12.6 us
    ppermute x6, starting transfers between devices, swap(): return lax.ppermute(value, ('sub', 'tile'), pairs)  9.43 us
    pallas_call x1, Pallas kernels, partial_image(): call(compress_kernel, 'compress', 60, [own] * (far - 1) + [extras], [smem...  5.21 us
    ppermute x1, starting transfers between devices, shards(): lax.ppermute(far_image, 'sub', [(one, one ^ half) for one in range(size)])  4.93 us
    ppermute x6, waiting for transfers between devices, swap(): return lax.ppermute(value, ('sub', 'tile'), pairs)  3.19 us
    pallas_call x1, Pallas kernels, partial_image(): call(near_image_kernel, 'near_image', 12, shape(half, jnp.float32), [smem...  2.48 us
    pallas_call x1, Pallas kernels, partial_image(): call(turn_kernel, 'turn', 12, [turned, turned], [vmem(), anywhere], flops...  2.35 us
    pallas_call x1, Pallas kernels, partial_image(): call(far_image_kernel, 'far_image', 12, [shape(half, jnp.bfloat16), shape...  2.31 us
  transfers between devices with their start and end apart: 7, of which 2 were waited for; matrix products, arithmetic and copies ran while one was open for 0% of the time, Pallas kernels for 14%

profile of v15, /device:TPU:1, one launch (start us, length us, event | category | flops | bytes accessed | tf_op | source)
XLA Modules:
  0.0 45.9 jit_solution(7680502599305344308)
XLA Ops:
  0.0 5.2 %compress.1 = (bf16[4,64,128]{2,1,0:T(8,128)(2,1)}, bf16[4,64,128]{2,1,0:T(8,128)(2,1)}, bf16[4,64,128]{2,1,0:T(8,128)(2,1)}, f32[768,128]{1,0:T(8,128)}) custom-call(s32[1]{0:T(128)} %bitcast.1.me_ref, s32[1]{0:T(128)} %bitcast.sub_ref, s32[2,16]{1,0:T(2,128)} %starts_ref.1, bf16[2,2048]{1,0:T(2,128)(2,1)} %chirp_hbm.1, f32[1,512]{1,0:T(1,128)} %rates_hbm.1, ...), custom_call_target="tpu_custom_call" | custom-call | flops 6000000000 | tf_op jit(solution)/shard_map/compress/pallas_call | solution.py:393
  5.2 5.3 %collective-permute-start = (bf16[4,64,128]{2,1,0:T(8,128)(2,1)}, bf16[4,64,128]{2,1,0:T(8,128)(2,1)S(1)}, u32[]{:S(2)}, u32[]{:S(2)}) collective-permute-start(bf16[4,64,128]{2,1,0:T(8,128)(2,1)} %get-tuple-element.23), channel_id=1, source_target_pairs={{0,8},{1,9},{2,10},{3,11},{4,12},{5,13},{6,14},{7,15},{8,0},{9,1},... | collective-permute-start | bytes 196616 | tf_op jit(solution)/shard_map/ppermute | solution.py:422
  10.5 0.0 collective-permute-start.1
  10.5 0.4 collective-permute-start.2
  10.9 0.0 copy-start.1
  10.9 1.0 %copy-done.1 = f32[768,128]{1,0:T(8,128)S(1)} copy-done((f32[768,128]{1,0:T(8,128)S(1)}, f32[768,128]{1,0:T(8,128)}, u32[]{:S(2)}) %copy-start.1) | copy-done | bytes 393240
  11.9 0.0 copy-start
  11.9 1.7 %phase.1 = (bf16[8,512,256]{2,1,0:T(8,128)(2,1)S(1)}, bf16[8,512,256]{2,1,0:T(8,128)(2,1)S(1)}, bf16[4,64,128]{2,1,0:T(8,128)(2,1)S(1)}) custom-call(f32[768,128]{1,0:T(8,128)S(1)} %copy-done.1), custom_call_target="tpu_custom_call" | custom-call | flops 4000000000 | tf_op jit(solution)/shard_map/phase/pallas_call | solution.py:426
  13.6 0.0 collective-permute-done.refs_1_.rest_1_
  13.6 1.1 %collective-permute-done.1.refs_2_.rest_2_ = bf16[4,64,128]{2,1,0:T(8,128)(2,1)S(1)} collective-permute-done((bf16[4,64,128]{2,1,0:T(8,128)(2,1)}, bf16[4,64,128]{2,1,0:T(8,128)(2,1)S(1)}, u32[]{:S(2)}, u32[]{:S(2)}) %collective-permute-start.1) | collective-permute-done | bytes 65568 | tf_op jit(solution)/shard_map/ppermute | solution.py:422
  14.7 0.0 collective-permute-done.2.refs_3_.rest_3_
  14.7 3.0 %collective-permute-start.4 = (bf16[4,64,128]{2,1,0:T(8,128)(2,1)S(1)}, bf16[4,64,128]{2,1,0:T(8,128)(2,1)S(1)}, u32[]{:S(2)}, u32[]{:S(2)}) collective-permute-start(bf16[4,64,128]{2,1,0:T(8,128)(2,1)S(1)} %get-tuple-element.29), channel_id=1, source_target_pairs={{0,3},{1,2},{2,1},{3,0},{4,7},{5,6},{6,5},{7,4},{8,11},{9,10},{10,... | collective-permute-start | bytes 196616 | tf_op jit(solution)/shard_map/ppermute | solution.py:422
  17.7 0.6 %collective-permute-start.5 = (bf16[4,64,128]{2,1,0:T(8,128)(2,1)S(1)}, bf16[4,64,128]{2,1,0:T(8,128)(2,1)S(1)}, u32[]{:S(2)}, u32[]{:S(2)}) collective-permute-start(bf16[4,64,128]{2,1,0:T(8,128)(2,1)S(1)} %get-tuple-element.30), channel_id=1, source_target_pairs={{0,2},{1,3},{2,0},{3,1},{4,6},{5,7},{6,4},{7,5},{8,10},{9,11},{10,... | collective-permute-start | bytes 196616 | tf_op jit(solution)/shard_map/ppermute | solution.py:422
  18.3 0.2 collective-permute-start.3
  18.5 0.0 copy-done
  18.5 2.3 %turn.1 = (bf16[2,64,128,128]{3,2,1,0:T(8,128)(2,1)S(1)}, bf16[2,64,128,128]{3,2,1,0:T(8,128)(2,1)S(1)}) custom-call(bf16[512,64,128]{2,1,0:T(8,128)(2,1)S(1)} %bitcast.15, bf16[4,64,128]{2,1,0:T(8,128)(2,1)S(1)} %get-tuple-element.26.after_ref), custom_call_target="tpu_custom_call" | custom-call | flops 4000000000 | tf_op jit(solution)/shard_map/turn/pallas_call | solution.py:437
  20.9 0.0 collective-permute-done.4.rest_5_
  20.9 0.0 collective-permute-done.5.rest_6_
  20.9 2.1 %collective-permute-done.3.rest_4_ = bf16[4,64,128]{2,1,0:T(8,128)(2,1)S(1)} collective-permute-done((bf16[4,64,128]{2,1,0:T(8,128)(2,1)S(1)}, bf16[4,64,128]{2,1,0:T(8,128)(2,1)S(1)}, u32[]{:S(2)}, u32[]{:S(2)}) %collective-permute-start.3) | collective-permute-done | bytes 65568 | tf_op jit(solution)/shard_map/ppermute | solution.py:422
  23.0 2.3 %far_image.1 = (bf16[4,16,128]{2,1,0:T(8,128)(2,1)S(1)}, bf16[2,256,512]{2,1,0:T(8,128)(2,1)S(1)}) custom-call(s32[1]{0:T(128)} %bitcast.1.me_ref, s32[1]{0:T(128)} %bitcast.sub_ref, bf16[8,512,256]{2,1,0:T(8,128)(2,1)S(1)} %get-tuple-element.20.after_ref.first_table_ref, bf16[8,512,256]{2,1,0:T(8,128)(2,1)S(1)} %get-tuple-element.21.second_table_ref, ...), custom_call_target="tpu_custom_call" | custom-call | flops 3000000000 | tf_op jit(solution)/shard_map/far_image/pallas_call | solution.py:444
  25.3 4.9 %collective-permute-start.6 = (bf16[4,16,128]{2,1,0:T(8,128)(2,1)S(1)}, bf16[4,16,128]{2,1,0:T(8,128)(2,1)S(1)}, u32[]{:S(2)}, u32[]{:S(2)}) collective-permute-start(bf16[4,16,128]{2,1,0:T(8,128)(2,1)S(1)} %get-tuple-element.32.after_ref), channel_id=1, source_target_pairs={{0,128},{16,144},{32,160},{48,176},{64,192},{80,208},{96,224},{112... | collective-permute-start | bytes 49160 | tf_op jit(solution)/shard_map/ppermute | solution.py:463
  30.2 2.5 %near_image.1 = f32[4,16,128]{2,1,0:T(8,128)S(1)} custom-call(s32[1]{0:T(128)} %bitcast.sub_ref, bf16[8,512,256]{2,1,0:T(8,128)(2,1)S(1)} %get-tuple-element.20.after_ref.first_table_ref, bf16[8,512,256]{2,1,0:T(8,128)(2,1)S(1)} %get-tuple-element.21.second_table_ref, bf16[2,64,128,128]{3,2,1,0:T(8,128)(2,1)S(1)} %get-tuple-element.27.first_weights_ref, ...), custom_call_target="tpu_custom_call" | custom-call | flops 3000000000 | tf_op jit(solution)/shard_map/near_image/pallas_call | solution.py:453
  32.7 0.0 collective-permute-done.6
  32.7 12.6 %all_to_all.5 = f32[8,8,128]{2,1,0:T(8,128)S(1)} all-to-all(f32[8,8,128]{2,1,0:T(8,128)S(1)} %bitcast.16), channel_id=1, replica_groups={{0,16,32,48,64,80,96,112},{128,144,160,176,192,208,224,240},{1,17,33,49..., dimensions={0} | all-to-all | bytes 65536 | tf_op jit(solution)/shard_map/all_to_all | solution.py:466
  45.3 0.6 %reduce_sum.9 = f32[8,128]{1,0:T(8,128)} reduce(f32[8,8,128]{2,1,0:T(8,128)S(1)} %all_to_all.5, f32[]{:T(128)} %constant.8.clone.1), dimensions={0}, to_apply=%region_0.0 | reduce | flops 7168 | bytes 36868 | tf_op jit(solution)/shard_map/reduce_sum | solution.py:467
  (2 shorter events, 0.0 us)
Async XLA Ops:
  5.2 8.4 %collective-permute-start = (bf16[4,64,128]{2,1,0:T(8,128)(2,1)}, bf16[4,64,128]{2,1,0:T(8,128)(2,1)S(1)}, u32[]{:S(2)}, u32[]{:S(2)}) collective-permute-start(bf16[4,64,128]{2,1,0:T(8,128)(2,1)} %get-tuple-element.23), channel_id=1, source_target_pairs={{0,8},{1,9},{2,10},{3,11},{4,12},{5,13},{6,14},{7,15},{8,0},{9,1},... | collective-permute-start | bytes 196616 | tf_op jit(solution)/shard_map/ppermute | solution.py:422
  10.5 4.2 %collective-permute-start.1 = (bf16[4,64,128]{2,1,0:T(8,128)(2,1)}, bf16[4,64,128]{2,1,0:T(8,128)(2,1)S(1)}, u32[]{:S(2)}, u32[]{:S(2)}) collective-permute-start(bf16[4,64,128]{2,1,0:T(8,128)(2,1)} %get-tuple-element.24), channel_id=1, source_target_pairs={{0,4},{1,5},{2,6},{3,7},{4,0},{5,1},{6,2},{7,3},{8,12},{9,13},{10,... | collective-permute-start | bytes 196616 | tf_op jit(solution)/shard_map/ppermute | solution.py:422
  10.5 4.2 %collective-permute-start.2 = (bf16[4,64,128]{2,1,0:T(8,128)(2,1)}, bf16[4,64,128]{2,1,0:T(8,128)(2,1)S(1)}, u32[]{:S(2)}, u32[]{:S(2)}) collective-permute-start(bf16[4,64,128]{2,1,0:T(8,128)(2,1)} %get-tuple-element.25), channel_id=1, source_target_pairs={{0,12},{1,13},{2,14},{3,15},{4,8},{5,9},{6,10},{7,11},{8,4},{9,5},... | collective-permute-start | bytes 196616 | tf_op jit(solution)/shard_map/ppermute | solution.py:422
  10.9 1.0 %copy-start.1 = (f32[768,128]{1,0:T(8,128)S(1)}, f32[768,128]{1,0:T(8,128)}, u32[]{:S(2)}) copy-start(f32[768,128]{1,0:T(8,128)} %get-tuple-element.19.extra_ref) | copy-start | bytes 1179652
  11.9 6.7 %copy-start = (bf16[2,2,128,4,2048]{4,3,2,1,0:T(4,128)(2,1)S(1)}, bf16[2,2,128,4,2048]{4,3,2,1,0:T(4,128)(2,1)}, u32[]{:S(2)}) copy-start(bf16[2,2,128,4,2048]{4,3,2,1,0:T(4,128)(2,1)} %param.11) | copy-start | bytes 25165828
  14.7 6.1 %collective-permute-start.4 = (bf16[4,64,128]{2,1,0:T(8,128)(2,1)S(1)}, bf16[4,64,128]{2,1,0:T(8,128)(2,1)S(1)}, u32[]{:S(2)}, u32[]{:S(2)}) collective-permute-start(bf16[4,64,128]{2,1,0:T(8,128)(2,1)S(1)} %get-tuple-element.29), channel_id=1, source_target_pairs={{0,3},{1,2},{2,1},{3,0},{4,7},{5,6},{6,5},{7,4},{8,11},{9,10},{10,... | collective-permute-start | bytes 196616 | tf_op jit(solution)/shard_map/ppermute | solution.py:422
  17.7 3.2 %collective-permute-start.5 = (bf16[4,64,128]{2,1,0:T(8,128)(2,1)S(1)}, bf16[4,64,128]{2,1,0:T(8,128)(2,1)S(1)}, u32[]{:S(2)}, u32[]{:S(2)}) collective-permute-start(bf16[4,64,128]{2,1,0:T(8,128)(2,1)S(1)} %get-tuple-element.30), channel_id=1, source_target_pairs={{0,2},{1,3},{2,0},{3,1},{4,6},{5,7},{6,4},{7,5},{8,10},{9,11},{10,... | collective-permute-start | bytes 196616 | tf_op jit(solution)/shard_map/ppermute | solution.py:422
  18.3 4.6 %collective-permute-start.3 = (bf16[4,64,128]{2,1,0:T(8,128)(2,1)S(1)}, bf16[4,64,128]{2,1,0:T(8,128)(2,1)S(1)}, u32[]{:S(2)}, u32[]{:S(2)}) collective-permute-start(bf16[4,64,128]{2,1,0:T(8,128)(2,1)S(1)} %get-tuple-element.26.after_ref), channel_id=1, source_target_pairs={{0,1},{1,0},{2,3},{3,2},{4,5},{5,4},{6,7},{7,6},{8,9},{9,8},{10,11... | collective-permute-start | bytes 196616 | tf_op jit(solution)/shard_map/ppermute | solution.py:422
  25.3 7.4 %collective-permute-start.6 = (bf16[4,16,128]{2,1,0:T(8,128)(2,1)S(1)}, bf16[4,16,128]{2,1,0:T(8,128)(2,1)S(1)}, u32[]{:S(2)}, u32[]{:S(2)}) collective-permute-start(bf16[4,16,128]{2,1,0:T(8,128)(2,1)S(1)} %get-tuple-element.32.after_ref), channel_id=1, source_target_pairs={{0,128},{16,144},{32,160},{48,176},{64,192},{80,208},{96,224},{112... | collective-permute-start | bytes 49160 | tf_op jit(solution)/shard_map/ppermute | solution.py:463

commit v16 on v15

--- a/solution.py
+++ b/solution.py
@@ -445,7 +445,7 @@
         far_image_kernel,
         "far_image",
         12,
-        [shape(half, jnp.bfloat16), shape((blocks, 2 * band, 2 * count), jnp.bfloat16)],
+        [shape(half, jnp.float32), shape((blocks, 2 * band, 2 * count), jnp.bfloat16)],
         [smem, smem] + [vmem()] * (4 + len(sources)),
         [pltpu.VMEM((tiles, 2 * pulses, band), jnp.bfloat16)] + focused,
         flops=3 * 10**9,
@@ -462,7 +462,7 @@
     half = size // 2
     came = lax.ppermute(far_image, "sub", [(one, one ^ half) for one in range(size)])
     groups = [list(range(half)), list(range(half, size))]
-    held = (near_image + came.astype(jnp.float32)).reshape(half, -1, LANES)
+    held = (near_image + came).reshape(half, -1, LANES)
     pieces = lax.all_to_all(held, "sub", 0, 0, axis_index_groups=groups, tiled=True)
     return jnp.sum(pieces, 0).reshape(2, -1, LANES)
 

time: 46.1 us -> 46.3 us (level)
  no operation moved by 1% of the time
where the time goes in v16:
time: 46.3 us; the launch traced here: 46.1 us
  starting transfers between devices  14.4 us (31%)
  Pallas kernels  14.1 us (30%)
  blocking collectives  12.8 us (28%)
  waiting for transfers between devices  3.2 us (7%)
  local copies, waits for them, and re-layouts  1 us (2%)
  other arithmetic  0.61 us (1%)
    all_to_all x1, blocking collectives, shards(): lax.all_to_all(held, 'sub', 0, 0, axis_index_groups=groups, tiled=True)  12.8 us
    ppermute x6, starting transfers between devices, swap(): return lax.ppermute(value, ('sub', 'tile'), pairs)  9.42 us
    pallas_call x1, Pallas kernels, partial_image(): call(compress_kernel, 'compress', 60, [own] * (far - 1) + [extras], [smem...  5.21 us
    ppermute x1, starting transfers between devices, shards(): lax.ppermute(far_image, 'sub', [(one, one ^ half) for one in range(size)])  4.93 us
    ppermute x6, waiting for transfers between devices, swap(): return lax.ppermute(value, ('sub', 'tile'), pairs)  3.19 us
    pallas_call x1, Pallas kernels, partial_image(): call(near_image_kernel, 'near_image', 12, shape(half, jnp.float32), [smem...  2.47 us
    pallas_call x1, Pallas kernels, partial_image(): call(turn_kernel, 'turn', 12, [turned, turned], [vmem(), anywhere], flops...  2.35 us
    pallas_call x1, Pallas kernels, partial_image(): call(far_image_kernel, 'far_image', 12, [shape(half, jnp.float32), shape(...  2.32 us
  transfers between devices with their start and end apart: 7, of which 2 were waited for; matrix products, arithmetic and copies ran while one was open for 0% of the time, Pallas kernels for 14%

profile of v16, /device:TPU:1, one launch (start us, length us, event | category | flops | bytes accessed | tf_op | source)
XLA Modules:
  0.0 46.1 jit_solution(3166299546763477396)
XLA Ops:
  0.0 5.2 %compress.1 = (bf16[4,64,128]{2,1,0:T(8,128)(2,1)}, bf16[4,64,128]{2,1,0:T(8,128)(2,1)}, bf16[4,64,128]{2,1,0:T(8,128)(2,1)}, f32[768,128]{1,0:T(8,128)}) custom-call(s32[1]{0:T(128)} %bitcast.1.me_ref, s32[1]{0:T(128)} %bitcast.sub_ref, s32[2,16]{1,0:T(2,128)} %starts_ref.1, bf16[2,2048]{1,0:T(2,128)(2,1)} %chirp_hbm.1, f32[1,512]{1,0:T(1,128)} %rates_hbm.1, ...), custom_call_target="tpu_custom_call" | custom-call | flops 6000000000 | tf_op jit(solution)/shard_map/compress/pallas_call | solution.py:393
  5.2 5.3 %collective-permute-start = (bf16[4,64,128]{2,1,0:T(8,128)(2,1)}, bf16[4,64,128]{2,1,0:T(8,128)(2,1)S(1)}, u32[]{:S(2)}, u32[]{:S(2)}) collective-permute-start(bf16[4,64,128]{2,1,0:T(8,128)(2,1)} %get-tuple-element.23), channel_id=1, source_target_pairs={{0,8},{1,9},{2,10},{3,11},{4,12},{5,13},{6,14},{7,15},{8,0},{9,1},... | collective-permute-start | bytes 196616 | tf_op jit(solution)/shard_map/ppermute | solution.py:422
  10.5 0.0 collective-permute-start.1
  10.5 0.4 collective-permute-start.2
  10.9 0.0 copy-start.1
  10.9 1.0 %copy-done.1 = f32[768,128]{1,0:T(8,128)S(1)} copy-done((f32[768,128]{1,0:T(8,128)S(1)}, f32[768,128]{1,0:T(8,128)}, u32[]{:S(2)}) %copy-start.1) | copy-done | bytes 393240
  11.9 0.0 copy-start
  11.9 1.7 %phase.1 = (bf16[8,512,256]{2,1,0:T(8,128)(2,1)S(1)}, bf16[8,512,256]{2,1,0:T(8,128)(2,1)S(1)}, bf16[4,64,128]{2,1,0:T(8,128)(2,1)S(1)}) custom-call(f32[768,128]{1,0:T(8,128)S(1)} %copy-done.1), custom_call_target="tpu_custom_call" | custom-call | flops 4000000000 | tf_op jit(solution)/shard_map/phase/pallas_call | solution.py:426
  13.6 0.0 collective-permute-done.refs_1_.rest_1_
  13.6 1.1 %collective-permute-done.1.refs_2_.rest_2_ = bf16[4,64,128]{2,1,0:T(8,128)(2,1)S(1)} collective-permute-done((bf16[4,64,128]{2,1,0:T(8,128)(2,1)}, bf16[4,64,128]{2,1,0:T(8,128)(2,1)S(1)}, u32[]{:S(2)}, u32[]{:S(2)}) %collective-permute-start.1) | collective-permute-done | bytes 65568 | tf_op jit(solution)/shard_map/ppermute | solution.py:422
  14.7 0.0 collective-permute-done.2.refs_3_.rest_3_
  14.7 3.0 %collective-permute-start.4 = (bf16[4,64,128]{2,1,0:T(8,128)(2,1)S(1)}, bf16[4,64,128]{2,1,0:T(8,128)(2,1)S(1)}, u32[]{:S(2)}, u32[]{:S(2)}) collective-permute-start(bf16[4,64,128]{2,1,0:T(8,128)(2,1)S(1)} %get-tuple-element.29), channel_id=1, source_target_pairs={{0,3},{1,2},{2,1},{3,0},{4,7},{5,6},{6,5},{7,4},{8,11},{9,10},{10,... | collective-permute-start | bytes 196616 | tf_op jit(solution)/shard_map/ppermute | solution.py:422
  17.7 0.6 %collective-permute-start.5 = (bf16[4,64,128]{2,1,0:T(8,128)(2,1)S(1)}, bf16[4,64,128]{2,1,0:T(8,128)(2,1)S(1)}, u32[]{:S(2)}, u32[]{:S(2)}) collective-permute-start(bf16[4,64,128]{2,1,0:T(8,128)(2,1)S(1)} %get-tuple-element.30), channel_id=1, source_target_pairs={{0,2},{1,3},{2,0},{3,1},{4,6},{5,7},{6,4},{7,5},{8,10},{9,11},{10,... | collective-permute-start | bytes 196616 | tf_op jit(solution)/shard_map/ppermute | solution.py:422
  18.3 0.2 collective-permute-start.3
  18.5 0.0 copy-done
  18.5 2.3 %turn.1 = (bf16[2,64,128,128]{3,2,1,0:T(8,128)(2,1)S(1)}, bf16[2,64,128,128]{3,2,1,0:T(8,128)(2,1)S(1)}) custom-call(bf16[512,64,128]{2,1,0:T(8,128)(2,1)S(1)} %bitcast.15, bf16[4,64,128]{2,1,0:T(8,128)(2,1)S(1)} %get-tuple-element.26.after_ref), custom_call_target="tpu_custom_call" | custom-call | flops 4000000000 | tf_op jit(solution)/shard_map/turn/pallas_call | solution.py:437
  20.9 0.0 collective-permute-done.4.rest_5_
  20.9 0.0 collective-permute-done.5.rest_6_
  20.9 2.1 %collective-permute-done.3.rest_4_ = bf16[4,64,128]{2,1,0:T(8,128)(2,1)S(1)} collective-permute-done((bf16[4,64,128]{2,1,0:T(8,128)(2,1)S(1)}, bf16[4,64,128]{2,1,0:T(8,128)(2,1)S(1)}, u32[]{:S(2)}, u32[]{:S(2)}) %collective-permute-start.3) | collective-permute-done | bytes 65568 | tf_op jit(solution)/shard_map/ppermute | solution.py:422
  23.0 2.3 %far_image.1 = (f32[4,16,128]{2,1,0:T(8,128)S(1)}, bf16[2,256,512]{2,1,0:T(8,128)(2,1)S(1)}) custom-call(s32[1]{0:T(128)} %bitcast.1.me_ref, s32[1]{0:T(128)} %bitcast.sub_ref, bf16[8,512,256]{2,1,0:T(8,128)(2,1)S(1)} %get-tuple-element.20.after_ref.first_table_ref, bf16[8,512,256]{2,1,0:T(8,128)(2,1)S(1)} %get-tuple-element.21.second_table_ref, ...), custom_call_target="tpu_custom_call" | custom-call | flops 3000000000 | tf_op jit(solution)/shard_map/far_image/pallas_call | solution.py:444
  25.3 4.9 %collective-permute-start.6 = (f32[4,16,128]{2,1,0:T(8,128)S(1)}, f32[4,16,128]{2,1,0:T(8,128)S(1)}, u32[]{:S(2)}, u32[]{:S(2)}) collective-permute-start(f32[4,16,128]{2,1,0:T(8,128)S(1)} %get-tuple-element.32.after_ref), channel_id=1, source_target_pairs={{0,128},{16,144},{32,160},{48,176},{64,192},{80,208},{96,224},{112... | collective-permute-start | bytes 98312 | tf_op jit(solution)/shard_map/ppermute | solution.py:463
  30.2 2.5 %near_image.1 = f32[4,16,128]{2,1,0:T(8,128)S(1)} custom-call(s32[1]{0:T(128)} %bitcast.sub_ref, bf16[8,512,256]{2,1,0:T(8,128)(2,1)S(1)} %get-tuple-element.20.after_ref.first_table_ref, bf16[8,512,256]{2,1,0:T(8,128)(2,1)S(1)} %get-tuple-element.21.second_table_ref, bf16[2,64,128,128]{3,2,1,0:T(8,128)(2,1)S(1)} %get-tuple-element.27.first_weights_ref, ...), custom_call_target="tpu_custom_call" | custom-call | flops 3000000000 | tf_op jit(solution)/shard_map/near_image/pallas_call | solution.py:453
  32.7 0.0 collective-permute-done.6
  32.7 12.8 %all_to_all.5 = f32[8,8,128]{2,1,0:T(8,128)S(1)} all-to-all(f32[8,8,128]{2,1,0:T(8,128)S(1)} %bitcast.16), channel_id=1, replica_groups={{0,16,32,48,64,80,96,112},{128,144,160,176,192,208,224,240},{1,17,33,49..., dimensions={0} | all-to-all | bytes 65536 | tf_op jit(solution)/shard_map/all_to_all | solution.py:466
  45.5 0.6 %reduce_sum.9 = f32[8,128]{1,0:T(8,128)} reduce(f32[8,8,128]{2,1,0:T(8,128)S(1)} %all_to_all.5, f32[]{:T(128)} %constant.8.clone.1), dimensions={0}, to_apply=%region_0.0 | reduce | flops 7168 | bytes 36868 | tf_op jit(solution)/shard_map/reduce_sum | solution.py:467
  (2 shorter events, 0.0 us)
Async XLA Ops:
  5.2 8.4 %collective-permute-start = (bf16[4,64,128]{2,1,0:T(8,128)(2,1)}, bf16[4,64,128]{2,1,0:T(8,128)(2,1)S(1)}, u32[]{:S(2)}, u32[]{:S(2)}) collective-permute-start(bf16[4,64,128]{2,1,0:T(8,128)(2,1)} %get-tuple-element.23), channel_id=1, source_target_pairs={{0,8},{1,9},{2,10},{3,11},{4,12},{5,13},{6,14},{7,15},{8,0},{9,1},... | collective-permute-start | bytes 196616 | tf_op jit(solution)/shard_map/ppermute | solution.py:422
  10.5 4.2 %collective-permute-start.1 = (bf16[4,64,128]{2,1,0:T(8,128)(2,1)}, bf16[4,64,128]{2,1,0:T(8,128)(2,1)S(1)}, u32[]{:S(2)}, u32[]{:S(2)}) collective-permute-start(bf16[4,64,128]{2,1,0:T(8,128)(2,1)} %get-tuple-element.24), channel_id=1, source_target_pairs={{0,4},{1,5},{2,6},{3,7},{4,0},{5,1},{6,2},{7,3},{8,12},{9,13},{10,... | collective-permute-start | bytes 196616 | tf_op jit(solution)/shard_map/ppermute | solution.py:422
  10.5 4.2 %collective-permute-start.2 = (bf16[4,64,128]{2,1,0:T(8,128)(2,1)}, bf16[4,64,128]{2,1,0:T(8,128)(2,1)S(1)}, u32[]{:S(2)}, u32[]{:S(2)}) collective-permute-start(bf16[4,64,128]{2,1,0:T(8,128)(2,1)} %get-tuple-element.25), channel_id=1, source_target_pairs={{0,12},{1,13},{2,14},{3,15},{4,8},{5,9},{6,10},{7,11},{8,4},{9,5},... | collective-permute-start | bytes 196616 | tf_op jit(solution)/shard_map/ppermute | solution.py:422
  10.9 1.0 %copy-start.1 = (f32[768,128]{1,0:T(8,128)S(1)}, f32[768,128]{1,0:T(8,128)}, u32[]{:S(2)}) copy-start(f32[768,128]{1,0:T(8,128)} %get-tuple-element.19.extra_ref) | copy-start | bytes 1179652
  11.9 6.7 %copy-start = (bf16[2,2,128,4,2048]{4,3,2,1,0:T(4,128)(2,1)S(1)}, bf16[2,2,128,4,2048]{4,3,2,1,0:T(4,128)(2,1)}, u32[]{:S(2)}) copy-start(bf16[2,2,128,4,2048]{4,3,2,1,0:T(4,128)(2,1)} %param.11) | copy-start | bytes 25165828
  14.7 6.1 %collective-permute-start.4 = (bf16[4,64,128]{2,1,0:T(8,128)(2,1)S(1)}, bf16[4,64,128]{2,1,0:T(8,128)(2,1)S(1)}, u32[]{:S(2)}, u32[]{:S(2)}) collective-permute-start(bf16[4,64,128]{2,1,0:T(8,128)(2,1)S(1)} %get-tuple-element.29), channel_id=1, source_target_pairs={{0,3},{1,2},{2,1},{3,0},{4,7},{5,6},{6,5},{7,4},{8,11},{9,10},{10,... | collective-permute-start | bytes 196616 | tf_op jit(solution)/shard_map/ppermute | solution.py:422
  17.7 3.2 %collective-permute-start.5 = (bf16[4,64,128]{2,1,0:T(8,128)(2,1)S(1)}, bf16[4,64,128]{2,1,0:T(8,128)(2,1)S(1)}, u32[]{:S(2)}, u32[]{:S(2)}) collective-permute-start(bf16[4,64,128]{2,1,0:T(8,128)(2,1)S(1)} %get-tuple-element.30), channel_id=1, source_target_pairs={{0,2},{1,3},{2,0},{3,1},{4,6},{5,7},{6,4},{7,5},{8,10},{9,11},{10,... | collective-permute-start | bytes 196616 | tf_op jit(solution)/shard_map/ppermute | solution.py:422
  18.3 4.6 %collective-permute-start.3 = (bf16[4,64,128]{2,1,0:T(8,128)(2,1)S(1)}, bf16[4,64,128]{2,1,0:T(8,128)(2,1)S(1)}, u32[]{:S(2)}, u32[]{:S(2)}) collective-permute-start(bf16[4,64,128]{2,1,0:T(8,128)(2,1)S(1)} %get-tuple-element.26.after_ref), channel_id=1, source_target_pairs={{0,1},{1,0},{2,3},{3,2},{4,5},{5,4},{6,7},{7,6},{8,9},{9,8},{10,11... | collective-permute-start | bytes 196616 | tf_op jit(solution)/shard_map/ppermute | solution.py:422
  25.3 7.4 %collective-permute-start.6 = (f32[4,16,128]{2,1,0:T(8,128)S(1)}, f32[4,16,128]{2,1,0:T(8,128)S(1)}, u32[]{:S(2)}, u32[]{:S(2)}) collective-permute-start(f32[4,16,128]{2,1,0:T(8,128)S(1)} %get-tuple-element.32.after_ref), channel_id=1, source_target_pairs={{0,128},{16,144},{32,160},{48,176},{64,192},{80,208},{96,224},{112... | collective-permute-start | bytes 98312 | tf_op jit(solution)/shard_map/ppermute | solution.py:463

commit v17 on v16

--- a/solution.py
+++ b/solution.py
@@ -342,6 +342,23 @@
     )
 
 
+ACROSS = (0, 2, 1, 3)
+
+
+def split_kernel(sub_ref, mine_ref, came_ref, *out_refs):
+    for distance, out_ref in zip(ACROSS, out_refs):
+        at = (sub_ref[0] >> 1 & 3) ^ distance
+        out_ref[...] = mine_ref[at] + came_ref[at]
+
+
+def join_kernel(sub_ref, *refs):
+    *piece_refs, keep_ref, send_ref = refs
+    total = (piece_refs[0][...] + piece_refs[1][...]) + (piece_refs[2][...] + piece_refs[3][...])
+    own_first = (sub_ref[0] & 1) == 0
+    keep_ref[...] = jnp.where(own_first, total[:8], total[8:])
+    send_ref[...] = jnp.where(own_first, total[8:], total[:8])
+
+
 def params(mib):
     return pltpu.CompilerParams(vmem_limit_bytes=mib * 1024 * 1024)
 
@@ -457,14 +474,21 @@
 
 
 def shards(*args):
-    _, far_image, near_image = partial_image(*args)
+    sub, far_image, near_image = partial_image(*args)
     size = 16
-    half = size // 2
-    came = lax.ppermute(far_image, "sub", [(one, one ^ half) for one in range(size)])
-    groups = [list(range(half)), list(range(half, size))]
-    held = (near_image + came).reshape(half, -1, LANES)
-    pieces = lax.all_to_all(held, "sub", 0, 0, axis_index_groups=groups, tiled=True)
-    return jnp.sum(pieces, 0).reshape(2, -1, LANES)
+
+    def swap(value, distance):
+        return lax.ppermute(value, "sub", [(one, one ^ distance) for one in range(size)])
+
+    smem = pl.BlockSpec(memory_space=pltpu.SMEM)
+    _, lines, _ = near_image.shape
+    pair = jax.ShapeDtypeStruct((lines, LANES), jnp.float32)
+    one = jax.ShapeDtypeStruct((lines // 2, LANES), jnp.float32)
+    came = swap(far_image, size // 2)
+    pieces = call(split_kernel, "split", 12, [pair] * 4, [smem, vmem(), vmem()])(sub, near_image, came)
+    pieces = [pieces[0]] + [swap(pieces[slot], 2 * ACROSS[slot]) for slot in range(1, 4)]
+    keep, send = call(join_kernel, "join", 12, [one, one], [smem] + [vmem()] * 4)(sub, *pieces)
+    return (keep + swap(send, 1)).reshape(2, -1, LANES)
 
 
 def solution(mesh):

time: 46.3 us -> 46.8 us (1.011)
  blocking collectives: 12.8 us -> 0 us
  starting transfers between devices: 14.4 us -> 23.7 us
  waiting for transfers between devices: 3.2 us -> 7.17 us
    all_to_all x1 -> x0, blocking collectives: 12.8 us -> none  [shards(): lax.all_to_all(held, 'sub', 0, 0, axis_index_groups=groups, tiled=True)]
    ppermute x1 -> x5, starting transfers between devices: 4.93 us -> 14.2 us  [swap(): lax.ppermute(value, 'sub', [(one, one ^ distance) for one in range(size)])]
    ppermute x1 -> x5, waiting for transfers between devices: 0.01 us -> 3.99 us  [swap(): lax.ppermute(value, 'sub', [(one, one ^ distance) for one in range(size)])]
    reduce_sum x1 -> x0, other arithmetic: 0.6 us -> none  [shards(): return jnp.sum(pieces, 0).reshape(2, -1, LANES)]
    add x1, other arithmetic: 0.01 us -> 0.59 us  [shards(): return (keep + swap(send, 1)).reshape(2, -1, LANES)]
  transfers between devices with their start and end apart: 7 -> 11, of which waited for: 2 -> 6; matrix products, arithmetic and copies ran while one was open for 0% -> 0% of each run, Pallas kernels for 14% -> 14%
where the time goes in v17:
time: 46.8 us; the launch traced here: 46.6 us
  starting transfers between devices  23.7 us (51%)
  Pallas kernels  14.1 us (30%)
  waiting for transfers between devices  7.17 us (15%)
  local copies, waits for them, and re-layouts  1 us (2%)
  other arithmetic  0.59 us (1%)
    ppermute x5, starting transfers between devices, swap(): lax.ppermute(value, 'sub', [(one, one ^ distance) for one in range(size)])  14.2 us
    ppermute x6, starting transfers between devices, swap(): return lax.ppermute(value, ('sub', 'tile'), pairs)  9.42 us
    pallas_call x1, Pallas kernels, partial_image(): call(compress_kernel, 'compress', 60, [own] * (far - 1) + [extras], [smem...  5.22 us
    ppermute x5, waiting for transfers between devices, swap(): lax.ppermute(value, 'sub', [(one, one ^ distance) for one in range(size)])  3.99 us
    ppermute x6, waiting for transfers between devices, swap(): return lax.ppermute(value, ('sub', 'tile'), pairs)  3.19 us
    pallas_call x1, Pallas kernels, partial_image(): call(near_image_kernel, 'near_image', 12, shape(half, jnp.float32), [smem...  2.47 us
    pallas_call x1, Pallas kernels, partial_image(): call(turn_kernel, 'turn', 12, [turned, turned], [vmem(), anywhere], flops...  2.35 us
    pallas_call x1, Pallas kernels, partial_image(): call(far_image_kernel, 'far_image', 12, [shape(half, jnp.float32), shape(...  2.32 us
  transfers between devices with their start and end apart: 11, of which 6 were waited for; matrix products, arithmetic and copies ran while one was open for 0% of the time, Pallas kernels for 14%

profile of v17, /device:TPU:1, one launch (start us, length us, event | category | flops | bytes accessed | tf_op | source)
XLA Modules:
  0.0 46.6 jit_solution(6409115572798464227)
XLA Ops:
  0.0 5.2 %compress.1 = (bf16[4,64,128]{2,1,0:T(8,128)(2,1)}, bf16[4,64,128]{2,1,0:T(8,128)(2,1)}, bf16[4,64,128]{2,1,0:T(8,128)(2,1)}, f32[768,128]{1,0:T(8,128)}) custom-call(s32[1]{0:T(128)} %bitcast.1.me_ref, s32[1]{0:T(128)} %bitcast.sub_ref, s32[2,16]{1,0:T(2,128)} %starts_ref.1, bf16[2,2048]{1,0:T(2,128)(2,1)} %chirp_hbm.1, f32[1,512]{1,0:T(1,128)} %rates_hbm.1, ...), custom_call_target="tpu_custom_call" | custom-call | flops 6000000000 | tf_op jit(solution)/shard_map/compress/pallas_call | solution.py:410
  5.2 5.3 %collective-permute-start = (bf16[4,64,128]{2,1,0:T(8,128)(2,1)}, bf16[4,64,128]{2,1,0:T(8,128)(2,1)S(1)}, u32[]{:S(2)}, u32[]{:S(2)}) collective-permute-start(bf16[4,64,128]{2,1,0:T(8,128)(2,1)} %get-tuple-element.29), channel_id=1, source_target_pairs={{0,8},{1,9},{2,10},{3,11},{4,12},{5,13},{6,14},{7,15},{8,0},{9,1},... | collective-permute-start | bytes 196616 | tf_op jit(solution)/shard_map/ppermute | solution.py:439
  10.5 0.0 collective-permute-start.1
  10.5 0.4 collective-permute-start.2
  10.9 0.0 copy-start.1
  10.9 1.0 %copy-done.1 = f32[768,128]{1,0:T(8,128)S(1)} copy-done((f32[768,128]{1,0:T(8,128)S(1)}, f32[768,128]{1,0:T(8,128)}, u32[]{:S(2)}) %copy-start.1) | copy-done | bytes 393240
  11.9 0.0 copy-start
  11.9 1.7 %phase.1 = (bf16[8,512,256]{2,1,0:T(8,128)(2,1)S(1)}, bf16[8,512,256]{2,1,0:T(8,128)(2,1)S(1)}, bf16[4,64,128]{2,1,0:T(8,128)(2,1)S(1)}) custom-call(f32[768,128]{1,0:T(8,128)S(1)} %copy-done.1), custom_call_target="tpu_custom_call" | custom-call | flops 4000000000 | tf_op jit(solution)/shard_map/phase/pallas_call | solution.py:443
  13.6 0.0 collective-permute-done.refs_1_.rest_1_
  13.6 1.1 %collective-permute-done.1.refs_2_.rest_2_ = bf16[4,64,128]{2,1,0:T(8,128)(2,1)S(1)} collective-permute-done((bf16[4,64,128]{2,1,0:T(8,128)(2,1)}, bf16[4,64,128]{2,1,0:T(8,128)(2,1)S(1)}, u32[]{:S(2)}, u32[]{:S(2)}) %collective-permute-start.1) | collective-permute-done | bytes 65568 | tf_op jit(solution)/shard_map/ppermute | solution.py:439
  14.7 0.0 collective-permute-done.2.refs_3_.rest_3_
  14.7 3.0 %collective-permute-start.4 = (bf16[4,64,128]{2,1,0:T(8,128)(2,1)S(1)}, bf16[4,64,128]{2,1,0:T(8,128)(2,1)S(1)}, u32[]{:S(2)}, u32[]{:S(2)}) collective-permute-start(bf16[4,64,128]{2,1,0:T(8,128)(2,1)S(1)} %get-tuple-element.35), channel_id=1, source_target_pairs={{0,3},{1,2},{2,1},{3,0},{4,7},{5,6},{6,5},{7,4},{8,11},{9,10},{10,... | collective-permute-start | bytes 196616 | tf_op jit(solution)/shard_map/ppermute | solution.py:439
  17.7 0.6 %collective-permute-start.5 = (bf16[4,64,128]{2,1,0:T(8,128)(2,1)S(1)}, bf16[4,64,128]{2,1,0:T(8,128)(2,1)S(1)}, u32[]{:S(2)}, u32[]{:S(2)}) collective-permute-start(bf16[4,64,128]{2,1,0:T(8,128)(2,1)S(1)} %get-tuple-element.36), channel_id=1, source_target_pairs={{0,2},{1,3},{2,0},{3,1},{4,6},{5,7},{6,4},{7,5},{8,10},{9,11},{10,... | collective-permute-start | bytes 196616 | tf_op jit(solution)/shard_map/ppermute | solution.py:439
  18.4 0.2 collective-permute-start.3
  18.5 0.0 copy-done
  18.5 2.3 %turn.1 = (bf16[2,64,128,128]{3,2,1,0:T(8,128)(2,1)S(1)}, bf16[2,64,128,128]{3,2,1,0:T(8,128)(2,1)S(1)}) custom-call(bf16[512,64,128]{2,1,0:T(8,128)(2,1)S(1)} %bitcast.14, bf16[4,64,128]{2,1,0:T(8,128)(2,1)S(1)} %get-tuple-element.32.after_ref), custom_call_target="tpu_custom_call" | custom-call | flops 4000000000 | tf_op jit(solution)/shard_map/turn/pallas_call | solution.py:454
  20.9 0.0 collective-permute-done.4.rest_5_
  20.9 0.0 collective-permute-done.5.rest_6_
  20.9 2.1 %collective-permute-done.3.rest_4_ = bf16[4,64,128]{2,1,0:T(8,128)(2,1)S(1)} collective-permute-done((bf16[4,64,128]{2,1,0:T(8,128)(2,1)S(1)}, bf16[4,64,128]{2,1,0:T(8,128)(2,1)S(1)}, u32[]{:S(2)}, u32[]{:S(2)}) %collective-permute-start.3) | collective-permute-done | bytes 65568 | tf_op jit(solution)/shard_map/ppermute | solution.py:439
  23.0 2.3 %far_image.1 = (f32[4,16,128]{2,1,0:T(8,128)S(1)}, bf16[2,256,512]{2,1,0:T(8,128)(2,1)S(1)}) custom-call(s32[1]{0:T(128)} %bitcast.1.me_ref, s32[1]{0:T(128)} %bitcast.sub_ref, bf16[8,512,256]{2,1,0:T(8,128)(2,1)S(1)} %get-tuple-element.26.after_ref.first_table_ref, bf16[8,512,256]{2,1,0:T(8,128)(2,1)S(1)} %get-tuple-element.27.second_table_ref, ...), custom_call_target="tpu_custom_call" | custom-call | flops 3000000000 | tf_op jit(solution)/shard_map/far_image/pallas_call | solution.py:461
  25.3 4.9 %collective-permute-start.6 = (f32[4,16,128]{2,1,0:T(8,128)S(1)}, f32[4,16,128]{2,1,0:T(8,128)S(1)}, u32[]{:S(2)}, u32[]{:S(2)}) collective-permute-start(f32[4,16,128]{2,1,0:T(8,128)S(1)} %get-tuple-element.38.after_ref), channel_id=1, source_target_pairs={{0,128},{16,144},{32,160},{48,176},{64,192},{80,208},{96,224},{112... | collective-permute-start | bytes 98312 | tf_op jit(solution)/shard_map/ppermute | solution.py:481
  30.2 2.5 %near_image.1.mine_ref = f32[4,16,128]{2,1,0:T(8,128)S(1)} custom-call(s32[1]{0:T(128)} %bitcast.sub_ref, bf16[8,512,256]{2,1,0:T(8,128)(2,1)S(1)} %get-tuple-element.26.after_ref.first_table_ref, bf16[8,512,256]{2,1,0:T(8,128)(2,1)S(1)} %get-tuple-element.27.second_table_ref, bf16[2,64,128,128]{3,2,1,0:T(8,128)(2,1)S(1)} %get-tuple-element.33.first_weights_ref, ...), custom_call_target="tpu_custom_call" | custom-call | flops 3000000000 | tf_op jit(solution)/shard_map/near_image/pallas_call | solution.py:470
  32.7 0.0 collective-permute-done.6.came_ref
  32.7 2.8 %collective-permute-start.7 = (f32[16,128]{1,0:T(8,128)S(1)}, f32[16,128]{1,0:T(8,128)S(1)}, u32[]{:S(2)}, u32[]{:S(2)}) collective-permute-start(f32[16,128]{1,0:T(8,128)S(1)} %get-tuple-element.40), channel_id=1, source_target_pairs={{0,64},{16,80},{32,96},{48,112},{64,0},{80,16},{96,32},{112,48},{1... | collective-permute-start | bytes 24584 | tf_op jit(solution)/shard_map/ppermute | solution.py:481
  35.6 0.3 collective-permute-start.8
  35.9 0.6 %collective-permute-start.9 = (f32[16,128]{1,0:T(8,128)S(1)}, f32[16,128]{1,0:T(8,128)S(1)}, u32[]{:S(2)}, u32[]{:S(2)}) collective-permute-start(f32[16,128]{1,0:T(8,128)S(1)} %get-tuple-element.42), channel_id=1, source_target_pairs={{0,96},{16,112},{32,64},{48,80},{64,32},{80,48},{96,0},{112,16},{1... | collective-permute-start | bytes 24584 | tf_op jit(solution)/shard_map/ppermute | solution.py:481
  36.4 0.4 collective-permute-done.7.refs_1_
  36.8 1.2 %collective-permute-done.8.refs_2_ = f32[16,128]{1,0:T(8,128)S(1)} collective-permute-done((f32[16,128]{1,0:T(8,128)S(1)}, f32[16,128]{1,0:T(8,128)S(1)}, u32[]{:S(2)}, u32[]{:S(2)}) %collective-permute-start.8) | collective-permute-done | bytes 8224 | tf_op jit(solution)/shard_map/ppermute | solution.py:481
  38.1 1.5 %collective-permute-done.9.refs_3_ = f32[16,128]{1,0:T(8,128)S(1)} collective-permute-done((f32[16,128]{1,0:T(8,128)S(1)}, f32[16,128]{1,0:T(8,128)S(1)}, u32[]{:S(2)}, u32[]{:S(2)}) %collective-permute-start.9) | collective-permute-done | bytes 8224 | tf_op jit(solution)/shard_map/ppermute | solution.py:481
  39.6 5.6 %collective-permute-start.10 = (f32[8,128]{1,0:T(8,128)S(1)}, f32[8,128]{1,0:T(8,128)S(1)}, u32[]{:S(2)}, u32[]{:S(2)}) collective-permute-start(f32[8,128]{1,0:T(8,128)S(1)} %get-tuple-element.44), channel_id=1, source_target_pairs={{0,16},{16,0},{32,48},{48,32},{64,80},{80,64},{96,112},{112,96},{1... | collective-permute-start | bytes 12296 | tf_op jit(solution)/shard_map/ppermute | solution.py:481
  45.2 0.8 %collective-permute-done.10 = f32[8,128]{1,0:T(8,128)S(1)} collective-permute-done((f32[8,128]{1,0:T(8,128)S(1)}, f32[8,128]{1,0:T(8,128)S(1)}, u32[]{:S(2)}, u32[]{:S(2)}) %collective-permute-start.10) | collective-permute-done | bytes 4128 | tf_op jit(solution)/shard_map/ppermute | solution.py:481
  46.0 0.6 %add.3 = f32[8,128]{1,0:T(8,128)} add(f32[8,128]{1,0:T(8,128)S(1)} %get-tuple-element.43, f32[8,128]{1,0:T(8,128)S(1)} %collective-permute-done.10) | non-fusion elementwise | flops 1024 | bytes 12288 | tf_op jit(solution)/shard_map/add | solution.py:491
  (3 shorter events, 0.0 us)
Async XLA Ops:
  5.2 8.4 %collective-permute-start = (bf16[4,64,128]{2,1,0:T(8,128)(2,1)}, bf16[4,64,128]{2,1,0:T(8,128)(2,1)S(1)}, u32[]{:S(2)}, u32[]{:S(2)}) collective-permute-start(bf16[4,64,128]{2,1,0:T(8,128)(2,1)} %get-tuple-element.29), channel_id=1, source_target_pairs={{0,8},{1,9},{2,10},{3,11},{4,12},{5,13},{6,14},{7,15},{8,0},{9,1},... | collective-permute-start | bytes 196616 | tf_op jit(solution)/shard_map/ppermute | solution.py:439
  10.5 4.2 %collective-permute-start.1 = (bf16[4,64,128]{2,1,0:T(8,128)(2,1)}, bf16[4,64,128]{2,1,0:T(8,128)(2,1)S(1)}, u32[]{:S(2)}, u32[]{:S(2)}) collective-permute-start(bf16[4,64,128]{2,1,0:T(8,128)(2,1)} %get-tuple-element.30), channel_id=1, source_target_pairs={{0,4},{1,5},{2,6},{3,7},{4,0},{5,1},{6,2},{7,3},{8,12},{9,13},{10,... | collective-permute-start | bytes 196616 | tf_op jit(solution)/shard_map/ppermute | solution.py:439
  10.5 4.2 %collective-permute-start.2 = (bf16[4,64,128]{2,1,0:T(8,128)(2,1)}, bf16[4,64,128]{2,1,0:T(8,128)(2,1)S(1)}, u32[]{:S(2)}, u32[]{:S(2)}) collective-permute-start(bf16[4,64,128]{2,1,0:T(8,128)(2,1)} %get-tuple-element.31), channel_id=1, source_target_pairs={{0,12},{1,13},{2,14},{3,15},{4,8},{5,9},{6,10},{7,11},{8,4},{9,5},... | collective-permute-start | bytes 196616 | tf_op jit(solution)/shard_map/ppermute | solution.py:439
  10.9 1.0 %copy-start.1 = (f32[768,128]{1,0:T(8,128)S(1)}, f32[768,128]{1,0:T(8,128)}, u32[]{:S(2)}) copy-start(f32[768,128]{1,0:T(8,128)} %get-tuple-element.25.extra_ref) | copy-start | bytes 1179652
  11.9 6.6 %copy-start = (bf16[2,2,128,4,2048]{4,3,2,1,0:T(4,128)(2,1)S(1)}, bf16[2,2,128,4,2048]{4,3,2,1,0:T(4,128)(2,1)}, u32[]{:S(2)}) copy-start(bf16[2,2,128,4,2048]{4,3,2,1,0:T(4,128)(2,1)} %param.11) | copy-start | bytes 25165828
  14.7 6.1 %collective-permute-start.4 = (bf16[4,64,128]{2,1,0:T(8,128)(2,1)S(1)}, bf16[4,64,128]{2,1,0:T(8,128)(2,1)S(1)}, u32[]{:S(2)}, u32[]{:S(2)}) collective-permute-start(bf16[4,64,128]{2,1,0:T(8,128)(2,1)S(1)} %get-tuple-element.35), channel_id=1, source_target_pairs={{0,3},{1,2},{2,1},{3,0},{4,7},{5,6},{6,5},{7,4},{8,11},{9,10},{10,... | collective-permute-start | bytes 196616 | tf_op jit(solution)/shard_map/ppermute | solution.py:439
  17.7 3.2 %collective-permute-start.5 = (bf16[4,64,128]{2,1,0:T(8,128)(2,1)S(1)}, bf16[4,64,128]{2,1,0:T(8,128)(2,1)S(1)}, u32[]{:S(2)}, u32[]{:S(2)}) collective-permute-start(bf16[4,64,128]{2,1,0:T(8,128)(2,1)S(1)} %get-tuple-element.36), channel_id=1, source_target_pairs={{0,2},{1,3},{2,0},{3,1},{4,6},{5,7},{6,4},{7,5},{8,10},{9,11},{10,... | collective-permute-start | bytes 196616 | tf_op jit(solution)/shard_map/ppermute | solution.py:439
  18.4 4.6 %collective-permute-start.3 = (bf16[4,64,128]{2,1,0:T(8,128)(2,1)S(1)}, bf16[4,64,128]{2,1,0:T(8,128)(2,1)S(1)}, u32[]{:S(2)}, u32[]{:S(2)}) collective-permute-start(bf16[4,64,128]{2,1,0:T(8,128)(2,1)S(1)} %get-tuple-element.32.after_ref), channel_id=1, source_target_pairs={{0,1},{1,0},{2,3},{3,2},{4,5},{5,4},{6,7},{7,6},{8,9},{9,8},{10,11... | collective-permute-start | bytes 196616 | tf_op jit(solution)/shard_map/ppermute | solution.py:439
  25.3 7.4 %collective-permute-start.6 = (f32[4,16,128]{2,1,0:T(8,128)S(1)}, f32[4,16,128]{2,1,0:T(8,128)S(1)}, u32[]{:S(2)}, u32[]{:S(2)}) collective-permute-start(f32[4,16,128]{2,1,0:T(8,128)S(1)} %get-tuple-element.38.after_ref), channel_id=1, source_target_pairs={{0,128},{16,144},{32,160},{48,176},{64,192},{80,208},{96,224},{112... | collective-permute-start | bytes 98312 | tf_op jit(solution)/shard_map/ppermute | solution.py:481
  32.7 4.1 %collective-permute-start.7 = (f32[16,128]{1,0:T(8,128)S(1)}, f32[16,128]{1,0:T(8,128)S(1)}, u32[]{:S(2)}, u32[]{:S(2)}) collective-permute-start(f32[16,128]{1,0:T(8,128)S(1)} %get-tuple-element.40), channel_id=1, source_target_pairs={{0,64},{16,80},{32,96},{48,112},{64,0},{80,16},{96,32},{112,48},{1... | collective-permute-start | bytes 24584 | tf_op jit(solution)/shard_map/ppermute | solution.py:481
  35.6 2.5 %collective-permute-start.8 = (f32[16,128]{1,0:T(8,128)S(1)}, f32[16,128]{1,0:T(8,128)S(1)}, u32[]{:S(2)}, u32[]{:S(2)}) collective-permute-start(f32[16,128]{1,0:T(8,128)S(1)} %get-tuple-element.41), channel_id=1, source_target_pairs={{0,32},{16,48},{32,0},{48,16},{64,96},{80,112},{96,64},{112,80},{1... | collective-permute-start | bytes 24584 | tf_op jit(solution)/shard_map/ppermute | solution.py:481
  35.9 3.7 %collective-permute-start.9 = (f32[16,128]{1,0:T(8,128)S(1)}, f32[16,128]{1,0:T(8,128)S(1)}, u32[]{:S(2)}, u32[]{:S(2)}) collective-permute-start(f32[16,128]{1,0:T(8,128)S(1)} %get-tuple-element.42), channel_id=1, source_target_pairs={{0,96},{16,112},{32,64},{48,80},{64,32},{80,48},{96,0},{112,16},{1... | collective-permute-start | bytes 24584 | tf_op jit(solution)/shard_map/ppermute | solution.py:481
  39.6 6.4 %collective-permute-start.10 = (f32[8,128]{1,0:T(8,128)S(1)}, f32[8,128]{1,0:T(8,128)S(1)}, u32[]{:S(2)}, u32[]{:S(2)}) collective-permute-start(f32[8,128]{1,0:T(8,128)S(1)} %get-tuple-element.44), channel_id=1, source_target_pairs={{0,16},{16,0},{32,48},{48,32},{64,80},{80,64},{96,112},{112,96},{1... | collective-permute-start | bytes 12296 | tf_op jit(solution)/shard_map/ppermute | solution.py:481
